TPU v7x, 128 devices: a whole 4x4x4 slice. The times are simulated.
128 devices in a mesh: seq: 8 (over x, core), head: 16 (over z, y).
Axes of the slice: x: 4, y: 4, z: 4, core: 2. Of those that a mesh axis runs over, the one named last changes fastest.
Arguments:
- tokens: bfloat16 [1024, 6144], P('seq'), may hold values from -6 to 6
- log_decay: float32 [1024, 32], P('seq', 'head'), may hold values from -1 to 0
- carried_state: float32 [32, 128, 128], P('head'), may hold values from -48 to 48
- q_weight: bfloat16 [6144, 4096], P(None, 'head'), may hold values from -0.078125 to 0.078125
- k_weight: bfloat16 [6144, 4096], P(None, 'head'), may hold values from -0.078125 to 0.078125
- v_weight: bfloat16 [6144, 4096], P(None, 'head'), may hold values from -0.078125 to 0.078125
- out_weight: bfloat16 [4096, 6144], P('head'), may hold values from -0.09375 to 0.09375
- final_gain: bfloat16 [6144], replicated, may hold values from 0.099609375 to 1.8984375
- vocab_weight: bfloat16 [6144, 131072], P(None, ('seq', 'head')), may hold values from -5 to 5
- targets: int32 [1024], replicated, may hold values from 0 to 131071
Outputs:
- loglik: float32 [1024], P('seq')
All inputs are finite; a program needn't handle non-finite values.
Results may differ from a plain program's by a relative error of at most 0.002.
Values may be sent and summed in bfloat16 or wider, within the bound.
No kernel may reach another device: no remote copies, remote signals or barrier semaphores. Data moves between devices by JAX's collectives and lax.ppermute only.
A program may use at most 128 MiB of HBM per device.

v0:
```python
import jax
import jax.numpy as jnp
from jax import lax
from jax.sharding import PartitionSpec as P


def prefix(array, axis, combine, identity):
    length, here = (lax.axis_size(axis), lax.axis_index(axis))
    everything = jax.tree.map(lambda part: lax.all_gather(part, axis), array)
    start = jax.tree.map(
        lambda part, zero: jnp.broadcast_to(jnp.asarray(zero, part.dtype), part.shape),
        array,
        identity,
    )

    def turn(k, before):
        reached = k < here
        new = combine(before, jax.tree.map(lambda part: part[k], everything))
        return jax.tree.map(lambda a, b: jnp.where(reached, a, b), new, before)

    return lax.fori_loop(0, length, turn, start)


def combine_states(earlier, later):
    return (earlier[0] * later[0], later[0][:, None, None] * earlier[1] + later[1])


def shards(
    tokens,
    log_decay,
    carried_state,
    q_weight,
    k_weight,
    v_weight,
    out_weight,
    final_gain,
    vocab_weight,
    targets,
):
    highest = lax.Precision.HIGHEST
    rows_here = tokens.shape[0]
    heads_here = carried_state.shape[0]
    head_size = carried_state.shape[1]
    view = (rows_here, heads_here, head_size)
    queries = (
        jnp.dot(tokens, q_weight, preferred_element_type=jnp.float32)
        .astype(jnp.bfloat16)
        .reshape(view)
    )
    keys_loc = (
        jnp.dot(tokens, k_weight, preferred_element_type=jnp.float32)
        .astype(jnp.bfloat16)
        .reshape(view)
    )
    values = (
        jnp.dot(tokens, v_weight, preferred_element_type=jnp.float32)
        .astype(jnp.bfloat16)
        .reshape(view)
    )
    cumul = jnp.cumsum(log_decay, axis=0)
    last_cum = cumul[-1]
    ends = jnp.exp(last_cum[None, :] - cumul)
    local_state = jnp.einsum(
        "thd,the->hde",
        keys_loc.astype(jnp.float32) * ends[:, :, None],
        values.astype(jnp.float32),
        precision=highest,
    )
    total_decay = jnp.exp(last_cum)
    prefix_decay, prefix_state = prefix(
        (total_decay, local_state),
        "seq",
        combine_states,
        (jnp.ones_like(total_decay), jnp.zeros_like(local_state)),
    )
    lower = jnp.arange(rows_here)[:, None] >= jnp.arange(rows_here)[None, :]
    scores = jnp.einsum("thd,shd->hts", queries, keys_loc, preferred_element_type=jnp.float32)
    diff = jnp.transpose(cumul[:, None, :] - cumul[None, :, :], (2, 0, 1))
    weight = (scores * jnp.exp(jnp.where(lower[None], diff, -1e30))).astype(jnp.bfloat16)
    intra = jnp.einsum("hts,shd->thd", weight, values, preferred_element_type=jnp.float32)
    state_in = prefix_decay[:, None, None] * carried_state + prefix_state
    inter = jnp.exp(cumul)[:, :, None] * jnp.einsum(
        "thd,hde->the", queries.astype(jnp.float32), state_in, precision=highest
    )
    attended = intra + inter
    normed_heads = attended * lax.rsqrt(
        jnp.mean(attended * attended, axis=-1, keepdims=True) + 1e-06
    )
    flat_heads = normed_heads.astype(jnp.bfloat16).reshape(rows_here, heads_here * head_size)
    rows_mine = rows_here // lax.axis_size("head")
    head_index = lax.axis_index("head")
    mixed_all = lax.psum(
        jnp.dot(flat_heads, out_weight, preferred_element_type=jnp.float32), "head"
    )
    mixed = lax.dynamic_slice_in_dim(mixed_all, head_index * rows_mine, rows_mine, 0)
    resid = (
        lax.dynamic_slice_in_dim(tokens, head_index * rows_mine, rows_mine, 0).astype(jnp.float32)
        + mixed
    )
    final_rows = (
        resid
        * lax.rsqrt(jnp.mean(resid * resid, axis=-1, keepdims=True) + 1e-06)
        * final_gain.astype(jnp.float32)
    )
    final_rows = final_rows.astype(jnp.bfloat16)
    vocab_local = vocab_weight.shape[1]
    offset = (lax.axis_index("seq") * lax.axis_size("head") + head_index) * vocab_local
    columns = jnp.arange(vocab_local, dtype=jnp.int32)
    logits = jnp.dot(
        lax.all_gather(final_rows, ("seq", "head"), axis=0, tiled=True),
        vocab_weight,
        preferred_element_type=jnp.float32,
    )
    top = jnp.max(logits, axis=1)
    total = jnp.sum(jnp.exp(logits - top[:, None]), axis=1)
    wanted = targets - offset
    hit = jnp.sum(jnp.where(columns[None, :] == wanted[:, None], logits, 0.0), axis=1)
    top_all = lax.pmax(top, ("seq", "head"))
    total_all, hit_all = lax.psum((total * jnp.exp(top - top_all), hit), ("seq", "head"))
    loglik = hit_all - top_all - jnp.log(total_all)
    return lax.dynamic_slice_in_dim(loglik, lax.axis_index("seq") * rows_here, rows_here, 0)


def solution(mesh):
    return jax.shard_map(
        shards,
        mesh=mesh,
        in_specs=(
            P("seq", None),
            P("seq", "head"),
            P("head", None, None),
            P(None, "head"),
            P(None, "head"),
            P(None, "head"),
            P("head", None),
            P(),
            P(None, ("seq", "head")),
            P(),
        ),
        out_specs=P("seq"),
        check_vma=False,
    )
```

profile of v0, /device:TPU:0, one launch (start us, length us, event | category | flops | bytes accessed | tf_op | source)
XLA Modules:
  0.0 384.7 jit_solution(14718534888018662489)
XLA Ops:
  6.5 0.9 copy.23
  7.5 0.2 reduce_window_sum.11
  7.7 3.0 convolution_convert_fusion
  10.7 0.1 copy.36
  10.8 2.9 fusion.4
  13.8 0.9 fusion.8
  14.7 10.6 %all-gather.1 = f32[8,1,2]{2,1,0:T(1,128)S(1)} all-gather(f32[1,1,2]{2,1,0:T(1,128)S(1)} %get-tuple-element.171), channel_id=1, replica_groups=mesh['seq'=8,'head'=16] {'seq'}, dimensions={0}, use_global_device_ids=true | all-gather | bytes 72 | tf_op jit(solution)/shard_map/all_gather | solution.py:9
  25.4 0.1 copy.24
  25.5 3.1 fusion.5
  28.6 12.0 %all-gather.7.cloned.1.call-done = f32[16,128,128]{2,1,0:T(8,128)} async-done(((f32[2,128,128]{2,1,0:T(8,128)}), f32[16,128,128]{2,1,0:T(8,128)}) %all-gather.7.cloned.1.call-update) | async-done | bytes 1048592 | tf_op jit(solution)/shard_map/all_gather | solution.py:9
  40.6 8.3 %while.16 = (s32[]{:T(128)}, f32[2]{0:T(128)S(1)}, f32[2,128,128]{2,1,0:T(8,128)S(1)}, s32[]{:T(128)}, f32[8,2]{1,0:T(8,128)S(1)}, /*index=5*/f32[8,2,128,128]{3,2,1,0:T(8,128)}, s32[]{:T(128)}, s32[]{:T(128)}) while((s32[]{:T(128)}, f32[2]{0:T(128)S(1)}, f32[2,128,128]{2,1,0:T(8,128)S(1)}, s32[]{:T(128)}, f32[8,2]{1,0:T(8,128)S(1)}, ...), condition=%wide.region_2.3_spmd.clone, body=%wide.region_1.2_spmd.clone.sunk | while | flops 131082 | bytes 393371 | solution.py:21
  40.6 1.0 fusion.48
  41.7 1.0 fusion.48
  42.7 1.0 fusion.48
  43.7 1.0 fusion.48
  44.8 1.0 fusion.48
  45.8 1.0 fusion.48
  46.9 1.0 fusion.48
  47.9 1.0 fusion.48
  48.9 1.9 fusion.1
  50.8 1.2 multiply_reduce_fusion.1
  52.1 2.3 fusion.35
  54.5 0.6 copy-done.1
  55.1 95.3 %all-reduce.3.cloned.1.call-done = f32[128,6144]{1,0:T(8,128)} async-done(((f32[128,6144]{1,0:T(8,128)}), f32[128,6144]{1,0:T(8,128)}) %all-reduce.3.cloned.1.call-update) | async-done | bytes 3145744 | tf_op jit(solution)/shard_map/psum | solution.py:92
  150.4 1.2 multiply_reduce_fusion
  151.6 1.7 multiply_convert_fusion
  153.3 72.3 %all-gather.5.cloned.1.call-done = bf16[1024,6144]{1,0:T(8,128)(2,1)} async-done(((bf16[8,6144]{1,0:T(8,128)(2,1)}), bf16[1024,6144]{1,0:T(8,128)(2,1)}) %all-gather.5.cloned.1.call-update) | async-done | bytes 12582928 | tf_op jit(solution)/shard_map/all_gather | solution.py:110
  225.7 19.4 %fusion.34 = (f32[1024]{0:T(1024)S(1)}, f32[1024,1024]{0,1:T(8,128)}) fusion(bf16[1024,6144]{1,0:T(8,128)(2,1)} %all-gather.5.cloned.1.call-done, bf16[6144,1024]{1,0:T(8,128)(2,1)} %param.20), kind=kOutput, calls=%fused_computation.57 | convolution fusion | flops 12885949440 | bytes 29364224 | tf_op jit(solution)/shard_map/dot_general | solution.py:109
  245.1 64.8 %pmax.7 = f32[1024]{0:T(1024)S(1)} all-reduce(f32[1024]{0:T(1024)S(1)} %get-tuple-element.174), channel_id=1, replica_groups=mesh['seq'=8,'head'=16] {'seq','head'}, use_global_device_ids=true, to_apply=%region_9.10 | all-reduce | flops 1024 | bytes 8192 | tf_op jit(solution)/shard_map/pmax | solution.py:118
  309.9 3.3 select_reduce_fusion
  313.2 64.4 %all-reduce = (f32[1024]{0:T(1024)S(1)}, f32[1024]{0:T(1024)S(1)}) all-reduce(f32[1024]{0:T(1024)S(1)} %exponential_multiply_fusion, f32[1024]{0:T(1024)S(1)} %get-tuple-element.150), channel_id=1, replica_groups=mesh['seq'=8,'head'=16] {'seq','head'}, use_global_device_ids=true, to_apply=%region_11.12 | all-reduce | flops 2048 | bytes 16384 | tf_op jit(solution)/shard_map/psum | solution.py:119
  377.6 0.6 dynamic_slice.25
  (33 shorter events, 0.5 us)
Async XLA Ops:
  6.5 45.5 %copy-start = (bf16[256,6144]{1,0:T(8,128)(2,1)S(1)}, bf16[256,6144]{1,0:T(8,128)(2,1)}, u32[]{:S(2)}) copy-start(bf16[256,6144]{1,0:T(8,128)(2,1)} %param.18) | copy-start | bytes 9437188
  6.5 34.1 %all-gather.7.cloned.1.call-start = ((), (), s32[]{:S(2)}) async-start(), calls=%async_computation.2 | async-start | bytes 1179648 | tf_op jit(solution)/shard_map/all_gather | solution.py:9
  14.7 135.7 %all-reduce.3.cloned.1.call-start = ((), (), s32[]{:S(2)}) async-start(), calls=%async_computation | async-start | bytes 6291456 | tf_op jit(solution)/shard_map/psum | solution.py:92
  54.4 0.7 copy-start.1
  54.4 98.9 %copy-start.2 = (s32[1024]{0:T(1024)S(1)}, s32[1024]{0:T(1024)}, u32[]{:S(2)}) copy-start(s32[1024]{0:T(1024)} %param.21) | copy-start | bytes 12292
  54.4 171.3 %all-gather.5.cloned.1.call-start = ((), (), s32[]{:S(2)}) async-start(), calls=%async_computation.1 | async-start | bytes 12681216 | tf_op jit(solution)/shard_map/all_gather | solution.py:110
Sparse Core Ops, SparseCore 0:
  14.8 25.7 all-gather.6
  54.5 95.8 all-reduce.2
  153.5 72.1 all-gather.4
where the time goes:
time: 386 us; the launch traced here: 385 us
  waiting for transfers between devices  180 us (47%)
  blocking collectives  140 us (36%)
  matrix products  34.7 us (9%)
  other arithmetic  14.5 us (4%)
  between operations  13.2 us (3%)
    psum x1, waiting for transfers between devices, shards(): lax.psum(jnp.dot(flat_heads, out_weight, preferred_element_type=jnp.float...  95.3 us
    all_gather x1, waiting for transfers between devices, shards(): lax.all_gather(final_rows, ('seq', 'head'), axis=0, tiled=True)  72.3 us
    pmax x1, blocking collectives, shards(): top_all = lax.pmax(top, ('seq', 'head'))  64.8 us
    psum x1, blocking collectives, shards(): lax.psum((total * jnp.exp(top - top_all), hit), ('seq', 'head'))  64.4 us
    dot_general x1, matrix products, shards(): jnp.dot(lax.all_gather(final_rows, ('seq', 'head'), axis=0, tiled=True),...  19.4 us
    all_gather x1, waiting for transfers between devices, prefix(): everything = jax.tree.map(lambda part: lax.all_gather(part, axis), array)  12 us
    all_gather x1, blocking collectives, prefix(): everything = jax.tree.map(lambda part: lax.all_gather(part, axis), array)  10.6 us
    select_n x16, other arithmetic, turn(): return jax.tree.map(lambda a, b: jnp.where(reached, a, b), new, before)  8.09 us
  transfers between devices with their start and end apart: 3, of which 3 were waited for; matrix products, arithmetic and copies ran while one was open for 1% of the time, Pallas kernels for 0%

commit v1 on v0

v1 whole, which is shorter than its diff:
```python
import jax
import jax.numpy as jnp
from jax import lax
from jax.sharding import Mesh, PartitionSpec as P

X, CORE, Z, Y = 4, 2, 4, 4
ALL = ("x", "core", "z", "y")
F32 = jnp.float32
BF16 = jnp.bfloat16


def move(array, target):
    pairs = []
    for i in range(X * CORE * Z * Y):
        at = (i // (CORE * Z * Y), i // (Z * Y) % CORE, i // Y % Z, i % Y)
        to = target(*at)
        if to is not None:
            pairs.append((i, ((to[0] * CORE + to[1]) * Z + to[2]) * Y + to[3]))
    return lax.ppermute(array, ALL, pairs)


def other_core(x, c, z, y):
    return (x, 1 - c, z, y)


def along_x(s):
    return lambda x, c, z, y: ((x + s) % X, c, z, y)


def along_y(s):
    return lambda x, c, z, y: (x, c, z, (y + s) % Y)


def along_z(s):
    return lambda x, c, z, y: (x, c, (z + s) % Z, y)


def along_first(s):
    return lambda x, c, z, y: (x, c, z, (y + s) % Y) if c == 0 else (x, c, (z + s) % Z, y)


def along_second(s):
    return lambda x, c, z, y: (x, c, (z + s) % Z, y) if c == 0 else (x, c, z, (y + s) % Y)


def later_x(s):
    return lambda x, c, z, y: (x + s, c, z, y) if x + s < X else None


def spread(block, here, target):
    rows = block.shape[0]
    parts = [block] + [move(block, target(s)) for s in (1, 3, 2)]
    whole = jnp.zeros((4 * rows,) + block.shape[1:], block.dtype)
    for s, part in zip((0, 1, 3, 2), parts):
        whole = lax.dynamic_update_slice_in_dim(whole, part, lax.rem(here + 4 - s, 4) * rows, 0)
    return whole


def merge(parts):
    top = parts[0][0]
    for p in parts[1:]:
        top = jnp.maximum(top, p[0])
    total = sum(p[1] * jnp.exp(p[0] - top) for p in parts)
    hit = sum(p[2] for p in parts)
    return jnp.stack([top, total, hit])


def shards(
    tokens,
    log_decay,
    carried_state,
    q_weight,
    k_weight,
    v_weight,
    out_weight,
    final_gain,
    vocab_weight,
    targets,
):
    highest = lax.Precision.HIGHEST
    x, c, z, y = (lax.axis_index(a) for a in ALL)
    rows_here = tokens.shape[0]
    heads_here = carried_state.shape[0]
    head_size = carried_state.shape[1]
    view = (rows_here, heads_here, head_size)

    keys = jnp.dot(tokens, k_weight, preferred_element_type=F32).astype(BF16).reshape(view)
    values = jnp.dot(tokens, v_weight, preferred_element_type=F32).astype(BF16).reshape(view)
    lower = jnp.arange(rows_here)[:, None] >= jnp.arange(rows_here)[None, :]
    cumul = jnp.dot(lower.astype(F32), log_decay, precision=highest)
    last_cum = cumul[-1]
    ends = jnp.exp(last_cum[None, :] - cumul)
    state = jnp.einsum(
        "thd,the->hde",
        keys.astype(F32) * ends[:, :, None],
        values.astype(F32),
        precision=highest,
    )
    decay = jnp.broadcast_to(jnp.exp(last_cum)[:, None, None], (heads_here, 8, head_size))
    mine = jnp.concatenate([state, decay], axis=1)
    theirs = move(mine, other_core)
    first = jnp.where(c == 0, mine, theirs)
    second = jnp.where(c == 0, theirs, mine)
    first_s, first_d = first[:, :head_size], first[:, head_size : head_size + 1]
    second_s, second_d = second[:, :head_size], second[:, head_size : head_size + 1]
    chip = jnp.concatenate(
        [second_d * first_s + second_s, second[:, head_size:] * first[:, head_size:]], axis=1
    )
    arrived = [(s, move(chip, later_x(s))) for s in (3, 2, 1)]

    queries = jnp.dot(tokens, q_weight, preferred_element_type=F32).astype(BF16).reshape(view)
    scores = jnp.einsum("thd,shd->hts", queries, keys, preferred_element_type=F32)
    diff = jnp.transpose(cumul[:, None, :] - cumul[None, :, :], (2, 0, 1))
    weight = (scores * jnp.exp(jnp.where(lower[None], diff, -1e30))).astype(BF16)
    intra = jnp.einsum("hts,shd->thd", weight, values, preferred_element_type=F32)

    state_in = carried_state
    for s, message in arrived:
        d = jnp.where(x >= s, message[:, head_size : head_size + 1], 1.0)
        state_in = d * state_in + message[:, :head_size]
    state_in = jnp.where(c == 1, first_d * state_in + first_s, state_in)
    inter = jnp.exp(cumul)[:, :, None] * jnp.einsum(
        "thd,hde->the", queries.astype(F32), state_in, precision=highest
    )
    attended = intra + inter
    normed_heads = attended * lax.rsqrt(
        jnp.mean(attended * attended, axis=-1, keepdims=True) + 1e-06
    )
    flat_heads = normed_heads.astype(BF16).reshape(rows_here, heads_here * head_size)

    n_head = Z * Y
    rows_mine = rows_here // n_head
    share = jnp.dot(flat_heads, out_weight, preferred_element_type=F32).astype(BF16)
    shares = lax.all_to_all(share.reshape(n_head, rows_mine, -1), ("z", "y"), 0, 0)
    mixed = jnp.sum(shares.astype(F32), axis=0)
    own_tokens = lax.dynamic_slice_in_dim(tokens, (z * Y + y) * rows_mine, rows_mine, 0)
    resid = own_tokens.astype(F32) + mixed
    final_rows = (
        resid
        * lax.rsqrt(jnp.mean(resid * resid, axis=-1, keepdims=True) + 1e-06)
        * final_gain.astype(F32)
    ).astype(BF16)

    vocab_local = vocab_weight.shape[1]
    offset = (((x * CORE + c) * Z + z) * Y + y) * vocab_local
    columns = jnp.arange(vocab_local, dtype=jnp.int32)
    wanted = (targets - offset).reshape(X, CORE, Z, Y, rows_mine)
    wanted_by = (
        jnp.transpose(wanted[:, 0], (1, 2, 0, 3)).reshape(Z, -1),
        jnp.transpose(wanted[:, 1], (2, 1, 0, 3)).reshape(Y, -1),
    )

    def score(rows, want):
        logits = jnp.dot(rows, vocab_weight, preferred_element_type=F32)
        top = jnp.max(logits, axis=1)
        total = jnp.sum(jnp.exp(logits - top[:, None]), axis=1)
        hit = jnp.sum(jnp.where(columns[None, :] == want[:, None], logits, 0.0), axis=1)
        return jnp.stack([top, total, hit])

    on_x = spread(final_rows, x, along_x)
    plane = jnp.where(c == 0, y, z)
    ours = spread(on_x, plane.astype(jnp.int32), along_first)
    blocks = [(0, ours)] + [(s, move(ours, along_second(s))) for s in (1, 3, 2)]
    stats = jnp.zeros((3, CORE, 4, 128), F32)
    for s, block in blocks:
        swapped = move(block, other_core)
        for rows, core, place in ((block, c, jnp.where(c == 0, z, y)), (swapped, 1 - c, jnp.where(c == 0, y, z))):
            place = lax.rem(place + 4 - s, 4)
            want = jnp.where(
                core == 0,
                lax.dynamic_index_in_dim(wanted_by[0], place, 0, False),
                lax.dynamic_index_in_dim(wanted_by[1], place, 0, False),
            )
            found = score(rows, want)
            stats = lax.dynamic_update_slice(stats, found[:, None, None], (0, core, place, 0))

    stats = stats.reshape(3, CORE * 4 * 128)
    stats = merge([stats, move(stats, other_core)])
    for along in (along_x, along_z, along_y):
        stats = merge([stats] + [move(stats, along(s)) for s in (1, 3, 2)])
    loglik = stats[2] - stats[0] - jnp.log(stats[1])
    loglik = loglik.reshape(CORE, 4, 4, X, rows_mine)
    loglik = lax.dynamic_index_in_dim(loglik, x, 3, False)
    loglik = jnp.where(c == 0, loglik[0], jnp.transpose(loglik[1], (1, 0, 2)))
    return loglik.reshape(rows_here)


def solution(mesh):
    fine = Mesh(mesh.devices.reshape(X, CORE, Z, Y), ALL)
    seq, head = (("x", "core"), ("z", "y"))
    return jax.shard_map(
        shards,
        mesh=fine,
        in_specs=(
            P(seq, None),
            P(seq, head),
            P(head, None, None),
            P(None, head),
            P(None, head),
            P(None, head),
            P(head, None),
            P(),
            P(None, ALL),
            P(),
        ),
        out_specs=P(seq),
        check_vma=False,
    )
```

time: 386 us -> 244 us (0.63)
  blocking collectives: 140 us -> 0 us
  waiting for transfers between devices: 180 us -> 58.3 us
  starting transfers between devices: 0.09 us -> 67.4 us
  local copies, waits for them, and re-layouts: 2.47 us -> 41.8 us
  matrix products: 34.7 us -> 54 us
  between operations: 13.2 us -> 0.85 us
  other arithmetic: 14.5 us -> 19.4 us
    psum x1 -> x0, waiting for transfers between devices: 95.3 us -> none  [shards(): lax.psum(jnp.dot(flat_heads, out_weight, preferred_element_type=jnp.float...]
    all_gather x2 -> x0, waiting for transfers between devices: 84.3 us -> none  [the longest x1 72.3 us: shards(): lax.all_gather(final_rows, ('seq', 'head'), axis=0, tiled=True)]
    pmax x1 -> x0, blocking collectives: 64.8 us -> none  [shards(): top_all = lax.pmax(top, ('seq', 'head'))]
    psum x1 -> x0, blocking collectives: 64.4 us -> none  [shards(): lax.psum((total * jnp.exp(top - top_all), hit), ('seq', 'head'))]
    ppermute x0 -> x27, starting transfers between devices: none -> 59.1 us  [move(): return lax.ppermute(array, ALL, pairs)]
    ppermute x0 -> x27, waiting for transfers between devices: none -> 35.5 us  [move(): return lax.ppermute(array, ALL, pairs)]
    squeeze x0 -> x33, local copies, waits for them, and re-layouts: none -> 28.5 us  [the longest x11 10.4 us: merge(): total = sum((p[1] * jnp.exp(p[0] - top) for p in parts))]
    all_to_all x0 -> x1, waiting for transfers between devices: none -> 22.8 us  [shards(): lax.all_to_all(share.reshape(n_head, rows_mine, -1), ('z', 'y'), 0, 0)]
  transfers between devices with their start and end apart: 3 -> 28, of which waited for: 3 -> 11; matrix products, arithmetic and copies ran while one was open for 1% -> 33% of each run, Pallas kernels for 0% -> 0%
where the time goes in v1:
time: 244 us; the launch traced here: 242 us
  starting transfers between devices  67.4 us (28%)
  waiting for transfers between devices  58.3 us (24%)
  matrix products  54 us (22%)
  local copies, waits for them, and re-layouts  41.8 us (17%)
  other arithmetic  19.4 us (8%)
    ppermute x27, starting transfers between devices, move(): return lax.ppermute(array, ALL, pairs)  59.1 us
    dot_general x8, matrix products, score(): logits = jnp.dot(rows, vocab_weight, preferred_element_type=F32)  42 us
    ppermute x27, waiting for transfers between devices, move(): return lax.ppermute(array, ALL, pairs)  35.5 us
    all_to_all x1, waiting for transfers between devices, shards(): lax.all_to_all(share.reshape(n_head, rows_mine, -1), ('z', 'y'), 0, 0)  22.8 us
    squeeze x11, local copies, waits for them, and re-layouts, merge(): total = sum((p[1] * jnp.exp(p[0] - top) for p in parts))  10.4 us
    squeeze x11, local copies, waits for them, and re-layouts, merge(): hit = sum((p[2] for p in parts))  9.65 us
    squeeze x10, local copies, waits for them, and re-layouts, merge(): top = jnp.maximum(top, p[0])  8.38 us
    all_to_all x1, starting transfers between devices, shards(): lax.all_to_all(share.reshape(n_head, rows_mine, -1), ('z', 'y'), 0, 0)  8.22 us
  transfers between devices with their start and end apart: 28, of which 11 were waited for; matrix products, arithmetic and copies ran while one was open for 33% of the time, Pallas kernels for 0%

profile of v1, /device:TPU:0, one launch (start us, length us, event | category | flops | bytes accessed | tf_op | source)
XLA Modules:
  0.0 241.7 jit_solution(15174909806863065966)
XLA Ops:
  1.8 2.9 %convolution_convert_fusion.1 = bf16[128,256]{1,0:T(8,128)(2,1)S(1)} fusion(bf16[128,6144]{1,0:T(8,128)(2,1)} %param.10, bf16[6144,256]{1,0:T(8,128)(2,1)} %param.14), kind=kOutput, calls=%fused_computation.8 | convolution fusion | flops 402685952 | bytes 4784128 | tf_op jit(solution)/shard_map/dot_general | solution.py:87
  4.9 3.1 %fusion.4 = bf16[16,2,8,128]{3,2,1,0:T(8,128)(2,1)S(1)} fusion(bf16[128,6144]{1,0:T(8,128)(2,1)} %param.10, bf16[6144,256]{1,0:T(8,128)(2,1)} %param.15), kind=kOutput, calls=%fused_computation.12 | convolution fusion | flops 402685952 | bytes 4784128 | tf_op jit(solution)/shard_map/dot_general | solution.py:88
  11.5 4.1 %collective-permute-start.1 = (f32[2,136,128]{2,1,0:T(8,128)}, f32[2,136,128]{2,1,0:T(8,128)}, u32[]{:S(2)}, u32[]{:S(2)}) collective-permute-start(f32[2,136,128]{2,1,0:T(8,128)} %pad_maximum_fusion.1), channel_id=1, source_target_pairs={{0,32},{1,33},{2,34},{3,35},{4,36},{5,37},{6,38},{7,39},{8,40},{9,... | collective-permute-start | bytes 417800 | tf_op jit(solution)/shard_map/ppermute | solution.py:19
  16.8 4.0 %collective-permute-start.2 = (f32[2,136,128]{2,1,0:T(8,128)}, f32[2,136,128]{2,1,0:T(8,128)S(1)}, u32[]{:S(2)}, u32[]{:S(2)}) collective-permute-start(f32[2,136,128]{2,1,0:T(8,128)} %pad_maximum_fusion.1), channel_id=1, source_target_pairs={{0,64},{1,65},{2,66},{3,67},{4,68},{5,69},{6,70},{7,71},{8,72},{9,... | collective-permute-start | bytes 417800 | tf_op jit(solution)/shard_map/ppermute | solution.py:19
  27.0 1.8 fusion
  28.7 8.2 %all-to-all-start = ((bf16[16,8,6144]{2,1,0:T(8,128)(2,1)}), bf16[16,8,6144]{2,1,0:T(8,128)(2,1)}, u32[]{:S(2)}, u32[]{:S(2)}) async-start(bf16[16,8,6144]{2,1,0:T(8,128)(2,1)} %fusion), calls=%async_computation | async-start | bytes 3145728 | tf_op jit(solution)/shard_map/all_to_all | solution.py:134
  37.6 22.8 %all-to-all-done = bf16[16,8,6144]{2,1,0:T(8,128)(2,1)} async-done(((bf16[16,8,6144]{2,1,0:T(8,128)(2,1)}), bf16[16,8,6144]{2,1,0:T(8,128)(2,1)}, u32[]{:S(2)}, u32[]{:S(2)}) %all-to-all-start) | async-done | bytes 1572896 | tf_op jit(solution)/shard_map/all_to_all | solution.py:134
  64.8 3.6 %collective-permute-start.5 = (bf16[8,6144]{1,0:T(8,128)(2,1)}, bf16[8,6144]{1,0:T(8,128)(2,1)S(1)}, u32[]{:S(2)}, u32[]{:S(2)}) collective-permute-start(bf16[8,6144]{1,0:T(8,128)(2,1)} %get-tuple-element.62), channel_id=1, source_target_pairs={{0,96},{1,97},{2,98},{3,99},{4,100},{5,101},{6,102},{7,103},{8,104... | collective-permute-start | bytes 294920 | tf_op jit(solution)/shard_map/ppermute | solution.py:19
  72.2 2.5 %collective-permute-done.6 = bf16[8,6144]{1,0:T(8,128)(2,1)S(1)} collective-permute-done((bf16[8,6144]{1,0:T(8,128)(2,1)}, bf16[8,6144]{1,0:T(8,128)(2,1)S(1)}, u32[]{:S(2)}, u32[]{:S(2)}) %collective-permute-start.6) | collective-permute-done | bytes 98336 | tf_op jit(solution)/shard_map/ppermute | solution.py:19
  74.8 3.2 %collective-permute-start.8 = (bf16[32,6144]{1,0:T(8,128)(2,1)S(1)}, bf16[32,6144]{1,0:T(8,128)(2,1)S(1)}, u32[]{:S(2)}, u32[]{:S(2)}) collective-permute-start(bf16[32,6144]{1,0:T(8,128)(2,1)S(1)} %constant_dynamic-update-slice_fusion.4), channel_id=1, source_target_pairs={{0,3},{1,0},{2,1},{3,2},{4,7},{5,4},{6,5},{7,6},{8,11},{9,8},{10,9... | collective-permute-start | bytes 1179656 | tf_op jit(solution)/shard_map/ppermute | solution.py:19
  80.1 7.9 %collective-permute-done.7 = bf16[32,6144]{1,0:T(8,128)(2,1)S(1)} collective-permute-done((bf16[32,6144]{1,0:T(8,128)(2,1)S(1)}, bf16[32,6144]{1,0:T(8,128)(2,1)S(1)}, u32[]{:S(2)}, u32[]{:S(2)}) %collective-permute-start.7) | collective-permute-done | bytes 393248 | tf_op jit(solution)/shard_map/ppermute | solution.py:19
  90.3 17.6 %collective-permute-start.15 = (bf16[128,6144]{1,0:T(8,128)(2,1)}, bf16[128,6144]{1,0:T(8,128)(2,1)}, u32[]{:S(2)}, u32[]{:S(2)}) collective-permute-start(bf16[128,6144]{1,0:T(8,128)(2,1)} %constant_dynamic-update-slice_fusion), channel_id=1, source_target_pairs={{0,8},{1,9},{2,10},{3,11},{4,12},{5,13},{6,14},{7,15},{8,0},{9,1},... | collective-permute-start | bytes 4718600 | tf_op jit(solution)/shard_map/ppermute | solution.py:19
  108.4 2.1 collective-permute-start.11
  110.5 7.1 %fusion.58 = (f32[128]{0:T(128)S(1)}, f32[128,1024]{1,0:T(8,128)S(1)}) fusion(bf16[128,6144]{1,0:T(8,128)(2,1)} %constant_dynamic-update-slice_fusion, bf16[6144,1024]{1,0:T(8,128)(2,1)} %param.18), kind=kOutput, calls=%fused_computation.213 | convolution fusion | flops 1610743680 | bytes 14680576 | tf_op jit(solution)/shard_map/dot_general | solution.py:154
  117.6 9.2 %collective-permute-done.15 = bf16[128,6144]{1,0:T(8,128)(2,1)} collective-permute-done((bf16[128,6144]{1,0:T(8,128)(2,1)}, bf16[128,6144]{1,0:T(8,128)(2,1)}, u32[]{:S(2)}, u32[]{:S(2)}) %collective-permute-start.15) | collective-permute-done | bytes 1572896 | tf_op jit(solution)/shard_map/ppermute | solution.py:19
  126.7 1.9 collective-permute-done.13
  128.7 7.7 %fusion.64 = (f32[128]{0:T(128)S(1)}, f32[128,1024]{1,0:T(8,128)}) fusion(bf16[128,6144]{1,0:T(8,128)(2,1)} %collective-permute-done.15, bf16[6144,1024]{1,0:T(8,128)(2,1)} %param.18), kind=kOutput, calls=%fused_computation.219 | convolution fusion | flops 1610743680 | bytes 14680576 | tf_op jit(solution)/shard_map/dot_general | solution.py:154
  136.3 7.2 %collective-permute-done.11 = bf16[128,6144]{1,0:T(8,128)(2,1)} collective-permute-done((bf16[128,6144]{1,0:T(8,128)(2,1)}, bf16[128,6144]{1,0:T(8,128)(2,1)}, u32[]{:S(2)}, u32[]{:S(2)}) %collective-permute-start.11) | collective-permute-done | bytes 1572896 | tf_op jit(solution)/shard_map/ppermute | solution.py:19
  143.5 4.0 %fusion.62 = (f32[128]{0:T(128)S(1)}, f32[128,1024]{1,0:T(8,128)}) fusion(bf16[128,6144]{1,0:T(8,128)(2,1)} %collective-permute-done.13, bf16[6144,1024]{1,0:T(8,128)(2,1)S(1)} %bitcast.170), kind=kOutput, calls=%fused_computation.217 | convolution fusion | flops 1610743680 | bytes 14680576 | tf_op jit(solution)/shard_map/dot_general | solution.py:154
  147.5 4.0 %fusion.60 = (f32[128]{0:T(128)S(1)}, f32[128,1024]{1,0:T(8,128)}) fusion(bf16[128,6144]{1,0:T(8,128)(2,1)} %collective-permute-done.11, bf16[6144,1024]{1,0:T(8,128)(2,1)S(1)} %bitcast.170), kind=kOutput, calls=%fused_computation.215 | convolution fusion | flops 1610743680 | bytes 14680576 | tf_op jit(solution)/shard_map/dot_general | solution.py:154
  151.5 1.9 fusion.59
  154.2 7.0 %fusion.65 = (f32[128]{0:T(128)S(1)}, f32[128,1024]{1,0:T(8,128)S(1)}) fusion(bf16[128,6144]{1,0:T(8,128)(2,1)} %collective-permute-done.16, bf16[6144,1024]{1,0:T(8,128)(2,1)} %param.18), kind=kOutput, calls=%fused_computation.220 | convolution fusion | flops 1610743680 | bytes 14680576 | tf_op jit(solution)/shard_map/dot_general | solution.py:154
  161.7 7.1 %fusion.63 = (f32[128]{0:T(128)S(1)}, f32[128,1024]{1,0:T(8,128)S(1)}) fusion(bf16[128,6144]{1,0:T(8,128)(2,1)} %collective-permute-done.14, bf16[6144,1024]{1,0:T(8,128)(2,1)} %param.18), kind=kOutput, calls=%fused_computation.218 | convolution fusion | flops 1610743680 | bytes 14680576 | tf_op jit(solution)/shard_map/dot_general | solution.py:154
  170.5 3.3 %fusion.61 = (f32[128]{0:T(128)S(1)}, f32[128,1024]{1,0:T(8,128)S(1)}) fusion(bf16[128,6144]{1,0:T(8,128)(2,1)} %collective-permute-done.12, bf16[6144,1024]{1,0:T(8,128)(2,1)S(1)} %bitcast.172), kind=kOutput, calls=%fused_computation.216 | convolution fusion | flops 1610743680 | bytes 14680576 | tf_op jit(solution)/shard_map/dot_general | solution.py:154
  176.0 6.9 %collective-permute-start.18 = (f32[3,1024]{1,0:T(4,128)S(1)}, f32[3,1024]{1,0:T(4,128)S(1)}, u32[]{:S(2)}, u32[]{:S(2)}) collective-permute-start(f32[3,1024]{1,0:T(4,128)S(1)} %pad_maximum_fusion.2), channel_id=1, source_target_pairs={{0,32},{1,33},{2,34},{3,35},{4,36},{5,37},{6,38},{7,39},{8,40},{9,... | collective-permute-start | bytes 36872 | tf_op jit(solution)/shard_map/ppermute | solution.py:19
  182.9 2.0 collective-permute-start.19
  188.3 1.9 collective-permute-done.20
  191.4 3.5 %collective-permute-start.21 = (f32[3,1024]{1,0:T(4,128)}, f32[3,1024]{1,0:T(4,128)}, u32[]{:S(2)}, u32[]{:S(2)}) collective-permute-start(f32[3,1024]{1,0:T(4,128)} %pad_maximum_fusion.3), channel_id=1, source_target_pairs={{0,4},{1,5},{2,6},{3,7},{4,8},{5,9},{6,10},{7,11},{8,12},{9,13},{1... | collective-permute-start | bytes 36872 | tf_op jit(solution)/shard_map/ppermute | solution.py:19
  194.9 2.7 %collective-permute-start.23 = (f32[3,1024]{1,0:T(4,128)}, f32[3,1024]{1,0:T(4,128)S(1)}, u32[]{:S(2)}, u32[]{:S(2)}) collective-permute-start(f32[3,1024]{1,0:T(4,128)} %pad_maximum_fusion.3), channel_id=1, source_target_pairs={{0,8},{1,9},{2,10},{3,11},{4,12},{5,13},{6,14},{7,15},{8,0},{9,1},... | collective-permute-start | bytes 36872 | tf_op jit(solution)/shard_map/ppermute | solution.py:19
  211.3 3.7 %collective-permute-start.25 = (f32[3,1024]{1,0:T(4,128)}, f32[3,1024]{1,0:T(4,128)}, u32[]{:S(2)}, u32[]{:S(2)}) collective-permute-start(f32[3,1024]{1,0:T(4,128)} %pad_maximum_fusion.4), channel_id=1, source_target_pairs={{0,3},{1,0},{2,1},{3,2},{4,7},{5,4},{6,5},{7,6},{8,11},{9,8},{10,9... | collective-permute-start | bytes 36872 | tf_op jit(solution)/shard_map/ppermute | solution.py:19
  227.8 1.9 multiply_add_fusion
  229.7 1.7 add_add_fusion
  (207 shorter events, 72.7 us)
Async XLA Ops:
  0.0 27.0 %copy-start = (bf16[256,6144]{1,0:T(8,128)(2,1)S(1)}, bf16[256,6144]{1,0:T(8,128)(2,1)}, u32[]{:S(2)}) copy-start(bf16[256,6144]{1,0:T(8,128)(2,1)} %param.16) | copy-start | bytes 9437188
  8.3 1.6 collective-permute-start
  11.5 10.6 %collective-permute-start.1 = (f32[2,136,128]{2,1,0:T(8,128)}, f32[2,136,128]{2,1,0:T(8,128)}, u32[]{:S(2)}, u32[]{:S(2)}) collective-permute-start(f32[2,136,128]{2,1,0:T(8,128)} %pad_maximum_fusion.1), channel_id=1, source_target_pairs={{0,32},{1,33},{2,34},{3,35},{4,36},{5,37},{6,38},{7,39},{8,40},{9,... | collective-permute-start | bytes 417800 | tf_op jit(solution)/shard_map/ppermute | solution.py:19
  16.8 7.3 %collective-permute-start.2 = (f32[2,136,128]{2,1,0:T(8,128)}, f32[2,136,128]{2,1,0:T(8,128)S(1)}, u32[]{:S(2)}, u32[]{:S(2)}) collective-permute-start(f32[2,136,128]{2,1,0:T(8,128)} %pad_maximum_fusion.1), channel_id=1, source_target_pairs={{0,64},{1,65},{2,66},{3,67},{4,68},{5,69},{6,70},{7,71},{8,72},{9,... | collective-permute-start | bytes 417800 | tf_op jit(solution)/shard_map/ppermute | solution.py:19
  20.8 4.8 %collective-permute-start.3 = (f32[2,136,128]{2,1,0:T(8,128)}, f32[2,136,128]{2,1,0:T(8,128)S(1)}, u32[]{:S(2)}, u32[]{:S(2)}) collective-permute-start(f32[2,136,128]{2,1,0:T(8,128)} %pad_maximum_fusion.1), channel_id=1, source_target_pairs={{0,96},{1,97},{2,98},{3,99},{4,100},{5,101},{6,102},{7,103},{8,104... | collective-permute-start | bytes 417800 | tf_op jit(solution)/shard_map/ppermute | solution.py:19
  28.7 31.7 %all-to-all-start = ((bf16[16,8,6144]{2,1,0:T(8,128)(2,1)}), bf16[16,8,6144]{2,1,0:T(8,128)(2,1)}, u32[]{:S(2)}, u32[]{:S(2)}) async-start(bf16[16,8,6144]{2,1,0:T(8,128)(2,1)} %fusion), calls=%async_computation | async-start | bytes 3145728 | tf_op jit(solution)/shard_map/all_to_all | solution.py:134
  64.8 6.5 %collective-permute-start.4 = (bf16[8,6144]{1,0:T(8,128)(2,1)}, bf16[8,6144]{1,0:T(8,128)(2,1)}, u32[]{:S(2)}, u32[]{:S(2)}) collective-permute-start(bf16[8,6144]{1,0:T(8,128)(2,1)} %get-tuple-element.62), channel_id=1, source_target_pairs={{0,32},{1,33},{2,34},{3,35},{4,36},{5,37},{6,38},{7,39},{8,40},{9,... | collective-permute-start | bytes 294920 | tf_op jit(solution)/shard_map/ppermute | solution.py:19
  64.8 7.4 %collective-permute-start.5 = (bf16[8,6144]{1,0:T(8,128)(2,1)}, bf16[8,6144]{1,0:T(8,128)(2,1)S(1)}, u32[]{:S(2)}, u32[]{:S(2)}) collective-permute-start(bf16[8,6144]{1,0:T(8,128)(2,1)} %get-tuple-element.62), channel_id=1, source_target_pairs={{0,96},{1,97},{2,98},{3,99},{4,100},{5,101},{6,102},{7,103},{8,104... | collective-permute-start | bytes 294920 | tf_op jit(solution)/shard_map/ppermute | solution.py:19
  68.4 6.3 %collective-permute-start.6 = (bf16[8,6144]{1,0:T(8,128)(2,1)}, bf16[8,6144]{1,0:T(8,128)(2,1)S(1)}, u32[]{:S(2)}, u32[]{:S(2)}) collective-permute-start(bf16[8,6144]{1,0:T(8,128)(2,1)} %get-tuple-element.62), channel_id=1, source_target_pairs={{0,64},{1,65},{2,66},{3,67},{4,68},{5,69},{6,70},{7,71},{8,72},{9,... | collective-permute-start | bytes 294920 | tf_op jit(solution)/shard_map/ppermute | solution.py:19
  74.7 13.3 %collective-permute-start.7 = (bf16[32,6144]{1,0:T(8,128)(2,1)S(1)}, bf16[32,6144]{1,0:T(8,128)(2,1)S(1)}, u32[]{:S(2)}, u32[]{:S(2)}) collective-permute-start(bf16[32,6144]{1,0:T(8,128)(2,1)S(1)} %constant_dynamic-update-slice_fusion.4), channel_id=1, source_target_pairs={{0,1},{1,2},{2,3},{3,0},{4,5},{5,6},{6,7},{7,4},{8,9},{9,10},{10,1... | collective-permute-start | bytes 1179656 | tf_op jit(solution)/shard_map/ppermute | solution.py:19
  74.8 14.0 %collective-permute-start.8 = (bf16[32,6144]{1,0:T(8,128)(2,1)S(1)}, bf16[32,6144]{1,0:T(8,128)(2,1)S(1)}, u32[]{:S(2)}, u32[]{:S(2)}) collective-permute-start(bf16[32,6144]{1,0:T(8,128)(2,1)S(1)} %constant_dynamic-update-slice_fusion.4), channel_id=1, source_target_pairs={{0,3},{1,0},{2,1},{3,2},{4,7},{5,4},{6,5},{7,6},{8,11},{9,8},{10,9... | collective-permute-start | bytes 1179656 | tf_op jit(solution)/shard_map/ppermute | solution.py:19
  78.0 11.6 %collective-permute-start.9 = (bf16[32,6144]{1,0:T(8,128)(2,1)S(1)}, bf16[32,6144]{1,0:T(8,128)(2,1)S(1)}, u32[]{:S(2)}, u32[]{:S(2)}) collective-permute-start(bf16[32,6144]{1,0:T(8,128)(2,1)S(1)} %constant_dynamic-update-slice_fusion.4), channel_id=1, source_target_pairs={{0,2},{1,3},{2,0},{3,1},{4,6},{5,7},{6,4},{7,5},{8,10},{9,11},{10,... | collective-permute-start | bytes 1179656 | tf_op jit(solution)/shard_map/ppermute | solution.py:19
  79.3 28.6 %copy-start.13 = (s32[1024]{0:T(1024)S(1)}, s32[1024]{0:T(1024)}, u32[]{:S(2)}) copy-start(s32[1024]{0:T(1024)} %param.19) | copy-start | bytes 12292
  90.3 36.4 %collective-permute-start.15 = (bf16[128,6144]{1,0:T(8,128)(2,1)}, bf16[128,6144]{1,0:T(8,128)(2,1)}, u32[]{:S(2)}, u32[]{:S(2)}) collective-permute-start(bf16[128,6144]{1,0:T(8,128)(2,1)} %constant_dynamic-update-slice_fusion), channel_id=1, source_target_pairs={{0,8},{1,9},{2,10},{3,11},{4,12},{5,13},{6,14},{7,15},{8,0},{9,1},... | collective-permute-start | bytes 4718600 | tf_op jit(solution)/shard_map/ppermute | solution.py:19
  107.9 20.7 %collective-permute-start.13 = (bf16[128,6144]{1,0:T(8,128)(2,1)}, bf16[128,6144]{1,0:T(8,128)(2,1)}, u32[]{:S(2)}, u32[]{:S(2)}) collective-permute-start(bf16[128,6144]{1,0:T(8,128)(2,1)} %constant_dynamic-update-slice_fusion), channel_id=1, source_target_pairs={{0,12},{1,13},{2,14},{3,15},{4,0},{5,1},{6,2},{7,3},{8,4},{9,5},{1... | collective-permute-start | bytes 4718600 | tf_op jit(solution)/shard_map/ppermute | solution.py:19
  108.4 35.1 %collective-permute-start.11 = (bf16[128,6144]{1,0:T(8,128)(2,1)}, bf16[128,6144]{1,0:T(8,128)(2,1)}, u32[]{:S(2)}, u32[]{:S(2)}) collective-permute-start(bf16[128,6144]{1,0:T(8,128)(2,1)} %constant_dynamic-update-slice_fusion), channel_id=1, source_target_pairs={{0,4},{1,5},{2,6},{3,7},{4,8},{5,9},{6,10},{7,11},{8,12},{9,13},{1... | collective-permute-start | bytes 4718600 | tf_op jit(solution)/shard_map/ppermute | solution.py:19
  110.5 41.0 %collective-permute-start.10 = (bf16[128,6144]{1,0:T(8,128)(2,1)}, bf16[128,6144]{1,0:T(8,128)(2,1)S(1)}, u32[]{:S(2)}, u32[]{:S(2)}) collective-permute-start(bf16[128,6144]{1,0:T(8,128)(2,1)} %constant_dynamic-update-slice_fusion), channel_id=1, source_target_pairs={{0,16},{1,17},{2,18},{3,19},{4,20},{5,21},{6,22},{7,23},{8,24},{9,... | collective-permute-start | bytes 4718600 | tf_op jit(solution)/shard_map/ppermute | solution.py:19
  110.5 33.0 %slice-start = ((s8[12582912]{0:T(1024)(128)(4,1)}), s8[4194304]{0:T(1024)(128)(4,1)S(1)}, s32[]{:S(2)}) async-start(s8[12582912]{0:T(1024)(128)(4,1)} %bitcast.169), calls=%async_computation.1 | async-start | bytes 8388608
  110.5 33.0 %slice-start.1 = ((s8[12582912]{0:T(1024)(128)(4,1)}), s8[4194304]{0:T(1024)(128)(4,1)S(1)}, s32[]{:S(2)}) async-start(s8[12582912]{0:T(1024)(128)(4,1)} %bitcast.169), calls=%async_computation.2 | async-start | bytes 8388608
  126.7 27.5 %collective-permute-start.16 = (bf16[128,6144]{1,0:T(8,128)(2,1)}, bf16[128,6144]{1,0:T(8,128)(2,1)}, u32[]{:S(2)}, u32[]{:S(2)}) collective-permute-start(bf16[128,6144]{1,0:T(8,128)(2,1)} %collective-permute-done.15), channel_id=1, source_target_pairs={{0,16},{1,17},{2,18},{3,19},{4,20},{5,21},{6,22},{7,23},{8,24},{9,... | collective-permute-start | bytes 4718600 | tf_op jit(solution)/shard_map/ppermute | solution.py:19
  128.7 33.0 %collective-permute-start.14 = (bf16[128,6144]{1,0:T(8,128)(2,1)}, bf16[128,6144]{1,0:T(8,128)(2,1)}, u32[]{:S(2)}, u32[]{:S(2)}) collective-permute-start(bf16[128,6144]{1,0:T(8,128)(2,1)} %collective-permute-done.13), channel_id=1, source_target_pairs={{0,16},{1,17},{2,18},{3,19},{4,20},{5,21},{6,22},{7,23},{8,24},{9,... | collective-permute-start | bytes 4718600 | tf_op jit(solution)/shard_map/ppermute | solution.py:19
  143.5 25.8 %collective-permute-start.12 = (bf16[128,6144]{1,0:T(8,128)(2,1)}, bf16[128,6144]{1,0:T(8,128)(2,1)}, u32[]{:S(2)}, u32[]{:S(2)}) collective-permute-start(bf16[128,6144]{1,0:T(8,128)(2,1)} %collective-permute-done.11), channel_id=1, source_target_pairs={{0,16},{1,17},{2,18},{3,19},{4,20},{5,21},{6,22},{7,23},{8,24},{9,... | collective-permute-start | bytes 4718600 | tf_op jit(solution)/shard_map/ppermute | solution.py:19
  174.5 1.4 collective-permute-start.17
  176.0 12.3 %collective-permute-start.18 = (f32[3,1024]{1,0:T(4,128)S(1)}, f32[3,1024]{1,0:T(4,128)S(1)}, u32[]{:S(2)}, u32[]{:S(2)}) collective-permute-start(f32[3,1024]{1,0:T(4,128)S(1)} %pad_maximum_fusion.2), channel_id=1, source_target_pairs={{0,32},{1,33},{2,34},{3,35},{4,36},{5,37},{6,38},{7,39},{8,40},{9,... | collective-permute-start | bytes 36872 | tf_op jit(solution)/shard_map/ppermute | solution.py:19
  182.9 5.4 %collective-permute-start.19 = (f32[3,1024]{1,0:T(4,128)S(1)}, f32[3,1024]{1,0:T(4,128)S(1)}, u32[]{:S(2)}, u32[]{:S(2)}) collective-permute-start(f32[3,1024]{1,0:T(4,128)S(1)} %pad_maximum_fusion.2), channel_id=1, source_target_pairs={{0,96},{1,97},{2,98},{3,99},{4,100},{5,101},{6,102},{7,103},{8,104... | collective-permute-start | bytes 36872 | tf_op jit(solution)/shard_map/ppermute | solution.py:19
  184.9 5.2 %collective-permute-start.20 = (f32[3,1024]{1,0:T(4,128)S(1)}, f32[3,1024]{1,0:T(4,128)S(1)}, u32[]{:S(2)}, u32[]{:S(2)}) collective-permute-start(f32[3,1024]{1,0:T(4,128)S(1)} %pad_maximum_fusion.2), channel_id=1, source_target_pairs={{0,64},{1,65},{2,66},{3,67},{4,68},{5,69},{6,70},{7,71},{8,72},{9,... | collective-permute-start | bytes 36872 | tf_op jit(solution)/shard_map/ppermute | solution.py:19
  191.4 17.7 %collective-permute-start.21 = (f32[3,1024]{1,0:T(4,128)}, f32[3,1024]{1,0:T(4,128)}, u32[]{:S(2)}, u32[]{:S(2)}) collective-permute-start(f32[3,1024]{1,0:T(4,128)} %pad_maximum_fusion.3), channel_id=1, source_target_pairs={{0,4},{1,5},{2,6},{3,7},{4,8},{5,9},{6,10},{7,11},{8,12},{9,13},{1... | collective-permute-start | bytes 36872 | tf_op jit(solution)/shard_map/ppermute | solution.py:19
  194.9 14.2 %collective-permute-start.22 = (f32[3,1024]{1,0:T(4,128)}, f32[3,1024]{1,0:T(4,128)}, u32[]{:S(2)}, u32[]{:S(2)}) collective-permute-start(f32[3,1024]{1,0:T(4,128)} %pad_maximum_fusion.3), channel_id=1, source_target_pairs={{0,12},{1,13},{2,14},{3,15},{4,0},{5,1},{6,2},{7,3},{8,4},{9,5},{1... | collective-permute-start | bytes 36872 | tf_op jit(solution)/shard_map/ppermute | solution.py:19
  194.9 14.2 %collective-permute-start.23 = (f32[3,1024]{1,0:T(4,128)}, f32[3,1024]{1,0:T(4,128)S(1)}, u32[]{:S(2)}, u32[]{:S(2)}) collective-permute-start(f32[3,1024]{1,0:T(4,128)} %pad_maximum_fusion.3), channel_id=1, source_target_pairs={{0,8},{1,9},{2,10},{3,11},{4,12},{5,13},{6,14},{7,15},{8,0},{9,1},... | collective-permute-start | bytes 36872 | tf_op jit(solution)/shard_map/ppermute | solution.py:19
  211.3 20.2 %collective-permute-start.26 = (f32[3,1024]{1,0:T(4,128)}, f32[3,1024]{1,0:T(4,128)}, u32[]{:S(2)}, u32[]{:S(2)}) collective-permute-start(f32[3,1024]{1,0:T(4,128)} %pad_maximum_fusion.4), channel_id=1, source_target_pairs={{0,2},{1,3},{2,0},{3,1},{4,6},{5,7},{6,4},{7,5},{8,10},{9,11},{10,... | collective-permute-start | bytes 36872 | tf_op jit(solution)/shard_map/ppermute | solution.py:19
  211.3 21.1 %collective-permute-start.25 = (f32[3,1024]{1,0:T(4,128)}, f32[3,1024]{1,0:T(4,128)}, u32[]{:S(2)}, u32[]{:S(2)}) collective-permute-start(f32[3,1024]{1,0:T(4,128)} %pad_maximum_fusion.4), channel_id=1, source_target_pairs={{0,3},{1,0},{2,1},{3,2},{4,7},{5,4},{6,5},{7,6},{8,11},{9,8},{10,9... | collective-permute-start | bytes 36872 | tf_op jit(solution)/shard_map/ppermute | solution.py:19
  215.0 18.5 %collective-permute-start.24 = (f32[3,1024]{1,0:T(4,128)}, f32[3,1024]{1,0:T(4,128)}, u32[]{:S(2)}, u32[]{:S(2)}) collective-permute-start(f32[3,1024]{1,0:T(4,128)} %pad_maximum_fusion.4), channel_id=1, source_target_pairs={{0,1},{1,2},{2,3},{3,0},{4,5},{5,6},{6,7},{7,4},{8,9},{9,10},{10,1... | collective-permute-start | bytes 36872 | tf_op jit(solution)/shard_map/ppermute | solution.py:19
  (17 other events, 122.4 us)

commit v2 on v1

v2 whole, which is shorter than its diff:
```python
import functools

import jax
import jax.numpy as jnp
from jax import lax
from jax.experimental import pallas as pl
from jax.experimental.pallas import tpu as pltpu
from jax.sharding import Mesh, PartitionSpec as P

X, CORE, Z, Y = 4, 2, 4, 4
ALL = ("x", "core", "z", "y")
F32 = jnp.float32
BF16 = jnp.bfloat16
HIGHEST = lax.Precision.HIGHEST


def move(array, target):
    pairs = []
    for i in range(X * CORE * Z * Y):
        at = (i // (CORE * Z * Y), i // (Z * Y) % CORE, i // Y % Z, i % Y)
        to = target(*at)
        if to is not None:
            pairs.append((i, ((to[0] * CORE + to[1]) * Z + to[2]) * Y + to[3]))
    return lax.ppermute(array, ALL, pairs)


def other_core(x, c, z, y):
    return (x, 1 - c, z, y)


def along_x(s):
    return lambda x, c, z, y: ((x + s) % X, c, z, y)


def along_y(s):
    return lambda x, c, z, y: (x, c, z, (y + s) % Y)


def along_z(s):
    return lambda x, c, z, y: (x, c, (z + s) % Z, y)


def along_p(s):
    return lambda x, c, z, y: (x, c, z, (y + s) % Y) if c == 0 else (x, c, (z + s) % Z, y)


def along_q(s):
    return lambda x, c, z, y: (x, c, (z + s) % Z, y) if c == 0 else (x, c, z, (y + s) % Y)


def later_x(s):
    return lambda x, c, z, y: (x + s, c, z, y) if x + s < X else None


def on_chip(shape, dtype):
    return pltpu.VMEM(shape, dtype)


def pin(array):
    return pltpu.with_memory_space_constraint(array, pltpu.VMEM)


SCALARS = pl.BlockSpec(memory_space=pltpu.SMEM)
WHOLE = pl.BlockSpec(memory_space=pltpu.VMEM)


def local(kernel, outs, scalars, *arrays, scratch=(), flops=0, bytes_=0, name=None):
    many = isinstance(outs, list)
    specs = [WHOLE] * len(outs) if many else WHOLE
    return pl.pallas_call(
        kernel,
        out_shape=outs,
        in_specs=[SCALARS] + [WHOLE] * len(arrays),
        out_specs=specs,
        scratch_shapes=list(scratch),
        compiler_params=pltpu.CompilerParams(vmem_limit_bytes=16 * 1024 * 1024),
        cost_estimate=pl.CostEstimate(flops=flops, bytes_accessed=bytes_, transcendentals=0),
        name=name,
    )(scalars, *[pin(a) for a in arrays])


def project_kernel(at, heads, weight, own, one, two, three, rolled):
    p = at[4]
    for s in range(4):
        start = pl.multiple_of((p + s) % 4 * 32, 32)
        rolled[pl.ds(32 * s, 32), :] = heads[pl.ds(start, 32), :]
    wide = 512 if weight.shape[1] % 512 == 0 else 128

    def step(n, carry):
        cols = pl.ds(pl.multiple_of(n * wide, wide), wide)
        out = jnp.dot(rolled[...], weight[:, cols], preferred_element_type=F32)
        own[:, cols] = out[:32]
        one[:, cols] = out[32:64].astype(BF16)
        two[:, cols] = out[64:96].astype(BF16)
        three[:, cols] = out[96:].astype(BF16)
        return carry

    lax.fori_loop(0, weight.shape[1] // wide, step, 0)


def partial_kernel(at, own, one, two, three, mine, first, second, third, total):
    q = at[5]
    total[...] = (
        own[...]
        + one[...].astype(F32)
        + two[...].astype(F32)
        + three[...].astype(F32)
    )
    for s, out in enumerate((mine, first, second, third)):
        start = pl.multiple_of((q + s) % 4 * 8, 8)
        out[...] = total[pl.ds(start, 8), :].astype(out.dtype)


def norm_kernel(at, own, one, two, three, tokens, gain, out):
    resid = (
        tokens[...]
        + own[...]
        + one[...].astype(F32)
        + two[...].astype(F32)
        + three[...].astype(F32)
    )
    scale = lax.rsqrt(jnp.mean(resid * resid, axis=1, keepdims=True) + 1e-06)
    out[...] = (resid * scale * gain[...].astype(F32)).astype(BF16)


def stack_kernel(at, a, b, c, d, out):
    rows = a.shape[0]
    out[0 : 2 * rows, :] = jnp.concatenate([a[...], b[...]], axis=0)
    out[2 * rows : 4 * rows, :] = jnp.concatenate([c[...], d[...]], axis=0)


def gather(block, target, scalars, name):
    parts = [move(block, target(s)) for s in (1, 2, 3)]
    rows, width = block.shape
    return local(
        stack_kernel,
        on_chip((4 * rows, width), block.dtype),
        scalars,
        block,
        *parts,
        bytes_=16 * rows * width,
        name=name,
    )


def score_kernel(shift, own, at, targets, rows, weight, out, logits):
    x = at[0]
    p, q, core = (at[4], at[5], at[1]) if own else (at[5], at[4], 1 - at[1])
    n_rows, width = rows.shape[0], weight.shape[1]
    tile = 256

    def step(n, carry):
        cols = pl.ds(pl.multiple_of(n * tile, tile), tile)
        logits[:, cols] = jnp.dot(rows[...], weight[:, cols], preferred_element_type=F32)
        return carry

    lax.fori_loop(0, width // tile, step, 0)
    i = lax.broadcasted_iota(jnp.int32, (n_rows, n_rows), 0)
    j = lax.broadcasted_iota(jnp.int32, (n_rows, n_rows), 1)
    lands = (
        (((p + 4 - i // 32) & 3) == j // 32)
        & (((x + 4 - (i // 8 & 3)) & 3) == (j // 8 & 3))
        & ((i & 7) == (j & 7))
    )
    place = core * 4 + ((q + 4 - shift) & 3)
    line = targets[pl.ds(place, 1), :] - at[6]
    want = jnp.sum(jnp.where(lands, line, 0), axis=1, keepdims=True)
    found = logits[...]
    top = jnp.max(found, axis=1, keepdims=True)
    total = jnp.sum(jnp.exp(found - top), axis=1, keepdims=True)
    column = lax.broadcasted_iota(jnp.int32, found.shape, 1)
    hit = jnp.sum(jnp.where(column == want, found, 0.0), axis=1, keepdims=True)
    both = jnp.where(j == 0, top, jnp.where(j == 1, total, jnp.where(j == 2, hit, 0.0)))
    turned = jnp.transpose(both)[:8]
    out[...] = jnp.dot(
        turned, lands.astype(F32), precision=HIGHEST, preferred_element_type=F32
    )


def place_kernel(at, *refs):
    blocks, out = refs[:-1], refs[-1]
    for k, block in enumerate(blocks):
        shift, own = k // 2, k % 2 == 0
        q, core = (at[5], at[1]) if own else (at[4], 1 - at[1])
        place = core * 4 + ((q + 4 - shift) & 3)
        for row in range(3):
            out[pl.ds(8 * row + place, 1), :] = block[row : row + 1, :]


def merged(parts):
    top = parts[0][0:8, :]
    for part in parts[1:]:
        top = jnp.maximum(top, part[0:8, :])
    total = sum(part[8:16, :] * jnp.exp(part[0:8, :] - top) for part in parts)
    hit = sum(part[16:24, :] for part in parts)
    return top, total, hit


def merge_kernel(at, *refs):
    top, total, hit = merged(refs[:-1])
    refs[-1][0:8, :] = top
    refs[-1][8:16, :] = total
    refs[-1][16:24, :] = hit


def finish_kernel(at, *refs):
    top, total, hit = merged(refs[:-2])
    out, found = refs[-2], refs[-1]
    found[...] = hit - top - jnp.log(total)
    i = lax.broadcasted_iota(jnp.int32, (128, 128), 0)
    j = lax.broadcasted_iota(jnp.int32, (128, 128), 1)
    here = jnp.zeros((1, 128), F32)
    for q in range(4):
        takes = (
            (i // 32 == j // 32)
            & ((i // 8 & 3) == at[0])
            & ((j // 8 & 3) == q)
            & ((i & 7) == (j & 7))
        )
        here = here + jnp.dot(
            found[pl.ds(at[1] * 4 + q, 1), :],
            takes.astype(F32),
            precision=HIGHEST,
            preferred_element_type=F32,
        )
    out[...] = here


def shards(
    tokens,
    log_decay,
    carried_state,
    q_weight,
    k_weight,
    v_weight,
    out_weight,
    final_gain,
    vocab_weight,
    targets,
):
    x, c, z, y = (lax.axis_index(a) for a in ALL)
    p, q = jnp.where(c == 0, y, z), jnp.where(c == 0, z, y)
    rows_here, width = tokens.shape
    heads_here = carried_state.shape[0]
    head_size = carried_state.shape[1]
    view = (rows_here, heads_here, head_size)
    vocab_local = vocab_weight.shape[1]
    offset = (((x * CORE + c) * Z + z) * Y + y) * vocab_local
    scalars = jnp.stack([x, c, z, y, p, q, offset, offset]).astype(jnp.int32)

    keys = jnp.dot(tokens, k_weight, preferred_element_type=F32).astype(BF16).reshape(view)
    values = jnp.dot(tokens, v_weight, preferred_element_type=F32).astype(BF16).reshape(view)
    lower = jnp.arange(rows_here)[:, None] >= jnp.arange(rows_here)[None, :]
    cumul = jnp.dot(lower.astype(F32), log_decay, precision=HIGHEST)
    last_cum = cumul[-1]
    ends = jnp.exp(last_cum[None, :] - cumul)
    state = jnp.einsum(
        "thd,the->hde",
        keys.astype(F32) * ends[:, :, None],
        values.astype(F32),
        precision=HIGHEST,
    )
    decay = jnp.broadcast_to(jnp.exp(last_cum)[:, None, None], (heads_here, 8, head_size))
    mine = jnp.concatenate([state, decay], axis=1)
    theirs = move(mine, other_core)
    first = jnp.where(c == 0, mine, theirs)
    second = jnp.where(c == 0, theirs, mine)
    first_s, first_d = first[:, :head_size], first[:, head_size : head_size + 1]
    second_s, second_d = second[:, :head_size], second[:, head_size : head_size + 1]
    chip = jnp.concatenate(
        [second_d * first_s + second_s, second[:, head_size:] * first[:, head_size:]], axis=1
    )
    arrived = [(s, move(chip, later_x(s))) for s in (3, 2, 1)]

    queries = jnp.dot(tokens, q_weight, preferred_element_type=F32).astype(BF16).reshape(view)
    scores = jnp.einsum("thd,shd->hts", queries, keys, preferred_element_type=F32)
    diff = jnp.transpose(cumul[:, None, :] - cumul[None, :, :], (2, 0, 1))
    weight = (scores * jnp.exp(jnp.where(lower[None], diff, -1e30))).astype(BF16)
    intra = jnp.einsum("hts,shd->thd", weight, values, preferred_element_type=F32)

    state_in = carried_state
    for s, message in arrived:
        d = jnp.where(x >= s, message[:, head_size : head_size + 1], 1.0)
        state_in = d * state_in + message[:, :head_size]
    state_in = jnp.where(c == 1, first_d * state_in + first_s, state_in)
    inter = jnp.exp(cumul)[:, :, None] * jnp.einsum(
        "thd,hde->the", queries.astype(F32), state_in, precision=HIGHEST
    )
    attended = intra + inter
    normed_heads = attended * lax.rsqrt(
        jnp.mean(attended * attended, axis=-1, keepdims=True) + 1e-06
    )
    flat_heads = normed_heads.astype(BF16).reshape(rows_here, heads_here * head_size)

    own, *sent = local(
        project_kernel,
        [on_chip((32, width), F32)] + [on_chip((32, width), BF16)] * 3,
        scalars,
        flat_heads,
        out_weight,
        scratch=[pltpu.VMEM(flat_heads.shape, BF16)],
        flops=2 * rows_here * flat_heads.shape[1] * width,
        bytes_=2 * width * (flat_heads.shape[1] + rows_here),
        name="project",
    )
    came = [move(part, along_p(s)) for s, part in zip((1, 2, 3), sent)]
    own, *sent = local(
        partial_kernel,
        [on_chip((8, width), F32)] + [on_chip((8, width), BF16)] * 3,
        scalars,
        own,
        *came,
        scratch=[pltpu.VMEM((32, width), F32)],
        bytes_=32 * width * 8,
        name="partial",
    )
    came = [move(part, along_q(s)) for s, part in zip((1, 2, 3), sent)]
    own_tokens = lax.dynamic_slice_in_dim(tokens, 32 * p + 8 * q, 8, 0).astype(F32)
    final_rows = local(
        norm_kernel,
        on_chip((8, width), BF16),
        scalars,
        own,
        *came,
        own_tokens,
        final_gain.reshape(1, width),
        bytes_=8 * width * 16,
        name="norm",
    )

    on_x = gather(final_rows, along_x, scalars, "stack_x")
    ours = gather(on_x, along_p, scalars, "stack_p")
    theirs = move(ours, other_core)
    ours, theirs = lax.optimization_barrier((ours, theirs))
    lines = jnp.transpose(targets.reshape(X, CORE, 4, 4, 8), (1, 3, 2, 0, 4)).reshape(8, 128)
    pairs = [(ours, theirs)]
    for s in (1, 3, 2):
        block = move(ours, along_q(s))
        pairs.append((block, move(block, other_core)))
    pairs = [pairs[0], pairs[1], pairs[3], pairs[2]]
    found = []
    for s, pair in enumerate(pairs):
        for mine_too, block in zip((True, False), pair):
            found.append(
                local(
                    functools.partial(score_kernel, s, mine_too),
                    on_chip((8, 128), F32),
                    scalars,
                    lines,
                    block,
                    vocab_weight,
                    scratch=[pltpu.VMEM((128, vocab_local), F32)],
                    flops=2 * 128 * width * vocab_local,
                    bytes_=2 * width * (128 + vocab_local),
                    name="score",
                )
            )
    stats = local(place_kernel, on_chip((24, 128), F32), scalars, *found, name="place")
    stats = local(
        merge_kernel, on_chip((24, 128), F32), scalars, stats, move(stats, other_core), name="merge"
    )
    for along in (along_x, along_z):
        parts = [stats] + [move(stats, along(s)) for s in (1, 3, 2)]
        stats = local(merge_kernel, on_chip((24, 128), F32), scalars, *parts, name="merge")
    parts = [stats] + [move(stats, along_y(s)) for s in (1, 3, 2)]
    loglik = local(
        finish_kernel,
        jax.ShapeDtypeStruct((1, 128), F32),
        scalars,
        *parts,
        scratch=[pltpu.VMEM((8, 128), F32)],
        name="finish",
    )
    return loglik.reshape(rows_here)


def solution(mesh):
    fine = Mesh(mesh.devices.reshape(X, CORE, Z, Y), ALL)
    seq, head = (("x", "core"), ("z", "y"))
    return jax.shard_map(
        shards,
        mesh=fine,
        in_specs=(
            P(seq, None),
            P(seq, head),
            P(head, None, None),
            P(None, head),
            P(None, head),
            P(None, head),
            P(head, None),
            P(),
            P(None, ALL),
            P(),
        ),
        out_specs=P(seq),
        check_vma=False,
    )
```

time: 244 us -> 210 us (0.86)
  Pallas kernels: 0 us -> 45.6 us
  matrix products: 54 us -> 9.97 us
  waiting for transfers between devices: 58.3 us -> 85.6 us
  starting transfers between devices: 67.4 us -> 44 us
  local copies, waits for them, and re-layouts: 41.8 us -> 19.1 us
  other arithmetic: 19.4 us -> 4.63 us
    ppermute x27 -> x33, waiting for transfers between devices: 35.5 us -> 85.6 us  [move(): return lax.ppermute(array, ALL, pairs)]
    pallas_call x0 -> x18, Pallas kernels: none -> 45.6 us  [local(): pl.pallas_call(kernel, out_shape=outs, in_specs=[SCALARS] + [WHOLE] * len...]
    dot_general x11 -> x2, matrix products: 46 us -> 2.31 us  [the longest x1 1.36 us: shards(): jnp.einsum('thd,hde->the', queries.astype(F32), state_in, precision=HIGHEST)]
    squeeze x33 -> x0, local copies, waits for them, and re-layouts: 28.5 us -> none  [the longest x11 10.4 us: merge(): total = sum((p[1] * jnp.exp(p[0] - top) for p in parts))]
    all_to_all x1 -> x0, waiting for transfers between devices: 22.8 us -> none  [shards(): lax.all_to_all(share.reshape(n_head, rows_mine, -1), ('z', 'y'), 0, 0)]
    unnamed x42 -> x34, local copies, waits for them, and re-layouts: 1.54 us -> 18.2 us
    ppermute x27 -> x33, starting transfers between devices: 59.1 us -> 44 us  [move(): return lax.ppermute(array, ALL, pairs)]
    all_to_all x1 -> x0, starting transfers between devices: 8.22 us -> none  [shards(): lax.all_to_all(share.reshape(n_head, rows_mine, -1), ('z', 'y'), 0, 0)]
  transfers between devices with their start and end apart: 28 -> 33, of which waited for: 11 -> 20; matrix products, arithmetic and copies ran while one was open for 33% -> 4% of each run, Pallas kernels for 0% -> 14%
where the time goes in v2:
time: 210 us; the launch traced here: 209 us
  waiting for transfers between devices  85.6 us (41%)
  Pallas kernels  45.6 us (22%)
  starting transfers between devices  44 us (21%)
  local copies, waits for them, and re-layouts  19.1 us (9%)
  matrix products  9.97 us (5%)
  other arithmetic  4.63 us (2%)
    ppermute x33, waiting for transfers between devices, move(): return lax.ppermute(array, ALL, pairs)  85.6 us
    pallas_call x18, Pallas kernels, local(): pl.pallas_call(kernel, out_shape=outs, in_specs=[SCALARS] + [WHOLE] * len...  45.6 us
    ppermute x33, starting transfers between devices, move(): return lax.ppermute(array, ALL, pairs)  44 us
    unnamed x34, local copies, waits for them, and re-layouts  18.2 us
  transfers between devices with their start and end apart: 33, of which 20 were waited for; matrix products, arithmetic and copies ran while one was open for 4% of the time, Pallas kernels for 14%

profile of v2, /device:TPU:0, one launch (start us, length us, event | category | flops | bytes accessed | tf_op | source)
XLA Modules:
  0.0 209.3 jit_solution(8430882266608885092)
XLA Ops:
  1.9 2.1 %fusion.3 = bf16[16,2,8,128]{3,2,1,0:T(8,128)(2,1)S(1)} fusion(bf16[128,6144]{1,0:T(8,128)(2,1)} %param.10, bf16[6144,256]{1,0:T(8,128)(2,1)S(1)} %copy-done), kind=kOutput, calls=%fused_computation.9 | convolution fusion | flops 402685952 | bytes 4784128 | tf_op jit(solution)/shard_map/dot_general | solution.py:252
  6.4 2.9 %fusion.4 = bf16[16,2,8,128]{3,2,1,0:T(8,128)(2,1)S(1)} fusion(bf16[128,6144]{1,0:T(8,128)(2,1)} %param.10, bf16[6144,256]{1,0:T(8,128)(2,1)} %param.13), kind=kOutput, calls=%fused_computation.10 | convolution fusion | flops 402685952 | bytes 4784128 | tf_op jit(solution)/shard_map/dot_general | solution.py:275
  11.8 5.4 %collective-permute-start.3 = (f32[2,136,128]{2,1,0:T(8,128)}, f32[2,136,128]{2,1,0:T(8,128)}, u32[]{:S(2)}, u32[]{:S(2)}) collective-permute-start(f32[2,136,128]{2,1,0:T(8,128)} %pad_maximum_fusion.1), channel_id=1, source_target_pairs={{0,96},{1,97},{2,98},{3,99},{4,100},{5,101},{6,102},{7,103},{8,104... | collective-permute-start | bytes 417800 | tf_op jit(solution)/shard_map/ppermute | solution.py:24
  24.6 2.6 %collective-permute-done.1 = f32[2,136,128]{2,1,0:T(8,128)S(1)} collective-permute-done((f32[2,136,128]{2,1,0:T(8,128)}, f32[2,136,128]{2,1,0:T(8,128)S(1)}, u32[]{:S(2)}, u32[]{:S(2)}) %collective-permute-start.1) | collective-permute-done | bytes 139296 | tf_op jit(solution)/shard_map/ppermute | solution.py:24
  30.6 3.9 %project.1 = (f32[32,6144]{1,0:T(8,128)S(1)}, bf16[32,6144]{1,0:T(8,128)(2,1)}, bf16[32,6144]{1,0:T(8,128)(2,1)}, bf16[32,6144]{1,0:T(8,128)(2,1)}) custom-call(s32[8]{0:T(128)S(1)} %stack.32.at, bf16[128,256]{1,0:T(8,128)(2,1)S(1)} %copy.26.heads, bf16[256,6144]{1,0:T(8,128)(2,1)S(1)} %copy-done.5), custom_call_target="tpu_custom_call" | custom-call | flops 402653184 | bytes 4718592 | tf_op jit(solution)/shard_map/project/pallas_call | solution.py:70
  36.9 2.9 %collective-permute-start.5 = (bf16[32,6144]{1,0:T(8,128)(2,1)}, bf16[32,6144]{1,0:T(8,128)(2,1)}, u32[]{:S(2)}, u32[]{:S(2)}) collective-permute-start(bf16[32,6144]{1,0:T(8,128)(2,1)} %get-tuple-element.17), channel_id=1, source_target_pairs={{0,2},{1,3},{2,0},{3,1},{4,6},{5,7},{6,4},{7,5},{8,10},{9,11},{10,... | collective-permute-start | bytes 1179656 | tf_op jit(solution)/shard_map/ppermute | solution.py:24
  41.2 3.4 %collective-permute-done.4.one = bf16[32,6144]{1,0:T(8,128)(2,1)S(1)} collective-permute-done((bf16[32,6144]{1,0:T(8,128)(2,1)}, bf16[32,6144]{1,0:T(8,128)(2,1)S(1)}, u32[]{:S(2)}, u32[]{:S(2)}) %collective-permute-start.4) | collective-permute-done | bytes 393248 | tf_op jit(solution)/shard_map/ppermute | solution.py:24
  44.6 5.6 %collective-permute-done.5.two = bf16[32,6144]{1,0:T(8,128)(2,1)} collective-permute-done((bf16[32,6144]{1,0:T(8,128)(2,1)}, bf16[32,6144]{1,0:T(8,128)(2,1)}, u32[]{:S(2)}, u32[]{:S(2)}) %collective-permute-start.5) | collective-permute-done | bytes 393248 | tf_op jit(solution)/shard_map/ppermute | solution.py:24
  54.7 3.6 %collective-permute-start.8 = (bf16[8,6144]{1,0:T(8,128)(2,1)S(1)}, bf16[8,6144]{1,0:T(8,128)(2,1)S(1)}, u32[]{:S(2)}, u32[]{:S(2)}) collective-permute-start(bf16[8,6144]{1,0:T(8,128)(2,1)S(1)} %get-tuple-element.21), channel_id=1, source_target_pairs={{0,8},{1,9},{2,10},{3,11},{4,12},{5,13},{6,14},{7,15},{8,0},{9,1},... | collective-permute-start | bytes 294920 | tf_op jit(solution)/shard_map/ppermute | solution.py:24
  63.9 4.2 %collective-permute-start.11 = (bf16[8,6144]{1,0:T(8,128)(2,1)S(1)}, bf16[8,6144]{1,0:T(8,128)(2,1)S(1)}, u32[]{:S(2)}, u32[]{:S(2)}) collective-permute-start(bf16[8,6144]{1,0:T(8,128)(2,1)S(1)} %norm.1.a), channel_id=1, source_target_pairs={{0,64},{1,65},{2,66},{3,67},{4,68},{5,69},{6,70},{7,71},{8,72},{9,... | collective-permute-start | bytes 294920 | tf_op jit(solution)/shard_map/ppermute | solution.py:24
  70.7 3.2 %collective-permute-done.10.b = bf16[8,6144]{1,0:T(8,128)(2,1)S(1)} collective-permute-done((bf16[8,6144]{1,0:T(8,128)(2,1)S(1)}, bf16[8,6144]{1,0:T(8,128)(2,1)S(1)}, u32[]{:S(2)}, u32[]{:S(2)}) %collective-permute-start.10) | collective-permute-done | bytes 98336 | tf_op jit(solution)/shard_map/ppermute | solution.py:24
  74.6 2.4 %collective-permute-start.15 = (bf16[32,6144]{1,0:T(8,128)(2,1)S(1)}, bf16[32,6144]{1,0:T(8,128)(2,1)S(1)}, u32[]{:S(2)}, u32[]{:S(2)}) collective-permute-start(bf16[32,6144]{1,0:T(8,128)(2,1)S(1)} %stack_x.1.a), channel_id=1, source_target_pairs={{0,3},{1,0},{2,1},{3,2},{4,7},{5,4},{6,5},{7,6},{8,11},{9,8},{10,9... | collective-permute-start | bytes 1179656 | tf_op jit(solution)/shard_map/ppermute | solution.py:24
  78.9 7.6 %collective-permute-done.15.d = bf16[32,6144]{1,0:T(8,128)(2,1)S(1)} collective-permute-done((bf16[32,6144]{1,0:T(8,128)(2,1)S(1)}, bf16[32,6144]{1,0:T(8,128)(2,1)S(1)}, u32[]{:S(2)}, u32[]{:S(2)}) %collective-permute-start.15) | collective-permute-done | bytes 393248 | tf_op jit(solution)/shard_map/ppermute | solution.py:24
  86.5 3.9 %collective-permute-done.13.b = bf16[32,6144]{1,0:T(8,128)(2,1)S(1)} collective-permute-done((bf16[32,6144]{1,0:T(8,128)(2,1)S(1)}, bf16[32,6144]{1,0:T(8,128)(2,1)S(1)}, u32[]{:S(2)}, u32[]{:S(2)}) %collective-permute-start.13) | collective-permute-done | bytes 393248 | tf_op jit(solution)/shard_map/ppermute | solution.py:24
  91.2 3.4 %collective-permute-done.16.rows = bf16[128,6144]{1,0:T(8,128)(2,1)S(1)} collective-permute-done((bf16[128,6144]{1,0:T(8,128)(2,1)S(1)}, bf16[128,6144]{1,0:T(8,128)(2,1)S(1)}, u32[]{:S(2)}, u32[]{:S(2)}) %collective-permute-start.16) | collective-permute-done | bytes 1572896 | tf_op jit(solution)/shard_map/ppermute | solution.py:24
  95.7 2.2 %collective-permute-start.21 = (bf16[128,6144]{1,0:T(8,128)(2,1)S(1)}, bf16[128,6144]{1,0:T(8,128)(2,1)}, u32[]{:S(2)}, u32[]{:S(2)}) collective-permute-start(bf16[128,6144]{1,0:T(8,128)(2,1)S(1)} %stack_p.1.rows), channel_id=1, source_target_pairs={{0,12},{1,13},{2,14},{3,15},{4,0},{5,1},{6,2},{7,3},{8,4},{9,5},{1... | collective-permute-start | bytes 4718600 | tf_op jit(solution)/shard_map/ppermute | solution.py:24
  100.0 32.7 %collective-permute-done.21.rows = bf16[128,6144]{1,0:T(8,128)(2,1)} collective-permute-done((bf16[128,6144]{1,0:T(8,128)(2,1)S(1)}, bf16[128,6144]{1,0:T(8,128)(2,1)}, u32[]{:S(2)}, u32[]{:S(2)}) %collective-permute-start.21) | collective-permute-done | bytes 1572896 | tf_op jit(solution)/shard_map/ppermute | solution.py:24
  133.3 3.5 %collective-permute-done.17.rows = bf16[128,6144]{1,0:T(8,128)(2,1)} collective-permute-done((bf16[128,6144]{1,0:T(8,128)(2,1)S(1)}, bf16[128,6144]{1,0:T(8,128)(2,1)}, u32[]{:S(2)}, u32[]{:S(2)}) %collective-permute-start.17) | collective-permute-done | bytes 1572896 | tf_op jit(solution)/shard_map/ppermute | solution.py:24
  137.1 4.6 %copy-done.1 = bf16[6144,1024]{1,0:T(8,128)(2,1)S(1)} copy-done((bf16[6144,1024]{1,0:T(8,128)(2,1)S(1)}, bf16[6144,1024]{1,0:T(8,128)(2,1)}, u32[]{:S(2)}) %copy-start.1) | copy-done | bytes 12582936
  143.1 3.7 %score.8.refs_0_ = f32[8,128]{1,0:T(8,128)S(1)} custom-call(s32[8]{0:T(128)S(1)} %stack.32.at, s32[8,128]{1,0:T(8,128)S(1)} %reshape.54.targets, bf16[128,6144]{1,0:T(8,128)(2,1)S(1)} %copy-done.4, bf16[6144,1024]{1,0:T(8,128)(2,1)S(1)} %copy-done.1), custom_call_target="tpu_custom_call" | custom-call | flops 1610612736 | bytes 14155776 | tf_op jit(solution)/shard_map/score/pallas_call | solution.py:70
  146.8 4.6 %copy-done.2 = bf16[6144,1024]{1,0:T(8,128)(2,1)S(1)} copy-done((bf16[6144,1024]{1,0:T(8,128)(2,1)S(1)}, bf16[6144,1024]{1,0:T(8,128)(2,1)}, u32[]{:S(2)}) %copy-start.2) | copy-done | bytes 12582936
  151.4 3.7 %score.9.refs_1_ = f32[8,128]{1,0:T(8,128)S(1)} custom-call(s32[8]{0:T(128)S(1)} %stack.32.at, s32[8,128]{1,0:T(8,128)S(1)} %reshape.54.targets, bf16[128,6144]{1,0:T(8,128)(2,1)S(1)} %copy-done.7, bf16[6144,1024]{1,0:T(8,128)(2,1)S(1)} %copy-done.2), custom_call_target="tpu_custom_call" | custom-call | flops 1610612736 | bytes 14155776 | tf_op jit(solution)/shard_map/score/pallas_call | solution.py:70
  155.1 4.5 %score.14.refs_6_ = f32[8,128]{1,0:T(8,128)S(1)} custom-call(s32[8]{0:T(128)S(1)} %stack.32.at, s32[8,128]{1,0:T(8,128)S(1)} %reshape.54.targets, bf16[128,6144]{1,0:T(8,128)(2,1)} %collective-permute-done.21.rows, bf16[6144,1024]{1,0:T(8,128)(2,1)S(1)} %copy-done.2), custom_call_target="tpu_custom_call" | custom-call | flops 1610612736 | bytes 14155776 | tf_op jit(solution)/shard_map/score/pallas_call | solution.py:70
  159.7 4.5 %score.12.refs_4_ = f32[8,128]{1,0:T(8,128)S(1)} custom-call(s32[8]{0:T(128)S(1)} %stack.32.at, s32[8,128]{1,0:T(8,128)S(1)} %reshape.54.targets, bf16[128,6144]{1,0:T(8,128)(2,1)} %collective-permute-done.19.rows, bf16[6144,1024]{1,0:T(8,128)(2,1)S(1)} %copy-done.2), custom_call_target="tpu_custom_call" | custom-call | flops 1610612736 | bytes 14155776 | tf_op jit(solution)/shard_map/score/pallas_call | solution.py:70
  164.2 4.5 %score.10.refs_2_ = f32[8,128]{1,0:T(8,128)S(1)} custom-call(s32[8]{0:T(128)S(1)} %stack.32.at, s32[8,128]{1,0:T(8,128)S(1)} %reshape.54.targets, bf16[128,6144]{1,0:T(8,128)(2,1)} %collective-permute-done.17.rows, bf16[6144,1024]{1,0:T(8,128)(2,1)S(1)} %copy-done.2), custom_call_target="tpu_custom_call" | custom-call | flops 1610612736 | bytes 14155776 | tf_op jit(solution)/shard_map/score/pallas_call | solution.py:70
  168.8 4.5 %score.15.refs_7_ = f32[8,128]{1,0:T(8,128)S(1)} custom-call(s32[8]{0:T(128)S(1)} %stack.32.at, s32[8,128]{1,0:T(8,128)S(1)} %reshape.54.targets, bf16[128,6144]{1,0:T(8,128)(2,1)} %collective-permute-done.22.rows, bf16[6144,1024]{1,0:T(8,128)(2,1)S(1)} %copy-done.2), custom_call_target="tpu_custom_call" | custom-call | flops 1610612736 | bytes 14155776 | tf_op jit(solution)/shard_map/score/pallas_call | solution.py:70
  173.3 4.5 %score.13.refs_5_ = f32[8,128]{1,0:T(8,128)S(1)} custom-call(s32[8]{0:T(128)S(1)} %stack.32.at, s32[8,128]{1,0:T(8,128)S(1)} %reshape.54.targets, bf16[128,6144]{1,0:T(8,128)(2,1)} %collective-permute-done.20.rows, bf16[6144,1024]{1,0:T(8,128)(2,1)S(1)} %copy-done.2), custom_call_target="tpu_custom_call" | custom-call | flops 1610612736 | bytes 14155776 | tf_op jit(solution)/shard_map/score/pallas_call | solution.py:70
  177.9 4.5 %score.11.refs_3_ = f32[8,128]{1,0:T(8,128)S(1)} custom-call(s32[8]{0:T(128)S(1)} %stack.32.at, s32[8,128]{1,0:T(8,128)S(1)} %reshape.54.targets, bf16[128,6144]{1,0:T(8,128)(2,1)} %collective-permute-done.18.rows, bf16[6144,1024]{1,0:T(8,128)(2,1)S(1)} %copy-done.2), custom_call_target="tpu_custom_call" | custom-call | flops 1610612736 | bytes 14155776 | tf_op jit(solution)/shard_map/score/pallas_call | solution.py:70
  187.8 2.5 %collective-permute-done.26.refs_3_ = f32[24,128]{1,0:T(8,128)S(1)} collective-permute-done((f32[24,128]{1,0:T(8,128)S(1)}, f32[24,128]{1,0:T(8,128)S(1)}, u32[]{:S(2)}, u32[]{:S(2)}) %collective-permute-start.26) | collective-permute-done | bytes 12320 | tf_op jit(solution)/shard_map/ppermute | solution.py:24
  190.2 2.3 %collective-permute-done.24.refs_1_ = f32[24,128]{1,0:T(8,128)S(1)} collective-permute-done((f32[24,128]{1,0:T(8,128)S(1)}, f32[24,128]{1,0:T(8,128)S(1)}, u32[]{:S(2)}, u32[]{:S(2)}) %collective-permute-start.24) | collective-permute-done | bytes 12320 | tf_op jit(solution)/shard_map/ppermute | solution.py:24
  195.6 2.8 %collective-permute-done.29.refs_3_ = f32[24,128]{1,0:T(8,128)S(1)} collective-permute-done((f32[24,128]{1,0:T(8,128)S(1)}, f32[24,128]{1,0:T(8,128)S(1)}, u32[]{:S(2)}, u32[]{:S(2)}) %collective-permute-start.29) | collective-permute-done | bytes 12320 | tf_op jit(solution)/shard_map/ppermute | solution.py:24
  205.5 2.3 %collective-permute-done.30.refs_1_ = f32[24,128]{1,0:T(8,128)S(1)} collective-permute-done((f32[24,128]{1,0:T(8,128)S(1)}, f32[24,128]{1,0:T(8,128)S(1)}, u32[]{:S(2)}, u32[]{:S(2)}) %collective-permute-start.30) | collective-permute-done | bytes 12320 | tf_op jit(solution)/shard_map/ppermute | solution.py:24
  (118 shorter events, 59.6 us)
Async XLA Ops:
  6.4 3.7 %collective-permute-start = (f32[2,136,128]{2,1,0:T(8,128)}, f32[2,136,128]{2,1,0:T(8,128)}, u32[]{:S(2)}, u32[]{:S(2)}) collective-permute-start(f32[2,136,128]{2,1,0:T(8,128)} %pad_maximum_fusion), channel_id=1, source_target_pairs={{0,16},{1,17},{2,18},{3,19},{4,20},{5,21},{6,22},{7,23},{8,24},{9,... | collective-permute-start | bytes 417800 | tf_op jit(solution)/shard_map/ppermute | solution.py:24
  11.8 10.6 %collective-permute-start.3 = (f32[2,136,128]{2,1,0:T(8,128)}, f32[2,136,128]{2,1,0:T(8,128)}, u32[]{:S(2)}, u32[]{:S(2)}) collective-permute-start(f32[2,136,128]{2,1,0:T(8,128)} %pad_maximum_fusion.1), channel_id=1, source_target_pairs={{0,96},{1,97},{2,98},{3,99},{4,100},{5,101},{6,102},{7,103},{8,104... | collective-permute-start | bytes 417800 | tf_op jit(solution)/shard_map/ppermute | solution.py:24
  19.0 5.6 %collective-permute-start.2 = (f32[2,136,128]{2,1,0:T(8,128)}, f32[2,136,128]{2,1,0:T(8,128)S(1)}, u32[]{:S(2)}, u32[]{:S(2)}) collective-permute-start(f32[2,136,128]{2,1,0:T(8,128)} %pad_maximum_fusion.1), channel_id=1, source_target_pairs={{0,64},{1,65},{2,66},{3,67},{4,68},{5,69},{6,70},{7,71},{8,72},{9,... | collective-permute-start | bytes 417800 | tf_op jit(solution)/shard_map/ppermute | solution.py:24
  20.3 6.9 %collective-permute-start.1 = (f32[2,136,128]{2,1,0:T(8,128)}, f32[2,136,128]{2,1,0:T(8,128)S(1)}, u32[]{:S(2)}, u32[]{:S(2)}) collective-permute-start(f32[2,136,128]{2,1,0:T(8,128)} %pad_maximum_fusion.1), channel_id=1, source_target_pairs={{0,32},{1,33},{2,34},{3,35},{4,36},{5,37},{6,38},{7,39},{8,40},{9,... | collective-permute-start | bytes 417800 | tf_op jit(solution)/shard_map/ppermute | solution.py:24
  35.4 9.2 %collective-permute-start.4 = (bf16[32,6144]{1,0:T(8,128)(2,1)}, bf16[32,6144]{1,0:T(8,128)(2,1)S(1)}, u32[]{:S(2)}, u32[]{:S(2)}) collective-permute-start(bf16[32,6144]{1,0:T(8,128)(2,1)} %get-tuple-element.16), channel_id=1, source_target_pairs={{0,1},{1,2},{2,3},{3,0},{4,5},{5,6},{6,7},{7,4},{8,9},{9,10},{10,1... | collective-permute-start | bytes 1179656 | tf_op jit(solution)/shard_map/ppermute | solution.py:24
  36.9 13.2 %collective-permute-start.5 = (bf16[32,6144]{1,0:T(8,128)(2,1)}, bf16[32,6144]{1,0:T(8,128)(2,1)}, u32[]{:S(2)}, u32[]{:S(2)}) collective-permute-start(bf16[32,6144]{1,0:T(8,128)(2,1)} %get-tuple-element.17), channel_id=1, source_target_pairs={{0,2},{1,3},{2,0},{3,1},{4,6},{5,7},{6,4},{7,5},{8,10},{9,11},{10,... | collective-permute-start | bytes 1179656 | tf_op jit(solution)/shard_map/ppermute | solution.py:24
  39.9 10.3 %collective-permute-start.6 = (bf16[32,6144]{1,0:T(8,128)(2,1)}, bf16[32,6144]{1,0:T(8,128)(2,1)}, u32[]{:S(2)}, u32[]{:S(2)}) collective-permute-start(bf16[32,6144]{1,0:T(8,128)(2,1)} %get-tuple-element.18), channel_id=1, source_target_pairs={{0,3},{1,0},{2,1},{3,2},{4,7},{5,4},{6,5},{7,6},{8,11},{9,8},{10,9... | collective-permute-start | bytes 1179656 | tf_op jit(solution)/shard_map/ppermute | solution.py:24
  52.7 7.5 %collective-permute-start.7 = (bf16[8,6144]{1,0:T(8,128)(2,1)S(1)}, bf16[8,6144]{1,0:T(8,128)(2,1)S(1)}, u32[]{:S(2)}, u32[]{:S(2)}) collective-permute-start(bf16[8,6144]{1,0:T(8,128)(2,1)S(1)} %get-tuple-element.20), channel_id=1, source_target_pairs={{0,4},{1,5},{2,6},{3,7},{4,8},{5,9},{6,10},{7,11},{8,12},{9,13},{1... | collective-permute-start | bytes 294920 | tf_op jit(solution)/shard_map/ppermute | solution.py:24
  54.7 7.2 %collective-permute-start.8 = (bf16[8,6144]{1,0:T(8,128)(2,1)S(1)}, bf16[8,6144]{1,0:T(8,128)(2,1)S(1)}, u32[]{:S(2)}, u32[]{:S(2)}) collective-permute-start(bf16[8,6144]{1,0:T(8,128)(2,1)S(1)} %get-tuple-element.21), channel_id=1, source_target_pairs={{0,8},{1,9},{2,10},{3,11},{4,12},{5,13},{6,14},{7,15},{8,0},{9,1},... | collective-permute-start | bytes 294920 | tf_op jit(solution)/shard_map/ppermute | solution.py:24
  58.3 4.6 %collective-permute-start.9 = (bf16[8,6144]{1,0:T(8,128)(2,1)S(1)}, bf16[8,6144]{1,0:T(8,128)(2,1)S(1)}, u32[]{:S(2)}, u32[]{:S(2)}) collective-permute-start(bf16[8,6144]{1,0:T(8,128)(2,1)S(1)} %get-tuple-element.22), channel_id=1, source_target_pairs={{0,12},{1,13},{2,14},{3,15},{4,0},{5,1},{6,2},{7,3},{8,4},{9,5},{1... | collective-permute-start | bytes 294920 | tf_op jit(solution)/shard_map/ppermute | solution.py:24
  63.6 5.3 %collective-permute-start.12 = (bf16[8,6144]{1,0:T(8,128)(2,1)S(1)}, bf16[8,6144]{1,0:T(8,128)(2,1)S(1)}, u32[]{:S(2)}, u32[]{:S(2)}) collective-permute-start(bf16[8,6144]{1,0:T(8,128)(2,1)S(1)} %norm.1.a), channel_id=1, source_target_pairs={{0,96},{1,97},{2,98},{3,99},{4,100},{5,101},{6,102},{7,103},{8,104... | collective-permute-start | bytes 294920 | tf_op jit(solution)/shard_map/ppermute | solution.py:24
  63.9 6.8 %collective-permute-start.11 = (bf16[8,6144]{1,0:T(8,128)(2,1)S(1)}, bf16[8,6144]{1,0:T(8,128)(2,1)S(1)}, u32[]{:S(2)}, u32[]{:S(2)}) collective-permute-start(bf16[8,6144]{1,0:T(8,128)(2,1)S(1)} %norm.1.a), channel_id=1, source_target_pairs={{0,64},{1,65},{2,66},{3,67},{4,68},{5,69},{6,70},{7,71},{8,72},{9,... | collective-permute-start | bytes 294920 | tf_op jit(solution)/shard_map/ppermute | solution.py:24
  68.1 5.8 %collective-permute-start.10 = (bf16[8,6144]{1,0:T(8,128)(2,1)S(1)}, bf16[8,6144]{1,0:T(8,128)(2,1)S(1)}, u32[]{:S(2)}, u32[]{:S(2)}) collective-permute-start(bf16[8,6144]{1,0:T(8,128)(2,1)S(1)} %norm.1.a), channel_id=1, source_target_pairs={{0,32},{1,33},{2,34},{3,35},{4,36},{5,37},{6,38},{7,39},{8,40},{9,... | collective-permute-start | bytes 294920 | tf_op jit(solution)/shard_map/ppermute | solution.py:24
  74.6 11.9 %collective-permute-start.15 = (bf16[32,6144]{1,0:T(8,128)(2,1)S(1)}, bf16[32,6144]{1,0:T(8,128)(2,1)S(1)}, u32[]{:S(2)}, u32[]{:S(2)}) collective-permute-start(bf16[32,6144]{1,0:T(8,128)(2,1)S(1)} %stack_x.1.a), channel_id=1, source_target_pairs={{0,3},{1,0},{2,1},{3,2},{4,7},{5,4},{6,5},{7,6},{8,11},{9,8},{10,9... | collective-permute-start | bytes 1179656 | tf_op jit(solution)/shard_map/ppermute | solution.py:24
  76.9 9.5 %collective-permute-start.14 = (bf16[32,6144]{1,0:T(8,128)(2,1)S(1)}, bf16[32,6144]{1,0:T(8,128)(2,1)S(1)}, u32[]{:S(2)}, u32[]{:S(2)}) collective-permute-start(bf16[32,6144]{1,0:T(8,128)(2,1)S(1)} %stack_x.1.a), channel_id=1, source_target_pairs={{0,2},{1,3},{2,0},{3,1},{4,6},{5,7},{6,4},{7,5},{8,10},{9,11},{10,... | collective-permute-start | bytes 1179656 | tf_op jit(solution)/shard_map/ppermute | solution.py:24
  78.3 12.1 %collective-permute-start.13 = (bf16[32,6144]{1,0:T(8,128)(2,1)S(1)}, bf16[32,6144]{1,0:T(8,128)(2,1)S(1)}, u32[]{:S(2)}, u32[]{:S(2)}) collective-permute-start(bf16[32,6144]{1,0:T(8,128)(2,1)S(1)} %stack_x.1.a), channel_id=1, source_target_pairs={{0,1},{1,2},{2,3},{3,0},{4,5},{5,6},{6,7},{7,4},{8,9},{9,10},{10,1... | collective-permute-start | bytes 1179656 | tf_op jit(solution)/shard_map/ppermute | solution.py:24
  91.1 3.5 %collective-permute-start.16 = (bf16[128,6144]{1,0:T(8,128)(2,1)S(1)}, bf16[128,6144]{1,0:T(8,128)(2,1)S(1)}, u32[]{:S(2)}, u32[]{:S(2)}) collective-permute-start(bf16[128,6144]{1,0:T(8,128)(2,1)S(1)} %stack_p.1.rows), channel_id=1, source_target_pairs={{0,16},{1,17},{2,18},{3,19},{4,20},{5,21},{6,22},{7,23},{8,24},{9,... | collective-permute-start | bytes 4718600 | tf_op jit(solution)/shard_map/ppermute | solution.py:24
  95.7 37.0 %collective-permute-start.21 = (bf16[128,6144]{1,0:T(8,128)(2,1)S(1)}, bf16[128,6144]{1,0:T(8,128)(2,1)}, u32[]{:S(2)}, u32[]{:S(2)}) collective-permute-start(bf16[128,6144]{1,0:T(8,128)(2,1)S(1)} %stack_p.1.rows), channel_id=1, source_target_pairs={{0,12},{1,13},{2,14},{3,15},{4,0},{5,1},{6,2},{7,3},{8,4},{9,5},{1... | collective-permute-start | bytes 4718600 | tf_op jit(solution)/shard_map/ppermute | solution.py:24
  97.9 34.8 %collective-permute-start.19 = (bf16[128,6144]{1,0:T(8,128)(2,1)S(1)}, bf16[128,6144]{1,0:T(8,128)(2,1)}, u32[]{:S(2)}, u32[]{:S(2)}) collective-permute-start(bf16[128,6144]{1,0:T(8,128)(2,1)S(1)} %stack_p.1.rows), channel_id=1, source_target_pairs={{0,8},{1,9},{2,10},{3,11},{4,12},{5,13},{6,14},{7,15},{8,0},{9,1},... | collective-permute-start | bytes 4718600 | tf_op jit(solution)/shard_map/ppermute | solution.py:24
  98.3 38.5 %collective-permute-start.17 = (bf16[128,6144]{1,0:T(8,128)(2,1)S(1)}, bf16[128,6144]{1,0:T(8,128)(2,1)}, u32[]{:S(2)}, u32[]{:S(2)}) collective-permute-start(bf16[128,6144]{1,0:T(8,128)(2,1)S(1)} %stack_p.1.rows), channel_id=1, source_target_pairs={{0,4},{1,5},{2,6},{3,7},{4,8},{5,9},{6,10},{7,11},{8,12},{9,13},{1... | collective-permute-start | bytes 4718600 | tf_op jit(solution)/shard_map/ppermute | solution.py:24
  132.8 36.0 %collective-permute-start.22 = (bf16[128,6144]{1,0:T(8,128)(2,1)}, bf16[128,6144]{1,0:T(8,128)(2,1)}, u32[]{:S(2)}, u32[]{:S(2)}) collective-permute-start(bf16[128,6144]{1,0:T(8,128)(2,1)} %collective-permute-done.21.rows), channel_id=1, source_target_pairs={{0,16},{1,17},{2,18},{3,19},{4,20},{5,21},{6,22},{7,23},{8,24},{9,... | collective-permute-start | bytes 4718600 | tf_op jit(solution)/shard_map/ppermute | solution.py:24
  132.8 40.6 %collective-permute-start.20 = (bf16[128,6144]{1,0:T(8,128)(2,1)}, bf16[128,6144]{1,0:T(8,128)(2,1)}, u32[]{:S(2)}, u32[]{:S(2)}) collective-permute-start(bf16[128,6144]{1,0:T(8,128)(2,1)} %collective-permute-done.19.rows), channel_id=1, source_target_pairs={{0,16},{1,17},{2,18},{3,19},{4,20},{5,21},{6,22},{7,23},{8,24},{9,... | collective-permute-start | bytes 4718600 | tf_op jit(solution)/shard_map/ppermute | solution.py:24
  136.8 41.1 %collective-permute-start.18 = (bf16[128,6144]{1,0:T(8,128)(2,1)}, bf16[128,6144]{1,0:T(8,128)(2,1)}, u32[]{:S(2)}, u32[]{:S(2)}) collective-permute-start(bf16[128,6144]{1,0:T(8,128)(2,1)} %collective-permute-done.17.rows), channel_id=1, source_target_pairs={{0,16},{1,17},{2,18},{3,19},{4,20},{5,21},{6,22},{7,23},{8,24},{9,... | collective-permute-start | bytes 4718600 | tf_op jit(solution)/shard_map/ppermute | solution.py:24
  185.0 5.3 %collective-permute-start.26 = (f32[24,128]{1,0:T(8,128)S(1)}, f32[24,128]{1,0:T(8,128)S(1)}, u32[]{:S(2)}, u32[]{:S(2)}) collective-permute-start(f32[24,128]{1,0:T(8,128)S(1)} %merge.3.refs_0_), channel_id=1, source_target_pairs={{0,64},{1,65},{2,66},{3,67},{4,68},{5,69},{6,70},{7,71},{8,72},{9,... | collective-permute-start | bytes 36872 | tf_op jit(solution)/shard_map/ppermute | solution.py:24
  185.7 4.5 %collective-permute-start.25 = (f32[24,128]{1,0:T(8,128)S(1)}, f32[24,128]{1,0:T(8,128)S(1)}, u32[]{:S(2)}, u32[]{:S(2)}) collective-permute-start(f32[24,128]{1,0:T(8,128)S(1)} %merge.3.refs_0_), channel_id=1, source_target_pairs={{0,96},{1,97},{2,98},{3,99},{4,100},{5,101},{6,102},{7,103},{8,104... | collective-permute-start | bytes 36872 | tf_op jit(solution)/shard_map/ppermute | solution.py:24
  187.6 4.9 %collective-permute-start.24 = (f32[24,128]{1,0:T(8,128)S(1)}, f32[24,128]{1,0:T(8,128)S(1)}, u32[]{:S(2)}, u32[]{:S(2)}) collective-permute-start(f32[24,128]{1,0:T(8,128)S(1)} %merge.3.refs_0_), channel_id=1, source_target_pairs={{0,32},{1,33},{2,34},{3,35},{4,36},{5,37},{6,38},{7,39},{8,40},{9,... | collective-permute-start | bytes 36872 | tf_op jit(solution)/shard_map/ppermute | solution.py:24
  193.1 5.3 %collective-permute-start.29 = (f32[24,128]{1,0:T(8,128)S(1)}, f32[24,128]{1,0:T(8,128)S(1)}, u32[]{:S(2)}, u32[]{:S(2)}) collective-permute-start(f32[24,128]{1,0:T(8,128)S(1)} %merge.4.refs_0_), channel_id=1, source_target_pairs={{0,8},{1,9},{2,10},{3,11},{4,12},{5,13},{6,14},{7,15},{8,0},{9,1},... | collective-permute-start | bytes 36872 | tf_op jit(solution)/shard_map/ppermute | solution.py:24
  193.5 4.8 %collective-permute-start.28 = (f32[24,128]{1,0:T(8,128)S(1)}, f32[24,128]{1,0:T(8,128)S(1)}, u32[]{:S(2)}, u32[]{:S(2)}) collective-permute-start(f32[24,128]{1,0:T(8,128)S(1)} %merge.4.refs_0_), channel_id=1, source_target_pairs={{0,12},{1,13},{2,14},{3,15},{4,0},{5,1},{6,2},{7,3},{8,4},{9,5},{1... | collective-permute-start | bytes 36872 | tf_op jit(solution)/shard_map/ppermute | solution.py:24
  194.7 4.9 %collective-permute-start.27 = (f32[24,128]{1,0:T(8,128)S(1)}, f32[24,128]{1,0:T(8,128)S(1)}, u32[]{:S(2)}, u32[]{:S(2)}) collective-permute-start(f32[24,128]{1,0:T(8,128)S(1)} %merge.4.refs_0_), channel_id=1, source_target_pairs={{0,4},{1,5},{2,6},{3,7},{4,8},{5,9},{6,10},{7,11},{8,12},{9,13},{1... | collective-permute-start | bytes 36872 | tf_op jit(solution)/shard_map/ppermute | solution.py:24
  200.2 5.3 %collective-permute-start.32 = (f32[24,128]{1,0:T(8,128)S(1)}, f32[24,128]{1,0:T(8,128)S(1)}, u32[]{:S(2)}, u32[]{:S(2)}) collective-permute-start(f32[24,128]{1,0:T(8,128)S(1)} %merge.5.refs_0_), channel_id=1, source_target_pairs={{0,2},{1,3},{2,0},{3,1},{4,6},{5,7},{6,4},{7,5},{8,10},{9,11},{10,... | collective-permute-start | bytes 36872 | tf_op jit(solution)/shard_map/ppermute | solution.py:24
  201.7 3.8 %collective-permute-start.31 = (f32[24,128]{1,0:T(8,128)S(1)}, f32[24,128]{1,0:T(8,128)S(1)}, u32[]{:S(2)}, u32[]{:S(2)}) collective-permute-start(f32[24,128]{1,0:T(8,128)S(1)} %merge.5.refs_0_), channel_id=1, source_target_pairs={{0,3},{1,0},{2,1},{3,2},{4,7},{5,4},{6,5},{7,6},{8,11},{9,8},{10,9... | collective-permute-start | bytes 36872 | tf_op jit(solution)/shard_map/ppermute | solution.py:24
  202.9 4.9 %collective-permute-start.30 = (f32[24,128]{1,0:T(8,128)S(1)}, f32[24,128]{1,0:T(8,128)S(1)}, u32[]{:S(2)}, u32[]{:S(2)}) collective-permute-start(f32[24,128]{1,0:T(8,128)S(1)} %merge.5.refs_0_), channel_id=1, source_target_pairs={{0,1},{1,2},{2,3},{3,0},{4,5},{5,6},{6,7},{7,4},{8,9},{9,10},{10,1... | collective-permute-start | bytes 36872 | tf_op jit(solution)/shard_map/ppermute | solution.py:24
  (18 other events, 121.2 us)

commit v3 on v2

--- a/solution.py
+++ b/solution.py
@@ -60,23 +60,40 @@
     return pltpu.with_memory_space_constraint(array, pltpu.VMEM)
 
 
+ANYWHERE = pl.BlockSpec(memory_space=pl.ANY)
 SCALARS = pl.BlockSpec(memory_space=pltpu.SMEM)
 WHOLE = pl.BlockSpec(memory_space=pltpu.VMEM)
 
 
-def local(kernel, outs, scalars, *arrays, scratch=(), flops=0, bytes_=0, name=None):
+def local(kernel, outs, scalars, *arrays, unread=(), scratch=(), flops=0, bytes_=0, mib=4, name=None):
     many = isinstance(outs, list)
     specs = [WHOLE] * len(outs) if many else WHOLE
     return pl.pallas_call(
         kernel,
         out_shape=outs,
-        in_specs=[SCALARS] + [WHOLE] * len(arrays),
+        in_specs=[SCALARS] + [WHOLE] * len(arrays) + [ANYWHERE] * len(unread),
         out_specs=specs,
         scratch_shapes=list(scratch),
-        compiler_params=pltpu.CompilerParams(vmem_limit_bytes=16 * 1024 * 1024),
+        compiler_params=pltpu.CompilerParams(vmem_limit_bytes=mib * 1024 * 1024),
         cost_estimate=pl.CostEstimate(flops=flops, bytes_accessed=bytes_, transcendentals=0),
         name=name,
-    )(scalars, *[pin(a) for a in arrays])
+    )(scalars, *[pin(a) for a in (*arrays, *unread)])
+
+
+def tie_kernel(a, b, out_a, out_b):
+    pass
+
+
+def tie(a, b):
+    return pl.pallas_call(
+        tie_kernel,
+        out_shape=[on_chip(a.shape, a.dtype), on_chip(b.shape, b.dtype)],
+        in_specs=[ANYWHERE] * 2,
+        out_specs=[ANYWHERE] * 2,
+        input_output_aliases={0: 0, 1: 1},
+        compiler_params=pltpu.CompilerParams(vmem_limit_bytes=1024 * 1024),
+        name="tie",
+    )(pin(a), pin(b))
 
 
 def project_kernel(at, heads, weight, own, one, two, three, rolled):
@@ -139,22 +156,15 @@
         block,
         *parts,
         bytes_=16 * rows * width,
+        mib=8,
         name=name,
     )
 
 
-def score_kernel(shift, own, at, targets, rows, weight, out, logits):
+def score_kernel(shift, own, at, targets, logits, rows, out):
     x = at[0]
     p, q, core = (at[4], at[5], at[1]) if own else (at[5], at[4], 1 - at[1])
-    n_rows, width = rows.shape[0], weight.shape[1]
-    tile = 256
-
-    def step(n, carry):
-        cols = pl.ds(pl.multiple_of(n * tile, tile), tile)
-        logits[:, cols] = jnp.dot(rows[...], weight[:, cols], preferred_element_type=F32)
-        return carry
-
-    lax.fori_loop(0, width // tile, step, 0)
+    n_rows = rows.shape[0]
     i = lax.broadcasted_iota(jnp.int32, (n_rows, n_rows), 0)
     j = lax.broadcasted_iota(jnp.int32, (n_rows, n_rows), 1)
     lands = (
@@ -301,6 +311,7 @@
         scratch=[pltpu.VMEM(flat_heads.shape, BF16)],
         flops=2 * rows_here * flat_heads.shape[1] * width,
         bytes_=2 * width * (flat_heads.shape[1] + rows_here),
+        mib=16,
         name="project",
     )
     came = [move(part, along_p(s)) for s, part in zip((1, 2, 3), sent)]
@@ -312,6 +323,7 @@
         *came,
         scratch=[pltpu.VMEM((32, width), F32)],
         bytes_=32 * width * 8,
+        mib=8,
         name="partial",
     )
     came = [move(part, along_q(s)) for s, part in zip((1, 2, 3), sent)]
@@ -331,7 +343,7 @@
     on_x = gather(final_rows, along_x, scalars, "stack_x")
     ours = gather(on_x, along_p, scalars, "stack_p")
     theirs = move(ours, other_core)
-    ours, theirs = lax.optimization_barrier((ours, theirs))
+    ours, theirs = tie(ours, theirs)
     lines = jnp.transpose(targets.reshape(X, CORE, 4, 4, 8), (1, 3, 2, 0, 4)).reshape(8, 128)
     pairs = [(ours, theirs)]
     for s in (1, 3, 2):
@@ -341,17 +353,16 @@
     found = []
     for s, pair in enumerate(pairs):
         for mine_too, block in zip((True, False), pair):
+            logits = jnp.dot(block, vocab_weight, preferred_element_type=F32)
             found.append(
                 local(
                     functools.partial(score_kernel, s, mine_too),
                     on_chip((8, 128), F32),
                     scalars,
                     lines,
-                    block,
-                    vocab_weight,
-                    scratch=[pltpu.VMEM((128, vocab_local), F32)],
-                    flops=2 * 128 * width * vocab_local,
-                    bytes_=2 * width * (128 + vocab_local),
+                    logits,
+                    unread=(block,),
+                    bytes_=4 * 128 * vocab_local,
                     name="score",
                 )
             )

time: 210 us -> 181 us (0.86)
  Pallas kernels: 45.6 us -> 20.5 us
  matrix products: 9.97 us -> 31.1 us
  waiting for transfers between devices: 85.6 us -> 71.4 us
  local copies, waits for them, and re-layouts: 19.1 us -> 6.19 us
  starting transfers between devices: 44 us -> 46.1 us
    pallas_call x18, Pallas kernels: 45.6 us -> 20.5 us  [local(): pl.pallas_call(kernel, out_shape=outs, in_specs=[SCALARS] + [WHOLE] * len...]
    dot_general x0 -> x8, matrix products: none -> 21.1 us  [shards(): logits = jnp.dot(block, vocab_weight, preferred_element_type=F32)]
    ppermute x33, waiting for transfers between devices: 85.6 us -> 71.4 us  [move(): return lax.ppermute(array, ALL, pairs)]
    unnamed x34 -> x28, local copies, waits for them, and re-layouts: 18.2 us -> 5.28 us
  transfers between devices with their start and end apart: 33 -> 33, of which waited for: 20 -> 20; matrix products, arithmetic and copies ran while one was open for 4% -> 15% of each run, Pallas kernels for 14% -> 4%
where the time goes in v3:
time: 181 us; the launch traced here: 180 us
  waiting for transfers between devices  71.4 us (39%)
  starting transfers between devices  46.1 us (25%)
  matrix products  31.1 us (17%)
  Pallas kernels  20.5 us (11%)
  local copies, waits for them, and re-layouts  6.19 us (3%)
  other arithmetic  4.65 us (3%)
    ppermute x33, waiting for transfers between devices, move(): return lax.ppermute(array, ALL, pairs)  71.4 us
    ppermute x33, starting transfers between devices, move(): return lax.ppermute(array, ALL, pairs)  46.1 us
    dot_general x8, matrix products, shards(): logits = jnp.dot(block, vocab_weight, preferred_element_type=F32)  21.1 us
    pallas_call x18, Pallas kernels, local(): pl.pallas_call(kernel, out_shape=outs, in_specs=[SCALARS] + [WHOLE] * len...  20.5 us
    unnamed x28, local copies, waits for them, and re-layouts  5.28 us
  transfers between devices with their start and end apart: 33, of which 20 were waited for; matrix products, arithmetic and copies ran while one was open for 15% of the time, Pallas kernels for 4%

profile of v3, /device:TPU:0, one launch (start us, length us, event | category | flops | bytes accessed | tf_op | source)
XLA Modules:
  0.0 180.2 jit_solution(14677282967312544828)
XLA Ops:
  1.9 2.1 %fusion.3 = bf16[16,2,8,128]{3,2,1,0:T(8,128)(2,1)S(1)} fusion(bf16[128,6144]{1,0:T(8,128)(2,1)} %param.10, bf16[6144,256]{1,0:T(8,128)(2,1)S(1)} %copy-done), kind=kOutput, calls=%fused_computation.9 | convolution fusion | flops 402685952 | bytes 4784128 | tf_op jit(solution)/shard_map/dot_general | solution.py:262
  6.4 2.9 %fusion.4 = bf16[16,2,8,128]{3,2,1,0:T(8,128)(2,1)S(1)} fusion(bf16[128,6144]{1,0:T(8,128)(2,1)} %param.10, bf16[6144,256]{1,0:T(8,128)(2,1)} %param.13), kind=kOutput, calls=%fused_computation.10 | convolution fusion | flops 402685952 | bytes 4784128 | tf_op jit(solution)/shard_map/dot_general | solution.py:285
  11.8 5.4 %collective-permute-start.3 = (f32[2,136,128]{2,1,0:T(8,128)}, f32[2,136,128]{2,1,0:T(8,128)}, u32[]{:S(2)}, u32[]{:S(2)}) collective-permute-start(f32[2,136,128]{2,1,0:T(8,128)} %pad_maximum_fusion.1), channel_id=1, source_target_pairs={{0,96},{1,97},{2,98},{3,99},{4,100},{5,101},{6,102},{7,103},{8,104... | collective-permute-start | bytes 417800 | tf_op jit(solution)/shard_map/ppermute | solution.py:24
  17.2 1.8 %convolution_bitcast_fusion.1 = f32[128,2,128]{0,2,1:T(8,128)} fusion(bf16[128,2,128]{0,2,1:T(8,128)(2,1)} %bitcast.71, f32[2,128]{1,0:T(2,128)} %bitcast.77, pred[128,128]{1,0:T(8,128)(4,1)} %iota_compare_fusion, bf16[16,2,8,128]{3,2,1,0:T(8,128)(2,1)S(1)} %fusion.4, bf16[16,2,8,128]{3,2,1,0:T(8,128)(2,1)S(1)} %fusion.3), kind=kOutput, calls=%fused_computation.2 | convolution fusion | flops 16908288 | bytes 345088 | tf_op jit(solution)/shard_map/hts,shd->thd/dot_general | solution.py:289
  20.3 2.1 %collective-permute-start.1 = (f32[2,136,128]{2,1,0:T(8,128)}, f32[2,136,128]{2,1,0:T(8,128)S(1)}, u32[]{:S(2)}, u32[]{:S(2)}) collective-permute-start(f32[2,136,128]{2,1,0:T(8,128)} %pad_maximum_fusion.1), channel_id=1, source_target_pairs={{0,32},{1,33},{2,34},{3,35},{4,36},{5,37},{6,38},{7,39},{8,40},{9,... | collective-permute-start | bytes 417800 | tf_op jit(solution)/shard_map/ppermute | solution.py:24
  24.6 2.6 %collective-permute-done.1 = f32[2,136,128]{2,1,0:T(8,128)S(1)} collective-permute-done((f32[2,136,128]{2,1,0:T(8,128)}, f32[2,136,128]{2,1,0:T(8,128)S(1)}, u32[]{:S(2)}, u32[]{:S(2)}) %collective-permute-start.1) | collective-permute-done | bytes 139296 | tf_op jit(solution)/shard_map/ppermute | solution.py:24
  28.7 1.9 %copy-done.1 = bf16[256,6144]{1,0:T(8,128)(2,1)S(1)} copy-done((bf16[256,6144]{1,0:T(8,128)(2,1)S(1)}, bf16[256,6144]{1,0:T(8,128)(2,1)}, u32[]{:S(2)}) %copy-start.1) | copy-done | bytes 3145752
  30.6 3.9 %project.1 = (f32[32,6144]{1,0:T(8,128)S(1)}, bf16[32,6144]{1,0:T(8,128)(2,1)}, bf16[32,6144]{1,0:T(8,128)(2,1)}, bf16[32,6144]{1,0:T(8,128)(2,1)}) custom-call(s32[8]{0:T(128)S(1)} %stack.32.at, bf16[128,256]{1,0:T(8,128)(2,1)S(1)} %copy.28.heads, bf16[256,6144]{1,0:T(8,128)(2,1)S(1)} %copy-done.1), custom_call_target="tpu_custom_call" | custom-call | flops 402653184 | bytes 4718592 | tf_op jit(solution)/shard_map/project/pallas_call | solution.py:71
  37.0 2.9 %collective-permute-start.5 = (bf16[32,6144]{1,0:T(8,128)(2,1)}, bf16[32,6144]{1,0:T(8,128)(2,1)}, u32[]{:S(2)}, u32[]{:S(2)}) collective-permute-start(bf16[32,6144]{1,0:T(8,128)(2,1)} %get-tuple-element.17), channel_id=1, source_target_pairs={{0,2},{1,3},{2,0},{3,1},{4,6},{5,7},{6,4},{7,5},{8,10},{9,11},{10,... | collective-permute-start | bytes 1179656 | tf_op jit(solution)/shard_map/ppermute | solution.py:24
  41.2 3.4 %collective-permute-done.4.one = bf16[32,6144]{1,0:T(8,128)(2,1)S(1)} collective-permute-done((bf16[32,6144]{1,0:T(8,128)(2,1)}, bf16[32,6144]{1,0:T(8,128)(2,1)S(1)}, u32[]{:S(2)}, u32[]{:S(2)}) %collective-permute-start.4) | collective-permute-done | bytes 393248 | tf_op jit(solution)/shard_map/ppermute | solution.py:24
  44.6 5.6 %collective-permute-done.5.two = bf16[32,6144]{1,0:T(8,128)(2,1)} collective-permute-done((bf16[32,6144]{1,0:T(8,128)(2,1)}, bf16[32,6144]{1,0:T(8,128)(2,1)}, u32[]{:S(2)}, u32[]{:S(2)}) %collective-permute-start.5) | collective-permute-done | bytes 393248 | tf_op jit(solution)/shard_map/ppermute | solution.py:24
  52.7 2.0 %collective-permute-start.7 = (bf16[8,6144]{1,0:T(8,128)(2,1)S(1)}, bf16[8,6144]{1,0:T(8,128)(2,1)S(1)}, u32[]{:S(2)}, u32[]{:S(2)}) collective-permute-start(bf16[8,6144]{1,0:T(8,128)(2,1)S(1)} %get-tuple-element.20), channel_id=1, source_target_pairs={{0,4},{1,5},{2,6},{3,7},{4,8},{5,9},{6,10},{7,11},{8,12},{9,13},{1... | collective-permute-start | bytes 294920 | tf_op jit(solution)/shard_map/ppermute | solution.py:24
  54.7 3.6 %collective-permute-start.8 = (bf16[8,6144]{1,0:T(8,128)(2,1)S(1)}, bf16[8,6144]{1,0:T(8,128)(2,1)S(1)}, u32[]{:S(2)}, u32[]{:S(2)}) collective-permute-start(bf16[8,6144]{1,0:T(8,128)(2,1)S(1)} %get-tuple-element.21), channel_id=1, source_target_pairs={{0,8},{1,9},{2,10},{3,11},{4,12},{5,13},{6,14},{7,15},{8,0},{9,1},... | collective-permute-start | bytes 294920 | tf_op jit(solution)/shard_map/ppermute | solution.py:24
  63.9 4.2 %collective-permute-start.11 = (bf16[8,6144]{1,0:T(8,128)(2,1)S(1)}, bf16[8,6144]{1,0:T(8,128)(2,1)S(1)}, u32[]{:S(2)}, u32[]{:S(2)}) collective-permute-start(bf16[8,6144]{1,0:T(8,128)(2,1)S(1)} %norm.1.a), channel_id=1, source_target_pairs={{0,64},{1,65},{2,66},{3,67},{4,68},{5,69},{6,70},{7,71},{8,72},{9,... | collective-permute-start | bytes 294920 | tf_op jit(solution)/shard_map/ppermute | solution.py:24
  70.8 3.2 %collective-permute-done.10.b = bf16[8,6144]{1,0:T(8,128)(2,1)S(1)} collective-permute-done((bf16[8,6144]{1,0:T(8,128)(2,1)S(1)}, bf16[8,6144]{1,0:T(8,128)(2,1)S(1)}, u32[]{:S(2)}, u32[]{:S(2)}) %collective-permute-start.10) | collective-permute-done | bytes 98336 | tf_op jit(solution)/shard_map/ppermute | solution.py:24
  74.6 2.4 %collective-permute-start.15 = (bf16[32,6144]{1,0:T(8,128)(2,1)S(1)}, bf16[32,6144]{1,0:T(8,128)(2,1)S(1)}, u32[]{:S(2)}, u32[]{:S(2)}) collective-permute-start(bf16[32,6144]{1,0:T(8,128)(2,1)S(1)} %stack_x.1.a), channel_id=1, source_target_pairs={{0,3},{1,0},{2,1},{3,2},{4,7},{5,4},{6,5},{7,6},{8,11},{9,8},{10,9... | collective-permute-start | bytes 1179656 | tf_op jit(solution)/shard_map/ppermute | solution.py:24
  78.9 7.6 %collective-permute-done.15.d = bf16[32,6144]{1,0:T(8,128)(2,1)S(1)} collective-permute-done((bf16[32,6144]{1,0:T(8,128)(2,1)S(1)}, bf16[32,6144]{1,0:T(8,128)(2,1)S(1)}, u32[]{:S(2)}, u32[]{:S(2)}) %collective-permute-start.15) | collective-permute-done | bytes 393248 | tf_op jit(solution)/shard_map/ppermute | solution.py:24
  86.5 3.9 %collective-permute-done.13.b = bf16[32,6144]{1,0:T(8,128)(2,1)S(1)} collective-permute-done((bf16[32,6144]{1,0:T(8,128)(2,1)S(1)}, bf16[32,6144]{1,0:T(8,128)(2,1)S(1)}, u32[]{:S(2)}, u32[]{:S(2)}) %collective-permute-start.13) | collective-permute-done | bytes 393248 | tf_op jit(solution)/shard_map/ppermute | solution.py:24
  90.5 1.8 %stack_p.1.a = bf16[128,6144]{1,0:T(8,128)(2,1)} custom-call(s32[8]{0:T(128)S(1)} %stack.32.at, bf16[32,6144]{1,0:T(8,128)(2,1)S(1)} %stack_x.1.a, bf16[32,6144]{1,0:T(8,128)(2,1)S(1)} %collective-permute-done.13.b, bf16[32,6144]{1,0:T(8,128)(2,1)S(1)} %collective-permute-done.14.c, bf16[32,6144]{1,0:T(8,128)(2,1)S(1)} %collective-permute-done.15.d), custom_call_target="tpu_custom_call" | custom-call | bytes 3145728 | tf_op jit(solution)/shard_map/stack_p/pallas_call | solution.py:71
  92.6 3.5 %collective-permute-done.16.b = bf16[128,6144]{1,0:T(8,128)(2,1)} collective-permute-done((bf16[128,6144]{1,0:T(8,128)(2,1)}, bf16[128,6144]{1,0:T(8,128)(2,1)}, u32[]{:S(2)}, u32[]{:S(2)}) %collective-permute-start.16) | collective-permute-done | bytes 1572896 | tf_op jit(solution)/shard_map/ppermute | solution.py:24
  96.0 2.2 %collective-permute-start.21 = (bf16[128,6144]{1,0:T(8,128)(2,1)}, bf16[128,6144]{1,0:T(8,128)(2,1)S(1)}, u32[]{:S(2)}, u32[]{:S(2)}) collective-permute-start(bf16[128,6144]{1,0:T(8,128)(2,1)} %get-tuple-element.23.rows), channel_id=1, source_target_pairs={{0,12},{1,13},{2,14},{3,15},{4,0},{5,1},{6,2},{7,3},{8,4},{9,5},{1... | collective-permute-start | bytes 4718600 | tf_op jit(solution)/shard_map/ppermute | solution.py:24
  99.1 7.0 %fusion.42.logits = f32[128,1024]{1,0:T(8,128)S(1)} fusion(bf16[128,6144]{1,0:T(8,128)(2,1)} %get-tuple-element.24.rows, bf16[6144,1024]{1,0:T(8,128)(2,1)} %param.18), kind=kOutput, calls=%fused_computation.65 | convolution fusion | flops 1610612736 | bytes 14680064 | tf_op jit(solution)/shard_map/dot_general | solution.py:356
  107.2 3.2 %fusion.41.logits = f32[128,1024]{1,0:T(8,128)S(1)} fusion(bf16[128,6144]{1,0:T(8,128)(2,1)} %get-tuple-element.23.rows, bf16[6144,1024]{1,0:T(8,128)(2,1)S(1)} %bitcast.67), kind=kOutput, calls=%fused_computation.64 | convolution fusion | flops 1610612736 | bytes 14680064 | tf_op jit(solution)/shard_map/dot_general | solution.py:356
  111.4 21.9 %collective-permute-done.21.rows = bf16[128,6144]{1,0:T(8,128)(2,1)S(1)} collective-permute-done((bf16[128,6144]{1,0:T(8,128)(2,1)}, bf16[128,6144]{1,0:T(8,128)(2,1)S(1)}, u32[]{:S(2)}, u32[]{:S(2)}) %collective-permute-start.21) | collective-permute-done | bytes 1572896 | tf_op jit(solution)/shard_map/ppermute | solution.py:24
  133.4 1.8 %fusion.47.logits = f32[128,1024]{1,0:T(8,128)S(1)} fusion(bf16[128,6144]{1,0:T(8,128)(2,1)S(1)} %collective-permute-done.21.rows, bf16[6144,1024]{1,0:T(8,128)(2,1)S(1)} %bitcast.67), kind=kOutput, calls=%fused_computation.70 | convolution fusion | flops 1610612736 | bytes 14680064 | tf_op jit(solution)/shard_map/dot_general | solution.py:356
  136.8 1.9 %fusion.45.logits = f32[128,1024]{1,0:T(8,128)S(1)} fusion(bf16[128,6144]{1,0:T(8,128)(2,1)S(1)} %collective-permute-done.19.rows, bf16[6144,1024]{1,0:T(8,128)(2,1)S(1)} %bitcast.67), kind=kOutput, calls=%fused_computation.68 | convolution fusion | flops 1610612736 | bytes 14680064 | tf_op jit(solution)/shard_map/dot_general | solution.py:356
  154.7 1.9 %collective-permute-start.25 = (f32[24,128]{1,0:T(8,128)S(1)}, f32[24,128]{1,0:T(8,128)S(1)}, u32[]{:S(2)}, u32[]{:S(2)}) collective-permute-start(f32[24,128]{1,0:T(8,128)S(1)} %merge.3.refs_0_), channel_id=1, source_target_pairs={{0,96},{1,97},{2,98},{3,99},{4,100},{5,101},{6,102},{7,103},{8,104... | collective-permute-start | bytes 36872 | tf_op jit(solution)/shard_map/ppermute | solution.py:24
  156.7 2.5 %collective-permute-done.26.refs_3_ = f32[24,128]{1,0:T(8,128)S(1)} collective-permute-done((f32[24,128]{1,0:T(8,128)S(1)}, f32[24,128]{1,0:T(8,128)S(1)}, u32[]{:S(2)}, u32[]{:S(2)}) %collective-permute-start.26) | collective-permute-done | bytes 12320 | tf_op jit(solution)/shard_map/ppermute | solution.py:24
  159.2 2.3 %collective-permute-done.24.refs_1_ = f32[24,128]{1,0:T(8,128)S(1)} collective-permute-done((f32[24,128]{1,0:T(8,128)S(1)}, f32[24,128]{1,0:T(8,128)S(1)}, u32[]{:S(2)}, u32[]{:S(2)}) %collective-permute-start.24) | collective-permute-done | bytes 12320 | tf_op jit(solution)/shard_map/ppermute | solution.py:24
  162.1 3.6 %collective-permute-start.28 = (f32[24,128]{1,0:T(8,128)S(1)}, f32[24,128]{1,0:T(8,128)S(1)}, u32[]{:S(2)}, u32[]{:S(2)}) collective-permute-start(f32[24,128]{1,0:T(8,128)S(1)} %merge.4.refs_0_), channel_id=1, source_target_pairs={{0,12},{1,13},{2,14},{3,15},{4,0},{5,1},{6,2},{7,3},{8,4},{9,5},{1... | collective-permute-start | bytes 36872 | tf_op jit(solution)/shard_map/ppermute | solution.py:24
  168.3 2.3 %collective-permute-done.27.refs_1_ = f32[24,128]{1,0:T(8,128)S(1)} collective-permute-done((f32[24,128]{1,0:T(8,128)S(1)}, f32[24,128]{1,0:T(8,128)S(1)}, u32[]{:S(2)}, u32[]{:S(2)}) %collective-permute-start.27) | collective-permute-done | bytes 12320 | tf_op jit(solution)/shard_map/ppermute | solution.py:24
  176.5 2.3 %collective-permute-done.30.refs_1_ = f32[24,128]{1,0:T(8,128)S(1)} collective-permute-done((f32[24,128]{1,0:T(8,128)S(1)}, f32[24,128]{1,0:T(8,128)S(1)}, u32[]{:S(2)}, u32[]{:S(2)}) %collective-permute-start.30) | collective-permute-done | bytes 12320 | tf_op jit(solution)/shard_map/ppermute | solution.py:24
  (122 shorter events, 60.1 us)
Async XLA Ops:
  6.4 3.7 %collective-permute-start = (f32[2,136,128]{2,1,0:T(8,128)}, f32[2,136,128]{2,1,0:T(8,128)}, u32[]{:S(2)}, u32[]{:S(2)}) collective-permute-start(f32[2,136,128]{2,1,0:T(8,128)} %pad_maximum_fusion), channel_id=1, source_target_pairs={{0,16},{1,17},{2,18},{3,19},{4,20},{5,21},{6,22},{7,23},{8,24},{9,... | collective-permute-start | bytes 417800 | tf_op jit(solution)/shard_map/ppermute | solution.py:24
  11.8 10.6 %collective-permute-start.3 = (f32[2,136,128]{2,1,0:T(8,128)}, f32[2,136,128]{2,1,0:T(8,128)}, u32[]{:S(2)}, u32[]{:S(2)}) collective-permute-start(f32[2,136,128]{2,1,0:T(8,128)} %pad_maximum_fusion.1), channel_id=1, source_target_pairs={{0,96},{1,97},{2,98},{3,99},{4,100},{5,101},{6,102},{7,103},{8,104... | collective-permute-start | bytes 417800 | tf_op jit(solution)/shard_map/ppermute | solution.py:24
  19.0 5.6 %collective-permute-start.2 = (f32[2,136,128]{2,1,0:T(8,128)}, f32[2,136,128]{2,1,0:T(8,128)S(1)}, u32[]{:S(2)}, u32[]{:S(2)}) collective-permute-start(f32[2,136,128]{2,1,0:T(8,128)} %pad_maximum_fusion.1), channel_id=1, source_target_pairs={{0,64},{1,65},{2,66},{3,67},{4,68},{5,69},{6,70},{7,71},{8,72},{9,... | collective-permute-start | bytes 417800 | tf_op jit(solution)/shard_map/ppermute | solution.py:24
  20.3 6.9 %collective-permute-start.1 = (f32[2,136,128]{2,1,0:T(8,128)}, f32[2,136,128]{2,1,0:T(8,128)S(1)}, u32[]{:S(2)}, u32[]{:S(2)}) collective-permute-start(f32[2,136,128]{2,1,0:T(8,128)} %pad_maximum_fusion.1), channel_id=1, source_target_pairs={{0,32},{1,33},{2,34},{3,35},{4,36},{5,37},{6,38},{7,39},{8,40},{9,... | collective-permute-start | bytes 417800 | tf_op jit(solution)/shard_map/ppermute | solution.py:24
  35.4 9.2 %collective-permute-start.4 = (bf16[32,6144]{1,0:T(8,128)(2,1)}, bf16[32,6144]{1,0:T(8,128)(2,1)S(1)}, u32[]{:S(2)}, u32[]{:S(2)}) collective-permute-start(bf16[32,6144]{1,0:T(8,128)(2,1)} %get-tuple-element.16), channel_id=1, source_target_pairs={{0,1},{1,2},{2,3},{3,0},{4,5},{5,6},{6,7},{7,4},{8,9},{9,10},{10,1... | collective-permute-start | bytes 1179656 | tf_op jit(solution)/shard_map/ppermute | solution.py:24
  37.0 13.2 %collective-permute-start.5 = (bf16[32,6144]{1,0:T(8,128)(2,1)}, bf16[32,6144]{1,0:T(8,128)(2,1)}, u32[]{:S(2)}, u32[]{:S(2)}) collective-permute-start(bf16[32,6144]{1,0:T(8,128)(2,1)} %get-tuple-element.17), channel_id=1, source_target_pairs={{0,2},{1,3},{2,0},{3,1},{4,6},{5,7},{6,4},{7,5},{8,10},{9,11},{10,... | collective-permute-start | bytes 1179656 | tf_op jit(solution)/shard_map/ppermute | solution.py:24
  39.9 10.3 %collective-permute-start.6 = (bf16[32,6144]{1,0:T(8,128)(2,1)}, bf16[32,6144]{1,0:T(8,128)(2,1)}, u32[]{:S(2)}, u32[]{:S(2)}) collective-permute-start(bf16[32,6144]{1,0:T(8,128)(2,1)} %get-tuple-element.18), channel_id=1, source_target_pairs={{0,3},{1,0},{2,1},{3,2},{4,7},{5,4},{6,5},{7,6},{8,11},{9,8},{10,9... | collective-permute-start | bytes 1179656 | tf_op jit(solution)/shard_map/ppermute | solution.py:24
  52.7 7.5 %collective-permute-start.7 = (bf16[8,6144]{1,0:T(8,128)(2,1)S(1)}, bf16[8,6144]{1,0:T(8,128)(2,1)S(1)}, u32[]{:S(2)}, u32[]{:S(2)}) collective-permute-start(bf16[8,6144]{1,0:T(8,128)(2,1)S(1)} %get-tuple-element.20), channel_id=1, source_target_pairs={{0,4},{1,5},{2,6},{3,7},{4,8},{5,9},{6,10},{7,11},{8,12},{9,13},{1... | collective-permute-start | bytes 294920 | tf_op jit(solution)/shard_map/ppermute | solution.py:24
  54.7 7.2 %collective-permute-start.8 = (bf16[8,6144]{1,0:T(8,128)(2,1)S(1)}, bf16[8,6144]{1,0:T(8,128)(2,1)S(1)}, u32[]{:S(2)}, u32[]{:S(2)}) collective-permute-start(bf16[8,6144]{1,0:T(8,128)(2,1)S(1)} %get-tuple-element.21), channel_id=1, source_target_pairs={{0,8},{1,9},{2,10},{3,11},{4,12},{5,13},{6,14},{7,15},{8,0},{9,1},... | collective-permute-start | bytes 294920 | tf_op jit(solution)/shard_map/ppermute | solution.py:24
  58.3 4.6 %collective-permute-start.9 = (bf16[8,6144]{1,0:T(8,128)(2,1)S(1)}, bf16[8,6144]{1,0:T(8,128)(2,1)S(1)}, u32[]{:S(2)}, u32[]{:S(2)}) collective-permute-start(bf16[8,6144]{1,0:T(8,128)(2,1)S(1)} %get-tuple-element.22), channel_id=1, source_target_pairs={{0,12},{1,13},{2,14},{3,15},{4,0},{5,1},{6,2},{7,3},{8,4},{9,5},{1... | collective-permute-start | bytes 294920 | tf_op jit(solution)/shard_map/ppermute | solution.py:24
  63.6 5.3 %collective-permute-start.12 = (bf16[8,6144]{1,0:T(8,128)(2,1)S(1)}, bf16[8,6144]{1,0:T(8,128)(2,1)S(1)}, u32[]{:S(2)}, u32[]{:S(2)}) collective-permute-start(bf16[8,6144]{1,0:T(8,128)(2,1)S(1)} %norm.1.a), channel_id=1, source_target_pairs={{0,96},{1,97},{2,98},{3,99},{4,100},{5,101},{6,102},{7,103},{8,104... | collective-permute-start | bytes 294920 | tf_op jit(solution)/shard_map/ppermute | solution.py:24
  63.9 6.8 %collective-permute-start.11 = (bf16[8,6144]{1,0:T(8,128)(2,1)S(1)}, bf16[8,6144]{1,0:T(8,128)(2,1)S(1)}, u32[]{:S(2)}, u32[]{:S(2)}) collective-permute-start(bf16[8,6144]{1,0:T(8,128)(2,1)S(1)} %norm.1.a), channel_id=1, source_target_pairs={{0,64},{1,65},{2,66},{3,67},{4,68},{5,69},{6,70},{7,71},{8,72},{9,... | collective-permute-start | bytes 294920 | tf_op jit(solution)/shard_map/ppermute | solution.py:24
  68.2 5.8 %collective-permute-start.10 = (bf16[8,6144]{1,0:T(8,128)(2,1)S(1)}, bf16[8,6144]{1,0:T(8,128)(2,1)S(1)}, u32[]{:S(2)}, u32[]{:S(2)}) collective-permute-start(bf16[8,6144]{1,0:T(8,128)(2,1)S(1)} %norm.1.a), channel_id=1, source_target_pairs={{0,32},{1,33},{2,34},{3,35},{4,36},{5,37},{6,38},{7,39},{8,40},{9,... | collective-permute-start | bytes 294920 | tf_op jit(solution)/shard_map/ppermute | solution.py:24
  74.6 11.9 %collective-permute-start.15 = (bf16[32,6144]{1,0:T(8,128)(2,1)S(1)}, bf16[32,6144]{1,0:T(8,128)(2,1)S(1)}, u32[]{:S(2)}, u32[]{:S(2)}) collective-permute-start(bf16[32,6144]{1,0:T(8,128)(2,1)S(1)} %stack_x.1.a), channel_id=1, source_target_pairs={{0,3},{1,0},{2,1},{3,2},{4,7},{5,4},{6,5},{7,6},{8,11},{9,8},{10,9... | collective-permute-start | bytes 1179656 | tf_op jit(solution)/shard_map/ppermute | solution.py:24
  77.0 9.5 %collective-permute-start.14 = (bf16[32,6144]{1,0:T(8,128)(2,1)S(1)}, bf16[32,6144]{1,0:T(8,128)(2,1)S(1)}, u32[]{:S(2)}, u32[]{:S(2)}) collective-permute-start(bf16[32,6144]{1,0:T(8,128)(2,1)S(1)} %stack_x.1.a), channel_id=1, source_target_pairs={{0,2},{1,3},{2,0},{3,1},{4,6},{5,7},{6,4},{7,5},{8,10},{9,11},{10,... | collective-permute-start | bytes 1179656 | tf_op jit(solution)/shard_map/ppermute | solution.py:24
  78.4 12.1 %collective-permute-start.13 = (bf16[32,6144]{1,0:T(8,128)(2,1)S(1)}, bf16[32,6144]{1,0:T(8,128)(2,1)S(1)}, u32[]{:S(2)}, u32[]{:S(2)}) collective-permute-start(bf16[32,6144]{1,0:T(8,128)(2,1)S(1)} %stack_x.1.a), channel_id=1, source_target_pairs={{0,1},{1,2},{2,3},{3,0},{4,5},{5,6},{6,7},{7,4},{8,9},{9,10},{10,1... | collective-permute-start | bytes 1179656 | tf_op jit(solution)/shard_map/ppermute | solution.py:24
  92.3 3.8 %collective-permute-start.16 = (bf16[128,6144]{1,0:T(8,128)(2,1)}, bf16[128,6144]{1,0:T(8,128)(2,1)}, u32[]{:S(2)}, u32[]{:S(2)}) collective-permute-start(bf16[128,6144]{1,0:T(8,128)(2,1)} %stack_p.1.a), channel_id=1, source_target_pairs={{0,16},{1,17},{2,18},{3,19},{4,20},{5,21},{6,22},{7,23},{8,24},{9,... | collective-permute-start | bytes 4718600 | tf_op jit(solution)/shard_map/ppermute | solution.py:24
  96.0 37.3 %collective-permute-start.21 = (bf16[128,6144]{1,0:T(8,128)(2,1)}, bf16[128,6144]{1,0:T(8,128)(2,1)S(1)}, u32[]{:S(2)}, u32[]{:S(2)}) collective-permute-start(bf16[128,6144]{1,0:T(8,128)(2,1)} %get-tuple-element.23.rows), channel_id=1, source_target_pairs={{0,12},{1,13},{2,14},{3,15},{4,0},{5,1},{6,2},{7,3},{8,4},{9,5},{1... | collective-permute-start | bytes 4718600 | tf_op jit(solution)/shard_map/ppermute | solution.py:24
  98.2 38.0 %collective-permute-start.19 = (bf16[128,6144]{1,0:T(8,128)(2,1)}, bf16[128,6144]{1,0:T(8,128)(2,1)S(1)}, u32[]{:S(2)}, u32[]{:S(2)}) collective-permute-start(bf16[128,6144]{1,0:T(8,128)(2,1)} %get-tuple-element.23.rows), channel_id=1, source_target_pairs={{0,8},{1,9},{2,10},{3,11},{4,12},{5,13},{6,14},{7,15},{8,0},{9,1},... | collective-permute-start | bytes 4718600 | tf_op jit(solution)/shard_map/ppermute | solution.py:24
  98.6 41.1 %collective-permute-start.17 = (bf16[128,6144]{1,0:T(8,128)(2,1)}, bf16[128,6144]{1,0:T(8,128)(2,1)S(1)}, u32[]{:S(2)}, u32[]{:S(2)}) collective-permute-start(bf16[128,6144]{1,0:T(8,128)(2,1)} %get-tuple-element.23.rows), channel_id=1, source_target_pairs={{0,4},{1,5},{2,6},{3,7},{4,8},{5,9},{6,10},{7,11},{8,12},{9,13},{1... | collective-permute-start | bytes 4718600 | tf_op jit(solution)/shard_map/ppermute | solution.py:24
  133.4 9.4 %collective-permute-start.22 = (bf16[128,6144]{1,0:T(8,128)(2,1)S(1)}, bf16[128,6144]{1,0:T(8,128)(2,1)S(1)}, u32[]{:S(2)}, u32[]{:S(2)}) collective-permute-start(bf16[128,6144]{1,0:T(8,128)(2,1)S(1)} %collective-permute-done.21.rows), channel_id=1, source_target_pairs={{0,16},{1,17},{2,18},{3,19},{4,20},{5,21},{6,22},{7,23},{8,24},{9,... | collective-permute-start | bytes 4718600 | tf_op jit(solution)/shard_map/ppermute | solution.py:24
  136.3 9.4 %collective-permute-start.20 = (bf16[128,6144]{1,0:T(8,128)(2,1)S(1)}, bf16[128,6144]{1,0:T(8,128)(2,1)S(1)}, u32[]{:S(2)}, u32[]{:S(2)}) collective-permute-start(bf16[128,6144]{1,0:T(8,128)(2,1)S(1)} %collective-permute-done.19.rows), channel_id=1, source_target_pairs={{0,16},{1,17},{2,18},{3,19},{4,20},{5,21},{6,22},{7,23},{8,24},{9,... | collective-permute-start | bytes 4718600 | tf_op jit(solution)/shard_map/ppermute | solution.py:24
  139.7 8.8 %collective-permute-start.18 = (bf16[128,6144]{1,0:T(8,128)(2,1)S(1)}, bf16[128,6144]{1,0:T(8,128)(2,1)S(1)}, u32[]{:S(2)}, u32[]{:S(2)}) collective-permute-start(bf16[128,6144]{1,0:T(8,128)(2,1)S(1)} %collective-permute-done.17.rows), channel_id=1, source_target_pairs={{0,16},{1,17},{2,18},{3,19},{4,20},{5,21},{6,22},{7,23},{8,24},{9,... | collective-permute-start | bytes 4718600 | tf_op jit(solution)/shard_map/ppermute | solution.py:24
  153.9 5.3 %collective-permute-start.26 = (f32[24,128]{1,0:T(8,128)S(1)}, f32[24,128]{1,0:T(8,128)S(1)}, u32[]{:S(2)}, u32[]{:S(2)}) collective-permute-start(f32[24,128]{1,0:T(8,128)S(1)} %merge.3.refs_0_), channel_id=1, source_target_pairs={{0,64},{1,65},{2,66},{3,67},{4,68},{5,69},{6,70},{7,71},{8,72},{9,... | collective-permute-start | bytes 36872 | tf_op jit(solution)/shard_map/ppermute | solution.py:24
  154.7 4.5 %collective-permute-start.25 = (f32[24,128]{1,0:T(8,128)S(1)}, f32[24,128]{1,0:T(8,128)S(1)}, u32[]{:S(2)}, u32[]{:S(2)}) collective-permute-start(f32[24,128]{1,0:T(8,128)S(1)} %merge.3.refs_0_), channel_id=1, source_target_pairs={{0,96},{1,97},{2,98},{3,99},{4,100},{5,101},{6,102},{7,103},{8,104... | collective-permute-start | bytes 36872 | tf_op jit(solution)/shard_map/ppermute | solution.py:24
  156.5 4.9 %collective-permute-start.24 = (f32[24,128]{1,0:T(8,128)S(1)}, f32[24,128]{1,0:T(8,128)S(1)}, u32[]{:S(2)}, u32[]{:S(2)}) collective-permute-start(f32[24,128]{1,0:T(8,128)S(1)} %merge.3.refs_0_), channel_id=1, source_target_pairs={{0,32},{1,33},{2,34},{3,35},{4,36},{5,37},{6,38},{7,39},{8,40},{9,... | collective-permute-start | bytes 36872 | tf_op jit(solution)/shard_map/ppermute | solution.py:24
  162.0 5.3 %collective-permute-start.29 = (f32[24,128]{1,0:T(8,128)S(1)}, f32[24,128]{1,0:T(8,128)S(1)}, u32[]{:S(2)}, u32[]{:S(2)}) collective-permute-start(f32[24,128]{1,0:T(8,128)S(1)} %merge.4.refs_0_), channel_id=1, source_target_pairs={{0,8},{1,9},{2,10},{3,11},{4,12},{5,13},{6,14},{7,15},{8,0},{9,1},... | collective-permute-start | bytes 36872 | tf_op jit(solution)/shard_map/ppermute | solution.py:24
  162.1 6.2 %collective-permute-start.28 = (f32[24,128]{1,0:T(8,128)S(1)}, f32[24,128]{1,0:T(8,128)S(1)}, u32[]{:S(2)}, u32[]{:S(2)}) collective-permute-start(f32[24,128]{1,0:T(8,128)S(1)} %merge.4.refs_0_), channel_id=1, source_target_pairs={{0,12},{1,13},{2,14},{3,15},{4,0},{5,1},{6,2},{7,3},{8,4},{9,5},{1... | collective-permute-start | bytes 36872 | tf_op jit(solution)/shard_map/ppermute | solution.py:24
  165.7 4.9 %collective-permute-start.27 = (f32[24,128]{1,0:T(8,128)S(1)}, f32[24,128]{1,0:T(8,128)S(1)}, u32[]{:S(2)}, u32[]{:S(2)}) collective-permute-start(f32[24,128]{1,0:T(8,128)S(1)} %merge.4.refs_0_), channel_id=1, source_target_pairs={{0,4},{1,5},{2,6},{3,7},{4,8},{5,9},{6,10},{7,11},{8,12},{9,13},{1... | collective-permute-start | bytes 36872 | tf_op jit(solution)/shard_map/ppermute | solution.py:24
  171.2 5.3 %collective-permute-start.32 = (f32[24,128]{1,0:T(8,128)S(1)}, f32[24,128]{1,0:T(8,128)S(1)}, u32[]{:S(2)}, u32[]{:S(2)}) collective-permute-start(f32[24,128]{1,0:T(8,128)S(1)} %merge.5.refs_0_), channel_id=1, source_target_pairs={{0,2},{1,3},{2,0},{3,1},{4,6},{5,7},{6,4},{7,5},{8,10},{9,11},{10,... | collective-permute-start | bytes 36872 | tf_op jit(solution)/shard_map/ppermute | solution.py:24
  172.7 3.8 %collective-permute-start.31 = (f32[24,128]{1,0:T(8,128)S(1)}, f32[24,128]{1,0:T(8,128)S(1)}, u32[]{:S(2)}, u32[]{:S(2)}) collective-permute-start(f32[24,128]{1,0:T(8,128)S(1)} %merge.5.refs_0_), channel_id=1, source_target_pairs={{0,3},{1,0},{2,1},{3,2},{4,7},{5,4},{6,5},{7,6},{8,11},{9,8},{10,9... | collective-permute-start | bytes 36872 | tf_op jit(solution)/shard_map/ppermute | solution.py:24
  173.9 4.9 %collective-permute-start.30 = (f32[24,128]{1,0:T(8,128)S(1)}, f32[24,128]{1,0:T(8,128)S(1)}, u32[]{:S(2)}, u32[]{:S(2)}) collective-permute-start(f32[24,128]{1,0:T(8,128)S(1)} %merge.5.refs_0_), channel_id=1, source_target_pairs={{0,1},{1,2},{2,3},{3,0},{4,5},{5,6},{6,7},{7,4},{8,9},{9,10},{10,1... | collective-permute-start | bytes 36872 | tf_op jit(solution)/shard_map/ppermute | solution.py:24
  (15 other events, 87.2 us)

commit v4 on v3

--- a/solution.py
+++ b/solution.py
@@ -28,16 +28,17 @@
     return (x, 1 - c, z, y)
 
 
+def near(axis, step):
+    def target(*at):
+        to = list(at)
+        to[axis] = (at[axis] + (1 if at[axis] % 2 == step else 3)) % 4
+        return tuple(to)
+
+    return target
+
+
 def along_x(s):
     return lambda x, c, z, y: ((x + s) % X, c, z, y)
-
-
-def along_y(s):
-    return lambda x, c, z, y: (x, c, z, (y + s) % Y)
-
-
-def along_z(s):
-    return lambda x, c, z, y: (x, c, (z + s) % Z, y)
 
 
 def along_p(s):
@@ -97,22 +98,17 @@
 
 
 def project_kernel(at, heads, weight, own, one, two, three, rolled):
-    p = at[4]
-    for s in range(4):
-        start = pl.multiple_of((p + s) % 4 * 32, 32)
-        rolled[pl.ds(32 * s, 32), :] = heads[pl.ds(start, 32), :]
-    wide = 512 if weight.shape[1] % 512 == 0 else 128
-
-    def step(n, carry):
-        cols = pl.ds(pl.multiple_of(n * wide, wide), wide)
-        out = jnp.dot(rolled[...], weight[:, cols], preferred_element_type=F32)
-        own[:, cols] = out[:32]
-        one[:, cols] = out[32:64].astype(BF16)
-        two[:, cols] = out[64:96].astype(BF16)
-        three[:, cols] = out[96:].astype(BF16)
-        return carry
-
-    lax.fori_loop(0, weight.shape[1] // wide, step, 0)
+    @pl.when(pl.program_id(0) == 0)
+    def _():
+        for s in range(4):
+            start = pl.multiple_of((at[4] + s) % 4 * 32, 32)
+            rolled[pl.ds(32 * s, 32), :] = heads[pl.ds(start, 32), :]
+
+    out = jnp.dot(rolled[...], weight[...], preferred_element_type=F32)
+    own[...] = out[:32]
+    one[...] = out[32:64].astype(BF16)
+    two[...] = out[64:96].astype(BF16)
+    three[...] = out[96:].astype(BF16)
 
 
 def partial_kernel(at, own, one, two, three, mine, first, second, third, total):
@@ -161,10 +157,12 @@
     )
 
 
-def score_kernel(shift, own, at, targets, logits, rows, out):
+def score_kernel(shift, own, parts, at, targets, *refs):
     x = at[0]
     p, q, core = (at[4], at[5], at[1]) if own else (at[5], at[4], 1 - at[1])
-    n_rows = rows.shape[0]
+    out = refs[-1]
+    found = jnp.concatenate([ref[...] for ref in refs[:parts]], axis=0)
+    n_rows = found.shape[0]
     i = lax.broadcasted_iota(jnp.int32, (n_rows, n_rows), 0)
     j = lax.broadcasted_iota(jnp.int32, (n_rows, n_rows), 1)
     lands = (
@@ -175,7 +173,6 @@
     place = core * 4 + ((q + 4 - shift) & 3)
     line = targets[pl.ds(place, 1), :] - at[6]
     want = jnp.sum(jnp.where(lands, line, 0), axis=1, keepdims=True)
-    found = logits[...]
     top = jnp.max(found, axis=1, keepdims=True)
     total = jnp.sum(jnp.exp(found - top), axis=1, keepdims=True)
     column = lax.broadcasted_iota(jnp.int32, found.shape, 1)
@@ -215,24 +212,14 @@
 
 def finish_kernel(at, *refs):
     top, total, hit = merged(refs[:-2])
-    out, found = refs[-2], refs[-1]
-    found[...] = hit - top - jnp.log(total)
-    i = lax.broadcasted_iota(jnp.int32, (128, 128), 0)
-    j = lax.broadcasted_iota(jnp.int32, (128, 128), 1)
+    out, turned = refs[-2], refs[-1]
+    found = hit - top - jnp.log(total)
+    lane = lax.broadcasted_iota(jnp.int32, (8, 128), 1)
     here = jnp.zeros((1, 128), F32)
     for q in range(4):
-        takes = (
-            (i // 32 == j // 32)
-            & ((i // 8 & 3) == at[0])
-            & ((j // 8 & 3) == q)
-            & ((i & 7) == (j & 7))
-        )
-        here = here + jnp.dot(
-            found[pl.ds(at[1] * 4 + q, 1), :],
-            takes.astype(F32),
-            precision=HIGHEST,
-            preferred_element_type=F32,
-        )
+        turn = (8 * q + 128 - 8 * at[0]) % 128
+        turned[...] = jnp.where((lane // 8 & 3) == q, pltpu.roll(found, turn, 1), 0.0)
+        here = here + turned[pl.ds(at[1] * 4 + q, 1), :]
     out[...] = here
 
 
@@ -302,18 +289,29 @@
     )
     flat_heads = normed_heads.astype(BF16).reshape(rows_here, heads_here * head_size)
 
-    own, *sent = local(
+    inner = flat_heads.shape[1]
+    wide = width // 6 if width % 768 == 0 else width
+    share = pl.BlockSpec((32, wide), lambda n: (0, n))
+    own, *sent = pl.pallas_call(
         project_kernel,
-        [on_chip((32, width), F32)] + [on_chip((32, width), BF16)] * 3,
-        scalars,
-        flat_heads,
-        out_weight,
-        scratch=[pltpu.VMEM(flat_heads.shape, BF16)],
-        flops=2 * rows_here * flat_heads.shape[1] * width,
-        bytes_=2 * width * (flat_heads.shape[1] + rows_here),
-        mib=16,
+        out_shape=[jax.ShapeDtypeStruct((32, width), F32)]
+        + [jax.ShapeDtypeStruct((32, width), BF16)] * 3,
+        grid=(width // wide,),
+        in_specs=[
+            SCALARS,
+            pl.BlockSpec((rows_here, inner), lambda n: (0, 0)),
+            pl.BlockSpec((inner, wide), lambda n: (0, n)),
+        ],
+        out_specs=[share] * 4,
+        scratch_shapes=[pltpu.VMEM((rows_here, inner), BF16)],
+        compiler_params=pltpu.CompilerParams(vmem_limit_bytes=8 * 1024 * 1024),
+        cost_estimate=pl.CostEstimate(
+            flops=2 * rows_here * inner * width,
+            bytes_accessed=2 * width * (inner + rows_here),
+            transcendentals=0,
+        ),
         name="project",
-    )
+    )(scalars, flat_heads, out_weight)
     came = [move(part, along_p(s)) for s, part in zip((1, 2, 3), sent)]
     own, *sent = local(
         partial_kernel,
@@ -345,35 +343,36 @@
     theirs = move(ours, other_core)
     ours, theirs = tie(ours, theirs)
     lines = jnp.transpose(targets.reshape(X, CORE, 4, 4, 8), (1, 3, 2, 0, 4)).reshape(8, 128)
-    pairs = [(ours, theirs)]
-    for s in (1, 3, 2):
-        block = move(ours, along_q(s))
-        pairs.append((block, move(block, other_core)))
-    pairs = [pairs[0], pairs[1], pairs[3], pairs[2]]
-    found = []
-    for s, pair in enumerate(pairs):
-        for mine_too, block in zip((True, False), pair):
-            logits = jnp.dot(block, vocab_weight, preferred_element_type=F32)
-            found.append(
-                local(
-                    functools.partial(score_kernel, s, mine_too),
-                    on_chip((8, 128), F32),
-                    scalars,
-                    lines,
-                    logits,
-                    unread=(block,),
-                    bytes_=4 * 128 * vocab_local,
-                    name="score",
-                )
+    up, down = move(ours, along_q(1)), move(ours, along_q(3))
+    half = up.shape[0] // 2
+    far = (move(up[:half], along_q(1)), move(down[half:], along_q(3)))
+    found = {}
+    for s, parts in ((0, (ours,)), (1, (up,)), (3, (down,)), (2, far)):
+        if s == 2:
+            parts, found = lax.optimization_barrier((parts, found))
+        swapped = (theirs,) if s == 0 else tuple(move(part, other_core) for part in parts)
+        for mine_too, blocks in ((True, parts), (False, swapped)):
+            logits = [jnp.dot(b, vocab_weight, preferred_element_type=F32) for b in blocks]
+            found[s, mine_too] = local(
+                functools.partial(score_kernel, s, mine_too, len(blocks)),
+                on_chip((8, 128), F32),
+                scalars,
+                lines,
+                *logits,
+                unread=blocks,
+                bytes_=4 * 128 * vocab_local,
+                name="score",
             )
+    found = [found[k // 2, k % 2 == 0] for k in range(8)]
     stats = local(place_kernel, on_chip((24, 128), F32), scalars, *found, name="place")
-    stats = local(
-        merge_kernel, on_chip((24, 128), F32), scalars, stats, move(stats, other_core), name="merge"
-    )
-    for along in (along_x, along_z):
-        parts = [stats] + [move(stats, along(s)) for s in (1, 3, 2)]
-        stats = local(merge_kernel, on_chip((24, 128), F32), scalars, *parts, name="merge")
-    parts = [stats] + [move(stats, along_y(s)) for s in (1, 3, 2)]
+    steps = [other_core]
+    for axis in (0, 2, 3):
+        steps += [near(axis, 0), near(axis, 1)]
+    for step in steps[:-1]:
+        stats = local(
+            merge_kernel, on_chip((24, 128), F32), scalars, stats, move(stats, step), name="merge"
+        )
+    parts = [stats, move(stats, steps[-1])]
     loglik = local(
         finish_kernel,
         jax.ShapeDtypeStruct((1, 128), F32),

time: 181 us -> 178 us (0.983)
  matrix products: 31.1 us -> 37.1 us
  waiting for transfers between devices: 71.4 us -> 66.7 us
  starting transfers between devices: 46.1 us -> 41.7 us
    dot_general x8 -> x10, matrix products: 21.1 us -> 26.8 us  [shards(): jnp.dot(b, vocab_weight, preferred_element_type=F32)]
    ppermute x33 -> x32, waiting for transfers between devices: 71.4 us -> 66.7 us  [move(): return lax.ppermute(array, ALL, pairs)]
    ppermute x33 -> x32, starting transfers between devices: 46.1 us -> 41.7 us  [move(): return lax.ppermute(array, ALL, pairs)]
    pallas_call x0 -> x1, Pallas kernels: none -> 3.78 us  [shards(): pl.pallas_call(project_kernel, out_shape=[jax.ShapeDtypeStruct((32, width...]
    pallas_call x18 -> x20, Pallas kernels: 20.5 us -> 18 us  [local(): pl.pallas_call(kernel, out_shape=outs, in_specs=[SCALARS] + [WHOLE] * len...]
  transfers between devices with their start and end apart: 33 -> 32, of which waited for: 20 -> 20; matrix products, arithmetic and copies ran while one was open for 15% -> 18% of each run, Pallas kernels for 4% -> 4%
where the time goes in v4:
time: 178 us
  waiting for transfers between devices  66.7 us (37%)
  starting transfers between devices  41.7 us (23%)
  matrix products  37.1 us (21%)
  Pallas kernels  21.7 us (12%)
  local copies, waits for them, and re-layouts  5.6 us (3%)
  other arithmetic  4.62 us (3%)
    ppermute x32, waiting for transfers between devices, move(): return lax.ppermute(array, ALL, pairs)  66.7 us
    ppermute x32, starting transfers between devices, move(): return lax.ppermute(array, ALL, pairs)  41.7 us
    dot_general x10, matrix products, shards(): jnp.dot(b, vocab_weight, preferred_element_type=F32)  26.8 us
    pallas_call x20, Pallas kernels, local(): pl.pallas_call(kernel, out_shape=outs, in_specs=[SCALARS] + [WHOLE] * len...  18 us
    unnamed x28, local copies, waits for them, and re-layouts  4.59 us
    pallas_call x1, Pallas kernels, shards(): pl.pallas_call(project_kernel, out_shape=[jax.ShapeDtypeStruct((32, width...  3.78 us
  transfers between devices with their start and end apart: 32, of which 20 were waited for; matrix products, arithmetic and copies ran while one was open for 18% of the time, Pallas kernels for 4%

profile of v4, /device:TPU:0, one launch (start us, length us, event | category | flops | bytes accessed | tf_op | source)
XLA Modules:
  0.0 178.0 jit_solution(432586459203777865)
XLA Ops:
  1.9 2.4 %fusion.3 = bf16[16,2,8,128]{3,2,1,0:T(8,128)(2,1)S(1)} fusion(bf16[128,6144]{1,0:T(8,128)(2,1)} %param.10, bf16[6144,256]{1,0:T(8,128)(2,1)S(1)} %copy-done), kind=kOutput, calls=%fused_computation.9 | convolution fusion | flops 402685952 | bytes 4784128 | tf_op jit(solution)/shard_map/dot_general | solution.py:249
  6.0 2.9 %fusion.4 = bf16[16,2,8,128]{3,2,1,0:T(8,128)(2,1)S(1)} fusion(bf16[128,6144]{1,0:T(8,128)(2,1)} %param.10, bf16[6144,256]{1,0:T(8,128)(2,1)} %param.13), kind=kOutput, calls=%fused_computation.10 | convolution fusion | flops 402685952 | bytes 4784128 | tf_op jit(solution)/shard_map/dot_general | solution.py:272
  11.4 5.4 %collective-permute-start.3 = (f32[2,136,128]{2,1,0:T(8,128)}, f32[2,136,128]{2,1,0:T(8,128)}, u32[]{:S(2)}, u32[]{:S(2)}) collective-permute-start(f32[2,136,128]{2,1,0:T(8,128)} %pad_maximum_fusion.1), channel_id=1, source_target_pairs={{0,96},{1,97},{2,98},{3,99},{4,100},{5,101},{6,102},{7,103},{8,104... | collective-permute-start | bytes 417800 | tf_op jit(solution)/shard_map/ppermute | solution.py:24
  19.9 2.1 %collective-permute-start.1 = (f32[2,136,128]{2,1,0:T(8,128)}, f32[2,136,128]{2,1,0:T(8,128)S(1)}, u32[]{:S(2)}, u32[]{:S(2)}) collective-permute-start(f32[2,136,128]{2,1,0:T(8,128)} %pad_maximum_fusion.1), channel_id=1, source_target_pairs={{0,32},{1,33},{2,34},{3,35},{4,36},{5,37},{6,38},{7,39},{8,40},{9,... | collective-permute-start | bytes 417800 | tf_op jit(solution)/shard_map/ppermute | solution.py:24
  24.2 2.6 %collective-permute-done.1 = f32[2,136,128]{2,1,0:T(8,128)S(1)} collective-permute-done((f32[2,136,128]{2,1,0:T(8,128)}, f32[2,136,128]{2,1,0:T(8,128)S(1)}, u32[]{:S(2)}, u32[]{:S(2)}) %collective-permute-start.1) | collective-permute-done | bytes 139296 | tf_op jit(solution)/shard_map/ppermute | solution.py:24
  30.2 3.8 %project.1 = (f32[32,6144]{1,0:T(8,128)S(1)}, bf16[32,6144]{1,0:T(8,128)(2,1)}, bf16[32,6144]{1,0:T(8,128)(2,1)}, bf16[32,6144]{1,0:T(8,128)(2,1)}) custom-call(s32[8]{0:T(128)S(1)} %stack.32.at, bf16[128,256]{1,0:T(8,128)(2,1)S(1)} %copy.28.heads, bf16[256,6144]{1,0:T(8,128)(2,1)S(1)} %copy-done.1), custom_call_target="tpu_custom_call" | custom-call | flops 402653184 | bytes 4718592 | tf_op jit(solution)/shard_map/project/pallas_call | solution.py:295
  36.5 2.9 %collective-permute-start.5 = (bf16[32,6144]{1,0:T(8,128)(2,1)}, bf16[32,6144]{1,0:T(8,128)(2,1)}, u32[]{:S(2)}, u32[]{:S(2)}) collective-permute-start(bf16[32,6144]{1,0:T(8,128)(2,1)} %get-tuple-element.25), channel_id=1, source_target_pairs={{0,2},{1,3},{2,0},{3,1},{4,6},{5,7},{6,4},{7,5},{8,10},{9,11},{10,... | collective-permute-start | bytes 1179656 | tf_op jit(solution)/shard_map/ppermute | solution.py:24
  40.7 3.4 %collective-permute-done.4.one = bf16[32,6144]{1,0:T(8,128)(2,1)S(1)} collective-permute-done((bf16[32,6144]{1,0:T(8,128)(2,1)}, bf16[32,6144]{1,0:T(8,128)(2,1)S(1)}, u32[]{:S(2)}, u32[]{:S(2)}) %collective-permute-start.4) | collective-permute-done | bytes 393248 | tf_op jit(solution)/shard_map/ppermute | solution.py:24
  44.1 5.6 %collective-permute-done.5.two = bf16[32,6144]{1,0:T(8,128)(2,1)} collective-permute-done((bf16[32,6144]{1,0:T(8,128)(2,1)}, bf16[32,6144]{1,0:T(8,128)(2,1)}, u32[]{:S(2)}, u32[]{:S(2)}) %collective-permute-start.5) | collective-permute-done | bytes 393248 | tf_op jit(solution)/shard_map/ppermute | solution.py:24
  54.2 3.6 %collective-permute-start.8 = (bf16[8,6144]{1,0:T(8,128)(2,1)S(1)}, bf16[8,6144]{1,0:T(8,128)(2,1)S(1)}, u32[]{:S(2)}, u32[]{:S(2)}) collective-permute-start(bf16[8,6144]{1,0:T(8,128)(2,1)S(1)} %get-tuple-element.29), channel_id=1, source_target_pairs={{0,8},{1,9},{2,10},{3,11},{4,12},{5,13},{6,14},{7,15},{8,0},{9,1},... | collective-permute-start | bytes 294920 | tf_op jit(solution)/shard_map/ppermute | solution.py:24
  63.4 4.2 %collective-permute-start.11 = (bf16[8,6144]{1,0:T(8,128)(2,1)S(1)}, bf16[8,6144]{1,0:T(8,128)(2,1)S(1)}, u32[]{:S(2)}, u32[]{:S(2)}) collective-permute-start(bf16[8,6144]{1,0:T(8,128)(2,1)S(1)} %norm.1.a), channel_id=1, source_target_pairs={{0,64},{1,65},{2,66},{3,67},{4,68},{5,69},{6,70},{7,71},{8,72},{9,... | collective-permute-start | bytes 294920 | tf_op jit(solution)/shard_map/ppermute | solution.py:24
  70.2 3.2 %collective-permute-done.10.b = bf16[8,6144]{1,0:T(8,128)(2,1)S(1)} collective-permute-done((bf16[8,6144]{1,0:T(8,128)(2,1)S(1)}, bf16[8,6144]{1,0:T(8,128)(2,1)S(1)}, u32[]{:S(2)}, u32[]{:S(2)}) %collective-permute-start.10) | collective-permute-done | bytes 98336 | tf_op jit(solution)/shard_map/ppermute | solution.py:24
  74.1 2.4 %collective-permute-start.15 = (bf16[32,6144]{1,0:T(8,128)(2,1)S(1)}, bf16[32,6144]{1,0:T(8,128)(2,1)S(1)}, u32[]{:S(2)}, u32[]{:S(2)}) collective-permute-start(bf16[32,6144]{1,0:T(8,128)(2,1)S(1)} %stack_x.1.a), channel_id=1, source_target_pairs={{0,3},{1,0},{2,1},{3,2},{4,7},{5,4},{6,5},{7,6},{8,11},{9,8},{10,9... | collective-permute-start | bytes 1179656 | tf_op jit(solution)/shard_map/ppermute | solution.py:24
  78.4 7.6 %collective-permute-done.15.d = bf16[32,6144]{1,0:T(8,128)(2,1)S(1)} collective-permute-done((bf16[32,6144]{1,0:T(8,128)(2,1)S(1)}, bf16[32,6144]{1,0:T(8,128)(2,1)S(1)}, u32[]{:S(2)}, u32[]{:S(2)}) %collective-permute-start.15) | collective-permute-done | bytes 393248 | tf_op jit(solution)/shard_map/ppermute | solution.py:24
  86.0 3.9 %collective-permute-done.13.b = bf16[32,6144]{1,0:T(8,128)(2,1)S(1)} collective-permute-done((bf16[32,6144]{1,0:T(8,128)(2,1)S(1)}, bf16[32,6144]{1,0:T(8,128)(2,1)S(1)}, u32[]{:S(2)}, u32[]{:S(2)}) %collective-permute-start.13) | collective-permute-done | bytes 393248 | tf_op jit(solution)/shard_map/ppermute | solution.py:24
  92.0 3.5 %collective-permute-done.16.b = bf16[128,6144]{1,0:T(8,128)(2,1)} collective-permute-done((bf16[128,6144]{1,0:T(8,128)(2,1)}, bf16[128,6144]{1,0:T(8,128)(2,1)}, u32[]{:S(2)}, u32[]{:S(2)}) %collective-permute-start.16) | collective-permute-done | bytes 1572896 | tf_op jit(solution)/shard_map/ppermute | solution.py:24
  95.5 2.2 %collective-permute-start.19 = (bf16[128,6144]{1,0:T(8,128)(2,1)}, bf16[128,6144]{1,0:T(8,128)(2,1)S(1)}, u32[]{:S(2)}, u32[]{:S(2)}) collective-permute-start(bf16[128,6144]{1,0:T(8,128)(2,1)} %get-tuple-element.31.refs_1_), channel_id=1, source_target_pairs={{0,12},{1,13},{2,14},{3,15},{4,0},{5,1},{6,2},{7,3},{8,4},{9,5},{1... | collective-permute-start | bytes 4718600 | tf_op jit(solution)/shard_map/ppermute | solution.py:24
  97.7 7.0 %fusion.41.refs_0_ = f32[128,1024]{1,0:T(8,128)S(1)} fusion(bf16[128,6144]{1,0:T(8,128)(2,1)} %get-tuple-element.32.refs_1_, bf16[6144,1024]{1,0:T(8,128)(2,1)} %param.18), kind=kOutput, calls=%fused_computation.64 | convolution fusion | flops 1610612736 | bytes 14680064 | tf_op jit(solution)/shard_map/dot_general | solution.py:355
  105.8 3.2 %fusion.42.refs_0_ = f32[128,1024]{1,0:T(8,128)S(1)} fusion(bf16[128,6144]{1,0:T(8,128)(2,1)} %get-tuple-element.31.refs_1_, bf16[6144,1024]{1,0:T(8,128)(2,1)S(1)} %bitcast.71), kind=kOutput, calls=%fused_computation.65 | convolution fusion | flops 1610612736 | bytes 14680064 | tf_op jit(solution)/shard_map/dot_general | solution.py:355
  110.1 6.1 %collective-permute-done.19.refs_1_ = bf16[128,6144]{1,0:T(8,128)(2,1)S(1)} collective-permute-done((bf16[128,6144]{1,0:T(8,128)(2,1)}, bf16[128,6144]{1,0:T(8,128)(2,1)S(1)}, u32[]{:S(2)}, u32[]{:S(2)}) %collective-permute-start.19) | collective-permute-done | bytes 1572896 | tf_op jit(solution)/shard_map/ppermute | solution.py:24
  116.2 3.5 %collective-permute-start.20 = (bf16[64,6144]{1,0:T(8,128)(2,1)S(1)}, bf16[64,6144]{1,0:T(8,128)(2,1)S(1)}, u32[]{:S(2)}, u32[]{:S(2)}) collective-permute-start(bf16[64,6144]{1,0:T(8,128)(2,1)S(1)} %slice.73), channel_id=1, source_target_pairs={{0,12},{1,13},{2,14},{3,15},{4,0},{5,1},{6,2},{7,3},{8,4},{9,5},{1... | collective-permute-start | bytes 2359304 | tf_op jit(solution)/shard_map/ppermute | solution.py:24
  133.0 2.3 %fusion.47.refs_0_ = f32[64,1024]{1,0:T(8,128)S(1)} fusion(bf16[64,6144]{1,0:T(8,128)(2,1)S(1)} %collective-permute-done.18.refs_2_, bf16[6144,1024]{1,0:T(8,128)(2,1)S(1)} %bitcast.71), kind=kOutput, calls=%fused_computation.70 | convolution fusion | flops 805306368 | bytes 13631488 | tf_op jit(solution)/shard_map/dot_general | solution.py:355
  136.2 2.3 %fusion.48.refs_1_ = f32[64,1024]{1,0:T(8,128)S(1)} fusion(bf16[64,6144]{1,0:T(8,128)(2,1)S(1)} %collective-permute-done.20.refs_3_, bf16[6144,1024]{1,0:T(8,128)(2,1)S(1)} %bitcast.71), kind=kOutput, calls=%fused_computation.71 | convolution fusion | flops 805306368 | bytes 13631488 | tf_op jit(solution)/shard_map/dot_general | solution.py:355
  139.6 2.3 %fusion.49.refs_0_ = f32[64,1024]{1,0:T(8,128)S(1)} fusion(bf16[64,6144]{1,0:T(8,128)(2,1)S(1)} %collective-permute-done.23.refs_2_, bf16[6144,1024]{1,0:T(8,128)(2,1)S(1)} %bitcast.71), kind=kOutput, calls=%fused_computation.72 | convolution fusion | flops 805306368 | bytes 13631488 | tf_op jit(solution)/shard_map/dot_general | solution.py:355
  142.0 2.3 %fusion.50.refs_1_ = f32[64,1024]{1,0:T(8,128)S(1)} fusion(bf16[64,6144]{1,0:T(8,128)(2,1)S(1)} %collective-permute-done.24.refs_3_, bf16[6144,1024]{1,0:T(8,128)(2,1)S(1)} %bitcast.71), kind=kOutput, calls=%fused_computation.73 | convolution fusion | flops 805306368 | bytes 13631488 | tf_op jit(solution)/shard_map/dot_general | solution.py:355
  147.8 3.7 %collective-permute-done.26.refs_1_ = f32[24,128]{1,0:T(8,128)S(1)} collective-permute-done((f32[24,128]{1,0:T(8,128)S(1)}, f32[24,128]{1,0:T(8,128)S(1)}, u32[]{:S(2)}, u32[]{:S(2)}) %collective-permute-start.26) | collective-permute-done | bytes 12320 | tf_op jit(solution)/shard_map/ppermute | solution.py:24
  152.4 4.6 %collective-permute-done.27.refs_1_ = f32[24,128]{1,0:T(8,128)S(1)} collective-permute-done((f32[24,128]{1,0:T(8,128)S(1)}, f32[24,128]{1,0:T(8,128)S(1)}, u32[]{:S(2)}, u32[]{:S(2)}) %collective-permute-start.27) | collective-permute-done | bytes 12320 | tf_op jit(solution)/shard_map/ppermute | solution.py:24
  157.7 3.7 %collective-permute-done.28.refs_1_ = f32[24,128]{1,0:T(8,128)S(1)} collective-permute-done((f32[24,128]{1,0:T(8,128)S(1)}, f32[24,128]{1,0:T(8,128)S(1)}, u32[]{:S(2)}, u32[]{:S(2)}) %collective-permute-start.28) | collective-permute-done | bytes 12320 | tf_op jit(solution)/shard_map/ppermute | solution.py:24
  161.9 2.2 %collective-permute-start.29 = (f32[24,128]{1,0:T(8,128)S(1)}, f32[24,128]{1,0:T(8,128)S(1)}, u32[]{:S(2)}, u32[]{:S(2)}) collective-permute-start(f32[24,128]{1,0:T(8,128)S(1)} %merge.9.refs_0_), channel_id=1, source_target_pairs={{0,12},{1,13},{2,14},{3,15},{4,8},{5,9},{6,10},{7,11},{8,4},{9,5},... | collective-permute-start | bytes 36872 | tf_op jit(solution)/shard_map/ppermute | solution.py:24
  164.2 2.7 %collective-permute-done.29.refs_1_ = f32[24,128]{1,0:T(8,128)S(1)} collective-permute-done((f32[24,128]{1,0:T(8,128)S(1)}, f32[24,128]{1,0:T(8,128)S(1)}, u32[]{:S(2)}, u32[]{:S(2)}) %collective-permute-start.29) | collective-permute-done | bytes 12320 | tf_op jit(solution)/shard_map/ppermute | solution.py:24
  167.6 3.7 %collective-permute-done.30.refs_1_ = f32[24,128]{1,0:T(8,128)S(1)} collective-permute-done((f32[24,128]{1,0:T(8,128)S(1)}, f32[24,128]{1,0:T(8,128)S(1)}, u32[]{:S(2)}, u32[]{:S(2)}) %collective-permute-start.30) | collective-permute-done | bytes 12320 | tf_op jit(solution)/shard_map/ppermute | solution.py:24
  172.5 4.3 %collective-permute-done.31.refs_1_ = f32[24,128]{1,0:T(8,128)S(1)} collective-permute-done((f32[24,128]{1,0:T(8,128)S(1)}, f32[24,128]{1,0:T(8,128)S(1)}, u32[]{:S(2)}, u32[]{:S(2)}) %collective-permute-start.31) | collective-permute-done | bytes 12320 | tf_op jit(solution)/shard_map/ppermute | solution.py:24
  (127 shorter events, 61.7 us)
Async XLA Ops:
  6.0 3.7 %collective-permute-start = (f32[2,136,128]{2,1,0:T(8,128)}, f32[2,136,128]{2,1,0:T(8,128)}, u32[]{:S(2)}, u32[]{:S(2)}) collective-permute-start(f32[2,136,128]{2,1,0:T(8,128)} %pad_maximum_fusion), channel_id=1, source_target_pairs={{0,16},{1,17},{2,18},{3,19},{4,20},{5,21},{6,22},{7,23},{8,24},{9,... | collective-permute-start | bytes 417800 | tf_op jit(solution)/shard_map/ppermute | solution.py:24
  11.4 10.6 %collective-permute-start.3 = (f32[2,136,128]{2,1,0:T(8,128)}, f32[2,136,128]{2,1,0:T(8,128)}, u32[]{:S(2)}, u32[]{:S(2)}) collective-permute-start(f32[2,136,128]{2,1,0:T(8,128)} %pad_maximum_fusion.1), channel_id=1, source_target_pairs={{0,96},{1,97},{2,98},{3,99},{4,100},{5,101},{6,102},{7,103},{8,104... | collective-permute-start | bytes 417800 | tf_op jit(solution)/shard_map/ppermute | solution.py:24
  18.6 5.6 %collective-permute-start.2 = (f32[2,136,128]{2,1,0:T(8,128)}, f32[2,136,128]{2,1,0:T(8,128)S(1)}, u32[]{:S(2)}, u32[]{:S(2)}) collective-permute-start(f32[2,136,128]{2,1,0:T(8,128)} %pad_maximum_fusion.1), channel_id=1, source_target_pairs={{0,64},{1,65},{2,66},{3,67},{4,68},{5,69},{6,70},{7,71},{8,72},{9,... | collective-permute-start | bytes 417800 | tf_op jit(solution)/shard_map/ppermute | solution.py:24
  19.9 6.9 %collective-permute-start.1 = (f32[2,136,128]{2,1,0:T(8,128)}, f32[2,136,128]{2,1,0:T(8,128)S(1)}, u32[]{:S(2)}, u32[]{:S(2)}) collective-permute-start(f32[2,136,128]{2,1,0:T(8,128)} %pad_maximum_fusion.1), channel_id=1, source_target_pairs={{0,32},{1,33},{2,34},{3,35},{4,36},{5,37},{6,38},{7,39},{8,40},{9,... | collective-permute-start | bytes 417800 | tf_op jit(solution)/shard_map/ppermute | solution.py:24
  34.9 9.2 %collective-permute-start.4 = (bf16[32,6144]{1,0:T(8,128)(2,1)}, bf16[32,6144]{1,0:T(8,128)(2,1)S(1)}, u32[]{:S(2)}, u32[]{:S(2)}) collective-permute-start(bf16[32,6144]{1,0:T(8,128)(2,1)} %get-tuple-element.24), channel_id=1, source_target_pairs={{0,1},{1,2},{2,3},{3,0},{4,5},{5,6},{6,7},{7,4},{8,9},{9,10},{10,1... | collective-permute-start | bytes 1179656 | tf_op jit(solution)/shard_map/ppermute | solution.py:24
  36.5 13.2 %collective-permute-start.5 = (bf16[32,6144]{1,0:T(8,128)(2,1)}, bf16[32,6144]{1,0:T(8,128)(2,1)}, u32[]{:S(2)}, u32[]{:S(2)}) collective-permute-start(bf16[32,6144]{1,0:T(8,128)(2,1)} %get-tuple-element.25), channel_id=1, source_target_pairs={{0,2},{1,3},{2,0},{3,1},{4,6},{5,7},{6,4},{7,5},{8,10},{9,11},{10,... | collective-permute-start | bytes 1179656 | tf_op jit(solution)/shard_map/ppermute | solution.py:24
  39.4 10.3 %collective-permute-start.6 = (bf16[32,6144]{1,0:T(8,128)(2,1)}, bf16[32,6144]{1,0:T(8,128)(2,1)}, u32[]{:S(2)}, u32[]{:S(2)}) collective-permute-start(bf16[32,6144]{1,0:T(8,128)(2,1)} %get-tuple-element.26), channel_id=1, source_target_pairs={{0,3},{1,0},{2,1},{3,2},{4,7},{5,4},{6,5},{7,6},{8,11},{9,8},{10,9... | collective-permute-start | bytes 1179656 | tf_op jit(solution)/shard_map/ppermute | solution.py:24
  52.2 7.5 %collective-permute-start.7 = (bf16[8,6144]{1,0:T(8,128)(2,1)S(1)}, bf16[8,6144]{1,0:T(8,128)(2,1)S(1)}, u32[]{:S(2)}, u32[]{:S(2)}) collective-permute-start(bf16[8,6144]{1,0:T(8,128)(2,1)S(1)} %get-tuple-element.28), channel_id=1, source_target_pairs={{0,4},{1,5},{2,6},{3,7},{4,8},{5,9},{6,10},{7,11},{8,12},{9,13},{1... | collective-permute-start | bytes 294920 | tf_op jit(solution)/shard_map/ppermute | solution.py:24
  54.2 7.2 %collective-permute-start.8 = (bf16[8,6144]{1,0:T(8,128)(2,1)S(1)}, bf16[8,6144]{1,0:T(8,128)(2,1)S(1)}, u32[]{:S(2)}, u32[]{:S(2)}) collective-permute-start(bf16[8,6144]{1,0:T(8,128)(2,1)S(1)} %get-tuple-element.29), channel_id=1, source_target_pairs={{0,8},{1,9},{2,10},{3,11},{4,12},{5,13},{6,14},{7,15},{8,0},{9,1},... | collective-permute-start | bytes 294920 | tf_op jit(solution)/shard_map/ppermute | solution.py:24
  57.8 4.6 %collective-permute-start.9 = (bf16[8,6144]{1,0:T(8,128)(2,1)S(1)}, bf16[8,6144]{1,0:T(8,128)(2,1)S(1)}, u32[]{:S(2)}, u32[]{:S(2)}) collective-permute-start(bf16[8,6144]{1,0:T(8,128)(2,1)S(1)} %get-tuple-element.30), channel_id=1, source_target_pairs={{0,12},{1,13},{2,14},{3,15},{4,0},{5,1},{6,2},{7,3},{8,4},{9,5},{1... | collective-permute-start | bytes 294920 | tf_op jit(solution)/shard_map/ppermute | solution.py:24
  63.1 5.3 %collective-permute-start.12 = (bf16[8,6144]{1,0:T(8,128)(2,1)S(1)}, bf16[8,6144]{1,0:T(8,128)(2,1)S(1)}, u32[]{:S(2)}, u32[]{:S(2)}) collective-permute-start(bf16[8,6144]{1,0:T(8,128)(2,1)S(1)} %norm.1.a), channel_id=1, source_target_pairs={{0,96},{1,97},{2,98},{3,99},{4,100},{5,101},{6,102},{7,103},{8,104... | collective-permute-start | bytes 294920 | tf_op jit(solution)/shard_map/ppermute | solution.py:24
  63.4 6.8 %collective-permute-start.11 = (bf16[8,6144]{1,0:T(8,128)(2,1)S(1)}, bf16[8,6144]{1,0:T(8,128)(2,1)S(1)}, u32[]{:S(2)}, u32[]{:S(2)}) collective-permute-start(bf16[8,6144]{1,0:T(8,128)(2,1)S(1)} %norm.1.a), channel_id=1, source_target_pairs={{0,64},{1,65},{2,66},{3,67},{4,68},{5,69},{6,70},{7,71},{8,72},{9,... | collective-permute-start | bytes 294920 | tf_op jit(solution)/shard_map/ppermute | solution.py:24
  67.6 5.8 %collective-permute-start.10 = (bf16[8,6144]{1,0:T(8,128)(2,1)S(1)}, bf16[8,6144]{1,0:T(8,128)(2,1)S(1)}, u32[]{:S(2)}, u32[]{:S(2)}) collective-permute-start(bf16[8,6144]{1,0:T(8,128)(2,1)S(1)} %norm.1.a), channel_id=1, source_target_pairs={{0,32},{1,33},{2,34},{3,35},{4,36},{5,37},{6,38},{7,39},{8,40},{9,... | collective-permute-start | bytes 294920 | tf_op jit(solution)/shard_map/ppermute | solution.py:24
  74.1 11.9 %collective-permute-start.15 = (bf16[32,6144]{1,0:T(8,128)(2,1)S(1)}, bf16[32,6144]{1,0:T(8,128)(2,1)S(1)}, u32[]{:S(2)}, u32[]{:S(2)}) collective-permute-start(bf16[32,6144]{1,0:T(8,128)(2,1)S(1)} %stack_x.1.a), channel_id=1, source_target_pairs={{0,3},{1,0},{2,1},{3,2},{4,7},{5,4},{6,5},{7,6},{8,11},{9,8},{10,9... | collective-permute-start | bytes 1179656 | tf_op jit(solution)/shard_map/ppermute | solution.py:24
  76.4 9.5 %collective-permute-start.14 = (bf16[32,6144]{1,0:T(8,128)(2,1)S(1)}, bf16[32,6144]{1,0:T(8,128)(2,1)S(1)}, u32[]{:S(2)}, u32[]{:S(2)}) collective-permute-start(bf16[32,6144]{1,0:T(8,128)(2,1)S(1)} %stack_x.1.a), channel_id=1, source_target_pairs={{0,2},{1,3},{2,0},{3,1},{4,6},{5,7},{6,4},{7,5},{8,10},{9,11},{10,... | collective-permute-start | bytes 1179656 | tf_op jit(solution)/shard_map/ppermute | solution.py:24
  77.8 12.1 %collective-permute-start.13 = (bf16[32,6144]{1,0:T(8,128)(2,1)S(1)}, bf16[32,6144]{1,0:T(8,128)(2,1)S(1)}, u32[]{:S(2)}, u32[]{:S(2)}) collective-permute-start(bf16[32,6144]{1,0:T(8,128)(2,1)S(1)} %stack_x.1.a), channel_id=1, source_target_pairs={{0,1},{1,2},{2,3},{3,0},{4,5},{5,6},{6,7},{7,4},{8,9},{9,10},{10,1... | collective-permute-start | bytes 1179656 | tf_op jit(solution)/shard_map/ppermute | solution.py:24
  91.8 3.8 %collective-permute-start.16 = (bf16[128,6144]{1,0:T(8,128)(2,1)}, bf16[128,6144]{1,0:T(8,128)(2,1)}, u32[]{:S(2)}, u32[]{:S(2)}) collective-permute-start(bf16[128,6144]{1,0:T(8,128)(2,1)} %stack_p.1.a), channel_id=1, source_target_pairs={{0,16},{1,17},{2,18},{3,19},{4,20},{5,21},{6,22},{7,23},{8,24},{9,... | collective-permute-start | bytes 4718600 | tf_op jit(solution)/shard_map/ppermute | solution.py:24
  95.5 20.6 %collective-permute-start.19 = (bf16[128,6144]{1,0:T(8,128)(2,1)}, bf16[128,6144]{1,0:T(8,128)(2,1)S(1)}, u32[]{:S(2)}, u32[]{:S(2)}) collective-permute-start(bf16[128,6144]{1,0:T(8,128)(2,1)} %get-tuple-element.31.refs_1_), channel_id=1, source_target_pairs={{0,12},{1,13},{2,14},{3,15},{4,0},{5,1},{6,2},{7,3},{8,4},{9,5},{1... | collective-permute-start | bytes 4718600 | tf_op jit(solution)/shard_map/ppermute | solution.py:24
  97.7 22.0 %collective-permute-start.17 = (bf16[128,6144]{1,0:T(8,128)(2,1)}, bf16[128,6144]{1,0:T(8,128)(2,1)S(1)}, u32[]{:S(2)}, u32[]{:S(2)}) collective-permute-start(bf16[128,6144]{1,0:T(8,128)(2,1)} %get-tuple-element.31.refs_1_), channel_id=1, source_target_pairs={{0,4},{1,5},{2,6},{3,7},{4,8},{5,9},{6,10},{7,11},{8,12},{9,13},{1... | collective-permute-start | bytes 4718600 | tf_op jit(solution)/shard_map/ppermute | solution.py:24
  116.2 15.8 %collective-permute-start.20 = (bf16[64,6144]{1,0:T(8,128)(2,1)S(1)}, bf16[64,6144]{1,0:T(8,128)(2,1)S(1)}, u32[]{:S(2)}, u32[]{:S(2)}) collective-permute-start(bf16[64,6144]{1,0:T(8,128)(2,1)S(1)} %slice.73), channel_id=1, source_target_pairs={{0,12},{1,13},{2,14},{3,15},{4,0},{5,1},{6,2},{7,3},{8,4},{9,5},{1... | collective-permute-start | bytes 2359304 | tf_op jit(solution)/shard_map/ppermute | solution.py:24
  119.8 13.3 %collective-permute-start.18 = (bf16[64,6144]{1,0:T(8,128)(2,1)S(1)}, bf16[64,6144]{1,0:T(8,128)(2,1)S(1)}, u32[]{:S(2)}, u32[]{:S(2)}) collective-permute-start(bf16[64,6144]{1,0:T(8,128)(2,1)S(1)} %slice.72), channel_id=1, source_target_pairs={{0,4},{1,5},{2,6},{3,7},{4,8},{5,9},{6,10},{7,11},{8,12},{9,13},{1... | collective-permute-start | bytes 2359304 | tf_op jit(solution)/shard_map/ppermute | solution.py:24
  119.8 6.4 %collective-permute-start.22 = (bf16[128,6144]{1,0:T(8,128)(2,1)S(1)}, bf16[128,6144]{1,0:T(8,128)(2,1)S(1)}, u32[]{:S(2)}, u32[]{:S(2)}) collective-permute-start(bf16[128,6144]{1,0:T(8,128)(2,1)S(1)} %collective-permute-done.19.refs_1_), channel_id=1, source_target_pairs={{0,16},{1,17},{2,18},{3,19},{4,20},{5,21},{6,22},{7,23},{8,24},{9,... | collective-permute-start | bytes 4718600 | tf_op jit(solution)/shard_map/ppermute | solution.py:24
  119.9 9.2 %collective-permute-start.21 = (bf16[128,6144]{1,0:T(8,128)(2,1)S(1)}, bf16[128,6144]{1,0:T(8,128)(2,1)S(1)}, u32[]{:S(2)}, u32[]{:S(2)}) collective-permute-start(bf16[128,6144]{1,0:T(8,128)(2,1)S(1)} %collective-permute-done.17.refs_1_), channel_id=1, source_target_pairs={{0,16},{1,17},{2,18},{3,19},{4,20},{5,21},{6,22},{7,23},{8,24},{9,... | collective-permute-start | bytes 4718600 | tf_op jit(solution)/shard_map/ppermute | solution.py:24
  133.0 6.6 %collective-permute-start.23 = (bf16[64,6144]{1,0:T(8,128)(2,1)S(1)}, bf16[64,6144]{1,0:T(8,128)(2,1)S(1)}, u32[]{:S(2)}, u32[]{:S(2)}) collective-permute-start(bf16[64,6144]{1,0:T(8,128)(2,1)S(1)} %collective-permute-done.18.refs_2_), channel_id=1, source_target_pairs={{0,16},{1,17},{2,18},{3,19},{4,20},{5,21},{6,22},{7,23},{8,24},{9,... | collective-permute-start | bytes 2359304 | tf_op jit(solution)/shard_map/ppermute | solution.py:24
  135.4 6.6 %collective-permute-start.24 = (bf16[64,6144]{1,0:T(8,128)(2,1)S(1)}, bf16[64,6144]{1,0:T(8,128)(2,1)S(1)}, u32[]{:S(2)}, u32[]{:S(2)}) collective-permute-start(bf16[64,6144]{1,0:T(8,128)(2,1)S(1)} %collective-permute-done.20.refs_3_), channel_id=1, source_target_pairs={{0,16},{1,17},{2,18},{3,19},{4,20},{5,21},{6,22},{7,23},{8,24},{9,... | collective-permute-start | bytes 2359304 | tf_op jit(solution)/shard_map/ppermute | solution.py:24
  145.9 1.3 collective-permute-start.25
  147.7 3.8 %collective-permute-start.26 = (f32[24,128]{1,0:T(8,128)S(1)}, f32[24,128]{1,0:T(8,128)S(1)}, u32[]{:S(2)}, u32[]{:S(2)}) collective-permute-start(f32[24,128]{1,0:T(8,128)S(1)} %merge.6.refs_0_), channel_id=1, source_target_pairs={{0,32},{1,33},{2,34},{3,35},{4,36},{5,37},{6,38},{7,39},{8,40},{9,... | collective-permute-start | bytes 36872 | tf_op jit(solution)/shard_map/ppermute | solution.py:24
  152.1 5.0 %collective-permute-start.27 = (f32[24,128]{1,0:T(8,128)S(1)}, f32[24,128]{1,0:T(8,128)S(1)}, u32[]{:S(2)}, u32[]{:S(2)}) collective-permute-start(f32[24,128]{1,0:T(8,128)S(1)} %merge.7.refs_0_), channel_id=1, source_target_pairs={{0,96},{1,97},{2,98},{3,99},{4,100},{5,101},{6,102},{7,103},{8,104... | collective-permute-start | bytes 36872 | tf_op jit(solution)/shard_map/ppermute | solution.py:24
  157.6 3.8 %collective-permute-start.28 = (f32[24,128]{1,0:T(8,128)S(1)}, f32[24,128]{1,0:T(8,128)S(1)}, u32[]{:S(2)}, u32[]{:S(2)}) collective-permute-start(f32[24,128]{1,0:T(8,128)S(1)} %merge.8.refs_0_), channel_id=1, source_target_pairs={{0,4},{1,5},{2,6},{3,7},{4,0},{5,1},{6,2},{7,3},{8,12},{9,13},{10,... | collective-permute-start | bytes 36872 | tf_op jit(solution)/shard_map/ppermute | solution.py:24
  161.9 5.0 %collective-permute-start.29 = (f32[24,128]{1,0:T(8,128)S(1)}, f32[24,128]{1,0:T(8,128)S(1)}, u32[]{:S(2)}, u32[]{:S(2)}) collective-permute-start(f32[24,128]{1,0:T(8,128)S(1)} %merge.9.refs_0_), channel_id=1, source_target_pairs={{0,12},{1,13},{2,14},{3,15},{4,8},{5,9},{6,10},{7,11},{8,4},{9,5},... | collective-permute-start | bytes 36872 | tf_op jit(solution)/shard_map/ppermute | solution.py:24
  167.5 3.8 %collective-permute-start.30 = (f32[24,128]{1,0:T(8,128)S(1)}, f32[24,128]{1,0:T(8,128)S(1)}, u32[]{:S(2)}, u32[]{:S(2)}) collective-permute-start(f32[24,128]{1,0:T(8,128)S(1)} %merge.10.refs_0_), channel_id=1, source_target_pairs={{0,1},{1,0},{2,3},{3,2},{4,5},{5,4},{6,7},{7,6},{8,9},{9,8},{10,11... | collective-permute-start | bytes 36872 | tf_op jit(solution)/shard_map/ppermute | solution.py:24
  171.8 5.0 %collective-permute-start.31 = (f32[24,128]{1,0:T(8,128)S(1)}, f32[24,128]{1,0:T(8,128)S(1)}, u32[]{:S(2)}, u32[]{:S(2)}) collective-permute-start(f32[24,128]{1,0:T(8,128)S(1)} %merge.11.refs_0_), channel_id=1, source_target_pairs={{0,3},{1,2},{2,1},{3,0},{4,7},{5,6},{6,5},{7,4},{8,11},{9,10},{10,... | collective-permute-start | bytes 36872 | tf_op jit(solution)/shard_map/ppermute | solution.py:24
  (14 other events, 117.9 us)

commit v5 on v4

--- a/solution.py
+++ b/solution.py
@@ -19,8 +19,7 @@
     for i in range(X * CORE * Z * Y):
         at = (i // (CORE * Z * Y), i // (Z * Y) % CORE, i // Y % Z, i % Y)
         to = target(*at)
-        if to is not None:
-            pairs.append((i, ((to[0] * CORE + to[1]) * Z + to[2]) * Y + to[3]))
+        pairs.append((i, ((to[0] * CORE + to[1]) * Z + to[2]) * Y + to[3]))
     return lax.ppermute(array, ALL, pairs)
 
 
@@ -49,10 +48,6 @@
     return lambda x, c, z, y: (x, c, (z + s) % Z, y) if c == 0 else (x, c, z, (y + s) % Y)
 
 
-def later_x(s):
-    return lambda x, c, z, y: (x + s, c, z, y) if x + s < X else None
-
-
 def on_chip(shape, dtype):
     return pltpu.VMEM(shape, dtype)
 
@@ -66,19 +61,19 @@
 WHOLE = pl.BlockSpec(memory_space=pltpu.VMEM)
 
 
-def local(kernel, outs, scalars, *arrays, unread=(), scratch=(), flops=0, bytes_=0, mib=4, name=None):
+def local(kernel, outs, scalars, *arrays, loose=(), unread=(), scratch=(), flops=0, bytes_=0, mib=4, name=None):
     many = isinstance(outs, list)
     specs = [WHOLE] * len(outs) if many else WHOLE
     return pl.pallas_call(
         kernel,
         out_shape=outs,
-        in_specs=[SCALARS] + [WHOLE] * len(arrays) + [ANYWHERE] * len(unread),
+        in_specs=[SCALARS] + [WHOLE] * len((*arrays, *loose)) + [ANYWHERE] * len(unread),
         out_specs=specs,
         scratch_shapes=list(scratch),
         compiler_params=pltpu.CompilerParams(vmem_limit_bytes=mib * 1024 * 1024),
         cost_estimate=pl.CostEstimate(flops=flops, bytes_accessed=bytes_, transcendentals=0),
         name=name,
-    )(scalars, *[pin(a) for a in (*arrays, *unread)])
+    )(scalars, *[pin(a) for a in arrays], *loose, *[pin(a) for a in unread])
 
 
 def tie_kernel(a, b, out_a, out_b):
@@ -111,7 +106,7 @@
     three[...] = out[96:].astype(BF16)
 
 
-def partial_kernel(at, own, one, two, three, mine, first, second, third, total):
+def partial_kernel(at, one, two, three, own, mine, first, second, third, total):
     q = at[5]
     total[...] = (
         own[...]
@@ -143,7 +138,7 @@
 
 
 def gather(block, target, scalars, name):
-    parts = [move(block, target(s)) for s in (1, 2, 3)]
+    parts = [move(block, target(s)) for s in (3, 2, 1)]
     rows, width = block.shape
     return local(
         stack_kernel,
@@ -157,70 +152,88 @@
     )
 
 
-def score_kernel(shift, own, parts, at, targets, *refs):
+def in_place(values, lane, p, x):
+    values = pltpu.roll(values, 32 * p, 1)
+    return jnp.where(
+        (lane & 31) >= 8 * x,
+        pltpu.roll(values, 8 * x, 1),
+        pltpu.roll(values, (8 * x + 96) % 128, 1),
+    )
+
+
+def as_gathered(values, lane, p, x):
+    values = pltpu.roll(values, (128 - 32 * p) % 128, 1)
+    return jnp.where(
+        (lane & 31) < 32 - 8 * x,
+        pltpu.roll(values, (128 - 8 * x) % 128, 1),
+        pltpu.roll(values, (160 - 8 * x) % 128, 1),
+    )
+
+
+def score_kernel(shift, at, targets, mine, theirs, rows_mine, rows_theirs, out_mine, out_theirs):
     x = at[0]
-    p, q, core = (at[4], at[5], at[1]) if own else (at[5], at[4], 1 - at[1])
-    out = refs[-1]
-    found = jnp.concatenate([ref[...] for ref in refs[:parts]], axis=0)
-    n_rows = found.shape[0]
-    i = lax.broadcasted_iota(jnp.int32, (n_rows, n_rows), 0)
-    j = lax.broadcasted_iota(jnp.int32, (n_rows, n_rows), 1)
-    lands = (
-        (((p + 4 - i // 32) & 3) == j // 32)
-        & (((x + 4 - (i // 8 & 3)) & 3) == (j // 8 & 3))
-        & ((i & 7) == (j & 7))
-    )
-    place = core * 4 + ((q + 4 - shift) & 3)
-    line = targets[pl.ds(place, 1), :] - at[6]
-    want = jnp.sum(jnp.where(lands, line, 0), axis=1, keepdims=True)
-    top = jnp.max(found, axis=1, keepdims=True)
-    total = jnp.sum(jnp.exp(found - top), axis=1, keepdims=True)
-    column = lax.broadcasted_iota(jnp.int32, found.shape, 1)
-    hit = jnp.sum(jnp.where(column == want, found, 0.0), axis=1, keepdims=True)
-    both = jnp.where(j == 0, top, jnp.where(j == 1, total, jnp.where(j == 2, hit, 0.0)))
-    turned = jnp.transpose(both)[:8]
-    out[...] = jnp.dot(
-        turned, lands.astype(F32), precision=HIGHEST, preferred_element_type=F32
-    )
+    lane = lax.broadcasted_iota(jnp.int32, (8, 128), 1)
+    i = lax.broadcasted_iota(jnp.int32, (128, 128), 0)
+    j = lax.broadcasted_iota(jnp.int32, (128, 128), 1)
+    for logits, out, p, q, core in (
+        (mine, out_mine, at[4], at[5], at[1]),
+        (theirs, out_theirs, at[5], at[4], 1 - at[1]),
+    ):
+        found = logits[...]
+        place = core * 4 + ((q + 4 - shift) & 3)
+        line = jnp.broadcast_to(targets[pl.ds(place, 1), :] - at[6], (8, 128))
+        line = as_gathered(line, lane, p, x)[:1]
+        want = jnp.sum(jnp.where(i == j, line, 0), axis=1, keepdims=True)
+        top = jnp.max(found, axis=1, keepdims=True)
+        total = jnp.sum(jnp.exp(found - top), axis=1, keepdims=True)
+        column = lax.broadcasted_iota(jnp.int32, found.shape, 1)
+        hit = jnp.sum(jnp.where(column == want, found, 0.0), axis=1, keepdims=True)
+        both = jnp.where(j == 0, top, jnp.where(j == 1, total, jnp.where(j == 2, hit, 0.0)))
+        out[...] = in_place(jnp.transpose(both)[:8], lane, p, x)
 
 
 def place_kernel(at, *refs):
-    blocks, out = refs[:-1], refs[-1]
+    blocks, out, held = refs[:-2], refs[-2], refs[-1]
     for k, block in enumerate(blocks):
         shift, own = k // 2, k % 2 == 0
         q, core = (at[5], at[1]) if own else (at[4], 1 - at[1])
         place = core * 4 + ((q + 4 - shift) & 3)
         for row in range(3):
-            out[pl.ds(8 * row + place, 1), :] = block[row : row + 1, :]
+            held[pl.ds(8 * row + place, 1), :] = block[row : row + 1, :]
+    lane = lax.broadcasted_iota(jnp.int32, (8, 128), 1)
+    for row in range(3):
+        values = held[8 * row : 8 * row + 8, :]
+        turned = {8 * k: pltpu.roll(values, 8 * k, 1) if k else values for k in range(16)}
+        for x in range(X):
+            picked = [
+                jnp.where((lane // 8 & 3) == q, turned[(8 * q - 8 * x) % 128], 0.0) for q in range(4)
+            ]
+            for core in range(CORE):
+                line = sum(picked[q][4 * core + q : 4 * core + q + 1, :] for q in range(4))
+                out[x * CORE + core, row : row + 1, :] = line
 
 
 def merged(parts):
-    top = parts[0][0:8, :]
+    top = parts[0][0:1]
     for part in parts[1:]:
-        top = jnp.maximum(top, part[0:8, :])
-    total = sum(part[8:16, :] * jnp.exp(part[0:8, :] - top) for part in parts)
-    hit = sum(part[16:24, :] for part in parts)
+        top = jnp.maximum(top, part[0:1])
+    total = sum(part[1:2] * jnp.exp(part[0:1] - top) for part in parts)
+    hit = sum(part[2:3] for part in parts)
     return top, total, hit
 
 
-def merge_kernel(at, *refs):
-    top, total, hit = merged(refs[:-1])
-    refs[-1][0:8, :] = top
-    refs[-1][8:16, :] = total
-    refs[-1][16:24, :] = hit
-
-
-def finish_kernel(at, *refs):
-    top, total, hit = merged(refs[:-2])
-    out, turned = refs[-2], refs[-1]
-    found = hit - top - jnp.log(total)
-    lane = lax.broadcasted_iota(jnp.int32, (8, 128), 1)
-    here = jnp.zeros((1, 128), F32)
-    for q in range(4):
-        turn = (8 * q + 128 - 8 * at[0]) % 128
-        turned[...] = jnp.where((lane // 8 & 3) == q, pltpu.roll(found, turn, 1), 0.0)
-        here = here + turned[pl.ds(at[1] * 4 + q, 1), :]
-    out[...] = here
+def block_kernel(at, found, out):
+    parts = [found[k] for k in range(X * CORE)]
+    out[0:1, :], out[1:2, :], out[2:3, :] = merged(parts)
+
+
+def merge_kernel(at, here, there, out):
+    out[0:1, :], out[1:2, :], out[2:3, :] = merged([here[...], there[...]])
+
+
+def finish_kernel(at, here, there, out):
+    top, total, hit = merged([here[...], there[...]])
+    out[...] = hit - top - jnp.log(total)
 
 
 def shards(
@@ -263,11 +276,19 @@
     first = jnp.where(c == 0, mine, theirs)
     second = jnp.where(c == 0, theirs, mine)
     first_s, first_d = first[:, :head_size], first[:, head_size : head_size + 1]
-    second_s, second_d = second[:, :head_size], second[:, head_size : head_size + 1]
+    second_s = second[:, :head_size]
+    second_d = second[:, head_size:]
+    both_d = second_d * first[:, head_size:]
+    coarse = both_d.astype(BF16)
     chip = jnp.concatenate(
-        [second_d * first_s + second_s, second[:, head_size:] * first[:, head_size:]], axis=1
-    )
-    arrived = [(s, move(chip, later_x(s))) for s in (3, 2, 1)]
+        [
+            (second_d[:, :1] * first_s + second_s).astype(BF16),
+            coarse,
+            (both_d - coarse.astype(F32)).astype(BF16),
+        ],
+        axis=1,
+    )
+    arrived = [(s, move(chip, along_x(s))) for s in (3, 2, 1)]
 
     queries = jnp.dot(tokens, q_weight, preferred_element_type=F32).astype(BF16).reshape(view)
     scores = jnp.einsum("thd,shd->hts", queries, keys, preferred_element_type=F32)
@@ -277,8 +298,10 @@
 
     state_in = carried_state
     for s, message in arrived:
-        d = jnp.where(x >= s, message[:, head_size : head_size + 1], 1.0)
-        state_in = d * state_in + message[:, :head_size]
+        message = message.astype(F32)
+        d = message[:, head_size : head_size + 1] + message[:, head_size + 8 : head_size + 9]
+        later = d * state_in + message[:, :head_size]
+        state_in = jnp.where(x >= s, later, state_in)
     state_in = jnp.where(c == 1, first_d * state_in + first_s, state_in)
     inter = jnp.exp(cumul)[:, :, None] * jnp.einsum(
         "thd,hde->the", queries.astype(F32), state_in, precision=HIGHEST
@@ -317,8 +340,8 @@
         partial_kernel,
         [on_chip((8, width), F32)] + [on_chip((8, width), BF16)] * 3,
         scalars,
-        own,
         *came,
+        loose=(own,),
         scratch=[pltpu.VMEM((32, width), F32)],
         bytes_=32 * width * 8,
         mib=8,
@@ -347,38 +370,47 @@
     half = up.shape[0] // 2
     far = (move(up[:half], along_q(1)), move(down[half:], along_q(3)))
     found = {}
-    for s, parts in ((0, (ours,)), (1, (up,)), (3, (down,)), (2, far)):
-        if s == 2:
-            parts, found = lax.optimization_barrier((parts, found))
-        swapped = (theirs,) if s == 0 else tuple(move(part, other_core) for part in parts)
-        for mine_too, blocks in ((True, parts), (False, swapped)):
-            logits = [jnp.dot(b, vocab_weight, preferred_element_type=F32) for b in blocks]
-            found[s, mine_too] = local(
-                functools.partial(score_kernel, s, mine_too, len(blocks)),
-                on_chip((8, 128), F32),
-                scalars,
-                lines,
-                *logits,
-                unread=blocks,
-                bytes_=4 * 128 * vocab_local,
-                name="score",
-            )
-    found = [found[k // 2, k % 2 == 0] for k in range(8)]
-    stats = local(place_kernel, on_chip((24, 128), F32), scalars, *found, name="place")
-    steps = [other_core]
-    for axis in (0, 2, 3):
-        steps += [near(axis, 0), near(axis, 1)]
+    for s, block in ((0, ours), (1, up), (3, down), (2, far)):
+        if s == 0:
+            swapped = theirs
+        elif s == 2:
+            block, found = lax.optimization_barrier((block, found))
+            swapped = jnp.concatenate([move(part, other_core) for part in block], axis=0)
+            block = jnp.concatenate(block, axis=0)
+        else:
+            swapped = move(block, other_core)
+        logits = [jnp.dot(b, vocab_weight, preferred_element_type=F32) for b in (block, swapped)]
+        found[s] = local(
+            functools.partial(score_kernel, s),
+            [on_chip((8, 128), F32)] * 2,
+            scalars,
+            lines,
+            *logits,
+            unread=(block, swapped),
+            bytes_=8 * 128 * vocab_local,
+            name="score",
+        )
+    sent = local(
+        place_kernel,
+        on_chip((X * CORE, 8, 128), F32),
+        scalars,
+        *[found[s][k] for s in range(4) for k in range(2)],
+        scratch=[pltpu.VMEM((24, 128), F32)],
+        name="place",
+    )
+    came = lax.all_to_all(sent, ("x", "core"), 0, 0)
+    stats = local(block_kernel, on_chip((8, 128), F32), scalars, came, name="block")
+    steps = [near(axis, step) for axis in (2, 3) for step in (0, 1)]
     for step in steps[:-1]:
         stats = local(
-            merge_kernel, on_chip((24, 128), F32), scalars, stats, move(stats, step), name="merge"
+            merge_kernel, on_chip((8, 128), F32), scalars, stats, move(stats, step), name="merge"
         )
-    parts = [stats, move(stats, steps[-1])]
     loglik = local(
         finish_kernel,
         jax.ShapeDtypeStruct((1, 128), F32),
         scalars,
-        *parts,
-        scratch=[pltpu.VMEM((8, 128), F32)],
+        stats,
+        move(stats, steps[-1]),
         name="finish",
     )
     return loglik.reshape(rows_here)

time: 178 us -> 163 us (0.916)
  waiting for transfers between devices: 66.7 us -> 53.9 us
  blocking collectives: 0 us -> 9.08 us
  matrix products: 37.1 us -> 31.8 us
  Pallas kernels: 21.7 us -> 16.9 us
  starting transfers between devices: 41.7 us -> 38.9 us
    ppermute x32 -> x29, waiting for transfers between devices: 66.7 us -> 53.9 us  [move(): return lax.ppermute(array, ALL, pairs)]
    all_to_all x0 -> x1, blocking collectives: none -> 9.08 us  [shards(): came = lax.all_to_all(sent, ('x', 'core'), 0, 0)]
    pallas_call x20 -> x14, Pallas kernels: 18 us -> 13.1 us  [local(): pl.pallas_call(kernel, out_shape=outs, in_specs=[SCALARS] + [WHOLE] * len...]
    dot_general x10 -> x8, matrix products: 26.8 us -> 22.5 us  [shards(): jnp.dot(b, vocab_weight, preferred_element_type=F32)]
    ppermute x32 -> x29, starting transfers between devices: 41.7 us -> 38.9 us  [move(): return lax.ppermute(array, ALL, pairs)]
    unnamed x28 -> x30, local copies, waits for them, and re-layouts: 4.59 us -> 5.36 us
  transfers between devices with their start and end apart: 32 -> 29, of which waited for: 20 -> 19; matrix products, arithmetic and copies ran while one was open for 18% -> 17% of each run, Pallas kernels for 4% -> 2%
where the time goes in v5:
time: 163 us; the launch traced here: 162 us
  waiting for transfers between devices  53.9 us (33%)
  starting transfers between devices  38.9 us (24%)
  matrix products  31.8 us (20%)
  Pallas kernels  16.9 us (10%)
  blocking collectives  9.08 us (6%)
  local copies, waits for them, and re-layouts  6.47 us (4%)
  other arithmetic  4.82 us (3%)
    ppermute x29, waiting for transfers between devices, move(): return lax.ppermute(array, ALL, pairs)  53.9 us
    ppermute x29, starting transfers between devices, move(): return lax.ppermute(array, ALL, pairs)  38.9 us
    dot_general x8, matrix products, shards(): jnp.dot(b, vocab_weight, preferred_element_type=F32)  22.5 us
    pallas_call x14, Pallas kernels, local(): pl.pallas_call(kernel, out_shape=outs, in_specs=[SCALARS] + [WHOLE] * len...  13.1 us
    all_to_all x1, blocking collectives, shards(): came = lax.all_to_all(sent, ('x', 'core'), 0, 0)  9.08 us
    unnamed x30, local copies, waits for them, and re-layouts  5.36 us
    pallas_call x1, Pallas kernels, shards(): pl.pallas_call(project_kernel, out_shape=[jax.ShapeDtypeStruct((32, width...  3.79 us
  transfers between devices with their start and end apart: 29, of which 19 were waited for; matrix products, arithmetic and copies ran while one was open for 17% of the time, Pallas kernels for 2%

profile of v5, /device:TPU:0, one launch (start us, length us, event | category | flops | bytes accessed | tf_op | source)
XLA Modules:
  0.0 162.3 jit_solution(9660667576995129385)
XLA Ops:
  1.9 2.1 %fusion.3 = bf16[16,2,8,128]{3,2,1,0:T(8,128)(2,1)S(1)} fusion(bf16[128,6144]{1,0:T(8,128)(2,1)} %param.10, bf16[6144,256]{1,0:T(8,128)(2,1)S(1)} %copy-done), kind=kOutput, calls=%fused_computation.9 | convolution fusion | flops 402685952 | bytes 4784128 | tf_op jit(solution)/shard_map/dot_general | solution.py:262
  6.4 2.9 %fusion.4 = bf16[16,2,8,128]{3,2,1,0:T(8,128)(2,1)S(1)} fusion(bf16[128,6144]{1,0:T(8,128)(2,1)} %param.10, bf16[6144,256]{1,0:T(8,128)(2,1)} %param.13), kind=kOutput, calls=%fused_computation.10 | convolution fusion | flops 402685952 | bytes 4784128 | tf_op jit(solution)/shard_map/dot_general | solution.py:293
  11.6 2.8 %collective-permute-start.3 = (bf16[2,144,128]{2,1,0:T(8,128)(2,1)}, bf16[2,144,128]{2,1,0:T(8,128)(2,1)}, u32[]{:S(2)}, u32[]{:S(2)}) collective-permute-start(bf16[2,144,128]{2,1,0:T(8,128)(2,1)} %pad_maximum_fusion.1), channel_id=1, source_target_pairs={{0,96},{1,97},{2,98},{3,99},{4,100},{5,101},{6,102},{7,103},{8,104... | collective-permute-start | bytes 221192 | tf_op jit(solution)/shard_map/ppermute | solution.py:23
  18.4 4.2 %collective-permute-done.2 = bf16[2,144,128]{2,1,0:T(8,128)(2,1)S(1)} collective-permute-done((bf16[2,144,128]{2,1,0:T(8,128)(2,1)}, bf16[2,144,128]{2,1,0:T(8,128)(2,1)S(1)}, u32[]{:S(2)}, u32[]{:S(2)}) %collective-permute-start.2) | collective-permute-done | bytes 73760 | tf_op jit(solution)/shard_map/ppermute | solution.py:23
  26.8 3.8 %project.1 = (f32[32,6144]{1,0:T(8,128)S(1)}, bf16[32,6144]{1,0:T(8,128)(2,1)}, bf16[32,6144]{1,0:T(8,128)(2,1)}, bf16[32,6144]{1,0:T(8,128)(2,1)}) custom-call(s32[8]{0:T(128)S(1)} %stack.32.at, bf16[128,256]{1,0:T(8,128)(2,1)S(1)} %copy.28.heads, bf16[256,6144]{1,0:T(8,128)(2,1)S(1)} %copy-done.1), custom_call_target="tpu_custom_call" | custom-call | flops 402653184 | bytes 4718592 | tf_op jit(solution)/shard_map/project/pallas_call | solution.py:318
  33.1 2.9 %collective-permute-start.5 = (bf16[32,6144]{1,0:T(8,128)(2,1)}, bf16[32,6144]{1,0:T(8,128)(2,1)}, u32[]{:S(2)}, u32[]{:S(2)}) collective-permute-start(bf16[32,6144]{1,0:T(8,128)(2,1)} %get-tuple-element.32), channel_id=1, source_target_pairs={{0,2},{1,3},{2,0},{3,1},{4,6},{5,7},{6,4},{7,5},{8,10},{9,11},{10,... | collective-permute-start | bytes 1179656 | tf_op jit(solution)/shard_map/ppermute | solution.py:23
  37.3 3.4 %collective-permute-done.4.one = bf16[32,6144]{1,0:T(8,128)(2,1)S(1)} collective-permute-done((bf16[32,6144]{1,0:T(8,128)(2,1)}, bf16[32,6144]{1,0:T(8,128)(2,1)S(1)}, u32[]{:S(2)}, u32[]{:S(2)}) %collective-permute-start.4) | collective-permute-done | bytes 393248 | tf_op jit(solution)/shard_map/ppermute | solution.py:23
  40.7 5.6 %collective-permute-done.5.two = bf16[32,6144]{1,0:T(8,128)(2,1)} collective-permute-done((bf16[32,6144]{1,0:T(8,128)(2,1)}, bf16[32,6144]{1,0:T(8,128)(2,1)}, u32[]{:S(2)}, u32[]{:S(2)}) %collective-permute-start.5) | collective-permute-done | bytes 393248 | tf_op jit(solution)/shard_map/ppermute | solution.py:23
  48.8 2.0 %collective-permute-start.7 = (bf16[8,6144]{1,0:T(8,128)(2,1)S(1)}, bf16[8,6144]{1,0:T(8,128)(2,1)S(1)}, u32[]{:S(2)}, u32[]{:S(2)}) collective-permute-start(bf16[8,6144]{1,0:T(8,128)(2,1)S(1)} %get-tuple-element.36), channel_id=1, source_target_pairs={{0,4},{1,5},{2,6},{3,7},{4,8},{5,9},{6,10},{7,11},{8,12},{9,13},{1... | collective-permute-start | bytes 294920 | tf_op jit(solution)/shard_map/ppermute | solution.py:23
  50.8 3.6 %collective-permute-start.8 = (bf16[8,6144]{1,0:T(8,128)(2,1)S(1)}, bf16[8,6144]{1,0:T(8,128)(2,1)S(1)}, u32[]{:S(2)}, u32[]{:S(2)}) collective-permute-start(bf16[8,6144]{1,0:T(8,128)(2,1)S(1)} %get-tuple-element.37), channel_id=1, source_target_pairs={{0,8},{1,9},{2,10},{3,11},{4,12},{5,13},{6,14},{7,15},{8,0},{9,1},... | collective-permute-start | bytes 294920 | tf_op jit(solution)/shard_map/ppermute | solution.py:23
  59.8 2.0 %collective-permute-start.11 = (bf16[8,6144]{1,0:T(8,128)(2,1)S(1)}, bf16[8,6144]{1,0:T(8,128)(2,1)S(1)}, u32[]{:S(2)}, u32[]{:S(2)}) collective-permute-start(bf16[8,6144]{1,0:T(8,128)(2,1)S(1)} %norm.1.a), channel_id=1, source_target_pairs={{0,64},{1,65},{2,66},{3,67},{4,68},{5,69},{6,70},{7,71},{8,72},{9,... | collective-permute-start | bytes 294920 | tf_op jit(solution)/shard_map/ppermute | solution.py:23
  63.3 3.4 %collective-permute-done.12.d = bf16[8,6144]{1,0:T(8,128)(2,1)S(1)} collective-permute-done((bf16[8,6144]{1,0:T(8,128)(2,1)S(1)}, bf16[8,6144]{1,0:T(8,128)(2,1)S(1)}, u32[]{:S(2)}, u32[]{:S(2)}) %collective-permute-start.12) | collective-permute-done | bytes 98336 | tf_op jit(solution)/shard_map/ppermute | solution.py:23
  69.9 2.1 %collective-permute-start.14 = (bf16[32,6144]{1,0:T(8,128)(2,1)S(1)}, bf16[32,6144]{1,0:T(8,128)(2,1)S(1)}, u32[]{:S(2)}, u32[]{:S(2)}) collective-permute-start(bf16[32,6144]{1,0:T(8,128)(2,1)S(1)} %stack_x.1.a), channel_id=1, source_target_pairs={{0,2},{1,3},{2,0},{3,1},{4,6},{5,7},{6,4},{7,5},{8,10},{9,11},{10,... | collective-permute-start | bytes 1179656 | tf_op jit(solution)/shard_map/ppermute | solution.py:23
  73.8 3.5 %collective-permute-done.15.d = bf16[32,6144]{1,0:T(8,128)(2,1)S(1)} collective-permute-done((bf16[32,6144]{1,0:T(8,128)(2,1)S(1)}, bf16[32,6144]{1,0:T(8,128)(2,1)S(1)}, u32[]{:S(2)}, u32[]{:S(2)}) %collective-permute-start.15) | collective-permute-done | bytes 393248 | tf_op jit(solution)/shard_map/ppermute | solution.py:23
  77.3 4.7 %collective-permute-done.14.c = bf16[32,6144]{1,0:T(8,128)(2,1)S(1)} collective-permute-done((bf16[32,6144]{1,0:T(8,128)(2,1)S(1)}, bf16[32,6144]{1,0:T(8,128)(2,1)S(1)}, u32[]{:S(2)}, u32[]{:S(2)}) %collective-permute-start.14) | collective-permute-done | bytes 393248 | tf_op jit(solution)/shard_map/ppermute | solution.py:23
  84.5 3.5 %collective-permute-done.16.b = bf16[128,6144]{1,0:T(8,128)(2,1)} collective-permute-done((bf16[128,6144]{1,0:T(8,128)(2,1)}, bf16[128,6144]{1,0:T(8,128)(2,1)}, u32[]{:S(2)}, u32[]{:S(2)}) %collective-permute-start.16) | collective-permute-done | bytes 1572896 | tf_op jit(solution)/shard_map/ppermute | solution.py:23
  88.0 2.3 %collective-permute-start.19 = (bf16[128,6144]{1,0:T(8,128)(2,1)}, bf16[128,6144]{1,0:T(8,128)(2,1)S(1)}, u32[]{:S(2)}, u32[]{:S(2)}) collective-permute-start(bf16[128,6144]{1,0:T(8,128)(2,1)} %get-tuple-element.39.rows_mine), channel_id=1, source_target_pairs={{0,12},{1,13},{2,14},{3,15},{4,0},{5,1},{6,2},{7,3},{8,4},{9,5},{1... | collective-permute-start | bytes 4718600 | tf_op jit(solution)/shard_map/ppermute | solution.py:23
  90.2 7.6 %fusion.53.mine = f32[128,1024]{1,0:T(8,128)S(1)} fusion(bf16[128,6144]{1,0:T(8,128)(2,1)} %get-tuple-element.39.rows_mine, bf16[6144,1024]{1,0:T(8,128)(2,1)} %param.18), kind=kOutput, calls=%fused_computation.77 | convolution fusion | flops 1610612736 | bytes 14680064 | tf_op jit(solution)/shard_map/dot_general | solution.py:382
  97.9 3.4 %fusion.54.theirs = f32[128,1024]{1,0:T(8,128)S(1)} fusion(bf16[128,6144]{1,0:T(8,128)(2,1)} %get-tuple-element.40.rows_theirs, bf16[6144,1024]{1,0:T(8,128)(2,1)S(1)} %bitcast.67), kind=kOutput, calls=%fused_computation.78 | convolution fusion | flops 1610612736 | bytes 14680064 | tf_op jit(solution)/shard_map/dot_general | solution.py:382
  102.4 6.2 %collective-permute-done.19.rows_mine = bf16[128,6144]{1,0:T(8,128)(2,1)S(1)} collective-permute-done((bf16[128,6144]{1,0:T(8,128)(2,1)}, bf16[128,6144]{1,0:T(8,128)(2,1)S(1)}, u32[]{:S(2)}, u32[]{:S(2)}) %collective-permute-start.19) | collective-permute-done | bytes 1572896 | tf_op jit(solution)/shard_map/ppermute | solution.py:23
  108.7 3.5 %collective-permute-start.20 = (bf16[64,6144]{1,0:T(8,128)(2,1)S(1)}, bf16[64,6144]{1,0:T(8,128)(2,1)S(1)}, u32[]{:S(2)}, u32[]{:S(2)}) collective-permute-start(bf16[64,6144]{1,0:T(8,128)(2,1)S(1)} %slice.89), channel_id=1, source_target_pairs={{0,12},{1,13},{2,14},{3,15},{4,0},{5,1},{6,2},{7,3},{8,4},{9,5},{1... | collective-permute-start | bytes 2359304 | tf_op jit(solution)/shard_map/ppermute | solution.py:23
  114.9 1.9 %fusion.55.mine = f32[128,1024]{1,0:T(8,128)S(1)} fusion(bf16[128,6144]{1,0:T(8,128)(2,1)S(1)} %collective-permute-done.17.rows_mine, bf16[6144,1024]{1,0:T(8,128)(2,1)S(1)} %bitcast.67), kind=kOutput, calls=%fused_computation.79 | convolution fusion | flops 1610612736 | bytes 14680064 | tf_op jit(solution)/shard_map/dot_general | solution.py:382
  116.8 1.9 %fusion.58.theirs = f32[128,1024]{1,0:T(8,128)S(1)} fusion(bf16[128,6144]{1,0:T(8,128)(2,1)S(1)} %collective-permute-done.22.rows_theirs, bf16[6144,1024]{1,0:T(8,128)(2,1)S(1)} %bitcast.67), kind=kOutput, calls=%fused_computation.82 | convolution fusion | flops 1610612736 | bytes 14680064 | tf_op jit(solution)/shard_map/dot_general | solution.py:382
  119.9 2.0 %fusion.56.theirs = f32[128,1024]{1,0:T(8,128)S(1)} fusion(bf16[128,6144]{1,0:T(8,128)(2,1)S(1)} %collective-permute-done.21.rows_theirs, bf16[6144,1024]{1,0:T(8,128)(2,1)S(1)} %bitcast.67), kind=kOutput, calls=%fused_computation.80 | convolution fusion | flops 1610612736 | bytes 14680064 | tf_op jit(solution)/shard_map/dot_general | solution.py:382
  123.0 2.5 %collective-permute-done.18 = bf16[64,6144]{1,0:T(8,128)(2,1)S(1)} collective-permute-done((bf16[64,6144]{1,0:T(8,128)(2,1)S(1)}, bf16[64,6144]{1,0:T(8,128)(2,1)S(1)}, u32[]{:S(2)}, u32[]{:S(2)}) %collective-permute-start.18) | collective-permute-done | bytes 786464 | tf_op jit(solution)/shard_map/ppermute | solution.py:23
  129.0 1.9 %fusion.60.theirs = f32[128,1024]{1,0:T(8,128)S(1)} fusion(bf16[128,6144]{1,0:T(8,128)(2,1)S(1)} %constant_dynamic-update-slice_fusion.2.rows_theirs, bf16[6144,1024]{1,0:T(8,128)(2,1)S(1)} %bitcast.67), kind=kOutput, calls=%fused_computation.84 | convolution fusion | flops 1610612736 | bytes 14680064 | tf_op jit(solution)/shard_map/dot_general | solution.py:382
  132.8 9.1 %all_to_all.5.found = f32[8,8,128]{2,1,0:T(8,128)S(1)} all-to-all(f32[8,8,128]{2,1,0:T(8,128)S(1)} %place.1), channel_id=1, replica_groups=mesh['x'=4,'core'=2,'z'=4,'y'=4] {'x','core'}, dimensions={0} | all-to-all | bytes 65536 | tf_op jit(solution)/shard_map/all_to_all | solution.py:401
  142.5 3.6 %collective-permute-done.25.there = f32[8,128]{1,0:T(8,128)S(1)} collective-permute-done((f32[8,128]{1,0:T(8,128)S(1)}, f32[8,128]{1,0:T(8,128)S(1)}, u32[]{:S(2)}, u32[]{:S(2)}) %collective-permute-start.25) | collective-permute-done | bytes 4128 | tf_op jit(solution)/shard_map/ppermute | solution.py:23
  147.5 4.1 %collective-permute-done.26.there = f32[8,128]{1,0:T(8,128)S(1)} collective-permute-done((f32[8,128]{1,0:T(8,128)S(1)}, f32[8,128]{1,0:T(8,128)S(1)}, u32[]{:S(2)}, u32[]{:S(2)}) %collective-permute-start.26) | collective-permute-done | bytes 4128 | tf_op jit(solution)/shard_map/ppermute | solution.py:23
  152.1 2.1 %collective-permute-start.27 = (f32[8,128]{1,0:T(8,128)S(1)}, f32[8,128]{1,0:T(8,128)S(1)}, u32[]{:S(2)}, u32[]{:S(2)}) collective-permute-start(f32[8,128]{1,0:T(8,128)S(1)} %merge.4.here), channel_id=1, source_target_pairs={{0,1},{1,0},{2,3},{3,2},{4,5},{5,4},{6,7},{7,6},{8,9},{9,8},{10,11... | collective-permute-start | bytes 12296 | tf_op jit(solution)/shard_map/ppermute | solution.py:23
  156.4 2.7 %collective-permute-start.28 = (f32[8,128]{1,0:T(8,128)S(1)}, f32[8,128]{1,0:T(8,128)S(1)}, u32[]{:S(2)}, u32[]{:S(2)}) collective-permute-start(f32[8,128]{1,0:T(8,128)S(1)} %merge.5.here), channel_id=1, source_target_pairs={{0,3},{1,2},{2,1},{3,0},{4,7},{5,6},{6,5},{7,4},{8,11},{9,10},{10,... | collective-permute-start | bytes 12296 | tf_op jit(solution)/shard_map/ppermute | solution.py:23
  159.1 2.2 %collective-permute-done.28.there = f32[8,128]{1,0:T(8,128)S(1)} collective-permute-done((f32[8,128]{1,0:T(8,128)S(1)}, f32[8,128]{1,0:T(8,128)S(1)}, u32[]{:S(2)}, u32[]{:S(2)}) %collective-permute-start.28) | collective-permute-done | bytes 4128 | tf_op jit(solution)/shard_map/ppermute | solution.py:23
  (121 shorter events, 52.3 us)
Async XLA Ops:
  6.4 3.6 %collective-permute-start = (f32[2,136,128]{2,1,0:T(8,128)}, f32[2,136,128]{2,1,0:T(8,128)}, u32[]{:S(2)}, u32[]{:S(2)}) collective-permute-start(f32[2,136,128]{2,1,0:T(8,128)} %pad_maximum_fusion), channel_id=1, source_target_pairs={{0,16},{1,17},{2,18},{3,19},{4,20},{5,21},{6,22},{7,23},{8,24},{9,... | collective-permute-start | bytes 417800 | tf_op jit(solution)/shard_map/ppermute | solution.py:23
  11.6 5.9 %collective-permute-start.3 = (bf16[2,144,128]{2,1,0:T(8,128)(2,1)}, bf16[2,144,128]{2,1,0:T(8,128)(2,1)}, u32[]{:S(2)}, u32[]{:S(2)}) collective-permute-start(bf16[2,144,128]{2,1,0:T(8,128)(2,1)} %pad_maximum_fusion.1), channel_id=1, source_target_pairs={{0,96},{1,97},{2,98},{3,99},{4,100},{5,101},{6,102},{7,103},{8,104... | collective-permute-start | bytes 221192 | tf_op jit(solution)/shard_map/ppermute | solution.py:23
  15.8 6.9 %collective-permute-start.2 = (bf16[2,144,128]{2,1,0:T(8,128)(2,1)}, bf16[2,144,128]{2,1,0:T(8,128)(2,1)S(1)}, u32[]{:S(2)}, u32[]{:S(2)}) collective-permute-start(bf16[2,144,128]{2,1,0:T(8,128)(2,1)} %pad_maximum_fusion.1), channel_id=1, source_target_pairs={{0,64},{1,65},{2,66},{3,67},{4,68},{5,69},{6,70},{7,71},{8,72},{9,... | collective-permute-start | bytes 221192 | tf_op jit(solution)/shard_map/ppermute | solution.py:23
  16.6 6.9 %collective-permute-start.1 = (bf16[2,144,128]{2,1,0:T(8,128)(2,1)}, bf16[2,144,128]{2,1,0:T(8,128)(2,1)S(1)}, u32[]{:S(2)}, u32[]{:S(2)}) collective-permute-start(bf16[2,144,128]{2,1,0:T(8,128)(2,1)} %pad_maximum_fusion.1), channel_id=1, source_target_pairs={{0,32},{1,33},{2,34},{3,35},{4,36},{5,37},{6,38},{7,39},{8,40},{9,... | collective-permute-start | bytes 221192 | tf_op jit(solution)/shard_map/ppermute | solution.py:23
  31.5 24.8 %copy-start.8 = (bf16[6144]{0:T(1024)(128)(2,1)S(1)}, bf16[6144]{0:T(1024)(128)(2,1)}, u32[]{:S(2)}) copy-start(bf16[6144]{0:T(1024)(128)(2,1)} %param.17) | copy-start | bytes 36868
  31.5 9.2 %collective-permute-start.4 = (bf16[32,6144]{1,0:T(8,128)(2,1)}, bf16[32,6144]{1,0:T(8,128)(2,1)S(1)}, u32[]{:S(2)}, u32[]{:S(2)}) collective-permute-start(bf16[32,6144]{1,0:T(8,128)(2,1)} %get-tuple-element.31), channel_id=1, source_target_pairs={{0,1},{1,2},{2,3},{3,0},{4,5},{5,6},{6,7},{7,4},{8,9},{9,10},{10,1... | collective-permute-start | bytes 1179656 | tf_op jit(solution)/shard_map/ppermute | solution.py:23
  33.1 13.2 %collective-permute-start.5 = (bf16[32,6144]{1,0:T(8,128)(2,1)}, bf16[32,6144]{1,0:T(8,128)(2,1)}, u32[]{:S(2)}, u32[]{:S(2)}) collective-permute-start(bf16[32,6144]{1,0:T(8,128)(2,1)} %get-tuple-element.32), channel_id=1, source_target_pairs={{0,2},{1,3},{2,0},{3,1},{4,6},{5,7},{6,4},{7,5},{8,10},{9,11},{10,... | collective-permute-start | bytes 1179656 | tf_op jit(solution)/shard_map/ppermute | solution.py:23
  36.0 10.3 %collective-permute-start.6 = (bf16[32,6144]{1,0:T(8,128)(2,1)}, bf16[32,6144]{1,0:T(8,128)(2,1)}, u32[]{:S(2)}, u32[]{:S(2)}) collective-permute-start(bf16[32,6144]{1,0:T(8,128)(2,1)} %get-tuple-element.33), channel_id=1, source_target_pairs={{0,3},{1,0},{2,1},{3,2},{4,7},{5,4},{6,5},{7,6},{8,11},{9,8},{10,9... | collective-permute-start | bytes 1179656 | tf_op jit(solution)/shard_map/ppermute | solution.py:23
  48.8 7.5 %collective-permute-start.7 = (bf16[8,6144]{1,0:T(8,128)(2,1)S(1)}, bf16[8,6144]{1,0:T(8,128)(2,1)S(1)}, u32[]{:S(2)}, u32[]{:S(2)}) collective-permute-start(bf16[8,6144]{1,0:T(8,128)(2,1)S(1)} %get-tuple-element.36), channel_id=1, source_target_pairs={{0,4},{1,5},{2,6},{3,7},{4,8},{5,9},{6,10},{7,11},{8,12},{9,13},{1... | collective-permute-start | bytes 294920 | tf_op jit(solution)/shard_map/ppermute | solution.py:23
  50.8 7.2 %collective-permute-start.8 = (bf16[8,6144]{1,0:T(8,128)(2,1)S(1)}, bf16[8,6144]{1,0:T(8,128)(2,1)S(1)}, u32[]{:S(2)}, u32[]{:S(2)}) collective-permute-start(bf16[8,6144]{1,0:T(8,128)(2,1)S(1)} %get-tuple-element.37), channel_id=1, source_target_pairs={{0,8},{1,9},{2,10},{3,11},{4,12},{5,13},{6,14},{7,15},{8,0},{9,1},... | collective-permute-start | bytes 294920 | tf_op jit(solution)/shard_map/ppermute | solution.py:23
  54.4 4.6 %collective-permute-start.9 = (bf16[8,6144]{1,0:T(8,128)(2,1)S(1)}, bf16[8,6144]{1,0:T(8,128)(2,1)S(1)}, u32[]{:S(2)}, u32[]{:S(2)}) collective-permute-start(bf16[8,6144]{1,0:T(8,128)(2,1)S(1)} %get-tuple-element.38), channel_id=1, source_target_pairs={{0,12},{1,13},{2,14},{3,15},{4,0},{5,1},{6,2},{7,3},{8,4},{9,5},{1... | collective-permute-start | bytes 294920 | tf_op jit(solution)/shard_map/ppermute | solution.py:23
  59.7 6.9 %collective-permute-start.12 = (bf16[8,6144]{1,0:T(8,128)(2,1)S(1)}, bf16[8,6144]{1,0:T(8,128)(2,1)S(1)}, u32[]{:S(2)}, u32[]{:S(2)}) collective-permute-start(bf16[8,6144]{1,0:T(8,128)(2,1)S(1)} %norm.1.a), channel_id=1, source_target_pairs={{0,32},{1,33},{2,34},{3,35},{4,36},{5,37},{6,38},{7,39},{8,40},{9,... | collective-permute-start | bytes 294920 | tf_op jit(solution)/shard_map/ppermute | solution.py:23
  59.8 6.9 %collective-permute-start.11 = (bf16[8,6144]{1,0:T(8,128)(2,1)S(1)}, bf16[8,6144]{1,0:T(8,128)(2,1)S(1)}, u32[]{:S(2)}, u32[]{:S(2)}) collective-permute-start(bf16[8,6144]{1,0:T(8,128)(2,1)S(1)} %norm.1.a), channel_id=1, source_target_pairs={{0,64},{1,65},{2,66},{3,67},{4,68},{5,69},{6,70},{7,71},{8,72},{9,... | collective-permute-start | bytes 294920 | tf_op jit(solution)/shard_map/ppermute | solution.py:23
  61.8 5.8 %collective-permute-start.10 = (bf16[8,6144]{1,0:T(8,128)(2,1)S(1)}, bf16[8,6144]{1,0:T(8,128)(2,1)S(1)}, u32[]{:S(2)}, u32[]{:S(2)}) collective-permute-start(bf16[8,6144]{1,0:T(8,128)(2,1)S(1)} %norm.1.a), channel_id=1, source_target_pairs={{0,96},{1,97},{2,98},{3,99},{4,100},{5,101},{6,102},{7,103},{8,104... | collective-permute-start | bytes 294920 | tf_op jit(solution)/shard_map/ppermute | solution.py:23
  68.2 16.0 %copy-start.9 = (s32[1024]{0:T(1024)S(1)}, s32[1024]{0:T(1024)}, u32[]{:S(2)}) copy-start(s32[1024]{0:T(1024)} %param.19) | copy-start | bytes 12292
  68.2 9.1 %collective-permute-start.15 = (bf16[32,6144]{1,0:T(8,128)(2,1)S(1)}, bf16[32,6144]{1,0:T(8,128)(2,1)S(1)}, u32[]{:S(2)}, u32[]{:S(2)}) collective-permute-start(bf16[32,6144]{1,0:T(8,128)(2,1)S(1)} %stack_x.1.a), channel_id=1, source_target_pairs={{0,1},{1,2},{2,3},{3,0},{4,5},{5,6},{6,7},{7,4},{8,9},{9,10},{10,1... | collective-permute-start | bytes 1179656 | tf_op jit(solution)/shard_map/ppermute | solution.py:23
  69.9 12.1 %collective-permute-start.14 = (bf16[32,6144]{1,0:T(8,128)(2,1)S(1)}, bf16[32,6144]{1,0:T(8,128)(2,1)S(1)}, u32[]{:S(2)}, u32[]{:S(2)}) collective-permute-start(bf16[32,6144]{1,0:T(8,128)(2,1)S(1)} %stack_x.1.a), channel_id=1, source_target_pairs={{0,2},{1,3},{2,0},{3,1},{4,6},{5,7},{6,4},{7,5},{8,10},{9,11},{10,... | collective-permute-start | bytes 1179656 | tf_op jit(solution)/shard_map/ppermute | solution.py:23
  72.0 10.4 %collective-permute-start.13 = (bf16[32,6144]{1,0:T(8,128)(2,1)S(1)}, bf16[32,6144]{1,0:T(8,128)(2,1)S(1)}, u32[]{:S(2)}, u32[]{:S(2)}) collective-permute-start(bf16[32,6144]{1,0:T(8,128)(2,1)S(1)} %stack_x.1.a), channel_id=1, source_target_pairs={{0,3},{1,0},{2,1},{3,2},{4,7},{5,4},{6,5},{7,6},{8,11},{9,8},{10,9... | collective-permute-start | bytes 1179656 | tf_op jit(solution)/shard_map/ppermute | solution.py:23
  84.2 3.8 %collective-permute-start.16 = (bf16[128,6144]{1,0:T(8,128)(2,1)}, bf16[128,6144]{1,0:T(8,128)(2,1)}, u32[]{:S(2)}, u32[]{:S(2)}) collective-permute-start(bf16[128,6144]{1,0:T(8,128)(2,1)} %stack_p.1.a), channel_id=1, source_target_pairs={{0,16},{1,17},{2,18},{3,19},{4,20},{5,21},{6,22},{7,23},{8,24},{9,... | collective-permute-start | bytes 4718600 | tf_op jit(solution)/shard_map/ppermute | solution.py:23
  88.0 9.9 %slice-start.2 = ((s8[12582912]{0:T(1024)(128)(4,1)}), s8[4194304]{0:T(1024)(128)(4,1)S(1)}, s32[]{:S(2)}) async-start(s8[12582912]{0:T(1024)(128)(4,1)} %bitcast.66), calls=%async_computation.3 | async-start | bytes 8388608
  88.0 20.7 %collective-permute-start.19 = (bf16[128,6144]{1,0:T(8,128)(2,1)}, bf16[128,6144]{1,0:T(8,128)(2,1)S(1)}, u32[]{:S(2)}, u32[]{:S(2)}) collective-permute-start(bf16[128,6144]{1,0:T(8,128)(2,1)} %get-tuple-element.39.rows_mine), channel_id=1, source_target_pairs={{0,12},{1,13},{2,14},{3,15},{4,0},{5,1},{6,2},{7,3},{8,4},{9,5},{1... | collective-permute-start | bytes 4718600 | tf_op jit(solution)/shard_map/ppermute | solution.py:23
  90.2 22.0 %collective-permute-start.17 = (bf16[128,6144]{1,0:T(8,128)(2,1)}, bf16[128,6144]{1,0:T(8,128)(2,1)S(1)}, u32[]{:S(2)}, u32[]{:S(2)}) collective-permute-start(bf16[128,6144]{1,0:T(8,128)(2,1)} %get-tuple-element.39.rows_mine), channel_id=1, source_target_pairs={{0,4},{1,5},{2,6},{3,7},{4,8},{5,9},{6,10},{7,11},{8,12},{9,13},{1... | collective-permute-start | bytes 4718600 | tf_op jit(solution)/shard_map/ppermute | solution.py:23
  108.7 14.3 %collective-permute-start.20 = (bf16[64,6144]{1,0:T(8,128)(2,1)S(1)}, bf16[64,6144]{1,0:T(8,128)(2,1)S(1)}, u32[]{:S(2)}, u32[]{:S(2)}) collective-permute-start(bf16[64,6144]{1,0:T(8,128)(2,1)S(1)} %slice.89), channel_id=1, source_target_pairs={{0,12},{1,13},{2,14},{3,15},{4,0},{5,1},{6,2},{7,3},{8,4},{9,5},{1... | collective-permute-start | bytes 2359304 | tf_op jit(solution)/shard_map/ppermute | solution.py:23
  112.3 13.3 %collective-permute-start.18 = (bf16[64,6144]{1,0:T(8,128)(2,1)S(1)}, bf16[64,6144]{1,0:T(8,128)(2,1)S(1)}, u32[]{:S(2)}, u32[]{:S(2)}) collective-permute-start(bf16[64,6144]{1,0:T(8,128)(2,1)S(1)} %slice.88), channel_id=1, source_target_pairs={{0,4},{1,5},{2,6},{3,7},{4,8},{5,9},{6,10},{7,11},{8,12},{9,13},{1... | collective-permute-start | bytes 2359304 | tf_op jit(solution)/shard_map/ppermute | solution.py:23
  112.3 4.5 %collective-permute-start.22 = (bf16[128,6144]{1,0:T(8,128)(2,1)S(1)}, bf16[128,6144]{1,0:T(8,128)(2,1)S(1)}, u32[]{:S(2)}, u32[]{:S(2)}) collective-permute-start(bf16[128,6144]{1,0:T(8,128)(2,1)S(1)} %collective-permute-done.19.rows_mine), channel_id=1, source_target_pairs={{0,16},{1,17},{2,18},{3,19},{4,20},{5,21},{6,22},{7,23},{8,24},{9,... | collective-permute-start | bytes 4718600 | tf_op jit(solution)/shard_map/ppermute | solution.py:23
  112.4 7.4 %collective-permute-start.21 = (bf16[128,6144]{1,0:T(8,128)(2,1)S(1)}, bf16[128,6144]{1,0:T(8,128)(2,1)S(1)}, u32[]{:S(2)}, u32[]{:S(2)}) collective-permute-start(bf16[128,6144]{1,0:T(8,128)(2,1)S(1)} %collective-permute-done.17.rows_mine), channel_id=1, source_target_pairs={{0,16},{1,17},{2,18},{3,19},{4,20},{5,21},{6,22},{7,23},{8,24},{9,... | collective-permute-start | bytes 4718600 | tf_op jit(solution)/shard_map/ppermute | solution.py:23
  125.5 2.9 %collective-permute-start.23 = (bf16[64,6144]{1,0:T(8,128)(2,1)S(1)}, bf16[64,6144]{1,0:T(8,128)(2,1)S(1)}, u32[]{:S(2)}, u32[]{:S(2)}) collective-permute-start(bf16[64,6144]{1,0:T(8,128)(2,1)S(1)} %collective-permute-done.18), channel_id=1, source_target_pairs={{0,16},{1,17},{2,18},{3,19},{4,20},{5,21},{6,22},{7,23},{8,24},{9,... | collective-permute-start | bytes 2359304 | tf_op jit(solution)/shard_map/ppermute | solution.py:23
  125.6 3.3 %collective-permute-start.24 = (bf16[64,6144]{1,0:T(8,128)(2,1)S(1)}, bf16[64,6144]{1,0:T(8,128)(2,1)S(1)}, u32[]{:S(2)}, u32[]{:S(2)}) collective-permute-start(bf16[64,6144]{1,0:T(8,128)(2,1)S(1)} %collective-permute-done.20), channel_id=1, source_target_pairs={{0,16},{1,17},{2,18},{3,19},{4,20},{5,21},{6,22},{7,23},{8,24},{9,... | collective-permute-start | bytes 2359304 | tf_op jit(solution)/shard_map/ppermute | solution.py:23
  142.4 3.7 %collective-permute-start.25 = (f32[8,128]{1,0:T(8,128)S(1)}, f32[8,128]{1,0:T(8,128)S(1)}, u32[]{:S(2)}, u32[]{:S(2)}) collective-permute-start(f32[8,128]{1,0:T(8,128)S(1)} %block.1.here), channel_id=1, source_target_pairs={{0,4},{1,5},{2,6},{3,7},{4,0},{5,1},{6,2},{7,3},{8,12},{9,13},{10,... | collective-permute-start | bytes 12296 | tf_op jit(solution)/shard_map/ppermute | solution.py:23
  146.7 4.9 %collective-permute-start.26 = (f32[8,128]{1,0:T(8,128)S(1)}, f32[8,128]{1,0:T(8,128)S(1)}, u32[]{:S(2)}, u32[]{:S(2)}) collective-permute-start(f32[8,128]{1,0:T(8,128)S(1)} %merge.3.here), channel_id=1, source_target_pairs={{0,12},{1,13},{2,14},{3,15},{4,8},{5,9},{6,10},{7,11},{8,4},{9,5},... | collective-permute-start | bytes 12296 | tf_op jit(solution)/shard_map/ppermute | solution.py:23
  152.1 3.7 %collective-permute-start.27 = (f32[8,128]{1,0:T(8,128)S(1)}, f32[8,128]{1,0:T(8,128)S(1)}, u32[]{:S(2)}, u32[]{:S(2)}) collective-permute-start(f32[8,128]{1,0:T(8,128)S(1)} %merge.4.here), channel_id=1, source_target_pairs={{0,1},{1,0},{2,3},{3,2},{4,5},{5,4},{6,7},{7,6},{8,9},{9,8},{10,11... | collective-permute-start | bytes 12296 | tf_op jit(solution)/shard_map/ppermute | solution.py:23
  156.4 4.9 %collective-permute-start.28 = (f32[8,128]{1,0:T(8,128)S(1)}, f32[8,128]{1,0:T(8,128)S(1)}, u32[]{:S(2)}, u32[]{:S(2)}) collective-permute-start(f32[8,128]{1,0:T(8,128)S(1)} %merge.5.here), channel_id=1, source_target_pairs={{0,3},{1,2},{2,1},{3,0},{4,7},{5,6},{6,5},{7,4},{8,11},{9,10},{10,... | collective-permute-start | bytes 12296 | tf_op jit(solution)/shard_map/ppermute | solution.py:23
  (11 other events, 38.8 us)

commit v6 on v5

--- a/solution.py
+++ b/solution.py
@@ -27,15 +27,6 @@
     return (x, 1 - c, z, y)
 
 
-def near(axis, step):
-    def target(*at):
-        to = list(at)
-        to[axis] = (at[axis] + (1 if at[axis] % 2 == step else 3)) % 4
-        return tuple(to)
-
-    return target
-
-
 def along_x(s):
     return lambda x, c, z, y: ((x + s) % X, c, z, y)
 
@@ -50,6 +41,14 @@
 
 def on_chip(shape, dtype):
     return pltpu.VMEM(shape, dtype)
+
+
+def in_hbm(shape, dtype):
+    return pltpu.HBM(shape, dtype)
+
+
+def leave(array):
+    return pltpu.with_memory_space_constraint(array, pltpu.HBM)
 
 
 def pin(array):
@@ -73,7 +72,7 @@
         compiler_params=pltpu.CompilerParams(vmem_limit_bytes=mib * 1024 * 1024),
         cost_estimate=pl.CostEstimate(flops=flops, bytes_accessed=bytes_, transcendentals=0),
         name=name,
-    )(scalars, *[pin(a) for a in arrays], *loose, *[pin(a) for a in unread])
+    )(scalars, *[pin(a) for a in arrays], *[leave(a) for a in loose], *[pin(a) for a in unread])
 
 
 def tie_kernel(a, b, out_a, out_b):
@@ -90,6 +89,31 @@
         compiler_params=pltpu.CompilerParams(vmem_limit_bytes=1024 * 1024),
         name="tie",
     )(pin(a), pin(b))
+
+
+def combine_kernel(at, mine, theirs, chip):
+    size = mine.shape[2]
+    low = at[1] == 0
+    for h in range(mine.shape[0]):
+        first = jnp.where(low, mine[h], theirs[h])
+        second = jnp.where(low, theirs[h], mine[h])
+        decay = jnp.broadcast_to((second[size:] * first[size:])[:1], (16, size))
+        coarse = decay.astype(BF16).astype(F32)
+        row = lax.broadcasted_iota(jnp.int32, (16, size), 0)
+        chip[h, :size, :] = (second[size : size + 1] * first[:size] + second[:size]).astype(BF16)
+        chip[h, size:, :] = jnp.where(row < 8, coarse, decay - coarse).astype(BF16)
+
+
+def state_kernel(at, carried, three, two, one, theirs, out):
+    size = carried.shape[2]
+    for h in range(carried.shape[0]):
+        state = carried[h]
+        for s, message in ((3, three), (2, two), (1, one)):
+            part = message[h].astype(F32)
+            decay = part[size : size + 1] + part[size + 8 : size + 9]
+            state = jnp.where(at[0] >= s, decay * state + part[:size], state)
+        part = theirs[h]
+        out[h] = jnp.where(at[1] == 1, part[size : size + 1] * state + part[:size], state)
 
 
 def project_kernel(at, heads, weight, own, one, two, three, rolled):
@@ -223,16 +247,13 @@
 
 
 def block_kernel(at, found, out):
-    parts = [found[k] for k in range(X * CORE)]
-    out[0:1, :], out[1:2, :], out[2:3, :] = merged(parts)
-
-
-def merge_kernel(at, here, there, out):
-    out[0:1, :], out[1:2, :], out[2:3, :] = merged([here[...], there[...]])
-
-
-def finish_kernel(at, here, there, out):
-    top, total, hit = merged([here[...], there[...]])
+    top, total, hit = merged([found[k] for k in range(X * CORE)])
+    for k in range(Z * Y):
+        out[k, 0:1, :], out[k, 1:2, :], out[k, 2:3, :] = top, total, hit
+
+
+def finish_kernel(at, found, out):
+    top, total, hit = merged([found[k] for k in range(Z * Y)])
     out[...] = hit - top - jnp.log(total)
 
 
@@ -273,36 +294,32 @@
     decay = jnp.broadcast_to(jnp.exp(last_cum)[:, None, None], (heads_here, 8, head_size))
     mine = jnp.concatenate([state, decay], axis=1)
     theirs = move(mine, other_core)
-    first = jnp.where(c == 0, mine, theirs)
-    second = jnp.where(c == 0, theirs, mine)
-    first_s, first_d = first[:, :head_size], first[:, head_size : head_size + 1]
-    second_s = second[:, :head_size]
-    second_d = second[:, head_size:]
-    both_d = second_d * first[:, head_size:]
-    coarse = both_d.astype(BF16)
-    chip = jnp.concatenate(
-        [
-            (second_d[:, :1] * first_s + second_s).astype(BF16),
-            coarse,
-            (both_d - coarse.astype(F32)).astype(BF16),
-        ],
-        axis=1,
-    )
+    chip = local(
+        combine_kernel,
+        on_chip((heads_here, head_size + 16, head_size), BF16),
+        scalars,
+        mine,
+        theirs,
+        name="combine",
+    )
+    tokens_then, chip = lax.optimization_barrier((tokens, chip))
     arrived = [(s, move(chip, along_x(s))) for s in (3, 2, 1)]
 
-    queries = jnp.dot(tokens, q_weight, preferred_element_type=F32).astype(BF16).reshape(view)
+    queries = jnp.dot(tokens_then, q_weight, preferred_element_type=F32).astype(BF16).reshape(view)
     scores = jnp.einsum("thd,shd->hts", queries, keys, preferred_element_type=F32)
     diff = jnp.transpose(cumul[:, None, :] - cumul[None, :, :], (2, 0, 1))
     weight = (scores * jnp.exp(jnp.where(lower[None], diff, -1e30))).astype(BF16)
     intra = jnp.einsum("hts,shd->thd", weight, values, preferred_element_type=F32)
 
-    state_in = carried_state
-    for s, message in arrived:
-        message = message.astype(F32)
-        d = message[:, head_size : head_size + 1] + message[:, head_size + 8 : head_size + 9]
-        later = d * state_in + message[:, :head_size]
-        state_in = jnp.where(x >= s, later, state_in)
-    state_in = jnp.where(c == 1, first_d * state_in + first_s, state_in)
+    state_in = local(
+        state_kernel,
+        on_chip(carried_state.shape, F32),
+        scalars,
+        carried_state,
+        *[message for _, message in arrived],
+        theirs,
+        name="state",
+    )
     inter = jnp.exp(cumul)[:, :, None] * jnp.einsum(
         "thd,hde->the", queries.astype(F32), state_in, precision=HIGHEST
     )
@@ -313,12 +330,11 @@
     flat_heads = normed_heads.astype(BF16).reshape(rows_here, heads_here * head_size)
 
     inner = flat_heads.shape[1]
-    wide = width // 6 if width % 768 == 0 else width
+    wide = width // 3 if width % 384 == 0 else width
     share = pl.BlockSpec((32, wide), lambda n: (0, n))
     own, *sent = pl.pallas_call(
         project_kernel,
-        out_shape=[jax.ShapeDtypeStruct((32, width), F32)]
-        + [jax.ShapeDtypeStruct((32, width), BF16)] * 3,
+        out_shape=[in_hbm((32, width), F32)] + [in_hbm((32, width), BF16)] * 3,
         grid=(width // wide,),
         in_specs=[
             SCALARS,
@@ -327,14 +343,14 @@
         ],
         out_specs=[share] * 4,
         scratch_shapes=[pltpu.VMEM((rows_here, inner), BF16)],
-        compiler_params=pltpu.CompilerParams(vmem_limit_bytes=8 * 1024 * 1024),
+        compiler_params=pltpu.CompilerParams(vmem_limit_bytes=12 * 1024 * 1024),
         cost_estimate=pl.CostEstimate(
             flops=2 * rows_here * inner * width,
             bytes_accessed=2 * width * (inner + rows_here),
             transcendentals=0,
         ),
         name="project",
-    )(scalars, flat_heads, out_weight)
+    )(scalars, flat_heads, leave(out_weight))
     came = [move(part, along_p(s)) for s, part in zip((1, 2, 3), sent)]
     own, *sent = local(
         partial_kernel,
@@ -399,19 +415,10 @@
         name="place",
     )
     came = lax.all_to_all(sent, ("x", "core"), 0, 0)
-    stats = local(block_kernel, on_chip((8, 128), F32), scalars, came, name="block")
-    steps = [near(axis, step) for axis in (2, 3) for step in (0, 1)]
-    for step in steps[:-1]:
-        stats = local(
-            merge_kernel, on_chip((8, 128), F32), scalars, stats, move(stats, step), name="merge"
-        )
+    sent = local(block_kernel, on_chip((Z * Y, 8, 128), F32), scalars, came, name="block")
+    came = lax.all_to_all(sent, ("z", "y"), 0, 0)
     loglik = local(
-        finish_kernel,
-        jax.ShapeDtypeStruct((1, 128), F32),
-        scalars,
-        stats,
-        move(stats, steps[-1]),
-        name="finish",
+        finish_kernel, jax.ShapeDtypeStruct((1, 128), F32), scalars, came, name="finish"
     )
     return loglik.reshape(rows_here)
 

time: 163 us -> 152 us (0.933)
  waiting for transfers between devices: 53.9 us -> 38.6 us
  blocking collectives: 9.08 us -> 20.8 us
  starting transfers between devices: 38.9 us -> 34.5 us
  local copies, waits for them, and re-layouts: 6.47 us -> 2.33 us
  other arithmetic: 4.82 us -> 1.03 us
  matrix products: 31.8 us -> 35.4 us
    ppermute x29 -> x25, waiting for transfers between devices: 53.9 us -> 38.6 us  [move(): return lax.ppermute(array, ALL, pairs)]
    all_to_all x0 -> x1, blocking collectives: none -> 11.9 us  [shards(): came = lax.all_to_all(sent, ('z', 'y'), 0, 0)]
    ppermute x29 -> x25, starting transfers between devices: 38.9 us -> 34.5 us  [move(): return lax.ppermute(array, ALL, pairs)]
    unnamed x30 -> x20, local copies, waits for them, and re-layouts: 5.36 us -> 1.1 us
    pallas_call x14 -> x13, Pallas kernels: 13.1 us -> 14 us  [local(): pl.pallas_call(kernel, out_shape=outs, in_specs=[SCALARS] + [WHOLE] * len...]
  transfers between devices with their start and end apart: 29 -> 25, of which waited for: 19 -> 14; matrix products, arithmetic and copies ran while one was open for 17% -> 18% of each run, Pallas kernels for 2% -> 2%
where the time goes in v6:
time: 152 us; the launch traced here: 151 us
  waiting for transfers between devices  38.6 us (25%)
  matrix products  35.4 us (23%)
  starting transfers between devices  34.5 us (23%)
  blocking collectives  20.8 us (14%)
  Pallas kernels  18.4 us (12%)
  local copies, waits for them, and re-layouts  2.33 us (2%)
    ppermute x25, waiting for transfers between devices, move(): return lax.ppermute(array, ALL, pairs)  38.6 us
    ppermute x25, starting transfers between devices, move(): return lax.ppermute(array, ALL, pairs)  34.5 us
    dot_general x8, matrix products, shards(): jnp.dot(b, vocab_weight, preferred_element_type=F32)  22.5 us
    pallas_call x13, Pallas kernels, local(): pl.pallas_call(kernel, out_shape=outs, in_specs=[SCALARS] + [WHOLE] * len...  14 us
    all_to_all x1, blocking collectives, shards(): came = lax.all_to_all(sent, ('z', 'y'), 0, 0)  11.9 us
    all_to_all x1, blocking collectives, shards(): came = lax.all_to_all(sent, ('x', 'core'), 0, 0)  8.98 us
    pallas_call x1, Pallas kernels, shards(): pl.pallas_call(project_kernel, out_shape=[in_hbm((32, width), F32)] + [in...  4.44 us
    dot_general x1, matrix products, shards(): jnp.dot(tokens_then, q_weight, preferred_element_type=F32).astype(BF16)  3.56 us
  transfers between devices with their start and end apart: 25, of which 14 were waited for; matrix products, arithmetic and copies ran while one was open for 18% of the time, Pallas kernels for 2%

profile of v6, /device:TPU:0, one launch (start us, length us, event | category | flops | bytes accessed | tf_op | source)
XLA Modules:
  0.0 151.5 jit_solution(2196500759154638646)
XLA Ops:
  1.9 2.0 %convolution_convert_fusion.1 = bf16[128,256]{1,0:T(8,128)(2,1)S(1)} fusion(bf16[128,6144]{1,0:T(8,128)(2,1)} %param.10, bf16[6144,256]{1,0:T(8,128)(2,1)S(1)} %copy-done), kind=kOutput, calls=%fused_computation.6 | convolution fusion | flops 402685952 | bytes 4784128 | tf_op jit(solution)/shard_map/dot_general | solution.py:282
  4.0 3.0 %convolution_convert_fusion.2 = bf16[128,256]{1,0:T(8,128)(2,1)S(1)} fusion(bf16[128,6144]{1,0:T(8,128)(2,1)} %param.10, bf16[6144,256]{1,0:T(8,128)(2,1)} %param.15), kind=kOutput, calls=%fused_computation.7 | convolution fusion | flops 402685952 | bytes 4784128 | tf_op jit(solution)/shard_map/dot_general | solution.py:283
  12.0 2.7 %collective-permute-start.2 = (bf16[2,144,128]{2,1,0:T(8,128)(2,1)}, bf16[2,144,128]{2,1,0:T(8,128)(2,1)}, u32[]{:S(2)}, u32[]{:S(2)}) collective-permute-start(bf16[2,144,128]{2,1,0:T(8,128)(2,1)} %combine.1), channel_id=1, source_target_pairs={{0,64},{1,65},{2,66},{3,67},{4,68},{5,69},{6,70},{7,71},{8,72},{9,... | collective-permute-start | bytes 221192 | tf_op jit(solution)/shard_map/ppermute | solution.py:23
  16.2 3.6 %fusion.3 = bf16[16,2,8,128]{3,2,1,0:T(8,128)(2,1)} fusion(bf16[128,6144]{1,0:T(8,128)(2,1)} %param.10, bf16[6144,256]{1,0:T(8,128)(2,1)} %param.13), kind=kOutput, calls=%fused_computation.9 | convolution fusion | flops 402685952 | bytes 4784128 | tf_op jit(solution)/shard_map/dot_general | solution.py:308
  19.8 1.9 %convolution_bitcast_fusion.1 = f32[128,2,128]{0,2,1:T(8,128)} fusion(bf16[128,2,128]{0,2,1:T(8,128)(2,1)} %bitcast.65, bf16[128,2,128]{0,2,1:T(8,128)(2,1)} %bitcast.63, f32[2,128]{1,0:T(2,128)S(1)} %bitcast.66, pred[128,128]{1,0:T(8,128)(4,1)S(1)} %iota_compare_fusion, bf16[16,2,8,128]{3,2,1,0:T(8,128)(2,1)} %fusion.3), kind=kOutput, calls=%fused_computation.2 | convolution fusion | flops 16908288 | bytes 345088 | tf_op jit(solution)/shard_map/hts,shd->thd/dot_general | solution.py:312
  24.1 4.4 %project.1 = (f32[32,6144]{1,0:T(8,128)}, bf16[32,6144]{1,0:T(8,128)(2,1)}, bf16[32,6144]{1,0:T(8,128)(2,1)}, bf16[32,6144]{1,0:T(8,128)(2,1)}) custom-call(s32[8]{0:T(128)S(1)} %stack.32.at, bf16[128,256]{1,0:T(8,128)(2,1)S(1)} %copy.28.heads, bf16[256,6144]{1,0:T(8,128)(2,1)} %weight.1), custom_call_target="tpu_custom_call" | custom-call | flops 402653184 | bytes 4718592 | tf_op jit(solution)/shard_map/project/pallas_call | solution.py:335
  30.1 2.9 %collective-permute-start.5 = (bf16[32,6144]{1,0:T(8,128)(2,1)}, bf16[32,6144]{1,0:T(8,128)(2,1)}, u32[]{:S(2)}, u32[]{:S(2)}) collective-permute-start(bf16[32,6144]{1,0:T(8,128)(2,1)} %get-tuple-element.36), channel_id=1, source_target_pairs={{0,2},{1,3},{2,0},{3,1},{4,6},{5,7},{6,4},{7,5},{8,10},{9,11},{10,... | collective-permute-start | bytes 1179656 | tf_op jit(solution)/shard_map/ppermute | solution.py:23
  34.4 3.4 %collective-permute-done.4.one = bf16[32,6144]{1,0:T(8,128)(2,1)S(1)} collective-permute-done((bf16[32,6144]{1,0:T(8,128)(2,1)}, bf16[32,6144]{1,0:T(8,128)(2,1)S(1)}, u32[]{:S(2)}, u32[]{:S(2)}) %collective-permute-start.4) | collective-permute-done | bytes 393248 | tf_op jit(solution)/shard_map/ppermute | solution.py:23
  37.8 5.6 %collective-permute-done.5.two = bf16[32,6144]{1,0:T(8,128)(2,1)} collective-permute-done((bf16[32,6144]{1,0:T(8,128)(2,1)}, bf16[32,6144]{1,0:T(8,128)(2,1)}, u32[]{:S(2)}, u32[]{:S(2)}) %collective-permute-start.5) | collective-permute-done | bytes 393248 | tf_op jit(solution)/shard_map/ppermute | solution.py:23
  45.0 2.0 %collective-permute-start.7 = (bf16[8,6144]{1,0:T(8,128)(2,1)S(1)}, bf16[8,6144]{1,0:T(8,128)(2,1)S(1)}, u32[]{:S(2)}, u32[]{:S(2)}) collective-permute-start(bf16[8,6144]{1,0:T(8,128)(2,1)S(1)} %get-tuple-element.40), channel_id=1, source_target_pairs={{0,4},{1,5},{2,6},{3,7},{4,8},{5,9},{6,10},{7,11},{8,12},{9,13},{1... | collective-permute-start | bytes 294920 | tf_op jit(solution)/shard_map/ppermute | solution.py:23
  47.0 3.6 %collective-permute-start.8 = (bf16[8,6144]{1,0:T(8,128)(2,1)S(1)}, bf16[8,6144]{1,0:T(8,128)(2,1)S(1)}, u32[]{:S(2)}, u32[]{:S(2)}) collective-permute-start(bf16[8,6144]{1,0:T(8,128)(2,1)S(1)} %get-tuple-element.41), channel_id=1, source_target_pairs={{0,8},{1,9},{2,10},{3,11},{4,12},{5,13},{6,14},{7,15},{8,0},{9,1},... | collective-permute-start | bytes 294920 | tf_op jit(solution)/shard_map/ppermute | solution.py:23
  59.4 3.5 %collective-permute-done.12.d = bf16[8,6144]{1,0:T(8,128)(2,1)S(1)} collective-permute-done((bf16[8,6144]{1,0:T(8,128)(2,1)S(1)}, bf16[8,6144]{1,0:T(8,128)(2,1)S(1)}, u32[]{:S(2)}, u32[]{:S(2)}) %collective-permute-start.12) | collective-permute-done | bytes 98336 | tf_op jit(solution)/shard_map/ppermute | solution.py:23
  66.1 2.1 %collective-permute-start.14 = (bf16[32,6144]{1,0:T(8,128)(2,1)S(1)}, bf16[32,6144]{1,0:T(8,128)(2,1)S(1)}, u32[]{:S(2)}, u32[]{:S(2)}) collective-permute-start(bf16[32,6144]{1,0:T(8,128)(2,1)S(1)} %stack_x.1.a), channel_id=1, source_target_pairs={{0,2},{1,3},{2,0},{3,1},{4,6},{5,7},{6,4},{7,5},{8,10},{9,11},{10,... | collective-permute-start | bytes 1179656 | tf_op jit(solution)/shard_map/ppermute | solution.py:23
  68.2 1.7 %collective-permute-start.13 = (bf16[32,6144]{1,0:T(8,128)(2,1)S(1)}, bf16[32,6144]{1,0:T(8,128)(2,1)S(1)}, u32[]{:S(2)}, u32[]{:S(2)}) collective-permute-start(bf16[32,6144]{1,0:T(8,128)(2,1)S(1)} %stack_x.1.a), channel_id=1, source_target_pairs={{0,3},{1,0},{2,1},{3,2},{4,7},{5,4},{6,5},{7,6},{8,11},{9,8},{10,9... | collective-permute-start | bytes 1179656 | tf_op jit(solution)/shard_map/ppermute | solution.py:23
  69.9 3.5 %collective-permute-done.15.d = bf16[32,6144]{1,0:T(8,128)(2,1)S(1)} collective-permute-done((bf16[32,6144]{1,0:T(8,128)(2,1)S(1)}, bf16[32,6144]{1,0:T(8,128)(2,1)S(1)}, u32[]{:S(2)}, u32[]{:S(2)}) %collective-permute-start.15) | collective-permute-done | bytes 393248 | tf_op jit(solution)/shard_map/ppermute | solution.py:23
  73.4 4.7 %collective-permute-done.14.c = bf16[32,6144]{1,0:T(8,128)(2,1)S(1)} collective-permute-done((bf16[32,6144]{1,0:T(8,128)(2,1)S(1)}, bf16[32,6144]{1,0:T(8,128)(2,1)S(1)}, u32[]{:S(2)}, u32[]{:S(2)}) %collective-permute-start.14) | collective-permute-done | bytes 393248 | tf_op jit(solution)/shard_map/ppermute | solution.py:23
  78.6 1.8 %stack_p.1.a = bf16[128,6144]{1,0:T(8,128)(2,1)} custom-call(s32[8]{0:T(128)S(1)} %stack.32.at, bf16[32,6144]{1,0:T(8,128)(2,1)S(1)} %stack_x.1.a, bf16[32,6144]{1,0:T(8,128)(2,1)S(1)} %collective-permute-done.13.b, bf16[32,6144]{1,0:T(8,128)(2,1)S(1)} %collective-permute-done.14.c, bf16[32,6144]{1,0:T(8,128)(2,1)S(1)} %collective-permute-done.15.d), custom_call_target="tpu_custom_call" | custom-call | bytes 3145728 | tf_op jit(solution)/shard_map/stack_p/pallas_call | solution.py:66
  80.7 3.5 %collective-permute-done.16.b = bf16[128,6144]{1,0:T(8,128)(2,1)} collective-permute-done((bf16[128,6144]{1,0:T(8,128)(2,1)}, bf16[128,6144]{1,0:T(8,128)(2,1)}, u32[]{:S(2)}, u32[]{:S(2)}) %collective-permute-start.16) | collective-permute-done | bytes 1572896 | tf_op jit(solution)/shard_map/ppermute | solution.py:23
  84.1 2.3 %collective-permute-start.19 = (bf16[128,6144]{1,0:T(8,128)(2,1)}, bf16[128,6144]{1,0:T(8,128)(2,1)S(1)}, u32[]{:S(2)}, u32[]{:S(2)}) collective-permute-start(bf16[128,6144]{1,0:T(8,128)(2,1)} %get-tuple-element.43.rows_mine), channel_id=1, source_target_pairs={{0,12},{1,13},{2,14},{3,15},{4,0},{5,1},{6,2},{7,3},{8,4},{9,5},{1... | collective-permute-start | bytes 4718600 | tf_op jit(solution)/shard_map/ppermute | solution.py:23
  86.4 7.6 %fusion.24.mine = f32[128,1024]{1,0:T(8,128)S(1)} fusion(bf16[128,6144]{1,0:T(8,128)(2,1)} %get-tuple-element.43.rows_mine, bf16[6144,1024]{1,0:T(8,128)(2,1)} %param.18), kind=kOutput, calls=%fused_computation.40 | convolution fusion | flops 1610612736 | bytes 14680064 | tf_op jit(solution)/shard_map/dot_general | solution.py:398
  94.1 3.4 %fusion.25.theirs = f32[128,1024]{1,0:T(8,128)S(1)} fusion(bf16[128,6144]{1,0:T(8,128)(2,1)} %get-tuple-element.44.rows_theirs, bf16[6144,1024]{1,0:T(8,128)(2,1)S(1)} %bitcast.59), kind=kOutput, calls=%fused_computation.41 | convolution fusion | flops 1610612736 | bytes 14680064 | tf_op jit(solution)/shard_map/dot_general | solution.py:398
  98.6 6.2 %collective-permute-done.19.rows_mine = bf16[128,6144]{1,0:T(8,128)(2,1)S(1)} collective-permute-done((bf16[128,6144]{1,0:T(8,128)(2,1)}, bf16[128,6144]{1,0:T(8,128)(2,1)S(1)}, u32[]{:S(2)}, u32[]{:S(2)}) %collective-permute-start.19) | collective-permute-done | bytes 1572896 | tf_op jit(solution)/shard_map/ppermute | solution.py:23
  104.9 3.5 %collective-permute-start.20 = (bf16[64,6144]{1,0:T(8,128)(2,1)S(1)}, bf16[64,6144]{1,0:T(8,128)(2,1)S(1)}, u32[]{:S(2)}, u32[]{:S(2)}) collective-permute-start(bf16[64,6144]{1,0:T(8,128)(2,1)S(1)} %slice.13), channel_id=1, source_target_pairs={{0,12},{1,13},{2,14},{3,15},{4,0},{5,1},{6,2},{7,3},{8,4},{9,5},{1... | collective-permute-start | bytes 2359304 | tf_op jit(solution)/shard_map/ppermute | solution.py:23
  109.1 1.9 %fusion.28.mine = f32[128,1024]{1,0:T(8,128)S(1)} fusion(bf16[128,6144]{1,0:T(8,128)(2,1)S(1)} %collective-permute-done.19.rows_mine, bf16[6144,1024]{1,0:T(8,128)(2,1)S(1)} %bitcast.59), kind=kOutput, calls=%fused_computation.44 | convolution fusion | flops 1610612736 | bytes 14680064 | tf_op jit(solution)/shard_map/dot_general | solution.py:398
  111.1 1.9 %fusion.26.mine = f32[128,1024]{1,0:T(8,128)S(1)} fusion(bf16[128,6144]{1,0:T(8,128)(2,1)S(1)} %collective-permute-done.17.rows_mine, bf16[6144,1024]{1,0:T(8,128)(2,1)S(1)} %bitcast.59), kind=kOutput, calls=%fused_computation.42 | convolution fusion | flops 1610612736 | bytes 14680064 | tf_op jit(solution)/shard_map/dot_general | solution.py:398
  113.0 1.9 %fusion.29.theirs = f32[128,1024]{1,0:T(8,128)S(1)} fusion(bf16[128,6144]{1,0:T(8,128)(2,1)S(1)} %collective-permute-done.22.rows_theirs, bf16[6144,1024]{1,0:T(8,128)(2,1)S(1)} %bitcast.59), kind=kOutput, calls=%fused_computation.45 | convolution fusion | flops 1610612736 | bytes 14680064 | tf_op jit(solution)/shard_map/dot_general | solution.py:398
  116.1 2.0 %fusion.27.theirs = f32[128,1024]{1,0:T(8,128)S(1)} fusion(bf16[128,6144]{1,0:T(8,128)(2,1)S(1)} %collective-permute-done.21.rows_theirs, bf16[6144,1024]{1,0:T(8,128)(2,1)S(1)} %bitcast.59), kind=kOutput, calls=%fused_computation.43 | convolution fusion | flops 1610612736 | bytes 14680064 | tf_op jit(solution)/shard_map/dot_general | solution.py:398
  119.2 2.5 %collective-permute-done.18 = bf16[64,6144]{1,0:T(8,128)(2,1)S(1)} collective-permute-done((bf16[64,6144]{1,0:T(8,128)(2,1)S(1)}, bf16[64,6144]{1,0:T(8,128)(2,1)S(1)}, u32[]{:S(2)}, u32[]{:S(2)}) %collective-permute-start.18) | collective-permute-done | bytes 786464 | tf_op jit(solution)/shard_map/ppermute | solution.py:23
  122.6 1.9 %fusion.30.mine = f32[128,1024]{1,0:T(8,128)S(1)} fusion(bf16[128,6144]{1,0:T(8,128)(2,1)S(1)} %constant_dynamic-update-slice_fusion.rows_mine, bf16[6144,1024]{1,0:T(8,128)(2,1)S(1)} %bitcast.59), kind=kOutput, calls=%fused_computation.46 | convolution fusion | flops 1610612736 | bytes 14680064 | tf_op jit(solution)/shard_map/dot_general | solution.py:398
  125.2 1.9 %fusion.31.theirs = f32[128,1024]{1,0:T(8,128)S(1)} fusion(bf16[128,6144]{1,0:T(8,128)(2,1)S(1)} %constant_dynamic-update-slice_fusion.2.rows_theirs, bf16[6144,1024]{1,0:T(8,128)(2,1)S(1)} %bitcast.59), kind=kOutput, calls=%fused_computation.47 | convolution fusion | flops 1610612736 | bytes 14680064 | tf_op jit(solution)/shard_map/dot_general | solution.py:398
  129.0 9.0 %all_to_all.10.found = f32[8,8,128]{2,1,0:T(8,128)S(1)} all-to-all(f32[8,8,128]{2,1,0:T(8,128)S(1)} %place.1), channel_id=1, replica_groups=mesh['x'=4,'core'=2,'z'=4,'y'=4] {'x','core'}, dimensions={0} | all-to-all | bytes 65536 | tf_op jit(solution)/shard_map/all_to_all | solution.py:417
  138.5 11.9 %all_to_all.11.found = f32[16,8,128]{2,1,0:T(8,128)S(1)} all-to-all(f32[16,8,128]{2,1,0:T(8,128)S(1)} %block.1), channel_id=1, replica_groups=mesh['x'=4,'core'=2,'z'=4,'y'=4] {'z','y'}, dimensions={0} | all-to-all | bytes 131072 | tf_op jit(solution)/shard_map/all_to_all | solution.py:419
  (92 shorter events, 37.3 us)
Async XLA Ops:
  4.0 3.1 %copy-start.2 = (bf16[128,256]{0,1:T(8,128)(2,1)}, bf16[128,256]{0,1:T(8,128)(2,1)S(1)}, u32[]{:S(2)}) copy-start(bf16[128,256]{0,1:T(8,128)(2,1)S(1)} %copy.27) | copy-start | bytes 196612
  7.8 1.4 collective-permute-start
  10.5 11.2 %copy-start.1 = (f32[2,128,128]{2,1,0:T(8,128)S(1)}, f32[2,128,128]{2,1,0:T(8,128)}, u32[]{:S(2)}) copy-start(f32[2,128,128]{2,1,0:T(8,128)} %carried.1) | copy-start | bytes 393220
  10.5 11.2 %collective-permute-start.3 = (bf16[2,144,128]{2,1,0:T(8,128)(2,1)}, bf16[2,144,128]{2,1,0:T(8,128)(2,1)S(1)}, u32[]{:S(2)}, u32[]{:S(2)}) collective-permute-start(bf16[2,144,128]{2,1,0:T(8,128)(2,1)} %combine.1), channel_id=1, source_target_pairs={{0,32},{1,33},{2,34},{3,35},{4,36},{5,37},{6,38},{7,39},{8,40},{9,... | collective-permute-start | bytes 221192 | tf_op jit(solution)/shard_map/ppermute | solution.py:23
  12.0 9.6 %collective-permute-start.2 = (bf16[2,144,128]{2,1,0:T(8,128)(2,1)}, bf16[2,144,128]{2,1,0:T(8,128)(2,1)}, u32[]{:S(2)}, u32[]{:S(2)}) collective-permute-start(bf16[2,144,128]{2,1,0:T(8,128)(2,1)} %combine.1), channel_id=1, source_target_pairs={{0,64},{1,65},{2,66},{3,67},{4,68},{5,69},{6,70},{7,71},{8,72},{9,... | collective-permute-start | bytes 221192 | tf_op jit(solution)/shard_map/ppermute | solution.py:23
  14.8 6.9 %collective-permute-start.1 = (bf16[2,144,128]{2,1,0:T(8,128)(2,1)}, bf16[2,144,128]{2,1,0:T(8,128)(2,1)}, u32[]{:S(2)}, u32[]{:S(2)}) collective-permute-start(bf16[2,144,128]{2,1,0:T(8,128)(2,1)} %combine.1), channel_id=1, source_target_pairs={{0,96},{1,97},{2,98},{3,99},{4,100},{5,101},{6,102},{7,103},{8,104... | collective-permute-start | bytes 221192 | tf_op jit(solution)/shard_map/ppermute | solution.py:23
  28.5 24.0 %copy-start.4 = (bf16[6144]{0:T(1024)(128)(2,1)S(1)}, bf16[6144]{0:T(1024)(128)(2,1)}, u32[]{:S(2)}) copy-start(bf16[6144]{0:T(1024)(128)(2,1)} %param.17) | copy-start | bytes 36868
  28.5 9.2 %collective-permute-start.4 = (bf16[32,6144]{1,0:T(8,128)(2,1)}, bf16[32,6144]{1,0:T(8,128)(2,1)S(1)}, u32[]{:S(2)}, u32[]{:S(2)}) collective-permute-start(bf16[32,6144]{1,0:T(8,128)(2,1)} %get-tuple-element.35), channel_id=1, source_target_pairs={{0,1},{1,2},{2,3},{3,0},{4,5},{5,6},{6,7},{7,4},{8,9},{9,10},{10,1... | collective-permute-start | bytes 1179656 | tf_op jit(solution)/shard_map/ppermute | solution.py:23
  30.1 13.2 %collective-permute-start.5 = (bf16[32,6144]{1,0:T(8,128)(2,1)}, bf16[32,6144]{1,0:T(8,128)(2,1)}, u32[]{:S(2)}, u32[]{:S(2)}) collective-permute-start(bf16[32,6144]{1,0:T(8,128)(2,1)} %get-tuple-element.36), channel_id=1, source_target_pairs={{0,2},{1,3},{2,0},{3,1},{4,6},{5,7},{6,4},{7,5},{8,10},{9,11},{10,... | collective-permute-start | bytes 1179656 | tf_op jit(solution)/shard_map/ppermute | solution.py:23
  33.0 10.3 %collective-permute-start.6 = (bf16[32,6144]{1,0:T(8,128)(2,1)}, bf16[32,6144]{1,0:T(8,128)(2,1)}, u32[]{:S(2)}, u32[]{:S(2)}) collective-permute-start(bf16[32,6144]{1,0:T(8,128)(2,1)} %get-tuple-element.37), channel_id=1, source_target_pairs={{0,3},{1,0},{2,1},{3,2},{4,7},{5,4},{6,5},{7,6},{8,11},{9,8},{10,9... | collective-permute-start | bytes 1179656 | tf_op jit(solution)/shard_map/ppermute | solution.py:23
  45.0 7.5 %collective-permute-start.7 = (bf16[8,6144]{1,0:T(8,128)(2,1)S(1)}, bf16[8,6144]{1,0:T(8,128)(2,1)S(1)}, u32[]{:S(2)}, u32[]{:S(2)}) collective-permute-start(bf16[8,6144]{1,0:T(8,128)(2,1)S(1)} %get-tuple-element.40), channel_id=1, source_target_pairs={{0,4},{1,5},{2,6},{3,7},{4,8},{5,9},{6,10},{7,11},{8,12},{9,13},{1... | collective-permute-start | bytes 294920 | tf_op jit(solution)/shard_map/ppermute | solution.py:23
  47.0 7.2 %collective-permute-start.8 = (bf16[8,6144]{1,0:T(8,128)(2,1)S(1)}, bf16[8,6144]{1,0:T(8,128)(2,1)S(1)}, u32[]{:S(2)}, u32[]{:S(2)}) collective-permute-start(bf16[8,6144]{1,0:T(8,128)(2,1)S(1)} %get-tuple-element.41), channel_id=1, source_target_pairs={{0,8},{1,9},{2,10},{3,11},{4,12},{5,13},{6,14},{7,15},{8,0},{9,1},... | collective-permute-start | bytes 294920 | tf_op jit(solution)/shard_map/ppermute | solution.py:23
  50.6 4.6 %collective-permute-start.9 = (bf16[8,6144]{1,0:T(8,128)(2,1)S(1)}, bf16[8,6144]{1,0:T(8,128)(2,1)S(1)}, u32[]{:S(2)}, u32[]{:S(2)}) collective-permute-start(bf16[8,6144]{1,0:T(8,128)(2,1)S(1)} %get-tuple-element.42), channel_id=1, source_target_pairs={{0,12},{1,13},{2,14},{3,15},{4,0},{5,1},{6,2},{7,3},{8,4},{9,5},{1... | collective-permute-start | bytes 294920 | tf_op jit(solution)/shard_map/ppermute | solution.py:23
  55.9 6.9 %collective-permute-start.12 = (bf16[8,6144]{1,0:T(8,128)(2,1)S(1)}, bf16[8,6144]{1,0:T(8,128)(2,1)S(1)}, u32[]{:S(2)}, u32[]{:S(2)}) collective-permute-start(bf16[8,6144]{1,0:T(8,128)(2,1)S(1)} %norm.1.a), channel_id=1, source_target_pairs={{0,32},{1,33},{2,34},{3,35},{4,36},{5,37},{6,38},{7,39},{8,40},{9,... | collective-permute-start | bytes 294920 | tf_op jit(solution)/shard_map/ppermute | solution.py:23
  56.6 6.3 %collective-permute-start.11 = (bf16[8,6144]{1,0:T(8,128)(2,1)S(1)}, bf16[8,6144]{1,0:T(8,128)(2,1)S(1)}, u32[]{:S(2)}, u32[]{:S(2)}) collective-permute-start(bf16[8,6144]{1,0:T(8,128)(2,1)S(1)} %norm.1.a), channel_id=1, source_target_pairs={{0,64},{1,65},{2,66},{3,67},{4,68},{5,69},{6,70},{7,71},{8,72},{9,... | collective-permute-start | bytes 294920 | tf_op jit(solution)/shard_map/ppermute | solution.py:23
  57.9 5.9 %collective-permute-start.10 = (bf16[8,6144]{1,0:T(8,128)(2,1)S(1)}, bf16[8,6144]{1,0:T(8,128)(2,1)S(1)}, u32[]{:S(2)}, u32[]{:S(2)}) collective-permute-start(bf16[8,6144]{1,0:T(8,128)(2,1)S(1)} %norm.1.a), channel_id=1, source_target_pairs={{0,96},{1,97},{2,98},{3,99},{4,100},{5,101},{6,102},{7,103},{8,104... | collective-permute-start | bytes 294920 | tf_op jit(solution)/shard_map/ppermute | solution.py:23
  64.4 16.0 %copy-start.5 = (s32[1024]{0:T(1024)S(1)}, s32[1024]{0:T(1024)}, u32[]{:S(2)}) copy-start(s32[1024]{0:T(1024)} %param.19) | copy-start | bytes 12292
  64.4 9.1 %collective-permute-start.15 = (bf16[32,6144]{1,0:T(8,128)(2,1)S(1)}, bf16[32,6144]{1,0:T(8,128)(2,1)S(1)}, u32[]{:S(2)}, u32[]{:S(2)}) collective-permute-start(bf16[32,6144]{1,0:T(8,128)(2,1)S(1)} %stack_x.1.a), channel_id=1, source_target_pairs={{0,1},{1,2},{2,3},{3,0},{4,5},{5,6},{6,7},{7,4},{8,9},{9,10},{10,1... | collective-permute-start | bytes 1179656 | tf_op jit(solution)/shard_map/ppermute | solution.py:23
  66.1 12.1 %collective-permute-start.14 = (bf16[32,6144]{1,0:T(8,128)(2,1)S(1)}, bf16[32,6144]{1,0:T(8,128)(2,1)S(1)}, u32[]{:S(2)}, u32[]{:S(2)}) collective-permute-start(bf16[32,6144]{1,0:T(8,128)(2,1)S(1)} %stack_x.1.a), channel_id=1, source_target_pairs={{0,2},{1,3},{2,0},{3,1},{4,6},{5,7},{6,4},{7,5},{8,10},{9,11},{10,... | collective-permute-start | bytes 1179656 | tf_op jit(solution)/shard_map/ppermute | solution.py:23
  68.2 10.3 %collective-permute-start.13 = (bf16[32,6144]{1,0:T(8,128)(2,1)S(1)}, bf16[32,6144]{1,0:T(8,128)(2,1)S(1)}, u32[]{:S(2)}, u32[]{:S(2)}) collective-permute-start(bf16[32,6144]{1,0:T(8,128)(2,1)S(1)} %stack_x.1.a), channel_id=1, source_target_pairs={{0,3},{1,0},{2,1},{3,2},{4,7},{5,4},{6,5},{7,6},{8,11},{9,8},{10,9... | collective-permute-start | bytes 1179656 | tf_op jit(solution)/shard_map/ppermute | solution.py:23
  80.4 3.8 %collective-permute-start.16 = (bf16[128,6144]{1,0:T(8,128)(2,1)}, bf16[128,6144]{1,0:T(8,128)(2,1)}, u32[]{:S(2)}, u32[]{:S(2)}) collective-permute-start(bf16[128,6144]{1,0:T(8,128)(2,1)} %stack_p.1.a), channel_id=1, source_target_pairs={{0,16},{1,17},{2,18},{3,19},{4,20},{5,21},{6,22},{7,23},{8,24},{9,... | collective-permute-start | bytes 4718600 | tf_op jit(solution)/shard_map/ppermute | solution.py:23
  84.1 9.9 %slice-start = ((s8[12582912]{0:T(1024)(128)(4,1)}), s8[4194304]{0:T(1024)(128)(4,1)S(1)}, s32[]{:S(2)}) async-start(s8[12582912]{0:T(1024)(128)(4,1)} %bitcast.58), calls=%async_computation.2 | async-start | bytes 8388608
  84.1 9.9 %slice-start.1 = ((s8[12582912]{0:T(1024)(128)(4,1)}), s8[4194304]{0:T(1024)(128)(4,1)S(1)}, s32[]{:S(2)}) async-start(s8[12582912]{0:T(1024)(128)(4,1)} %bitcast.58), calls=%async_computation.3 | async-start | bytes 8388608
  84.1 9.9 %slice-start.2 = ((s8[12582912]{0:T(1024)(128)(4,1)}), s8[4194304]{0:T(1024)(128)(4,1)S(1)}, s32[]{:S(2)}) async-start(s8[12582912]{0:T(1024)(128)(4,1)} %bitcast.58), calls=%async_computation.4 | async-start | bytes 8388608
  84.1 20.7 %collective-permute-start.19 = (bf16[128,6144]{1,0:T(8,128)(2,1)}, bf16[128,6144]{1,0:T(8,128)(2,1)S(1)}, u32[]{:S(2)}, u32[]{:S(2)}) collective-permute-start(bf16[128,6144]{1,0:T(8,128)(2,1)} %get-tuple-element.43.rows_mine), channel_id=1, source_target_pairs={{0,12},{1,13},{2,14},{3,15},{4,0},{5,1},{6,2},{7,3},{8,4},{9,5},{1... | collective-permute-start | bytes 4718600 | tf_op jit(solution)/shard_map/ppermute | solution.py:23
  86.4 22.0 %collective-permute-start.17 = (bf16[128,6144]{1,0:T(8,128)(2,1)}, bf16[128,6144]{1,0:T(8,128)(2,1)S(1)}, u32[]{:S(2)}, u32[]{:S(2)}) collective-permute-start(bf16[128,6144]{1,0:T(8,128)(2,1)} %get-tuple-element.43.rows_mine), channel_id=1, source_target_pairs={{0,4},{1,5},{2,6},{3,7},{4,8},{5,9},{6,10},{7,11},{8,12},{9,13},{1... | collective-permute-start | bytes 4718600 | tf_op jit(solution)/shard_map/ppermute | solution.py:23
  104.9 14.3 %collective-permute-start.20 = (bf16[64,6144]{1,0:T(8,128)(2,1)S(1)}, bf16[64,6144]{1,0:T(8,128)(2,1)S(1)}, u32[]{:S(2)}, u32[]{:S(2)}) collective-permute-start(bf16[64,6144]{1,0:T(8,128)(2,1)S(1)} %slice.13), channel_id=1, source_target_pairs={{0,12},{1,13},{2,14},{3,15},{4,0},{5,1},{6,2},{7,3},{8,4},{9,5},{1... | collective-permute-start | bytes 2359304 | tf_op jit(solution)/shard_map/ppermute | solution.py:23
  108.4 13.3 %collective-permute-start.18 = (bf16[64,6144]{1,0:T(8,128)(2,1)S(1)}, bf16[64,6144]{1,0:T(8,128)(2,1)S(1)}, u32[]{:S(2)}, u32[]{:S(2)}) collective-permute-start(bf16[64,6144]{1,0:T(8,128)(2,1)S(1)} %slice.12), channel_id=1, source_target_pairs={{0,4},{1,5},{2,6},{3,7},{4,8},{5,9},{6,10},{7,11},{8,12},{9,13},{1... | collective-permute-start | bytes 2359304 | tf_op jit(solution)/shard_map/ppermute | solution.py:23
  108.5 4.5 %collective-permute-start.22 = (bf16[128,6144]{1,0:T(8,128)(2,1)S(1)}, bf16[128,6144]{1,0:T(8,128)(2,1)S(1)}, u32[]{:S(2)}, u32[]{:S(2)}) collective-permute-start(bf16[128,6144]{1,0:T(8,128)(2,1)S(1)} %collective-permute-done.19.rows_mine), channel_id=1, source_target_pairs={{0,16},{1,17},{2,18},{3,19},{4,20},{5,21},{6,22},{7,23},{8,24},{9,... | collective-permute-start | bytes 4718600 | tf_op jit(solution)/shard_map/ppermute | solution.py:23
  108.6 7.4 %collective-permute-start.21 = (bf16[128,6144]{1,0:T(8,128)(2,1)S(1)}, bf16[128,6144]{1,0:T(8,128)(2,1)S(1)}, u32[]{:S(2)}, u32[]{:S(2)}) collective-permute-start(bf16[128,6144]{1,0:T(8,128)(2,1)S(1)} %collective-permute-done.17.rows_mine), channel_id=1, source_target_pairs={{0,16},{1,17},{2,18},{3,19},{4,20},{5,21},{6,22},{7,23},{8,24},{9,... | collective-permute-start | bytes 4718600 | tf_op jit(solution)/shard_map/ppermute | solution.py:23
  121.7 2.9 %collective-permute-start.23 = (bf16[64,6144]{1,0:T(8,128)(2,1)S(1)}, bf16[64,6144]{1,0:T(8,128)(2,1)S(1)}, u32[]{:S(2)}, u32[]{:S(2)}) collective-permute-start(bf16[64,6144]{1,0:T(8,128)(2,1)S(1)} %collective-permute-done.18), channel_id=1, source_target_pairs={{0,16},{1,17},{2,18},{3,19},{4,20},{5,21},{6,22},{7,23},{8,24},{9,... | collective-permute-start | bytes 2359304 | tf_op jit(solution)/shard_map/ppermute | solution.py:23
  121.8 3.4 %collective-permute-start.24 = (bf16[64,6144]{1,0:T(8,128)(2,1)S(1)}, bf16[64,6144]{1,0:T(8,128)(2,1)S(1)}, u32[]{:S(2)}, u32[]{:S(2)}) collective-permute-start(bf16[64,6144]{1,0:T(8,128)(2,1)S(1)} %collective-permute-done.20), channel_id=1, source_target_pairs={{0,16},{1,17},{2,18},{3,19},{4,20},{5,21},{6,22},{7,23},{8,24},{9,... | collective-permute-start | bytes 2359304 | tf_op jit(solution)/shard_map/ppermute | solution.py:23
  (2 other events, 2.5 us)

commit v7 on v6

--- a/solution.py
+++ b/solution.py
@@ -75,20 +75,10 @@
     )(scalars, *[pin(a) for a in arrays], *[leave(a) for a in loose], *[pin(a) for a in unread])
 
 
-def tie_kernel(a, b, out_a, out_b):
-    pass
-
-
-def tie(a, b):
-    return pl.pallas_call(
-        tie_kernel,
-        out_shape=[on_chip(a.shape, a.dtype), on_chip(b.shape, b.dtype)],
-        in_specs=[ANYWHERE] * 2,
-        out_specs=[ANYWHERE] * 2,
-        input_output_aliases={0: 0, 1: 1},
-        compiler_params=pltpu.CompilerParams(vmem_limit_bytes=1024 * 1024),
-        name="tie",
-    )(pin(a), pin(b))
+def load_kernel(source, out, done):
+    copy = pltpu.make_async_copy(source, out, done)
+    copy.start()
+    copy.wait()
 
 
 def combine_kernel(at, mine, theirs, chip):
@@ -194,7 +184,7 @@
     )
 
 
-def score_kernel(shift, at, targets, mine, theirs, rows_mine, rows_theirs, out_mine, out_theirs):
+def score_kernel(low, high, at, targets, mine, theirs, rows_mine, rows_theirs, out_mine, out_theirs):
     x = at[0]
     lane = lax.broadcasted_iota(jnp.int32, (8, 128), 1)
     i = lax.broadcasted_iota(jnp.int32, (128, 128), 0)
@@ -204,9 +194,11 @@
         (theirs, out_theirs, at[5], at[4], 1 - at[1]),
     ):
         found = logits[...]
-        place = core * 4 + ((q + 4 - shift) & 3)
-        line = jnp.broadcast_to(targets[pl.ds(place, 1), :] - at[6], (8, 128))
-        line = as_gathered(line, lane, p, x)[:1]
+        lines = []
+        for shift in (low, high):
+            line = targets[pl.ds(core * 4 + ((q + 4 - shift) & 3), 1), :] - at[6]
+            lines.append(as_gathered(jnp.broadcast_to(line, (8, 128)), lane, p, x))
+        line = jnp.where(lane < 64, *lines)[:1]
         want = jnp.sum(jnp.where(i == j, line, 0), axis=1, keepdims=True)
         top = jnp.max(found, axis=1, keepdims=True)
         total = jnp.sum(jnp.exp(found - top), axis=1, keepdims=True)
@@ -218,13 +210,20 @@
 
 def place_kernel(at, *refs):
     blocks, out, held = refs[:-2], refs[-2], refs[-1]
-    for k, block in enumerate(blocks):
-        shift, own = k // 2, k % 2 == 0
-        q, core = (at[5], at[1]) if own else (at[4], 1 - at[1])
-        place = core * 4 + ((q + 4 - shift) & 3)
-        for row in range(3):
-            held[pl.ds(8 * row + place, 1), :] = block[row : row + 1, :]
     lane = lax.broadcasted_iota(jnp.int32, (8, 128), 1)
+    for k in range(2):
+        p, q, core = (at[4], at[5], at[1]) if k == 0 else (at[5], at[4], 1 - at[1])
+        here, early, late, far = (blocks[2 * g + k][...] for g in range(4))
+        low = ((lane // 32 + 4 - p) & 3) < 2
+        for shift, values in (
+            (0, here),
+            (1, jnp.where(low, early, late)),
+            (2, far),
+            (3, jnp.where(low, late, early)),
+        ):
+            place = core * 4 + ((q + 4 - shift) & 3)
+            for row in range(3):
+                held[pl.ds(8 * row + place, 1), :] = values[row : row + 1, :]
     for row in range(3):
         values = held[8 * row : 8 * row + 8, :]
         turned = {8 * k: pltpu.roll(values, 8 * k, 1) if k else values for k in range(16)}
@@ -378,26 +377,40 @@
     )
 
     on_x = gather(final_rows, along_x, scalars, "stack_x")
+    on_x, source = lax.optimization_barrier((on_x, vocab_weight))
+    vocab = pl.pallas_call(
+        load_kernel,
+        out_shape=on_chip(vocab_weight.shape, BF16),
+        in_specs=[pl.BlockSpec(memory_space=pltpu.HBM)],
+        out_specs=ANYWHERE,
+        scratch_shapes=[pltpu.SemaphoreType.DMA],
+        compiler_params=pltpu.CompilerParams(vmem_limit_bytes=1024 * 1024),
+        cost_estimate=pl.CostEstimate(
+            flops=0, bytes_accessed=4 * width * vocab_local, transcendentals=0
+        ),
+        name="load",
+    )(leave(source))
     ours = gather(on_x, along_p, scalars, "stack_p")
     theirs = move(ours, other_core)
-    ours, theirs = tie(ours, theirs)
+    ours, theirs = lax.optimization_barrier((ours, theirs))
     lines = jnp.transpose(targets.reshape(X, CORE, 4, 4, 8), (1, 3, 2, 0, 4)).reshape(8, 128)
-    up, down = move(ours, along_q(1)), move(ours, along_q(3))
-    half = up.shape[0] // 2
-    far = (move(up[:half], along_q(1)), move(down[half:], along_q(3)))
-    found = {}
-    for s, block in ((0, ours), (1, up), (3, down), (2, far)):
-        if s == 0:
+    half = ours.shape[0] // 2
+    low, high = ours[:half], ours[half:]
+    early = (move(low, along_q(1)), move(high, along_q(3)))
+    late = (move(low, along_q(3)), move(high, along_q(1)))
+    far = (move(early[0], along_q(1)), move(early[1], along_q(3)))
+    found = []
+    for s, block in (((0, 0), ours), ((1, 3), early), ((3, 1), late), ((2, 2), far)):
+        if s == (0, 0):
             swapped = theirs
-        elif s == 2:
-            block, found = lax.optimization_barrier((block, found))
-            swapped = jnp.concatenate([move(part, other_core) for part in block], axis=0)
+        else:
+            if s != (1, 3):
+                block, found = lax.optimization_barrier((block, found))
             block = jnp.concatenate(block, axis=0)
-        else:
             swapped = move(block, other_core)
-        logits = [jnp.dot(b, vocab_weight, preferred_element_type=F32) for b in (block, swapped)]
-        found[s] = local(
-            functools.partial(score_kernel, s),
+        logits = [jnp.dot(b, vocab, preferred_element_type=F32) for b in (block, swapped)]
+        found += local(
+            functools.partial(score_kernel, *s),
             [on_chip((8, 128), F32)] * 2,
             scalars,
             lines,
@@ -410,7 +423,7 @@
         place_kernel,
         on_chip((X * CORE, 8, 128), F32),
         scalars,
-        *[found[s][k] for s in range(4) for k in range(2)],
+        *found,
         scratch=[pltpu.VMEM((24, 128), F32)],
         name="place",
     )

time: 152 us -> 157 us (1.033)
  waiting for transfers between devices: 38.6 us -> 52.5 us
  matrix products: 35.4 us -> 24.7 us
  Pallas kernels: 18.4 us -> 20.6 us
    ppermute x25 -> x26, waiting for transfers between devices: 38.6 us -> 52.5 us  [move(): return lax.ppermute(array, ALL, pairs)]
    dot_general x8, matrix products: 22.5 us -> 15.3 us  [shards(): jnp.dot(b, vocab, preferred_element_type=F32)]
    pallas_call x1, Pallas kernels: 0.01 us -> 4.59 us  [shards(): pl.pallas_call(load_kernel, out_shape=on_chip(vocab_weight.shape, BF16),...]
    pallas_call x13, Pallas kernels: 14 us -> 11.6 us  [local(): pl.pallas_call(kernel, out_shape=outs, in_specs=[SCALARS] + [WHOLE] * len...]
    ppermute x25 -> x26, starting transfers between devices: 34.5 us -> 33.7 us  [move(): return lax.ppermute(array, ALL, pairs)]
  transfers between devices with their start and end apart: 25 -> 26, of which waited for: 14 -> 16; matrix products, arithmetic and copies ran while one was open for 18% -> 11% of each run, Pallas kernels for 2% -> 5%
where the time goes in v7:
time: 157 us
  waiting for transfers between devices  52.5 us (33%)
  starting transfers between devices  33.7 us (21%)
  matrix products  24.7 us (16%)
  blocking collectives  21.5 us (14%)
  Pallas kernels  20.6 us (13%)
  local copies, waits for them, and re-layouts  2.1 us (1%)
    ppermute x26, waiting for transfers between devices, move(): return lax.ppermute(array, ALL, pairs)  52.5 us
    ppermute x26, starting transfers between devices, move(): return lax.ppermute(array, ALL, pairs)  33.7 us
    dot_general x8, matrix products, shards(): jnp.dot(b, vocab, preferred_element_type=F32)  15.3 us
    all_to_all x1, blocking collectives, shards(): came = lax.all_to_all(sent, ('z', 'y'), 0, 0)  13.4 us
    pallas_call x13, Pallas kernels, local(): pl.pallas_call(kernel, out_shape=outs, in_specs=[SCALARS] + [WHOLE] * len...  11.6 us
    all_to_all x1, blocking collectives, shards(): came = lax.all_to_all(sent, ('x', 'core'), 0, 0)  8.1 us
    pallas_call x1, Pallas kernels, shards(): pl.pallas_call(load_kernel, out_shape=on_chip(vocab_weight.shape, BF16),...  4.59 us
    pallas_call x1, Pallas kernels, shards(): pl.pallas_call(project_kernel, out_shape=[in_hbm((32, width), F32)] + [in...  4.42 us
  transfers between devices with their start and end apart: 26, of which 16 were waited for; matrix products, arithmetic and copies ran while one was open for 11% of the time, Pallas kernels for 5%

profile of v7, /device:TPU:0, one launch (start us, length us, event | category | flops | bytes accessed | tf_op | source)
XLA Modules:
  0.0 156.6 jit_solution(11665909194775068)
XLA Ops:
  1.9 2.0 %convolution_convert_fusion.2 = bf16[128,256]{1,0:T(8,128)(2,1)S(1)} fusion(bf16[128,6144]{1,0:T(8,128)(2,1)} %param.10, bf16[6144,256]{1,0:T(8,128)(2,1)S(1)} %copy-done), kind=kOutput, calls=%fused_computation.7 | convolution fusion | flops 402685952 | bytes 4784128 | tf_op jit(solution)/shard_map/dot_general | solution.py:282
  4.0 3.1 %convolution_convert_fusion.1 = bf16[128,256]{1,0:T(8,128)(2,1)S(1)} fusion(bf16[128,6144]{1,0:T(8,128)(2,1)} %param.10, bf16[6144,256]{1,0:T(8,128)(2,1)} %param.14), kind=kOutput, calls=%fused_computation.6 | convolution fusion | flops 402685952 | bytes 4784128 | tf_op jit(solution)/shard_map/dot_general | solution.py:281
  9.6 2.9 %collective-permute-start.1 = (bf16[2,144,128]{2,1,0:T(8,128)(2,1)S(1)}, bf16[2,144,128]{2,1,0:T(8,128)(2,1)S(1)}, u32[]{:S(2)}, u32[]{:S(2)}) collective-permute-start(bf16[2,144,128]{2,1,0:T(8,128)(2,1)S(1)} %combine.1), channel_id=1, source_target_pairs={{0,96},{1,97},{2,98},{3,99},{4,100},{5,101},{6,102},{7,103},{8,104... | collective-permute-start | bytes 221192 | tf_op jit(solution)/shard_map/ppermute | solution.py:23
  14.2 2.5 %fusion.3 = bf16[16,2,8,128]{3,2,1,0:T(8,128)(2,1)S(1)} fusion(bf16[128,6144]{1,0:T(8,128)(2,1)S(1)} %copy-done.3, bf16[6144,256]{1,0:T(8,128)(2,1)} %param.13), kind=kOutput, calls=%fused_computation.9 | convolution fusion | flops 402685952 | bytes 4784128 | tf_op jit(solution)/shard_map/dot_general | solution.py:307
  17.0 1.9 %collective-permute-done.2.two = bf16[2,144,128]{2,1,0:T(8,128)(2,1)S(1)} collective-permute-done((bf16[2,144,128]{2,1,0:T(8,128)(2,1)S(1)}, bf16[2,144,128]{2,1,0:T(8,128)(2,1)S(1)}, u32[]{:S(2)}, u32[]{:S(2)}) %collective-permute-start.2) | collective-permute-done | bytes 73760 | tf_op jit(solution)/shard_map/ppermute | solution.py:23
  20.7 4.4 %project.1 = (f32[32,6144]{1,0:T(8,128)}, bf16[32,6144]{1,0:T(8,128)(2,1)}, bf16[32,6144]{1,0:T(8,128)(2,1)}, bf16[32,6144]{1,0:T(8,128)(2,1)}) custom-call(s32[8]{0:T(128)S(1)} %stack.32.at, bf16[128,256]{1,0:T(8,128)(2,1)S(1)} %copy.26.heads, bf16[256,6144]{1,0:T(8,128)(2,1)} %weight.1), custom_call_target="tpu_custom_call" | custom-call | flops 402653184 | bytes 4718592 | tf_op jit(solution)/shard_map/project/pallas_call | solution.py:334
  26.7 2.9 %collective-permute-start.5 = (bf16[32,6144]{1,0:T(8,128)(2,1)}, bf16[32,6144]{1,0:T(8,128)(2,1)S(1)}, u32[]{:S(2)}, u32[]{:S(2)}) collective-permute-start(bf16[32,6144]{1,0:T(8,128)(2,1)} %get-tuple-element.44), channel_id=1, source_target_pairs={{0,2},{1,3},{2,0},{3,1},{4,6},{5,7},{6,4},{7,5},{8,10},{9,11},{10,... | collective-permute-start | bytes 1179656 | tf_op jit(solution)/shard_map/ppermute | solution.py:23
  31.0 3.4 %collective-permute-done.4.one = bf16[32,6144]{1,0:T(8,128)(2,1)S(1)} collective-permute-done((bf16[32,6144]{1,0:T(8,128)(2,1)}, bf16[32,6144]{1,0:T(8,128)(2,1)S(1)}, u32[]{:S(2)}, u32[]{:S(2)}) %collective-permute-start.4) | collective-permute-done | bytes 393248 | tf_op jit(solution)/shard_map/ppermute | solution.py:23
  34.3 5.5 %collective-permute-done.5.two = bf16[32,6144]{1,0:T(8,128)(2,1)S(1)} collective-permute-done((bf16[32,6144]{1,0:T(8,128)(2,1)}, bf16[32,6144]{1,0:T(8,128)(2,1)S(1)}, u32[]{:S(2)}, u32[]{:S(2)}) %collective-permute-start.5) | collective-permute-done | bytes 393248 | tf_op jit(solution)/shard_map/ppermute | solution.py:23
  41.3 2.0 %collective-permute-start.7 = (bf16[8,6144]{1,0:T(8,128)(2,1)S(1)}, bf16[8,6144]{1,0:T(8,128)(2,1)S(1)}, u32[]{:S(2)}, u32[]{:S(2)}) collective-permute-start(bf16[8,6144]{1,0:T(8,128)(2,1)S(1)} %get-tuple-element.48), channel_id=1, source_target_pairs={{0,4},{1,5},{2,6},{3,7},{4,8},{5,9},{6,10},{7,11},{8,12},{9,13},{1... | collective-permute-start | bytes 294920 | tf_op jit(solution)/shard_map/ppermute | solution.py:23
  43.2 3.6 %collective-permute-start.8 = (bf16[8,6144]{1,0:T(8,128)(2,1)S(1)}, bf16[8,6144]{1,0:T(8,128)(2,1)S(1)}, u32[]{:S(2)}, u32[]{:S(2)}) collective-permute-start(bf16[8,6144]{1,0:T(8,128)(2,1)S(1)} %get-tuple-element.49), channel_id=1, source_target_pairs={{0,8},{1,9},{2,10},{3,11},{4,12},{5,13},{6,14},{7,15},{8,0},{9,1},... | collective-permute-start | bytes 294920 | tf_op jit(solution)/shard_map/ppermute | solution.py:23
  54.6 2.2 %collective-permute-done.10.b = bf16[8,6144]{1,0:T(8,128)(2,1)S(1)} collective-permute-done((bf16[8,6144]{1,0:T(8,128)(2,1)S(1)}, bf16[8,6144]{1,0:T(8,128)(2,1)S(1)}, u32[]{:S(2)}, u32[]{:S(2)}) %collective-permute-start.10) | collective-permute-done | bytes 98336 | tf_op jit(solution)/shard_map/ppermute | solution.py:23
  56.8 2.1 %collective-permute-done.11.c = bf16[8,6144]{1,0:T(8,128)(2,1)S(1)} collective-permute-done((bf16[8,6144]{1,0:T(8,128)(2,1)S(1)}, bf16[8,6144]{1,0:T(8,128)(2,1)S(1)}, u32[]{:S(2)}, u32[]{:S(2)}) %collective-permute-start.11) | collective-permute-done | bytes 98336 | tf_op jit(solution)/shard_map/ppermute | solution.py:23
  60.6 2.4 %collective-permute-start.13 = (bf16[32,6144]{1,0:T(8,128)(2,1)S(1)}, bf16[32,6144]{1,0:T(8,128)(2,1)S(1)}, u32[]{:S(2)}, u32[]{:S(2)}) collective-permute-start(bf16[32,6144]{1,0:T(8,128)(2,1)S(1)} %stack_x.1.a), channel_id=1, source_target_pairs={{0,3},{1,0},{2,1},{3,2},{4,7},{5,4},{6,5},{7,6},{8,11},{9,8},{10,9... | collective-permute-start | bytes 1179656 | tf_op jit(solution)/shard_map/ppermute | solution.py:23
  64.9 7.6 %collective-permute-done.13.b = bf16[32,6144]{1,0:T(8,128)(2,1)S(1)} collective-permute-done((bf16[32,6144]{1,0:T(8,128)(2,1)S(1)}, bf16[32,6144]{1,0:T(8,128)(2,1)S(1)}, u32[]{:S(2)}, u32[]{:S(2)}) %collective-permute-start.13) | collective-permute-done | bytes 393248 | tf_op jit(solution)/shard_map/ppermute | solution.py:23
  72.5 3.9 %collective-permute-done.15.d = bf16[32,6144]{1,0:T(8,128)(2,1)S(1)} collective-permute-done((bf16[32,6144]{1,0:T(8,128)(2,1)S(1)}, bf16[32,6144]{1,0:T(8,128)(2,1)S(1)}, u32[]{:S(2)}, u32[]{:S(2)}) %collective-permute-start.15) | collective-permute-done | bytes 393248 | tf_op jit(solution)/shard_map/ppermute | solution.py:23
  77.5 4.6 %load.1 = bf16[6144,1024]{1,0:T(8,128)(2,1)S(1)} custom-call(bf16[6144,1024]{1,0:T(8,128)(2,1)} %source), custom_call_target="tpu_custom_call" | custom-call | bytes 25165824 | tf_op jit(solution)/shard_map/load/pallas_call | solution.py:381
  82.8 2.7 %collective-permute-start.21 = (bf16[64,6144]{1,0:T(8,128)(2,1)S(1)}, bf16[64,6144]{1,0:T(8,128)(2,1)S(1)}, u32[]{:S(2)}, u32[]{:S(2)}) collective-permute-start(bf16[64,6144]{1,0:T(8,128)(2,1)S(1)} %get-tuple-element.78), channel_id=1, source_target_pairs={{0,12},{1,13},{2,14},{3,15},{4,0},{5,1},{6,2},{7,3},{8,4},{9,5},{1... | collective-permute-start | bytes 2359304 | tf_op jit(solution)/shard_map/ppermute | solution.py:23
  87.5 1.9 %fusion.25.mine = f32[128,1024]{1,0:T(8,128)S(1)} fusion(bf16[128,6144]{1,0:T(8,128)(2,1)S(1)} %stack_p.1.rows_mine, bf16[6144,1024]{1,0:T(8,128)(2,1)S(1)} %load.1), kind=kOutput, calls=%fused_computation.43 | convolution fusion | flops 1610612736 | bytes 14680064 | tf_op jit(solution)/shard_map/dot_general | solution.py:411
  89.5 6.0 %collective-permute-done.17 = bf16[64,6144]{1,0:T(8,128)(2,1)S(1)} collective-permute-done((bf16[64,6144]{1,0:T(8,128)(2,1)S(1)}, bf16[64,6144]{1,0:T(8,128)(2,1)S(1)}, u32[]{:S(2)}, u32[]{:S(2)}) %collective-permute-start.17) | collective-permute-done | bytes 786464 | tf_op jit(solution)/shard_map/ppermute | solution.py:23
  95.5 7.9 %collective-permute-done.19 = bf16[64,6144]{1,0:T(8,128)(2,1)S(1)} collective-permute-done((bf16[64,6144]{1,0:T(8,128)(2,1)S(1)}, bf16[64,6144]{1,0:T(8,128)(2,1)S(1)}, u32[]{:S(2)}, u32[]{:S(2)}) %collective-permute-start.19) | collective-permute-done | bytes 786464 | tf_op jit(solution)/shard_map/ppermute | solution.py:23
  103.6 1.9 %fusion.26.theirs = f32[128,1024]{1,0:T(8,128)S(1)} fusion(bf16[128,6144]{1,0:T(8,128)(2,1)S(1)} %collective-permute-done.16.rows_theirs, bf16[6144,1024]{1,0:T(8,128)(2,1)S(1)} %load.1), kind=kOutput, calls=%fused_computation.44 | convolution fusion | flops 1610612736 | bytes 14680064 | tf_op jit(solution)/shard_map/dot_general | solution.py:411
  106.7 1.9 %fusion.27.mine = f32[128,1024]{1,0:T(8,128)S(1)} fusion(bf16[128,6144]{1,0:T(8,128)(2,1)S(1)} %constant_dynamic-update-slice_fusion.rows_mine, bf16[6144,1024]{1,0:T(8,128)(2,1)S(1)} %load.1), kind=kOutput, calls=%fused_computation.45 | convolution fusion | flops 1610612736 | bytes 14680064 | tf_op jit(solution)/shard_map/dot_general | solution.py:411
  108.6 1.9 %fusion.28.theirs = f32[128,1024]{1,0:T(8,128)S(1)} fusion(bf16[128,6144]{1,0:T(8,128)(2,1)S(1)} %collective-permute-done.23.rows_theirs, bf16[6144,1024]{1,0:T(8,128)(2,1)S(1)} %load.1), kind=kOutput, calls=%fused_computation.46 | convolution fusion | flops 1610612736 | bytes 14680064 | tf_op jit(solution)/shard_map/dot_general | solution.py:411
  113.2 2.8 %collective-permute-start.20 = (bf16[64,6144]{1,0:T(8,128)(2,1)S(1)}, bf16[64,6144]{1,0:T(8,128)(2,1)S(1)}, u32[]{:S(2)}, u32[]{:S(2)}) collective-permute-start(bf16[64,6144]{1,0:T(8,128)(2,1)S(1)} %collective-permute-done.19), channel_id=1, source_target_pairs={{0,12},{1,13},{2,14},{3,15},{4,0},{5,1},{6,2},{7,3},{8,4},{9,5},{1... | collective-permute-start | bytes 2359304 | tf_op jit(solution)/shard_map/ppermute | solution.py:23
  116.1 1.9 %fusion.29.mine = f32[128,1024]{1,0:T(8,128)S(1)} fusion(bf16[128,6144]{1,0:T(8,128)(2,1)S(1)} %constant_dynamic-update-slice_fusion.2.rows_mine, bf16[6144,1024]{1,0:T(8,128)(2,1)S(1)} %load.1), kind=kOutput, calls=%fused_computation.47 | convolution fusion | flops 1610612736 | bytes 14680064 | tf_op jit(solution)/shard_map/dot_general | solution.py:411
  118.0 1.9 %fusion.30.theirs = f32[128,1024]{1,0:T(8,128)S(1)} fusion(bf16[128,6144]{1,0:T(8,128)(2,1)S(1)} %collective-permute-done.24.rows_theirs, bf16[6144,1024]{1,0:T(8,128)(2,1)S(1)} %load.1), kind=kOutput, calls=%fused_computation.48 | convolution fusion | flops 1610612736 | bytes 14680064 | tf_op jit(solution)/shard_map/dot_general | solution.py:411
  121.1 4.9 %collective-permute-done.18 = bf16[64,6144]{1,0:T(8,128)(2,1)S(1)} collective-permute-done((bf16[64,6144]{1,0:T(8,128)(2,1)S(1)}, bf16[64,6144]{1,0:T(8,128)(2,1)S(1)}, u32[]{:S(2)}, u32[]{:S(2)}) %collective-permute-start.18) | collective-permute-done | bytes 786464 | tf_op jit(solution)/shard_map/ppermute | solution.py:23
  126.3 1.9 %fusion.31.mine = f32[128,1024]{1,0:T(8,128)S(1)} fusion(bf16[128,6144]{1,0:T(8,128)(2,1)S(1)} %constant_dynamic-update-slice_fusion.4.rows_mine, bf16[6144,1024]{1,0:T(8,128)(2,1)S(1)} %load.1), kind=kOutput, calls=%fused_computation.49 | convolution fusion | flops 1610612736 | bytes 14680064 | tf_op jit(solution)/shard_map/dot_general | solution.py:411
  129.7 1.9 %fusion.32.theirs = f32[128,1024]{1,0:T(8,128)S(1)} fusion(bf16[128,6144]{1,0:T(8,128)(2,1)S(1)} %collective-permute-done.25.rows_theirs, bf16[6144,1024]{1,0:T(8,128)(2,1)S(1)} %load.1), kind=kOutput, calls=%fused_computation.50 | convolution fusion | flops 1610612736 | bytes 14680064 | tf_op jit(solution)/shard_map/dot_general | solution.py:411
  133.4 8.1 %all_to_all.10.found = f32[8,8,128]{2,1,0:T(8,128)S(1)} all-to-all(f32[8,8,128]{2,1,0:T(8,128)S(1)} %place.1), channel_id=1, replica_groups=mesh['x'=4,'core'=2,'z'=4,'y'=4] {'x','core'}, dimensions={0} | all-to-all | bytes 65536 | tf_op jit(solution)/shard_map/all_to_all | solution.py:430
  142.1 13.4 %all_to_all.11.found = f32[16,8,128]{2,1,0:T(8,128)S(1)} all-to-all(f32[16,8,128]{2,1,0:T(8,128)S(1)} %block.1), channel_id=1, replica_groups=mesh['x'=4,'core'=2,'z'=4,'y'=4] {'z','y'}, dimensions={0} | all-to-all | bytes 131072 | tf_op jit(solution)/shard_map/all_to_all | solution.py:432
  (88 shorter events, 38.2 us)
Async XLA Ops:
  0.0 1.9 %copy-start = (bf16[6144,256]{1,0:T(8,128)(2,1)S(1)}, bf16[6144,256]{1,0:T(8,128)(2,1)}, u32[]{:S(2)}) copy-start(bf16[6144,256]{1,0:T(8,128)(2,1)} %param.15) | copy-start | bytes 9437188
  4.0 10.2 %copy-start.3 = (bf16[128,6144]{1,0:T(8,128)(2,1)S(1)}, bf16[128,6144]{1,0:T(8,128)(2,1)}, u32[]{:S(2)}) copy-start(bf16[128,6144]{1,0:T(8,128)(2,1)} %param.10) | copy-start | bytes 4718596
  7.6 1.4 collective-permute-start
  9.6 10.1 %copy-start.2 = (f32[2,128,128]{2,1,0:T(8,128)S(1)}, f32[2,128,128]{2,1,0:T(8,128)}, u32[]{:S(2)}) copy-start(f32[2,128,128]{2,1,0:T(8,128)} %carried.1) | copy-start | bytes 393220
  9.6 7.4 %collective-permute-start.1 = (bf16[2,144,128]{2,1,0:T(8,128)(2,1)S(1)}, bf16[2,144,128]{2,1,0:T(8,128)(2,1)S(1)}, u32[]{:S(2)}, u32[]{:S(2)}) collective-permute-start(bf16[2,144,128]{2,1,0:T(8,128)(2,1)S(1)} %combine.1), channel_id=1, source_target_pairs={{0,96},{1,97},{2,98},{3,99},{4,100},{5,101},{6,102},{7,103},{8,104... | collective-permute-start | bytes 221192 | tf_op jit(solution)/shard_map/ppermute | solution.py:23
  12.5 6.4 %collective-permute-start.2 = (bf16[2,144,128]{2,1,0:T(8,128)(2,1)S(1)}, bf16[2,144,128]{2,1,0:T(8,128)(2,1)S(1)}, u32[]{:S(2)}, u32[]{:S(2)}) collective-permute-start(bf16[2,144,128]{2,1,0:T(8,128)(2,1)S(1)} %combine.1), channel_id=1, source_target_pairs={{0,64},{1,65},{2,66},{3,67},{4,68},{5,69},{6,70},{7,71},{8,72},{9,... | collective-permute-start | bytes 221192 | tf_op jit(solution)/shard_map/ppermute | solution.py:23
  13.3 6.3 %collective-permute-start.3 = (bf16[2,144,128]{2,1,0:T(8,128)(2,1)S(1)}, bf16[2,144,128]{2,1,0:T(8,128)(2,1)S(1)}, u32[]{:S(2)}, u32[]{:S(2)}) collective-permute-start(bf16[2,144,128]{2,1,0:T(8,128)(2,1)S(1)} %combine.1), channel_id=1, source_target_pairs={{0,32},{1,33},{2,34},{3,35},{4,36},{5,37},{6,38},{7,39},{8,40},{9,... | collective-permute-start | bytes 221192 | tf_op jit(solution)/shard_map/ppermute | solution.py:23
  25.1 23.6 %copy-start.4 = (bf16[6144]{0:T(1024)(128)(2,1)S(1)}, bf16[6144]{0:T(1024)(128)(2,1)}, u32[]{:S(2)}) copy-start(bf16[6144]{0:T(1024)(128)(2,1)} %param.17) | copy-start | bytes 36868
  25.1 9.2 %collective-permute-start.4 = (bf16[32,6144]{1,0:T(8,128)(2,1)}, bf16[32,6144]{1,0:T(8,128)(2,1)S(1)}, u32[]{:S(2)}, u32[]{:S(2)}) collective-permute-start(bf16[32,6144]{1,0:T(8,128)(2,1)} %get-tuple-element.43), channel_id=1, source_target_pairs={{0,1},{1,2},{2,3},{3,0},{4,5},{5,6},{6,7},{7,4},{8,9},{9,10},{10,1... | collective-permute-start | bytes 1179656 | tf_op jit(solution)/shard_map/ppermute | solution.py:23
  26.7 13.1 %collective-permute-start.5 = (bf16[32,6144]{1,0:T(8,128)(2,1)}, bf16[32,6144]{1,0:T(8,128)(2,1)S(1)}, u32[]{:S(2)}, u32[]{:S(2)}) collective-permute-start(bf16[32,6144]{1,0:T(8,128)(2,1)} %get-tuple-element.44), channel_id=1, source_target_pairs={{0,2},{1,3},{2,0},{3,1},{4,6},{5,7},{6,4},{7,5},{8,10},{9,11},{10,... | collective-permute-start | bytes 1179656 | tf_op jit(solution)/shard_map/ppermute | solution.py:23
  29.6 10.2 %collective-permute-start.6 = (bf16[32,6144]{1,0:T(8,128)(2,1)}, bf16[32,6144]{1,0:T(8,128)(2,1)S(1)}, u32[]{:S(2)}, u32[]{:S(2)}) collective-permute-start(bf16[32,6144]{1,0:T(8,128)(2,1)} %get-tuple-element.45), channel_id=1, source_target_pairs={{0,3},{1,0},{2,1},{3,2},{4,7},{5,4},{6,5},{7,6},{8,11},{9,8},{10,9... | collective-permute-start | bytes 1179656 | tf_op jit(solution)/shard_map/ppermute | solution.py:23
  41.3 7.5 %collective-permute-start.7 = (bf16[8,6144]{1,0:T(8,128)(2,1)S(1)}, bf16[8,6144]{1,0:T(8,128)(2,1)S(1)}, u32[]{:S(2)}, u32[]{:S(2)}) collective-permute-start(bf16[8,6144]{1,0:T(8,128)(2,1)S(1)} %get-tuple-element.48), channel_id=1, source_target_pairs={{0,4},{1,5},{2,6},{3,7},{4,8},{5,9},{6,10},{7,11},{8,12},{9,13},{1... | collective-permute-start | bytes 294920 | tf_op jit(solution)/shard_map/ppermute | solution.py:23
  43.2 7.2 %collective-permute-start.8 = (bf16[8,6144]{1,0:T(8,128)(2,1)S(1)}, bf16[8,6144]{1,0:T(8,128)(2,1)S(1)}, u32[]{:S(2)}, u32[]{:S(2)}) collective-permute-start(bf16[8,6144]{1,0:T(8,128)(2,1)S(1)} %get-tuple-element.49), channel_id=1, source_target_pairs={{0,8},{1,9},{2,10},{3,11},{4,12},{5,13},{6,14},{7,15},{8,0},{9,1},... | collective-permute-start | bytes 294920 | tf_op jit(solution)/shard_map/ppermute | solution.py:23
  46.8 4.6 %collective-permute-start.9 = (bf16[8,6144]{1,0:T(8,128)(2,1)S(1)}, bf16[8,6144]{1,0:T(8,128)(2,1)S(1)}, u32[]{:S(2)}, u32[]{:S(2)}) collective-permute-start(bf16[8,6144]{1,0:T(8,128)(2,1)S(1)} %get-tuple-element.50), channel_id=1, source_target_pairs={{0,12},{1,13},{2,14},{3,15},{4,0},{5,1},{6,2},{7,3},{8,4},{9,5},{1... | collective-permute-start | bytes 294920 | tf_op jit(solution)/shard_map/ppermute | solution.py:23
  52.2 4.7 %collective-permute-start.10 = (bf16[8,6144]{1,0:T(8,128)(2,1)S(1)}, bf16[8,6144]{1,0:T(8,128)(2,1)S(1)}, u32[]{:S(2)}, u32[]{:S(2)}) collective-permute-start(bf16[8,6144]{1,0:T(8,128)(2,1)S(1)} %norm.1.a), channel_id=1, source_target_pairs={{0,96},{1,97},{2,98},{3,99},{4,100},{5,101},{6,102},{7,103},{8,104... | collective-permute-start | bytes 294920 | tf_op jit(solution)/shard_map/ppermute | solution.py:23
  52.8 6.2 %collective-permute-start.11 = (bf16[8,6144]{1,0:T(8,128)(2,1)S(1)}, bf16[8,6144]{1,0:T(8,128)(2,1)S(1)}, u32[]{:S(2)}, u32[]{:S(2)}) collective-permute-start(bf16[8,6144]{1,0:T(8,128)(2,1)S(1)} %norm.1.a), channel_id=1, source_target_pairs={{0,64},{1,65},{2,66},{3,67},{4,68},{5,69},{6,70},{7,71},{8,72},{9,... | collective-permute-start | bytes 294920 | tf_op jit(solution)/shard_map/ppermute | solution.py:23
  53.6 6.4 %collective-permute-start.12 = (bf16[8,6144]{1,0:T(8,128)(2,1)S(1)}, bf16[8,6144]{1,0:T(8,128)(2,1)S(1)}, u32[]{:S(2)}, u32[]{:S(2)}) collective-permute-start(bf16[8,6144]{1,0:T(8,128)(2,1)S(1)} %norm.1.a), channel_id=1, source_target_pairs={{0,32},{1,33},{2,34},{3,35},{4,36},{5,37},{6,38},{7,39},{8,40},{9,... | collective-permute-start | bytes 294920 | tf_op jit(solution)/shard_map/ppermute | solution.py:23
  60.6 16.6 %copy-start.5 = (s32[1024]{0:T(1024)S(1)}, s32[1024]{0:T(1024)}, u32[]{:S(2)}) copy-start(s32[1024]{0:T(1024)} %param.19) | copy-start | bytes 12292
  60.6 11.9 %collective-permute-start.13 = (bf16[32,6144]{1,0:T(8,128)(2,1)S(1)}, bf16[32,6144]{1,0:T(8,128)(2,1)S(1)}, u32[]{:S(2)}, u32[]{:S(2)}) collective-permute-start(bf16[32,6144]{1,0:T(8,128)(2,1)S(1)} %stack_x.1.a), channel_id=1, source_target_pairs={{0,3},{1,0},{2,1},{3,2},{4,7},{5,4},{6,5},{7,6},{8,11},{9,8},{10,9... | collective-permute-start | bytes 1179656 | tf_op jit(solution)/shard_map/ppermute | solution.py:23
  62.9 9.5 %collective-permute-start.14 = (bf16[32,6144]{1,0:T(8,128)(2,1)S(1)}, bf16[32,6144]{1,0:T(8,128)(2,1)S(1)}, u32[]{:S(2)}, u32[]{:S(2)}) collective-permute-start(bf16[32,6144]{1,0:T(8,128)(2,1)S(1)} %stack_x.1.a), channel_id=1, source_target_pairs={{0,2},{1,3},{2,0},{3,1},{4,6},{5,7},{6,4},{7,5},{8,10},{9,11},{10,... | collective-permute-start | bytes 1179656 | tf_op jit(solution)/shard_map/ppermute | solution.py:23
  64.4 12.1 %collective-permute-start.15 = (bf16[32,6144]{1,0:T(8,128)(2,1)S(1)}, bf16[32,6144]{1,0:T(8,128)(2,1)S(1)}, u32[]{:S(2)}, u32[]{:S(2)}) collective-permute-start(bf16[32,6144]{1,0:T(8,128)(2,1)S(1)} %stack_x.1.a), channel_id=1, source_target_pairs={{0,1},{1,2},{2,3},{3,0},{4,5},{5,6},{6,7},{7,4},{8,9},{9,10},{10,1... | collective-permute-start | bytes 1179656 | tf_op jit(solution)/shard_map/ppermute | solution.py:23
  77.1 5.0 %collective-permute-start.16 = (bf16[128,6144]{1,0:T(8,128)(2,1)S(1)}, bf16[128,6144]{1,0:T(8,128)(2,1)S(1)}, u32[]{:S(2)}, u32[]{:S(2)}) collective-permute-start(bf16[128,6144]{1,0:T(8,128)(2,1)S(1)} %stack_p.1.rows_mine), channel_id=1, source_target_pairs={{0,16},{1,17},{2,18},{3,19},{4,20},{5,21},{6,22},{7,23},{8,24},{9,... | collective-permute-start | bytes 4718600 | tf_op jit(solution)/shard_map/ppermute | solution.py:23
  82.2 13.3 %collective-permute-start.17 = (bf16[64,6144]{1,0:T(8,128)(2,1)S(1)}, bf16[64,6144]{1,0:T(8,128)(2,1)S(1)}, u32[]{:S(2)}, u32[]{:S(2)}) collective-permute-start(bf16[64,6144]{1,0:T(8,128)(2,1)S(1)} %get-tuple-element.78), channel_id=1, source_target_pairs={{0,4},{1,5},{2,6},{3,7},{4,8},{5,9},{6,10},{7,11},{8,12},{9,13},{1... | collective-permute-start | bytes 2359304 | tf_op jit(solution)/shard_map/ppermute | solution.py:23
  82.8 28.9 %collective-permute-start.21 = (bf16[64,6144]{1,0:T(8,128)(2,1)S(1)}, bf16[64,6144]{1,0:T(8,128)(2,1)S(1)}, u32[]{:S(2)}, u32[]{:S(2)}) collective-permute-start(bf16[64,6144]{1,0:T(8,128)(2,1)S(1)} %get-tuple-element.78), channel_id=1, source_target_pairs={{0,12},{1,13},{2,14},{3,15},{4,0},{5,1},{6,2},{7,3},{8,4},{9,5},{1... | collective-permute-start | bytes 2359304 | tf_op jit(solution)/shard_map/ppermute | solution.py:23
  85.5 17.9 %collective-permute-start.19 = (bf16[64,6144]{1,0:T(8,128)(2,1)S(1)}, bf16[64,6144]{1,0:T(8,128)(2,1)S(1)}, u32[]{:S(2)}, u32[]{:S(2)}) collective-permute-start(bf16[64,6144]{1,0:T(8,128)(2,1)S(1)} %get-tuple-element.77), channel_id=1, source_target_pairs={{0,12},{1,13},{2,14},{3,15},{4,0},{5,1},{6,2},{7,3},{8,4},{9,5},{1... | collective-permute-start | bytes 2359304 | tf_op jit(solution)/shard_map/ppermute | solution.py:23
  86.5 25.2 %collective-permute-start.22 = (bf16[64,6144]{1,0:T(8,128)(2,1)S(1)}, bf16[64,6144]{1,0:T(8,128)(2,1)S(1)}, u32[]{:S(2)}, u32[]{:S(2)}) collective-permute-start(bf16[64,6144]{1,0:T(8,128)(2,1)S(1)} %get-tuple-element.77), channel_id=1, source_target_pairs={{0,4},{1,5},{2,6},{3,7},{4,8},{5,9},{6,10},{7,11},{8,12},{9,13},{1... | collective-permute-start | bytes 2359304 | tf_op jit(solution)/shard_map/ppermute | solution.py:23
  103.5 5.1 %collective-permute-start.23 = (bf16[128,6144]{1,0:T(8,128)(2,1)S(1)}, bf16[128,6144]{1,0:T(8,128)(2,1)S(1)}, u32[]{:S(2)}, u32[]{:S(2)}) collective-permute-start(bf16[128,6144]{1,0:T(8,128)(2,1)S(1)} %constant_dynamic-update-slice_fusion.rows_mine), channel_id=1, source_target_pairs={{0,16},{1,17},{2,18},{3,19},{4,20},{5,21},{6,22},{7,23},{8,24},{9,... | collective-permute-start | bytes 4718600 | tf_op jit(solution)/shard_map/ppermute | solution.py:23
  111.8 6.2 %collective-permute-start.24 = (bf16[128,6144]{1,0:T(8,128)(2,1)S(1)}, bf16[128,6144]{1,0:T(8,128)(2,1)S(1)}, u32[]{:S(2)}, u32[]{:S(2)}) collective-permute-start(bf16[128,6144]{1,0:T(8,128)(2,1)S(1)} %constant_dynamic-update-slice_fusion.2.rows_mine), channel_id=1, source_target_pairs={{0,16},{1,17},{2,18},{3,19},{4,20},{5,21},{6,22},{7,23},{8,24},{9,... | collective-permute-start | bytes 4718600 | tf_op jit(solution)/shard_map/ppermute | solution.py:23
  112.4 13.7 %collective-permute-start.18 = (bf16[64,6144]{1,0:T(8,128)(2,1)S(1)}, bf16[64,6144]{1,0:T(8,128)(2,1)S(1)}, u32[]{:S(2)}, u32[]{:S(2)}) collective-permute-start(bf16[64,6144]{1,0:T(8,128)(2,1)S(1)} %collective-permute-done.17), channel_id=1, source_target_pairs={{0,4},{1,5},{2,6},{3,7},{4,8},{5,9},{6,10},{7,11},{8,12},{9,13},{1... | collective-permute-start | bytes 2359304 | tf_op jit(solution)/shard_map/ppermute | solution.py:23
  113.2 12.8 %collective-permute-start.20 = (bf16[64,6144]{1,0:T(8,128)(2,1)S(1)}, bf16[64,6144]{1,0:T(8,128)(2,1)S(1)}, u32[]{:S(2)}, u32[]{:S(2)}) collective-permute-start(bf16[64,6144]{1,0:T(8,128)(2,1)S(1)} %collective-permute-done.19), channel_id=1, source_target_pairs={{0,12},{1,13},{2,14},{3,15},{4,0},{5,1},{6,2},{7,3},{8,4},{9,5},{1... | collective-permute-start | bytes 2359304 | tf_op jit(solution)/shard_map/ppermute | solution.py:23
  126.2 3.5 %collective-permute-start.25 = (bf16[128,6144]{1,0:T(8,128)(2,1)S(1)}, bf16[128,6144]{1,0:T(8,128)(2,1)S(1)}, u32[]{:S(2)}, u32[]{:S(2)}) collective-permute-start(bf16[128,6144]{1,0:T(8,128)(2,1)S(1)} %constant_dynamic-update-slice_fusion.4.rows_mine), channel_id=1, source_target_pairs={{0,16},{1,17},{2,18},{3,19},{4,20},{5,21},{6,22},{7,23},{8,24},{9,... | collective-permute-start | bytes 4718600 | tf_op jit(solution)/shard_map/ppermute | solution.py:23
  129.6 26.9 %copy-start.1 = (bf16[6144,256]{1,0:T(8,128)(2,1)S(1)}, bf16[6144,256]{1,0:T(8,128)(2,1)}, u32[]{:S(2)}) copy-start(bf16[6144,256]{1,0:T(8,128)(2,1)} %param.15) | copy-start | bytes 9437188

commit v8 on v7

--- a/solution.py
+++ b/solution.py
@@ -397,28 +397,39 @@
     half = ours.shape[0] // 2
     low, high = ours[:half], ours[half:]
     early = (move(low, along_q(1)), move(high, along_q(3)))
+    first = jnp.dot(ours, vocab, preferred_element_type=F32)
+    low, high, first = lax.optimization_barrier((low, high, first))
     late = (move(low, along_q(3)), move(high, along_q(1)))
     far = (move(early[0], along_q(1)), move(early[1], along_q(3)))
-    found = []
-    for s, block in (((0, 0), ours), ((1, 3), early), ((3, 1), late), ((2, 2), far)):
-        if s == (0, 0):
-            swapped = theirs
-        else:
-            if s != (1, 3):
-                block, found = lax.optimization_barrier((block, found))
-            block = jnp.concatenate(block, axis=0)
-            swapped = move(block, other_core)
-        logits = [jnp.dot(b, vocab, preferred_element_type=F32) for b in (block, swapped)]
-        found += local(
-            functools.partial(score_kernel, *s),
+    def dot(rows):
+        return jnp.dot(rows, vocab, preferred_element_type=F32)
+
+    def score(shifts, blocks, logits):
+        return local(
+            functools.partial(score_kernel, *shifts),
             [on_chip((8, 128), F32)] * 2,
             scalars,
             lines,
             *logits,
-            unread=(block, swapped),
+            unread=blocks,
             bytes_=8 * 128 * vocab_local,
             name="score",
         )
+
+    def both(parts):
+        joined = jnp.concatenate(parts, axis=0)
+        return joined, move(joined, other_core)
+
+    found = score((0, 0), (ours, theirs), (first, dot(theirs)))
+    blocks = both(early)
+    found += score((1, 3), blocks, [dot(b) for b in blocks])
+    late, found = lax.optimization_barrier((late, found))
+    blocks = both(late)
+    first = dot(blocks[0])
+    far, first = lax.optimization_barrier((far, first))
+    found += score((3, 1), blocks, (first, dot(blocks[1])))
+    blocks = both(far)
+    found += score((2, 2), blocks, [dot(b) for b in blocks])
     sent = local(
         place_kernel,
         on_chip((X * CORE, 8, 128), F32),

time: 157 us -> 145 us (0.924)
  waiting for transfers between devices: 52.5 us -> 41.2 us
    ppermute x26, waiting for transfers between devices: 52.5 us -> 41.2 us  [move(): return lax.ppermute(array, ALL, pairs)]
  transfers between devices with their start and end apart: 26 -> 26, of which waited for: 16 -> 14; matrix products, arithmetic and copies ran while one was open for 11% -> 12% of each run, Pallas kernels for 5% -> 5%
where the time goes in v8:
time: 145 us
  waiting for transfers between devices  41.2 us (28%)
  starting transfers between devices  33.1 us (23%)
  matrix products  24.4 us (17%)
  blocking collectives  21.9 us (15%)
  Pallas kernels  20.6 us (14%)
  local copies, waits for them, and re-layouts  2.1 us (1%)
    ppermute x26, waiting for transfers between devices, move(): return lax.ppermute(array, ALL, pairs)  41.2 us
    ppermute x26, starting transfers between devices, move(): return lax.ppermute(array, ALL, pairs)  33.1 us
    all_to_all x1, blocking collectives, shards(): came = lax.all_to_all(sent, ('z', 'y'), 0, 0)  13.7 us
    dot_general x7, matrix products, dot(): return jnp.dot(rows, vocab, preferred_element_type=F32)  13.2 us
    pallas_call x13, Pallas kernels, local(): pl.pallas_call(kernel, out_shape=outs, in_specs=[SCALARS] + [WHOLE] * len...  11.6 us
    all_to_all x1, blocking collectives, shards(): came = lax.all_to_all(sent, ('x', 'core'), 0, 0)  8.2 us
    pallas_call x1, Pallas kernels, shards(): pl.pallas_call(load_kernel, out_shape=on_chip(vocab_weight.shape, BF16),...  4.59 us
    pallas_call x1, Pallas kernels, shards(): pl.pallas_call(project_kernel, out_shape=[in_hbm((32, width), F32)] + [in...  4.42 us
  transfers between devices with their start and end apart: 26, of which 14 were waited for; matrix products, arithmetic and copies ran while one was open for 12% of the time, Pallas kernels for 5%

profile of v8, /device:TPU:0, one launch (start us, length us, event | category | flops | bytes accessed | tf_op | source)
XLA Modules:
  0.0 144.8 jit_solution(17060745363047692238)
XLA Ops:
  1.9 2.0 %convolution_convert_fusion.2 = bf16[128,256]{1,0:T(8,128)(2,1)S(1)} fusion(bf16[128,6144]{1,0:T(8,128)(2,1)} %param.10, bf16[6144,256]{1,0:T(8,128)(2,1)S(1)} %copy-done), kind=kOutput, calls=%fused_computation.7 | convolution fusion | flops 402685952 | bytes 4784128 | tf_op jit(solution)/shard_map/dot_general | solution.py:282
  4.0 3.1 %convolution_convert_fusion.1 = bf16[128,256]{1,0:T(8,128)(2,1)S(1)} fusion(bf16[128,6144]{1,0:T(8,128)(2,1)} %param.10, bf16[6144,256]{1,0:T(8,128)(2,1)} %param.14), kind=kOutput, calls=%fused_computation.6 | convolution fusion | flops 402685952 | bytes 4784128 | tf_op jit(solution)/shard_map/dot_general | solution.py:281
  9.6 2.9 %collective-permute-start.1 = (bf16[2,144,128]{2,1,0:T(8,128)(2,1)S(1)}, bf16[2,144,128]{2,1,0:T(8,128)(2,1)S(1)}, u32[]{:S(2)}, u32[]{:S(2)}) collective-permute-start(bf16[2,144,128]{2,1,0:T(8,128)(2,1)S(1)} %combine.1), channel_id=1, source_target_pairs={{0,96},{1,97},{2,98},{3,99},{4,100},{5,101},{6,102},{7,103},{8,104... | collective-permute-start | bytes 221192 | tf_op jit(solution)/shard_map/ppermute | solution.py:23
  14.2 2.5 %fusion.3 = bf16[16,2,8,128]{3,2,1,0:T(8,128)(2,1)S(1)} fusion(bf16[128,6144]{1,0:T(8,128)(2,1)S(1)} %copy-done.3, bf16[6144,256]{1,0:T(8,128)(2,1)} %param.13), kind=kOutput, calls=%fused_computation.9 | convolution fusion | flops 402685952 | bytes 4784128 | tf_op jit(solution)/shard_map/dot_general | solution.py:307
  17.0 1.9 %collective-permute-done.2.two = bf16[2,144,128]{2,1,0:T(8,128)(2,1)S(1)} collective-permute-done((bf16[2,144,128]{2,1,0:T(8,128)(2,1)S(1)}, bf16[2,144,128]{2,1,0:T(8,128)(2,1)S(1)}, u32[]{:S(2)}, u32[]{:S(2)}) %collective-permute-start.2) | collective-permute-done | bytes 73760 | tf_op jit(solution)/shard_map/ppermute | solution.py:23
  20.7 4.4 %project.1 = (f32[32,6144]{1,0:T(8,128)}, bf16[32,6144]{1,0:T(8,128)(2,1)}, bf16[32,6144]{1,0:T(8,128)(2,1)}, bf16[32,6144]{1,0:T(8,128)(2,1)}) custom-call(s32[8]{0:T(128)S(1)} %stack.32.at, bf16[128,256]{1,0:T(8,128)(2,1)S(1)} %copy.26.heads, bf16[256,6144]{1,0:T(8,128)(2,1)} %weight.1), custom_call_target="tpu_custom_call" | custom-call | flops 402653184 | bytes 4718592 | tf_op jit(solution)/shard_map/project/pallas_call | solution.py:334
  26.7 2.9 %collective-permute-start.5 = (bf16[32,6144]{1,0:T(8,128)(2,1)}, bf16[32,6144]{1,0:T(8,128)(2,1)S(1)}, u32[]{:S(2)}, u32[]{:S(2)}) collective-permute-start(bf16[32,6144]{1,0:T(8,128)(2,1)} %get-tuple-element.42), channel_id=1, source_target_pairs={{0,2},{1,3},{2,0},{3,1},{4,6},{5,7},{6,4},{7,5},{8,10},{9,11},{10,... | collective-permute-start | bytes 1179656 | tf_op jit(solution)/shard_map/ppermute | solution.py:23
  31.0 3.4 %collective-permute-done.4.one = bf16[32,6144]{1,0:T(8,128)(2,1)S(1)} collective-permute-done((bf16[32,6144]{1,0:T(8,128)(2,1)}, bf16[32,6144]{1,0:T(8,128)(2,1)S(1)}, u32[]{:S(2)}, u32[]{:S(2)}) %collective-permute-start.4) | collective-permute-done | bytes 393248 | tf_op jit(solution)/shard_map/ppermute | solution.py:23
  34.3 5.5 %collective-permute-done.5.two = bf16[32,6144]{1,0:T(8,128)(2,1)S(1)} collective-permute-done((bf16[32,6144]{1,0:T(8,128)(2,1)}, bf16[32,6144]{1,0:T(8,128)(2,1)S(1)}, u32[]{:S(2)}, u32[]{:S(2)}) %collective-permute-start.5) | collective-permute-done | bytes 393248 | tf_op jit(solution)/shard_map/ppermute | solution.py:23
  41.3 2.0 %collective-permute-start.7 = (bf16[8,6144]{1,0:T(8,128)(2,1)S(1)}, bf16[8,6144]{1,0:T(8,128)(2,1)S(1)}, u32[]{:S(2)}, u32[]{:S(2)}) collective-permute-start(bf16[8,6144]{1,0:T(8,128)(2,1)S(1)} %get-tuple-element.46), channel_id=1, source_target_pairs={{0,4},{1,5},{2,6},{3,7},{4,8},{5,9},{6,10},{7,11},{8,12},{9,13},{1... | collective-permute-start | bytes 294920 | tf_op jit(solution)/shard_map/ppermute | solution.py:23
  43.2 3.6 %collective-permute-start.8 = (bf16[8,6144]{1,0:T(8,128)(2,1)S(1)}, bf16[8,6144]{1,0:T(8,128)(2,1)S(1)}, u32[]{:S(2)}, u32[]{:S(2)}) collective-permute-start(bf16[8,6144]{1,0:T(8,128)(2,1)S(1)} %get-tuple-element.47), channel_id=1, source_target_pairs={{0,8},{1,9},{2,10},{3,11},{4,12},{5,13},{6,14},{7,15},{8,0},{9,1},... | collective-permute-start | bytes 294920 | tf_op jit(solution)/shard_map/ppermute | solution.py:23
  48.8 1.7 %collective-permute-done.8.two = bf16[8,6144]{1,0:T(8,128)(2,1)S(1)} collective-permute-done((bf16[8,6144]{1,0:T(8,128)(2,1)S(1)}, bf16[8,6144]{1,0:T(8,128)(2,1)S(1)}, u32[]{:S(2)}, u32[]{:S(2)}) %collective-permute-start.8) | collective-permute-done | bytes 98336 | tf_op jit(solution)/shard_map/ppermute | solution.py:23
  54.6 2.2 %collective-permute-done.10.b = bf16[8,6144]{1,0:T(8,128)(2,1)S(1)} collective-permute-done((bf16[8,6144]{1,0:T(8,128)(2,1)S(1)}, bf16[8,6144]{1,0:T(8,128)(2,1)S(1)}, u32[]{:S(2)}, u32[]{:S(2)}) %collective-permute-start.10) | collective-permute-done | bytes 98336 | tf_op jit(solution)/shard_map/ppermute | solution.py:23
  56.8 2.1 %collective-permute-done.11.c = bf16[8,6144]{1,0:T(8,128)(2,1)S(1)} collective-permute-done((bf16[8,6144]{1,0:T(8,128)(2,1)S(1)}, bf16[8,6144]{1,0:T(8,128)(2,1)S(1)}, u32[]{:S(2)}, u32[]{:S(2)}) %collective-permute-start.11) | collective-permute-done | bytes 98336 | tf_op jit(solution)/shard_map/ppermute | solution.py:23
  60.6 2.4 %collective-permute-start.13 = (bf16[32,6144]{1,0:T(8,128)(2,1)S(1)}, bf16[32,6144]{1,0:T(8,128)(2,1)S(1)}, u32[]{:S(2)}, u32[]{:S(2)}) collective-permute-start(bf16[32,6144]{1,0:T(8,128)(2,1)S(1)} %stack_x.1.a), channel_id=1, source_target_pairs={{0,3},{1,0},{2,1},{3,2},{4,7},{5,4},{6,5},{7,6},{8,11},{9,8},{10,9... | collective-permute-start | bytes 1179656 | tf_op jit(solution)/shard_map/ppermute | solution.py:23
  64.9 7.6 %collective-permute-done.13.b = bf16[32,6144]{1,0:T(8,128)(2,1)S(1)} collective-permute-done((bf16[32,6144]{1,0:T(8,128)(2,1)S(1)}, bf16[32,6144]{1,0:T(8,128)(2,1)S(1)}, u32[]{:S(2)}, u32[]{:S(2)}) %collective-permute-start.13) | collective-permute-done | bytes 393248 | tf_op jit(solution)/shard_map/ppermute | solution.py:23
  72.5 3.9 %collective-permute-done.15.d = bf16[32,6144]{1,0:T(8,128)(2,1)S(1)} collective-permute-done((bf16[32,6144]{1,0:T(8,128)(2,1)S(1)}, bf16[32,6144]{1,0:T(8,128)(2,1)S(1)}, u32[]{:S(2)}, u32[]{:S(2)}) %collective-permute-start.15) | collective-permute-done | bytes 393248 | tf_op jit(solution)/shard_map/ppermute | solution.py:23
  77.5 4.6 %load.1 = bf16[6144,1024]{1,0:T(8,128)(2,1)S(1)} custom-call(bf16[6144,1024]{1,0:T(8,128)(2,1)} %source), custom_call_target="tpu_custom_call" | custom-call | bytes 25165824 | tf_op jit(solution)/shard_map/load/pallas_call | solution.py:381
  82.8 2.7 %collective-permute-start.20 = (bf16[64,6144]{1,0:T(8,128)(2,1)S(1)}, bf16[64,6144]{1,0:T(8,128)(2,1)S(1)}, u32[]{:S(2)}, u32[]{:S(2)}) collective-permute-start(bf16[64,6144]{1,0:T(8,128)(2,1)S(1)} %get-tuple-element.53), channel_id=1, source_target_pairs={{0,12},{1,13},{2,14},{3,15},{4,0},{5,1},{6,2},{7,3},{8,4},{9,5},{1... | collective-permute-start | bytes 2359304 | tf_op jit(solution)/shard_map/ppermute | solution.py:23
  85.5 1.9 %fusion.25.mine = f32[128,1024]{1,0:T(8,128)S(1)} fusion(bf16[128,6144]{1,0:T(8,128)(2,1)S(1)} %stack_p.1.rows_mine, bf16[6144,1024]{1,0:T(8,128)(2,1)S(1)} %load.1), kind=kOutput, calls=%fused_computation.43 | convolution fusion | flops 1610612736 | bytes 14680064 | tf_op jit(solution)/shard_map/dot_general | solution.py:400
  89.5 5.9 %collective-permute-done.19 = bf16[64,6144]{1,0:T(8,128)(2,1)S(1)} collective-permute-done((bf16[64,6144]{1,0:T(8,128)(2,1)S(1)}, bf16[64,6144]{1,0:T(8,128)(2,1)S(1)}, u32[]{:S(2)}, u32[]{:S(2)}) %collective-permute-start.19) | collective-permute-done | bytes 786464 | tf_op jit(solution)/shard_map/ppermute | solution.py:23
  95.7 1.9 %fusion.26.theirs = f32[128,1024]{1,0:T(8,128)S(1)} fusion(bf16[128,6144]{1,0:T(8,128)(2,1)S(1)} %collective-permute-done.16.rows_theirs, bf16[6144,1024]{1,0:T(8,128)(2,1)S(1)} %load.1), kind=kOutput, calls=%fused_computation.44 | convolution fusion | flops 1610612736 | bytes 14680064 | tf_op jit(solution)/shard_map/dot_general | solution.py:405
  99.1 2.9 %collective-permute-start.23 = (bf16[64,6144]{1,0:T(8,128)(2,1)S(1)}, bf16[64,6144]{1,0:T(8,128)(2,1)S(1)}, u32[]{:S(2)}, u32[]{:S(2)}) collective-permute-start(bf16[64,6144]{1,0:T(8,128)(2,1)S(1)} %collective-permute-done.20), channel_id=1, source_target_pairs={{0,12},{1,13},{2,14},{3,15},{4,0},{5,1},{6,2},{7,3},{8,4},{9,5},{1... | collective-permute-start | bytes 2359304 | tf_op jit(solution)/shard_map/ppermute | solution.py:23
  102.0 1.9 %fusion.27.mine = f32[128,1024]{1,0:T(8,128)S(1)} fusion(bf16[128,6144]{1,0:T(8,128)(2,1)S(1)} %constant_dynamic-update-slice_fusion.rows_mine, bf16[6144,1024]{1,0:T(8,128)(2,1)S(1)} %load.1), kind=kOutput, calls=%fused_computation.45 | convolution fusion | flops 1610612736 | bytes 14680064 | tf_op jit(solution)/shard_map/dot_general | solution.py:405
  103.9 1.9 %fusion.28.theirs = f32[128,1024]{1,0:T(8,128)S(1)} fusion(bf16[128,6144]{1,0:T(8,128)(2,1)S(1)} %collective-permute-done.21.rows_theirs, bf16[6144,1024]{1,0:T(8,128)(2,1)S(1)} %load.1), kind=kOutput, calls=%fused_computation.46 | convolution fusion | flops 1610612736 | bytes 14680064 | tf_op jit(solution)/shard_map/dot_general | solution.py:405
  107.5 1.9 %fusion.29.mine = f32[128,1024]{1,0:T(8,128)S(1)} fusion(bf16[128,6144]{1,0:T(8,128)(2,1)S(1)} %constant_dynamic-update-slice_fusion.2.rows_mine, bf16[6144,1024]{1,0:T(8,128)(2,1)S(1)} %load.1), kind=kOutput, calls=%fused_computation.47 | convolution fusion | flops 1610612736 | bytes 14680064 | tf_op jit(solution)/shard_map/dot_general | solution.py:405
  109.3 3.0 %collective-permute-done.22 = bf16[64,6144]{1,0:T(8,128)(2,1)S(1)} collective-permute-done((bf16[64,6144]{1,0:T(8,128)(2,1)S(1)}, bf16[64,6144]{1,0:T(8,128)(2,1)S(1)}, u32[]{:S(2)}, u32[]{:S(2)}) %collective-permute-start.22) | collective-permute-done | bytes 786464 | tf_op jit(solution)/shard_map/ppermute | solution.py:23
  112.5 1.9 %fusion.31.mine = f32[128,1024]{1,0:T(8,128)S(1)} fusion(bf16[128,6144]{1,0:T(8,128)(2,1)S(1)} %constant_dynamic-update-slice_fusion.4.rows_mine, bf16[6144,1024]{1,0:T(8,128)(2,1)S(1)} %load.1), kind=kOutput, calls=%fused_computation.49 | convolution fusion | flops 1610612736 | bytes 14680064 | tf_op jit(solution)/shard_map/dot_general | solution.py:405
  114.4 1.9 %fusion.30.theirs = f32[128,1024]{1,0:T(8,128)S(1)} fusion(bf16[128,6144]{1,0:T(8,128)(2,1)S(1)} %collective-permute-done.24.rows_theirs, bf16[6144,1024]{1,0:T(8,128)(2,1)S(1)} %load.1), kind=kOutput, calls=%fused_computation.48 | convolution fusion | flops 1610612736 | bytes 14680064 | tf_op jit(solution)/shard_map/dot_general | solution.py:405
  116.3 1.9 %fusion.32.theirs = f32[128,1024]{1,0:T(8,128)S(1)} fusion(bf16[128,6144]{1,0:T(8,128)(2,1)S(1)} %collective-permute-done.25.rows_theirs, bf16[6144,1024]{1,0:T(8,128)(2,1)S(1)} %load.1), kind=kOutput, calls=%fused_computation.50 | convolution fusion | flops 1610612736 | bytes 14680064 | tf_op jit(solution)/shard_map/dot_general | solution.py:405
  121.3 8.2 %all_to_all.10.found = f32[8,8,128]{2,1,0:T(8,128)S(1)} all-to-all(f32[8,8,128]{2,1,0:T(8,128)S(1)} %place.1), channel_id=1, replica_groups=mesh['x'=4,'core'=2,'z'=4,'y'=4] {'x','core'}, dimensions={0} | all-to-all | bytes 65536 | tf_op jit(solution)/shard_map/all_to_all | solution.py:441
  130.0 13.7 %all_to_all.11.found = f32[16,8,128]{2,1,0:T(8,128)S(1)} all-to-all(f32[16,8,128]{2,1,0:T(8,128)S(1)} %block.1), channel_id=1, replica_groups=mesh['x'=4,'core'=2,'z'=4,'y'=4] {'z','y'}, dimensions={0} | all-to-all | bytes 131072 | tf_op jit(solution)/shard_map/all_to_all | solution.py:443
  (88 shorter events, 34.4 us)
Async XLA Ops:
  0.0 1.9 %copy-start = (bf16[6144,256]{1,0:T(8,128)(2,1)S(1)}, bf16[6144,256]{1,0:T(8,128)(2,1)}, u32[]{:S(2)}) copy-start(bf16[6144,256]{1,0:T(8,128)(2,1)} %param.15) | copy-start | bytes 9437188
  4.0 10.2 %copy-start.3 = (bf16[128,6144]{1,0:T(8,128)(2,1)S(1)}, bf16[128,6144]{1,0:T(8,128)(2,1)}, u32[]{:S(2)}) copy-start(bf16[128,6144]{1,0:T(8,128)(2,1)} %param.10) | copy-start | bytes 4718596
  7.6 1.4 collective-permute-start
  9.6 10.1 %copy-start.2 = (f32[2,128,128]{2,1,0:T(8,128)S(1)}, f32[2,128,128]{2,1,0:T(8,128)}, u32[]{:S(2)}) copy-start(f32[2,128,128]{2,1,0:T(8,128)} %carried.1) | copy-start | bytes 393220
  9.6 7.4 %collective-permute-start.1 = (bf16[2,144,128]{2,1,0:T(8,128)(2,1)S(1)}, bf16[2,144,128]{2,1,0:T(8,128)(2,1)S(1)}, u32[]{:S(2)}, u32[]{:S(2)}) collective-permute-start(bf16[2,144,128]{2,1,0:T(8,128)(2,1)S(1)} %combine.1), channel_id=1, source_target_pairs={{0,96},{1,97},{2,98},{3,99},{4,100},{5,101},{6,102},{7,103},{8,104... | collective-permute-start | bytes 221192 | tf_op jit(solution)/shard_map/ppermute | solution.py:23
  12.5 6.4 %collective-permute-start.2 = (bf16[2,144,128]{2,1,0:T(8,128)(2,1)S(1)}, bf16[2,144,128]{2,1,0:T(8,128)(2,1)S(1)}, u32[]{:S(2)}, u32[]{:S(2)}) collective-permute-start(bf16[2,144,128]{2,1,0:T(8,128)(2,1)S(1)} %combine.1), channel_id=1, source_target_pairs={{0,64},{1,65},{2,66},{3,67},{4,68},{5,69},{6,70},{7,71},{8,72},{9,... | collective-permute-start | bytes 221192 | tf_op jit(solution)/shard_map/ppermute | solution.py:23
  13.3 6.3 %collective-permute-start.3 = (bf16[2,144,128]{2,1,0:T(8,128)(2,1)S(1)}, bf16[2,144,128]{2,1,0:T(8,128)(2,1)S(1)}, u32[]{:S(2)}, u32[]{:S(2)}) collective-permute-start(bf16[2,144,128]{2,1,0:T(8,128)(2,1)S(1)} %combine.1), channel_id=1, source_target_pairs={{0,32},{1,33},{2,34},{3,35},{4,36},{5,37},{6,38},{7,39},{8,40},{9,... | collective-permute-start | bytes 221192 | tf_op jit(solution)/shard_map/ppermute | solution.py:23
  25.1 23.6 %copy-start.4 = (bf16[6144]{0:T(1024)(128)(2,1)S(1)}, bf16[6144]{0:T(1024)(128)(2,1)}, u32[]{:S(2)}) copy-start(bf16[6144]{0:T(1024)(128)(2,1)} %param.17) | copy-start | bytes 36868
  25.1 9.2 %collective-permute-start.4 = (bf16[32,6144]{1,0:T(8,128)(2,1)}, bf16[32,6144]{1,0:T(8,128)(2,1)S(1)}, u32[]{:S(2)}, u32[]{:S(2)}) collective-permute-start(bf16[32,6144]{1,0:T(8,128)(2,1)} %get-tuple-element.41), channel_id=1, source_target_pairs={{0,1},{1,2},{2,3},{3,0},{4,5},{5,6},{6,7},{7,4},{8,9},{9,10},{10,1... | collective-permute-start | bytes 1179656 | tf_op jit(solution)/shard_map/ppermute | solution.py:23
  26.7 13.1 %collective-permute-start.5 = (bf16[32,6144]{1,0:T(8,128)(2,1)}, bf16[32,6144]{1,0:T(8,128)(2,1)S(1)}, u32[]{:S(2)}, u32[]{:S(2)}) collective-permute-start(bf16[32,6144]{1,0:T(8,128)(2,1)} %get-tuple-element.42), channel_id=1, source_target_pairs={{0,2},{1,3},{2,0},{3,1},{4,6},{5,7},{6,4},{7,5},{8,10},{9,11},{10,... | collective-permute-start | bytes 1179656 | tf_op jit(solution)/shard_map/ppermute | solution.py:23
  29.6 10.2 %collective-permute-start.6 = (bf16[32,6144]{1,0:T(8,128)(2,1)}, bf16[32,6144]{1,0:T(8,128)(2,1)S(1)}, u32[]{:S(2)}, u32[]{:S(2)}) collective-permute-start(bf16[32,6144]{1,0:T(8,128)(2,1)} %get-tuple-element.43), channel_id=1, source_target_pairs={{0,3},{1,0},{2,1},{3,2},{4,7},{5,4},{6,5},{7,6},{8,11},{9,8},{10,9... | collective-permute-start | bytes 1179656 | tf_op jit(solution)/shard_map/ppermute | solution.py:23
  41.3 7.5 %collective-permute-start.7 = (bf16[8,6144]{1,0:T(8,128)(2,1)S(1)}, bf16[8,6144]{1,0:T(8,128)(2,1)S(1)}, u32[]{:S(2)}, u32[]{:S(2)}) collective-permute-start(bf16[8,6144]{1,0:T(8,128)(2,1)S(1)} %get-tuple-element.46), channel_id=1, source_target_pairs={{0,4},{1,5},{2,6},{3,7},{4,8},{5,9},{6,10},{7,11},{8,12},{9,13},{1... | collective-permute-start | bytes 294920 | tf_op jit(solution)/shard_map/ppermute | solution.py:23
  43.2 7.2 %collective-permute-start.8 = (bf16[8,6144]{1,0:T(8,128)(2,1)S(1)}, bf16[8,6144]{1,0:T(8,128)(2,1)S(1)}, u32[]{:S(2)}, u32[]{:S(2)}) collective-permute-start(bf16[8,6144]{1,0:T(8,128)(2,1)S(1)} %get-tuple-element.47), channel_id=1, source_target_pairs={{0,8},{1,9},{2,10},{3,11},{4,12},{5,13},{6,14},{7,15},{8,0},{9,1},... | collective-permute-start | bytes 294920 | tf_op jit(solution)/shard_map/ppermute | solution.py:23
  46.8 4.6 %collective-permute-start.9 = (bf16[8,6144]{1,0:T(8,128)(2,1)S(1)}, bf16[8,6144]{1,0:T(8,128)(2,1)S(1)}, u32[]{:S(2)}, u32[]{:S(2)}) collective-permute-start(bf16[8,6144]{1,0:T(8,128)(2,1)S(1)} %get-tuple-element.48), channel_id=1, source_target_pairs={{0,12},{1,13},{2,14},{3,15},{4,0},{5,1},{6,2},{7,3},{8,4},{9,5},{1... | collective-permute-start | bytes 294920 | tf_op jit(solution)/shard_map/ppermute | solution.py:23
  52.2 4.7 %collective-permute-start.10 = (bf16[8,6144]{1,0:T(8,128)(2,1)S(1)}, bf16[8,6144]{1,0:T(8,128)(2,1)S(1)}, u32[]{:S(2)}, u32[]{:S(2)}) collective-permute-start(bf16[8,6144]{1,0:T(8,128)(2,1)S(1)} %norm.1.a), channel_id=1, source_target_pairs={{0,96},{1,97},{2,98},{3,99},{4,100},{5,101},{6,102},{7,103},{8,104... | collective-permute-start | bytes 294920 | tf_op jit(solution)/shard_map/ppermute | solution.py:23
  52.8 6.2 %collective-permute-start.11 = (bf16[8,6144]{1,0:T(8,128)(2,1)S(1)}, bf16[8,6144]{1,0:T(8,128)(2,1)S(1)}, u32[]{:S(2)}, u32[]{:S(2)}) collective-permute-start(bf16[8,6144]{1,0:T(8,128)(2,1)S(1)} %norm.1.a), channel_id=1, source_target_pairs={{0,64},{1,65},{2,66},{3,67},{4,68},{5,69},{6,70},{7,71},{8,72},{9,... | collective-permute-start | bytes 294920 | tf_op jit(solution)/shard_map/ppermute | solution.py:23
  53.6 6.4 %collective-permute-start.12 = (bf16[8,6144]{1,0:T(8,128)(2,1)S(1)}, bf16[8,6144]{1,0:T(8,128)(2,1)S(1)}, u32[]{:S(2)}, u32[]{:S(2)}) collective-permute-start(bf16[8,6144]{1,0:T(8,128)(2,1)S(1)} %norm.1.a), channel_id=1, source_target_pairs={{0,32},{1,33},{2,34},{3,35},{4,36},{5,37},{6,38},{7,39},{8,40},{9,... | collective-permute-start | bytes 294920 | tf_op jit(solution)/shard_map/ppermute | solution.py:23
  60.6 16.6 %copy-start.5 = (s32[1024]{0:T(1024)S(1)}, s32[1024]{0:T(1024)}, u32[]{:S(2)}) copy-start(s32[1024]{0:T(1024)} %param.19) | copy-start | bytes 12292
  60.6 11.9 %collective-permute-start.13 = (bf16[32,6144]{1,0:T(8,128)(2,1)S(1)}, bf16[32,6144]{1,0:T(8,128)(2,1)S(1)}, u32[]{:S(2)}, u32[]{:S(2)}) collective-permute-start(bf16[32,6144]{1,0:T(8,128)(2,1)S(1)} %stack_x.1.a), channel_id=1, source_target_pairs={{0,3},{1,0},{2,1},{3,2},{4,7},{5,4},{6,5},{7,6},{8,11},{9,8},{10,9... | collective-permute-start | bytes 1179656 | tf_op jit(solution)/shard_map/ppermute | solution.py:23
  62.9 9.5 %collective-permute-start.14 = (bf16[32,6144]{1,0:T(8,128)(2,1)S(1)}, bf16[32,6144]{1,0:T(8,128)(2,1)S(1)}, u32[]{:S(2)}, u32[]{:S(2)}) collective-permute-start(bf16[32,6144]{1,0:T(8,128)(2,1)S(1)} %stack_x.1.a), channel_id=1, source_target_pairs={{0,2},{1,3},{2,0},{3,1},{4,6},{5,7},{6,4},{7,5},{8,10},{9,11},{10,... | collective-permute-start | bytes 1179656 | tf_op jit(solution)/shard_map/ppermute | solution.py:23
  64.4 12.1 %collective-permute-start.15 = (bf16[32,6144]{1,0:T(8,128)(2,1)S(1)}, bf16[32,6144]{1,0:T(8,128)(2,1)S(1)}, u32[]{:S(2)}, u32[]{:S(2)}) collective-permute-start(bf16[32,6144]{1,0:T(8,128)(2,1)S(1)} %stack_x.1.a), channel_id=1, source_target_pairs={{0,1},{1,2},{2,3},{3,0},{4,5},{5,6},{6,7},{7,4},{8,9},{9,10},{10,1... | collective-permute-start | bytes 1179656 | tf_op jit(solution)/shard_map/ppermute | solution.py:23
  77.1 5.0 %collective-permute-start.16 = (bf16[128,6144]{1,0:T(8,128)(2,1)S(1)}, bf16[128,6144]{1,0:T(8,128)(2,1)S(1)}, u32[]{:S(2)}, u32[]{:S(2)}) collective-permute-start(bf16[128,6144]{1,0:T(8,128)(2,1)S(1)} %stack_p.1.rows_mine), channel_id=1, source_target_pairs={{0,16},{1,17},{2,18},{3,19},{4,20},{5,21},{6,22},{7,23},{8,24},{9,... | collective-permute-start | bytes 4718600 | tf_op jit(solution)/shard_map/ppermute | solution.py:23
  82.2 13.3 %collective-permute-start.19 = (bf16[64,6144]{1,0:T(8,128)(2,1)S(1)}, bf16[64,6144]{1,0:T(8,128)(2,1)S(1)}, u32[]{:S(2)}, u32[]{:S(2)}) collective-permute-start(bf16[64,6144]{1,0:T(8,128)(2,1)S(1)} %get-tuple-element.52), channel_id=1, source_target_pairs={{0,4},{1,5},{2,6},{3,7},{4,8},{5,9},{6,10},{7,11},{8,12},{9,13},{1... | collective-permute-start | bytes 2359304 | tf_op jit(solution)/shard_map/ppermute | solution.py:23
  82.8 12.7 %collective-permute-start.20 = (bf16[64,6144]{1,0:T(8,128)(2,1)S(1)}, bf16[64,6144]{1,0:T(8,128)(2,1)S(1)}, u32[]{:S(2)}, u32[]{:S(2)}) collective-permute-start(bf16[64,6144]{1,0:T(8,128)(2,1)S(1)} %get-tuple-element.53), channel_id=1, source_target_pairs={{0,12},{1,13},{2,14},{3,15},{4,0},{5,1},{6,2},{7,3},{8,4},{9,5},{1... | collective-permute-start | bytes 2359304 | tf_op jit(solution)/shard_map/ppermute | solution.py:23
  87.4 19.6 %collective-permute-start.17 = (bf16[64,6144]{1,0:T(8,128)(2,1)S(1)}, bf16[64,6144]{1,0:T(8,128)(2,1)S(1)}, u32[]{:S(2)}, u32[]{:S(2)}) collective-permute-start(bf16[64,6144]{1,0:T(8,128)(2,1)S(1)} %get-tuple-element.52), channel_id=1, source_target_pairs={{0,12},{1,13},{2,14},{3,15},{4,0},{5,1},{6,2},{7,3},{8,4},{9,5},{1... | collective-permute-start | bytes 2359304 | tf_op jit(solution)/shard_map/ppermute | solution.py:23
  88.5 18.5 %collective-permute-start.18 = (bf16[64,6144]{1,0:T(8,128)(2,1)S(1)}, bf16[64,6144]{1,0:T(8,128)(2,1)S(1)}, u32[]{:S(2)}, u32[]{:S(2)}) collective-permute-start(bf16[64,6144]{1,0:T(8,128)(2,1)S(1)} %get-tuple-element.53), channel_id=1, source_target_pairs={{0,4},{1,5},{2,6},{3,7},{4,8},{5,9},{6,10},{7,11},{8,12},{9,13},{1... | collective-permute-start | bytes 2359304 | tf_op jit(solution)/shard_map/ppermute | solution.py:23
  95.6 8.3 %collective-permute-start.21 = (bf16[128,6144]{1,0:T(8,128)(2,1)S(1)}, bf16[128,6144]{1,0:T(8,128)(2,1)S(1)}, u32[]{:S(2)}, u32[]{:S(2)}) collective-permute-start(bf16[128,6144]{1,0:T(8,128)(2,1)S(1)} %constant_dynamic-update-slice_fusion.rows_mine), channel_id=1, source_target_pairs={{0,16},{1,17},{2,18},{3,19},{4,20},{5,21},{6,22},{7,23},{8,24},{9,... | collective-permute-start | bytes 4718600 | tf_op jit(solution)/shard_map/ppermute | solution.py:23
  98.8 13.6 %collective-permute-start.22 = (bf16[64,6144]{1,0:T(8,128)(2,1)S(1)}, bf16[64,6144]{1,0:T(8,128)(2,1)S(1)}, u32[]{:S(2)}, u32[]{:S(2)}) collective-permute-start(bf16[64,6144]{1,0:T(8,128)(2,1)S(1)} %collective-permute-done.19), channel_id=1, source_target_pairs={{0,4},{1,5},{2,6},{3,7},{4,8},{5,9},{6,10},{7,11},{8,12},{9,13},{1... | collective-permute-start | bytes 2359304 | tf_op jit(solution)/shard_map/ppermute | solution.py:23
  99.1 13.2 %collective-permute-start.23 = (bf16[64,6144]{1,0:T(8,128)(2,1)S(1)}, bf16[64,6144]{1,0:T(8,128)(2,1)S(1)}, u32[]{:S(2)}, u32[]{:S(2)}) collective-permute-start(bf16[64,6144]{1,0:T(8,128)(2,1)S(1)} %collective-permute-done.20), channel_id=1, source_target_pairs={{0,12},{1,13},{2,14},{3,15},{4,0},{5,1},{6,2},{7,3},{8,4},{9,5},{1... | collective-permute-start | bytes 2359304 | tf_op jit(solution)/shard_map/ppermute | solution.py:23
  107.1 7.3 %collective-permute-start.24 = (bf16[128,6144]{1,0:T(8,128)(2,1)S(1)}, bf16[128,6144]{1,0:T(8,128)(2,1)S(1)}, u32[]{:S(2)}, u32[]{:S(2)}) collective-permute-start(bf16[128,6144]{1,0:T(8,128)(2,1)S(1)} %constant_dynamic-update-slice_fusion.2.rows_mine), channel_id=1, source_target_pairs={{0,16},{1,17},{2,18},{3,19},{4,20},{5,21},{6,22},{7,23},{8,24},{9,... | collective-permute-start | bytes 4718600 | tf_op jit(solution)/shard_map/ppermute | solution.py:23
  112.4 3.9 %collective-permute-start.25 = (bf16[128,6144]{1,0:T(8,128)(2,1)S(1)}, bf16[128,6144]{1,0:T(8,128)(2,1)S(1)}, u32[]{:S(2)}, u32[]{:S(2)}) collective-permute-start(bf16[128,6144]{1,0:T(8,128)(2,1)S(1)} %constant_dynamic-update-slice_fusion.4.rows_mine), channel_id=1, source_target_pairs={{0,16},{1,17},{2,18},{3,19},{4,20},{5,21},{6,22},{7,23},{8,24},{9,... | collective-permute-start | bytes 4718600 | tf_op jit(solution)/shard_map/ppermute | solution.py:23
  118.2 26.6 %copy-start.1 = (bf16[6144,256]{1,0:T(8,128)(2,1)S(1)}, bf16[6144,256]{1,0:T(8,128)(2,1)}, u32[]{:S(2)}) copy-start(bf16[6144,256]{1,0:T(8,128)(2,1)} %param.15) | copy-start | bytes 9437188

commit v9 on v8

--- a/solution.py
+++ b/solution.py
@@ -81,6 +81,48 @@
     copy.wait()
 
 
+def heads_kernel(count, tokens, *refs):
+    weights, outs, totals = refs[:count], refs[count : 2 * count], refs[2 * count :]
+    step = pl.program_id(0)
+    for weight, out, total in zip(weights, outs, totals):
+        part = jnp.dot(tokens[...], weight[...], preferred_element_type=F32)
+
+        @pl.when(step == 0)
+        def _():
+            total[...] = part
+
+        @pl.when(step > 0)
+        def _():
+            total[...] += part
+
+        @pl.when(step == pl.num_programs(0) - 1)
+        def _():
+            out[...] = total[...].astype(BF16)
+
+
+def heads(tokens, *weights):
+    rows, width = tokens.shape
+    columns = weights[0].shape[1]
+    count = len(weights)
+    deep = width // 6 if width % 768 == 0 else width
+    return pl.pallas_call(
+        functools.partial(heads_kernel, count),
+        out_shape=[jax.ShapeDtypeStruct((rows, columns), BF16)] * count,
+        grid=(width // deep,),
+        in_specs=[pl.BlockSpec((rows, deep), lambda n: (0, n))]
+        + [pl.BlockSpec((deep, columns), lambda n: (n, 0))] * count,
+        out_specs=[pl.BlockSpec((rows, columns), lambda n: (0, 0))] * count,
+        scratch_shapes=[pltpu.VMEM((rows, columns), F32)] * count,
+        compiler_params=pltpu.CompilerParams(vmem_limit_bytes=8 * 1024 * 1024),
+        cost_estimate=pl.CostEstimate(
+            flops=2 * rows * width * columns * count,
+            bytes_accessed=2 * width * (rows + columns * count),
+            transcendentals=0,
+        ),
+        name="heads",
+    )(leave(tokens), *[leave(w) for w in weights])
+
+
 def combine_kernel(at, mine, theirs, chip):
     size = mine.shape[2]
     low = at[1] == 0
@@ -109,9 +151,9 @@
 def project_kernel(at, heads, weight, own, one, two, three, rolled):
     @pl.when(pl.program_id(0) == 0)
     def _():
-        for s in range(4):
+        for k, s in enumerate((0, 2, 1, 3)):
             start = pl.multiple_of((at[4] + s) % 4 * 32, 32)
-            rolled[pl.ds(32 * s, 32), :] = heads[pl.ds(start, 32), :]
+            rolled[pl.ds(32 * k, 32), :] = heads[pl.ds(start, 32), :]
 
     out = jnp.dot(rolled[...], weight[...], preferred_element_type=F32)
     own[...] = out[:32]
@@ -128,7 +170,7 @@
         + two[...].astype(F32)
         + three[...].astype(F32)
     )
-    for s, out in enumerate((mine, first, second, third)):
+    for s, out in ((0, mine), (2, first), (1, second), (3, third)):
         start = pl.multiple_of((q + s) % 4 * 8, 8)
         out[...] = total[pl.ds(start, 8), :].astype(out.dtype)
 
@@ -145,14 +187,24 @@
     out[...] = (resid * scale * gain[...].astype(F32)).astype(BF16)
 
 
-def stack_kernel(at, a, b, c, d, out):
-    rows = a.shape[0]
-    out[0 : 2 * rows, :] = jnp.concatenate([a[...], b[...]], axis=0)
-    out[2 * rows : 4 * rows, :] = jnp.concatenate([c[...], d[...]], axis=0)
-
-
-def gather(block, target, scalars, name):
-    parts = [move(block, target(s)) for s in (3, 2, 1)]
+def stack_kernel(at, *refs):
+    *parts, out = refs
+    if parts[0].shape[0] % 16:
+        parts = [jnp.concatenate([a[...], b[...]], axis=0) for a, b in zip(parts[::2], parts[1::2])]
+    row = 0
+    for part in parts:
+        out[row : row + part.shape[0], :] = part[...]
+        row += part.shape[0]
+
+
+def gather(block, target, scalars, name, forward=False):
+    if forward:
+        half = block.shape[0] // 2
+        up, down = move(block, target(1)), move(block, target(3))
+        parts = [down, move(up[:half], target(1)), move(down[half:], target(3)), up]
+    else:
+        far, after, before = (move(block, target(s)) for s in (2, 3, 1))
+        parts = [after, far, before]
     rows, width = block.shape
     return local(
         stack_kernel,
@@ -278,8 +330,7 @@
     offset = (((x * CORE + c) * Z + z) * Y + y) * vocab_local
     scalars = jnp.stack([x, c, z, y, p, q, offset, offset]).astype(jnp.int32)
 
-    keys = jnp.dot(tokens, k_weight, preferred_element_type=F32).astype(BF16).reshape(view)
-    values = jnp.dot(tokens, v_weight, preferred_element_type=F32).astype(BF16).reshape(view)
+    keys, values = (part.reshape(view) for part in heads(tokens, k_weight, v_weight))
     lower = jnp.arange(rows_here)[:, None] >= jnp.arange(rows_here)[None, :]
     cumul = jnp.dot(lower.astype(F32), log_decay, precision=HIGHEST)
     last_cum = cumul[-1]
@@ -304,7 +355,7 @@
     tokens_then, chip = lax.optimization_barrier((tokens, chip))
     arrived = [(s, move(chip, along_x(s))) for s in (3, 2, 1)]
 
-    queries = jnp.dot(tokens_then, q_weight, preferred_element_type=F32).astype(BF16).reshape(view)
+    queries = heads(tokens_then, q_weight)[0].reshape(view)
     scores = jnp.einsum("thd,shd->hts", queries, keys, preferred_element_type=F32)
     diff = jnp.transpose(cumul[:, None, :] - cumul[None, :, :], (2, 0, 1))
     weight = (scores * jnp.exp(jnp.where(lower[None], diff, -1e30))).astype(BF16)
@@ -350,7 +401,7 @@
         ),
         name="project",
     )(scalars, flat_heads, leave(out_weight))
-    came = [move(part, along_p(s)) for s, part in zip((1, 2, 3), sent)]
+    came = [move(part, along_p(s)) for s, part in zip((2, 1, 3), sent)]
     own, *sent = local(
         partial_kernel,
         [on_chip((8, width), F32)] + [on_chip((8, width), BF16)] * 3,
@@ -362,7 +413,7 @@
         mib=8,
         name="partial",
     )
-    came = [move(part, along_q(s)) for s, part in zip((1, 2, 3), sent)]
+    came = [move(part, along_q(s)) for s, part in zip((2, 1, 3), sent)]
     own_tokens = lax.dynamic_slice_in_dim(tokens, 32 * p + 8 * q, 8, 0).astype(F32)
     final_rows = local(
         norm_kernel,
@@ -390,7 +441,7 @@
         ),
         name="load",
     )(leave(source))
-    ours = gather(on_x, along_p, scalars, "stack_p")
+    ours = gather(on_x, along_p, scalars, "stack_p", True)
     theirs = move(ours, other_core)
     ours, theirs = lax.optimization_barrier((ours, theirs))
     lines = jnp.transpose(targets.reshape(X, CORE, 4, 4, 8), (1, 3, 2, 0, 4)).reshape(8, 128)

time: 145 us -> 148 us (1.021)
  Pallas kernels: 20.6 us -> 31.6 us
  matrix products: 24.4 us -> 15.3 us
  waiting for transfers between devices: 41.2 us -> 35.3 us
  starting transfers between devices: 33.1 us -> 38.2 us
    pallas_call x0 -> x2, Pallas kernels: none -> 11 us  [heads(): pl.pallas_call(functools.partial(heads_kernel, count), out_shape=[jax.Sha...]
    dot_general x3 -> x0, matrix products: 7.51 us -> none  [the longest x1 3.06 us: shards(): jnp.dot(tokens, k_weight, preferred_element_type=F32).astype(BF16)]
    ppermute x26 -> x27, waiting for transfers between devices: 41.2 us -> 35.3 us  [move(): return lax.ppermute(array, ALL, pairs)]
    ppermute x26 -> x27, starting transfers between devices: 33.1 us -> 38.2 us  [move(): return lax.ppermute(array, ALL, pairs)]
  transfers between devices with their start and end apart: 26 -> 27, of which waited for: 14 -> 13; matrix products, arithmetic and copies ran while one was open for 12% -> 10% of each run, Pallas kernels for 5% -> 8%
where the time goes in v9:
time: 148 us; the launch traced here: 147 us
  starting transfers between devices  38.2 us (26%)
  waiting for transfers between devices  35.3 us (24%)
  Pallas kernels  31.6 us (21%)
  blocking collectives  23.1 us (16%)
  matrix products  15.3 us (10%)
  local copies, waits for them, and re-layouts  2.17 us (1%)
    ppermute x27, starting transfers between devices, move(): return lax.ppermute(array, ALL, pairs)  38.2 us
    ppermute x27, waiting for transfers between devices, move(): return lax.ppermute(array, ALL, pairs)  35.3 us
    all_to_all x1, blocking collectives, shards(): came = lax.all_to_all(sent, ('z', 'y'), 0, 0)  15.1 us
    dot_general x7, matrix products, dot(): return jnp.dot(rows, vocab, preferred_element_type=F32)  12.5 us
    pallas_call x13, Pallas kernels, local(): pl.pallas_call(kernel, out_shape=outs, in_specs=[SCALARS] + [WHOLE] * len...  11.6 us
    pallas_call x2, Pallas kernels, heads(): pl.pallas_call(functools.partial(heads_kernel, count), out_shape=[jax.Sha...  11 us
    all_to_all x1, blocking collectives, shards(): came = lax.all_to_all(sent, ('x', 'core'), 0, 0)  7.97 us
    pallas_call x1, Pallas kernels, shards(): pl.pallas_call(load_kernel, out_shape=on_chip(vocab_weight.shape, BF16),...  4.59 us
  transfers between devices with their start and end apart: 27, of which 13 were waited for; matrix products, arithmetic and copies ran while one was open for 10% of the time, Pallas kernels for 8%

profile of v9, /device:TPU:0, one launch (start us, length us, event | category | flops | bytes accessed | tf_op | source)
XLA Modules:
  0.0 147.2 jit_solution(3054534262403251182)
XLA Ops:
  1.1 6.5 %heads.2 = (bf16[128,256]{1,0:T(8,128)(2,1)S(1)}, bf16[128,256]{1,0:T(8,128)(2,1)S(1)}) custom-call(bf16[128,6144]{1,0:T(8,128)(2,1)} %tokens.2, bf16[6144,256]{1,0:T(8,128)(2,1)} %refs_0_.2, bf16[6144,256]{1,0:T(8,128)(2,1)} %refs_1_.1), custom_call_target="tpu_custom_call" | custom-call | flops 805306368 | bytes 7864320 | tf_op jit(solution)/shard_map/heads/pallas_call | solution.py:108
  10.2 2.9 %collective-permute-start.1 = (bf16[2,144,128]{2,1,0:T(8,128)(2,1)S(1)}, bf16[2,144,128]{2,1,0:T(8,128)(2,1)S(1)}, u32[]{:S(2)}, u32[]{:S(2)}) collective-permute-start(bf16[2,144,128]{2,1,0:T(8,128)(2,1)S(1)} %combine.1), channel_id=1, source_target_pairs={{0,96},{1,97},{2,98},{3,99},{4,100},{5,101},{6,102},{7,103},{8,104... | collective-permute-start | bytes 221192 | tf_op jit(solution)/shard_map/ppermute | solution.py:23
  14.8 4.5 %heads.3 = bf16[128,256]{1,0:T(8,128)(2,1)S(1)} custom-call(bf16[128,6144]{1,0:T(8,128)(2,1)} %tokens.2, bf16[6144,256]{1,0:T(8,128)(2,1)} %refs_0_.3), custom_call_target="tpu_custom_call" | custom-call | flops 402653184 | bytes 4718592 | tf_op jit(solution)/shard_map/heads/pallas_call | solution.py:108
  21.4 4.5 %project.1 = (f32[32,6144]{1,0:T(8,128)}, bf16[32,6144]{1,0:T(8,128)(2,1)}, bf16[32,6144]{1,0:T(8,128)(2,1)}, bf16[32,6144]{1,0:T(8,128)(2,1)}) custom-call(s32[8]{0:T(128)S(1)} %stack.32.at, bf16[128,256]{1,0:T(8,128)(2,1)S(1)} %copy.26.heads, bf16[256,6144]{1,0:T(8,128)(2,1)} %weight.1), custom_call_target="tpu_custom_call" | custom-call | flops 402653184 | bytes 4718592 | tf_op jit(solution)/shard_map/project/pallas_call | solution.py:385
  25.8 3.2 %collective-permute-start.4 = (bf16[32,6144]{1,0:T(8,128)(2,1)}, bf16[32,6144]{1,0:T(8,128)(2,1)S(1)}, u32[]{:S(2)}, u32[]{:S(2)}) collective-permute-start(bf16[32,6144]{1,0:T(8,128)(2,1)} %get-tuple-element.45), channel_id=1, source_target_pairs={{0,2},{1,3},{2,0},{3,1},{4,6},{5,7},{6,4},{7,5},{8,10},{9,11},{10,... | collective-permute-start | bytes 1179656 | tf_op jit(solution)/shard_map/ppermute | solution.py:23
  29.7 2.6 %collective-permute-start.6 = (bf16[32,6144]{1,0:T(8,128)(2,1)}, bf16[32,6144]{1,0:T(8,128)(2,1)S(1)}, u32[]{:S(2)}, u32[]{:S(2)}) collective-permute-start(bf16[32,6144]{1,0:T(8,128)(2,1)} %get-tuple-element.47), channel_id=1, source_target_pairs={{0,3},{1,0},{2,1},{3,2},{4,7},{5,4},{6,5},{7,6},{8,11},{9,8},{10,9... | collective-permute-start | bytes 1179656 | tf_op jit(solution)/shard_map/ppermute | solution.py:23
  32.3 3.2 %collective-permute-done.4.one = bf16[32,6144]{1,0:T(8,128)(2,1)S(1)} collective-permute-done((bf16[32,6144]{1,0:T(8,128)(2,1)}, bf16[32,6144]{1,0:T(8,128)(2,1)S(1)}, u32[]{:S(2)}, u32[]{:S(2)}) %collective-permute-start.4) | collective-permute-done | bytes 393248 | tf_op jit(solution)/shard_map/ppermute | solution.py:23
  35.4 4.1 %collective-permute-done.5.two = bf16[32,6144]{1,0:T(8,128)(2,1)S(1)} collective-permute-done((bf16[32,6144]{1,0:T(8,128)(2,1)}, bf16[32,6144]{1,0:T(8,128)(2,1)S(1)}, u32[]{:S(2)}, u32[]{:S(2)}) %collective-permute-start.5) | collective-permute-done | bytes 393248 | tf_op jit(solution)/shard_map/ppermute | solution.py:23
  41.3 4.0 %collective-permute-start.7 = (bf16[8,6144]{1,0:T(8,128)(2,1)S(1)}, bf16[8,6144]{1,0:T(8,128)(2,1)S(1)}, u32[]{:S(2)}, u32[]{:S(2)}) collective-permute-start(bf16[8,6144]{1,0:T(8,128)(2,1)S(1)} %get-tuple-element.50), channel_id=1, source_target_pairs={{0,8},{1,9},{2,10},{3,11},{4,12},{5,13},{6,14},{7,15},{8,0},{9,1},... | collective-permute-start | bytes 294920 | tf_op jit(solution)/shard_map/ppermute | solution.py:23
  46.3 2.2 %collective-permute-start.9 = (bf16[8,6144]{1,0:T(8,128)(2,1)S(1)}, bf16[8,6144]{1,0:T(8,128)(2,1)S(1)}, u32[]{:S(2)}, u32[]{:S(2)}) collective-permute-start(bf16[8,6144]{1,0:T(8,128)(2,1)S(1)} %get-tuple-element.52), channel_id=1, source_target_pairs={{0,12},{1,13},{2,14},{3,15},{4,0},{5,1},{6,2},{7,3},{8,4},{9,5},{1... | collective-permute-start | bytes 294920 | tf_op jit(solution)/shard_map/ppermute | solution.py:23
  51.8 1.9 %collective-permute-start.10 = (bf16[8,6144]{1,0:T(8,128)(2,1)S(1)}, bf16[8,6144]{1,0:T(8,128)(2,1)S(1)}, u32[]{:S(2)}, u32[]{:S(2)}) collective-permute-start(bf16[8,6144]{1,0:T(8,128)(2,1)S(1)} %norm.1.refs_0_), channel_id=1, source_target_pairs={{0,96},{1,97},{2,98},{3,99},{4,100},{5,101},{6,102},{7,103},{8,104... | collective-permute-start | bytes 294920 | tf_op jit(solution)/shard_map/ppermute | solution.py:23
  56.9 2.9 %collective-permute-done.11.refs_2_ = bf16[8,6144]{1,0:T(8,128)(2,1)S(1)} collective-permute-done((bf16[8,6144]{1,0:T(8,128)(2,1)S(1)}, bf16[8,6144]{1,0:T(8,128)(2,1)S(1)}, u32[]{:S(2)}, u32[]{:S(2)}) %collective-permute-start.11) | collective-permute-done | bytes 98336 | tf_op jit(solution)/shard_map/ppermute | solution.py:23
  63.1 1.8 %collective-permute-start.13 = (bf16[32,6144]{1,0:T(8,128)(2,1)S(1)}, bf16[32,6144]{1,0:T(8,128)(2,1)S(1)}, u32[]{:S(2)}, u32[]{:S(2)}) collective-permute-start(bf16[32,6144]{1,0:T(8,128)(2,1)S(1)} %stack_x.1.refs_0_), channel_id=1, source_target_pairs={{0,3},{1,0},{2,1},{3,2},{4,7},{5,4},{6,5},{7,6},{8,11},{9,8},{10,9... | collective-permute-start | bytes 1179656 | tf_op jit(solution)/shard_map/ppermute | solution.py:23
  65.0 5.8 %collective-permute-done.14.refs_4_ = bf16[32,6144]{1,0:T(8,128)(2,1)S(1)} collective-permute-done((bf16[32,6144]{1,0:T(8,128)(2,1)S(1)}, bf16[32,6144]{1,0:T(8,128)(2,1)S(1)}, u32[]{:S(2)}, u32[]{:S(2)}) %collective-permute-start.14) | collective-permute-done | bytes 393248 | tf_op jit(solution)/shard_map/ppermute | solution.py:23
  71.0 3.1 %collective-permute-start.16 = (bf16[16,6144]{1,0:T(8,128)(2,1)S(1)}, bf16[16,6144]{1,0:T(8,128)(2,1)S(1)}, u32[]{:S(2)}, u32[]{:S(2)}) collective-permute-start(bf16[16,6144]{1,0:T(8,128)(2,1)S(1)} %slice.21), channel_id=1, source_target_pairs={{0,3},{1,0},{2,1},{3,2},{4,7},{5,4},{6,5},{7,6},{8,11},{9,8},{10,9... | collective-permute-start | bytes 589832 | tf_op jit(solution)/shard_map/ppermute | solution.py:23
  74.1 3.5 %collective-permute-done.15.refs_2_ = bf16[16,6144]{1,0:T(8,128)(2,1)S(1)} collective-permute-done((bf16[16,6144]{1,0:T(8,128)(2,1)S(1)}, bf16[16,6144]{1,0:T(8,128)(2,1)S(1)}, u32[]{:S(2)}, u32[]{:S(2)}) %collective-permute-start.15) | collective-permute-done | bytes 196640 | tf_op jit(solution)/shard_map/ppermute | solution.py:23
  78.7 4.6 %load.1 = bf16[6144,1024]{1,0:T(8,128)(2,1)S(1)} custom-call(bf16[6144,1024]{1,0:T(8,128)(2,1)} %source), custom_call_target="tpu_custom_call" | custom-call | bytes 25165824 | tf_op jit(solution)/shard_map/load/pallas_call | solution.py:432
  83.5 3.3 %collective-permute-start.21 = (bf16[64,6144]{1,0:T(8,128)(2,1)S(1)}, bf16[64,6144]{1,0:T(8,128)(2,1)S(1)}, u32[]{:S(2)}, u32[]{:S(2)}) collective-permute-start(bf16[64,6144]{1,0:T(8,128)(2,1)S(1)} %get-tuple-element.57), channel_id=1, source_target_pairs={{0,12},{1,13},{2,14},{3,15},{4,0},{5,1},{6,2},{7,3},{8,4},{9,5},{1... | collective-permute-start | bytes 2359304 | tf_op jit(solution)/shard_map/ppermute | solution.py:23
  86.8 1.8 %fusion.24.mine = f32[128,1024]{1,0:T(8,128)S(1)} fusion(bf16[128,6144]{1,0:T(8,128)(2,1)S(1)} %stack_p.1.rows_mine, bf16[6144,1024]{1,0:T(8,128)(2,1)S(1)} %load.1), kind=kOutput, calls=%fused_computation.39 | convolution fusion | flops 1610612736 | bytes 14680064 | tf_op jit(solution)/shard_map/dot_general | solution.py:451
  88.6 2.2 %collective-permute-start.18 = (bf16[64,6144]{1,0:T(8,128)(2,1)S(1)}, bf16[64,6144]{1,0:T(8,128)(2,1)S(1)}, u32[]{:S(2)}, u32[]{:S(2)}) collective-permute-start(bf16[64,6144]{1,0:T(8,128)(2,1)S(1)} %get-tuple-element.56), channel_id=1, source_target_pairs={{0,12},{1,13},{2,14},{3,15},{4,0},{5,1},{6,2},{7,3},{8,4},{9,5},{1... | collective-permute-start | bytes 2359304 | tf_op jit(solution)/shard_map/ppermute | solution.py:23
  90.9 5.8 %collective-permute-done.20 = bf16[64,6144]{1,0:T(8,128)(2,1)S(1)} collective-permute-done((bf16[64,6144]{1,0:T(8,128)(2,1)S(1)}, bf16[64,6144]{1,0:T(8,128)(2,1)S(1)}, u32[]{:S(2)}, u32[]{:S(2)}) %collective-permute-start.20) | collective-permute-done | bytes 786464 | tf_op jit(solution)/shard_map/ppermute | solution.py:23
  96.9 1.8 %fusion.25.theirs = f32[128,1024]{1,0:T(8,128)S(1)} fusion(bf16[128,6144]{1,0:T(8,128)(2,1)S(1)} %collective-permute-done.17.rows_theirs, bf16[6144,1024]{1,0:T(8,128)(2,1)S(1)} %load.1), kind=kOutput, calls=%fused_computation.40 | convolution fusion | flops 1610612736 | bytes 14680064 | tf_op jit(solution)/shard_map/dot_general | solution.py:456
  101.2 1.9 %collective-permute-start.24 = (bf16[64,6144]{1,0:T(8,128)(2,1)S(1)}, bf16[64,6144]{1,0:T(8,128)(2,1)S(1)}, u32[]{:S(2)}, u32[]{:S(2)}) collective-permute-start(bf16[64,6144]{1,0:T(8,128)(2,1)S(1)} %collective-permute-done.21), channel_id=1, source_target_pairs={{0,12},{1,13},{2,14},{3,15},{4,0},{5,1},{6,2},{7,3},{8,4},{9,5},{1... | collective-permute-start | bytes 2359304 | tf_op jit(solution)/shard_map/ppermute | solution.py:23
  103.1 1.8 %fusion.26.mine = f32[128,1024]{1,0:T(8,128)S(1)} fusion(bf16[128,6144]{1,0:T(8,128)(2,1)S(1)} %constant_dynamic-update-slice_fusion.rows_mine, bf16[6144,1024]{1,0:T(8,128)(2,1)S(1)} %load.1), kind=kOutput, calls=%fused_computation.41 | convolution fusion | flops 1610612736 | bytes 14680064 | tf_op jit(solution)/shard_map/dot_general | solution.py:456
  104.9 1.8 %fusion.27.theirs = f32[128,1024]{1,0:T(8,128)S(1)} fusion(bf16[128,6144]{1,0:T(8,128)(2,1)S(1)} %collective-permute-done.22.rows_theirs, bf16[6144,1024]{1,0:T(8,128)(2,1)S(1)} %load.1), kind=kOutput, calls=%fused_computation.42 | convolution fusion | flops 1610612736 | bytes 14680064 | tf_op jit(solution)/shard_map/dot_general | solution.py:456
  108.4 1.8 %fusion.28.mine = f32[128,1024]{1,0:T(8,128)S(1)} fusion(bf16[128,6144]{1,0:T(8,128)(2,1)S(1)} %constant_dynamic-update-slice_fusion.2.rows_mine, bf16[6144,1024]{1,0:T(8,128)(2,1)S(1)} %load.1), kind=kOutput, calls=%fused_computation.43 | convolution fusion | flops 1610612736 | bytes 14680064 | tf_op jit(solution)/shard_map/dot_general | solution.py:456
  110.2 3.3 %collective-permute-done.23 = bf16[64,6144]{1,0:T(8,128)(2,1)S(1)} collective-permute-done((bf16[64,6144]{1,0:T(8,128)(2,1)S(1)}, bf16[64,6144]{1,0:T(8,128)(2,1)S(1)}, u32[]{:S(2)}, u32[]{:S(2)}) %collective-permute-start.23) | collective-permute-done | bytes 786464 | tf_op jit(solution)/shard_map/ppermute | solution.py:23
  114.0 1.8 %fusion.30.mine = f32[128,1024]{1,0:T(8,128)S(1)} fusion(bf16[128,6144]{1,0:T(8,128)(2,1)S(1)} %constant_dynamic-update-slice_fusion.4.rows_mine, bf16[6144,1024]{1,0:T(8,128)(2,1)S(1)} %load.1), kind=kOutput, calls=%fused_computation.45 | convolution fusion | flops 1610612736 | bytes 14680064 | tf_op jit(solution)/shard_map/dot_general | solution.py:456
  115.8 1.8 %fusion.29.theirs = f32[128,1024]{1,0:T(8,128)S(1)} fusion(bf16[128,6144]{1,0:T(8,128)(2,1)S(1)} %collective-permute-done.25.rows_theirs, bf16[6144,1024]{1,0:T(8,128)(2,1)S(1)} %load.1), kind=kOutput, calls=%fused_computation.44 | convolution fusion | flops 1610612736 | bytes 14680064 | tf_op jit(solution)/shard_map/dot_general | solution.py:456
  117.6 1.8 %fusion.31.theirs = f32[128,1024]{1,0:T(8,128)S(1)} fusion(bf16[128,6144]{1,0:T(8,128)(2,1)S(1)} %collective-permute-done.26.rows_theirs, bf16[6144,1024]{1,0:T(8,128)(2,1)S(1)} %load.1), kind=kOutput, calls=%fused_computation.46 | convolution fusion | flops 1610612736 | bytes 14680064 | tf_op jit(solution)/shard_map/dot_general | solution.py:456
  122.4 8.0 %all_to_all.10.found = f32[8,8,128]{2,1,0:T(8,128)S(1)} all-to-all(f32[8,8,128]{2,1,0:T(8,128)S(1)} %place.1), channel_id=1, replica_groups=mesh['x'=4,'core'=2,'z'=4,'y'=4] {'x','core'}, dimensions={0} | all-to-all | bytes 65536 | tf_op jit(solution)/shard_map/all_to_all | solution.py:492
  131.0 15.1 %all_to_all.11.found = f32[16,8,128]{2,1,0:T(8,128)S(1)} all-to-all(f32[16,8,128]{2,1,0:T(8,128)S(1)} %block.1), channel_id=1, replica_groups=mesh['x'=4,'core'=2,'z'=4,'y'=4] {'z','y'}, dimensions={0} | all-to-all | bytes 131072 | tf_op jit(solution)/shard_map/all_to_all | solution.py:494
  (89 shorter events, 31.6 us)
Async XLA Ops:
  0.0 0.7 copy-start
  8.2 1.4 collective-permute-start
  10.2 10.0 %copy-start.2 = (f32[2,128,128]{2,1,0:T(8,128)S(1)}, f32[2,128,128]{2,1,0:T(8,128)}, u32[]{:S(2)}) copy-start(f32[2,128,128]{2,1,0:T(8,128)} %carried.1) | copy-start | bytes 393220
  10.2 9.4 %collective-permute-start.1 = (bf16[2,144,128]{2,1,0:T(8,128)(2,1)S(1)}, bf16[2,144,128]{2,1,0:T(8,128)(2,1)S(1)}, u32[]{:S(2)}, u32[]{:S(2)}) collective-permute-start(bf16[2,144,128]{2,1,0:T(8,128)(2,1)S(1)} %combine.1), channel_id=1, source_target_pairs={{0,96},{1,97},{2,98},{3,99},{4,100},{5,101},{6,102},{7,103},{8,104... | collective-permute-start | bytes 221192 | tf_op jit(solution)/shard_map/ppermute | solution.py:23
  13.1 6.5 %collective-permute-start.2 = (bf16[2,144,128]{2,1,0:T(8,128)(2,1)S(1)}, bf16[2,144,128]{2,1,0:T(8,128)(2,1)S(1)}, u32[]{:S(2)}, u32[]{:S(2)}) collective-permute-start(bf16[2,144,128]{2,1,0:T(8,128)(2,1)S(1)} %combine.1), channel_id=1, source_target_pairs={{0,64},{1,65},{2,66},{3,67},{4,68},{5,69},{6,70},{7,71},{8,72},{9,... | collective-permute-start | bytes 221192 | tf_op jit(solution)/shard_map/ppermute | solution.py:23
  13.9 6.3 %collective-permute-start.3 = (bf16[2,144,128]{2,1,0:T(8,128)(2,1)S(1)}, bf16[2,144,128]{2,1,0:T(8,128)(2,1)S(1)}, u32[]{:S(2)}, u32[]{:S(2)}) collective-permute-start(bf16[2,144,128]{2,1,0:T(8,128)(2,1)S(1)} %combine.1), channel_id=1, source_target_pairs={{0,32},{1,33},{2,34},{3,35},{4,36},{5,37},{6,38},{7,39},{8,40},{9,... | collective-permute-start | bytes 221192 | tf_op jit(solution)/shard_map/ppermute | solution.py:23
  25.8 23.6 %copy-start.3 = (bf16[6144]{0:T(1024)(128)(2,1)S(1)}, bf16[6144]{0:T(1024)(128)(2,1)}, u32[]{:S(2)}) copy-start(bf16[6144]{0:T(1024)(128)(2,1)} %param.17) | copy-start | bytes 36868
  25.8 9.6 %collective-permute-start.4 = (bf16[32,6144]{1,0:T(8,128)(2,1)}, bf16[32,6144]{1,0:T(8,128)(2,1)S(1)}, u32[]{:S(2)}, u32[]{:S(2)}) collective-permute-start(bf16[32,6144]{1,0:T(8,128)(2,1)} %get-tuple-element.45), channel_id=1, source_target_pairs={{0,2},{1,3},{2,0},{3,1},{4,6},{5,7},{6,4},{7,5},{8,10},{9,11},{10,... | collective-permute-start | bytes 1179656 | tf_op jit(solution)/shard_map/ppermute | solution.py:23
  29.0 10.5 %collective-permute-start.5 = (bf16[32,6144]{1,0:T(8,128)(2,1)}, bf16[32,6144]{1,0:T(8,128)(2,1)S(1)}, u32[]{:S(2)}, u32[]{:S(2)}) collective-permute-start(bf16[32,6144]{1,0:T(8,128)(2,1)} %get-tuple-element.46), channel_id=1, source_target_pairs={{0,1},{1,2},{2,3},{3,0},{4,5},{5,6},{6,7},{7,4},{8,9},{9,10},{10,1... | collective-permute-start | bytes 1179656 | tf_op jit(solution)/shard_map/ppermute | solution.py:23
  29.7 10.2 %collective-permute-start.6 = (bf16[32,6144]{1,0:T(8,128)(2,1)}, bf16[32,6144]{1,0:T(8,128)(2,1)S(1)}, u32[]{:S(2)}, u32[]{:S(2)}) collective-permute-start(bf16[32,6144]{1,0:T(8,128)(2,1)} %get-tuple-element.47), channel_id=1, source_target_pairs={{0,3},{1,0},{2,1},{3,2},{4,7},{5,4},{6,5},{7,6},{8,11},{9,8},{10,9... | collective-permute-start | bytes 1179656 | tf_op jit(solution)/shard_map/ppermute | solution.py:23
  41.3 8.1 %collective-permute-start.7 = (bf16[8,6144]{1,0:T(8,128)(2,1)S(1)}, bf16[8,6144]{1,0:T(8,128)(2,1)S(1)}, u32[]{:S(2)}, u32[]{:S(2)}) collective-permute-start(bf16[8,6144]{1,0:T(8,128)(2,1)S(1)} %get-tuple-element.50), channel_id=1, source_target_pairs={{0,8},{1,9},{2,10},{3,11},{4,12},{5,13},{6,14},{7,15},{8,0},{9,1},... | collective-permute-start | bytes 294920 | tf_op jit(solution)/shard_map/ppermute | solution.py:23
  45.3 5.8 %collective-permute-start.8 = (bf16[8,6144]{1,0:T(8,128)(2,1)S(1)}, bf16[8,6144]{1,0:T(8,128)(2,1)S(1)}, u32[]{:S(2)}, u32[]{:S(2)}) collective-permute-start(bf16[8,6144]{1,0:T(8,128)(2,1)S(1)} %get-tuple-element.51), channel_id=1, source_target_pairs={{0,4},{1,5},{2,6},{3,7},{4,8},{5,9},{6,10},{7,11},{8,12},{9,13},{1... | collective-permute-start | bytes 294920 | tf_op jit(solution)/shard_map/ppermute | solution.py:23
  46.3 4.8 %collective-permute-start.9 = (bf16[8,6144]{1,0:T(8,128)(2,1)S(1)}, bf16[8,6144]{1,0:T(8,128)(2,1)S(1)}, u32[]{:S(2)}, u32[]{:S(2)}) collective-permute-start(bf16[8,6144]{1,0:T(8,128)(2,1)S(1)} %get-tuple-element.52), channel_id=1, source_target_pairs={{0,12},{1,13},{2,14},{3,15},{4,0},{5,1},{6,2},{7,3},{8,4},{9,5},{1... | collective-permute-start | bytes 294920 | tf_op jit(solution)/shard_map/ppermute | solution.py:23
  51.8 5.1 %collective-permute-start.10 = (bf16[8,6144]{1,0:T(8,128)(2,1)S(1)}, bf16[8,6144]{1,0:T(8,128)(2,1)S(1)}, u32[]{:S(2)}, u32[]{:S(2)}) collective-permute-start(bf16[8,6144]{1,0:T(8,128)(2,1)S(1)} %norm.1.refs_0_), channel_id=1, source_target_pairs={{0,96},{1,97},{2,98},{3,99},{4,100},{5,101},{6,102},{7,103},{8,104... | collective-permute-start | bytes 294920 | tf_op jit(solution)/shard_map/ppermute | solution.py:23
  53.7 6.1 %collective-permute-start.11 = (bf16[8,6144]{1,0:T(8,128)(2,1)S(1)}, bf16[8,6144]{1,0:T(8,128)(2,1)S(1)}, u32[]{:S(2)}, u32[]{:S(2)}) collective-permute-start(bf16[8,6144]{1,0:T(8,128)(2,1)S(1)} %norm.1.refs_0_), channel_id=1, source_target_pairs={{0,64},{1,65},{2,66},{3,67},{4,68},{5,69},{6,70},{7,71},{8,72},{9,... | collective-permute-start | bytes 294920 | tf_op jit(solution)/shard_map/ppermute | solution.py:23
  55.2 5.8 %collective-permute-start.12 = (bf16[8,6144]{1,0:T(8,128)(2,1)S(1)}, bf16[8,6144]{1,0:T(8,128)(2,1)S(1)}, u32[]{:S(2)}, u32[]{:S(2)}) collective-permute-start(bf16[8,6144]{1,0:T(8,128)(2,1)S(1)} %norm.1.refs_0_), channel_id=1, source_target_pairs={{0,32},{1,33},{2,34},{3,35},{4,36},{5,37},{6,38},{7,39},{8,40},{9,... | collective-permute-start | bytes 294920 | tf_op jit(solution)/shard_map/ppermute | solution.py:23
  61.7 9.1 %collective-permute-start.14 = (bf16[32,6144]{1,0:T(8,128)(2,1)S(1)}, bf16[32,6144]{1,0:T(8,128)(2,1)S(1)}, u32[]{:S(2)}, u32[]{:S(2)}) collective-permute-start(bf16[32,6144]{1,0:T(8,128)(2,1)S(1)} %stack_x.1.refs_0_), channel_id=1, source_target_pairs={{0,1},{1,2},{2,3},{3,0},{4,5},{5,6},{6,7},{7,4},{8,9},{9,10},{10,1... | collective-permute-start | bytes 1179656 | tf_op jit(solution)/shard_map/ppermute | solution.py:23
  63.1 7.9 %collective-permute-start.13 = (bf16[32,6144]{1,0:T(8,128)(2,1)S(1)}, bf16[32,6144]{1,0:T(8,128)(2,1)S(1)}, u32[]{:S(2)}, u32[]{:S(2)}) collective-permute-start(bf16[32,6144]{1,0:T(8,128)(2,1)S(1)} %stack_x.1.refs_0_), channel_id=1, source_target_pairs={{0,3},{1,0},{2,1},{3,2},{4,7},{5,4},{6,5},{7,6},{8,11},{9,8},{10,9... | collective-permute-start | bytes 1179656 | tf_op jit(solution)/shard_map/ppermute | solution.py:23
  70.7 6.9 %collective-permute-start.15 = (bf16[16,6144]{1,0:T(8,128)(2,1)S(1)}, bf16[16,6144]{1,0:T(8,128)(2,1)S(1)}, u32[]{:S(2)}, u32[]{:S(2)}) collective-permute-start(bf16[16,6144]{1,0:T(8,128)(2,1)S(1)} %slice.20), channel_id=1, source_target_pairs={{0,1},{1,2},{2,3},{3,0},{4,5},{5,6},{6,7},{7,4},{8,9},{9,10},{10,1... | collective-permute-start | bytes 589832 | tf_op jit(solution)/shard_map/ppermute | solution.py:23
  71.0 7.4 %copy-start.4 = (s32[1024]{0:T(1024)S(1)}, s32[1024]{0:T(1024)}, u32[]{:S(2)}) copy-start(s32[1024]{0:T(1024)} %param.19) | copy-start | bytes 12292
  71.0 6.7 %collective-permute-start.16 = (bf16[16,6144]{1,0:T(8,128)(2,1)S(1)}, bf16[16,6144]{1,0:T(8,128)(2,1)S(1)}, u32[]{:S(2)}, u32[]{:S(2)}) collective-permute-start(bf16[16,6144]{1,0:T(8,128)(2,1)S(1)} %slice.21), channel_id=1, source_target_pairs={{0,3},{1,0},{2,1},{3,2},{4,7},{5,4},{6,5},{7,6},{8,11},{9,8},{10,9... | collective-permute-start | bytes 589832 | tf_op jit(solution)/shard_map/ppermute | solution.py:23
  78.3 5.0 %collective-permute-start.17 = (bf16[128,6144]{1,0:T(8,128)(2,1)S(1)}, bf16[128,6144]{1,0:T(8,128)(2,1)S(1)}, u32[]{:S(2)}, u32[]{:S(2)}) collective-permute-start(bf16[128,6144]{1,0:T(8,128)(2,1)S(1)} %stack_p.1.rows_mine), channel_id=1, source_target_pairs={{0,16},{1,17},{2,18},{3,19},{4,20},{5,21},{6,22},{7,23},{8,24},{9,... | collective-permute-start | bytes 4718600 | tf_op jit(solution)/shard_map/ppermute | solution.py:23
  83.4 13.3 %collective-permute-start.20 = (bf16[64,6144]{1,0:T(8,128)(2,1)S(1)}, bf16[64,6144]{1,0:T(8,128)(2,1)S(1)}, u32[]{:S(2)}, u32[]{:S(2)}) collective-permute-start(bf16[64,6144]{1,0:T(8,128)(2,1)S(1)} %get-tuple-element.56), channel_id=1, source_target_pairs={{0,4},{1,5},{2,6},{3,7},{4,8},{5,9},{6,10},{7,11},{8,12},{9,13},{1... | collective-permute-start | bytes 2359304 | tf_op jit(solution)/shard_map/ppermute | solution.py:23
  83.5 13.2 %collective-permute-start.21 = (bf16[64,6144]{1,0:T(8,128)(2,1)S(1)}, bf16[64,6144]{1,0:T(8,128)(2,1)S(1)}, u32[]{:S(2)}, u32[]{:S(2)}) collective-permute-start(bf16[64,6144]{1,0:T(8,128)(2,1)S(1)} %get-tuple-element.57), channel_id=1, source_target_pairs={{0,12},{1,13},{2,14},{3,15},{4,0},{5,1},{6,2},{7,3},{8,4},{9,5},{1... | collective-permute-start | bytes 2359304 | tf_op jit(solution)/shard_map/ppermute | solution.py:23
  88.6 19.3 %collective-permute-start.18 = (bf16[64,6144]{1,0:T(8,128)(2,1)S(1)}, bf16[64,6144]{1,0:T(8,128)(2,1)S(1)}, u32[]{:S(2)}, u32[]{:S(2)}) collective-permute-start(bf16[64,6144]{1,0:T(8,128)(2,1)S(1)} %get-tuple-element.56), channel_id=1, source_target_pairs={{0,12},{1,13},{2,14},{3,15},{4,0},{5,1},{6,2},{7,3},{8,4},{9,5},{1... | collective-permute-start | bytes 2359304 | tf_op jit(solution)/shard_map/ppermute | solution.py:23
  90.8 17.1 %collective-permute-start.19 = (bf16[64,6144]{1,0:T(8,128)(2,1)S(1)}, bf16[64,6144]{1,0:T(8,128)(2,1)S(1)}, u32[]{:S(2)}, u32[]{:S(2)}) collective-permute-start(bf16[64,6144]{1,0:T(8,128)(2,1)S(1)} %get-tuple-element.57), channel_id=1, source_target_pairs={{0,4},{1,5},{2,6},{3,7},{4,8},{5,9},{6,10},{7,11},{8,12},{9,13},{1... | collective-permute-start | bytes 2359304 | tf_op jit(solution)/shard_map/ppermute | solution.py:23
  96.8 8.1 %collective-permute-start.22 = (bf16[128,6144]{1,0:T(8,128)(2,1)S(1)}, bf16[128,6144]{1,0:T(8,128)(2,1)S(1)}, u32[]{:S(2)}, u32[]{:S(2)}) collective-permute-start(bf16[128,6144]{1,0:T(8,128)(2,1)S(1)} %constant_dynamic-update-slice_fusion.rows_mine), channel_id=1, source_target_pairs={{0,16},{1,17},{2,18},{3,19},{4,20},{5,21},{6,22},{7,23},{8,24},{9,... | collective-permute-start | bytes 4718600 | tf_op jit(solution)/shard_map/ppermute | solution.py:23
  99.9 13.7 %collective-permute-start.23 = (bf16[64,6144]{1,0:T(8,128)(2,1)S(1)}, bf16[64,6144]{1,0:T(8,128)(2,1)S(1)}, u32[]{:S(2)}, u32[]{:S(2)}) collective-permute-start(bf16[64,6144]{1,0:T(8,128)(2,1)S(1)} %collective-permute-done.20), channel_id=1, source_target_pairs={{0,4},{1,5},{2,6},{3,7},{4,8},{5,9},{6,10},{7,11},{8,12},{9,13},{1... | collective-permute-start | bytes 2359304 | tf_op jit(solution)/shard_map/ppermute | solution.py:23
  101.2 12.3 %collective-permute-start.24 = (bf16[64,6144]{1,0:T(8,128)(2,1)S(1)}, bf16[64,6144]{1,0:T(8,128)(2,1)S(1)}, u32[]{:S(2)}, u32[]{:S(2)}) collective-permute-start(bf16[64,6144]{1,0:T(8,128)(2,1)S(1)} %collective-permute-done.21), channel_id=1, source_target_pairs={{0,12},{1,13},{2,14},{3,15},{4,0},{5,1},{6,2},{7,3},{8,4},{9,5},{1... | collective-permute-start | bytes 2359304 | tf_op jit(solution)/shard_map/ppermute | solution.py:23
  108.1 7.7 %collective-permute-start.25 = (bf16[128,6144]{1,0:T(8,128)(2,1)S(1)}, bf16[128,6144]{1,0:T(8,128)(2,1)S(1)}, u32[]{:S(2)}, u32[]{:S(2)}) collective-permute-start(bf16[128,6144]{1,0:T(8,128)(2,1)S(1)} %constant_dynamic-update-slice_fusion.2.rows_mine), channel_id=1, source_target_pairs={{0,16},{1,17},{2,18},{3,19},{4,20},{5,21},{6,22},{7,23},{8,24},{9,... | collective-permute-start | bytes 4718600 | tf_op jit(solution)/shard_map/ppermute | solution.py:23
  113.7 3.9 %collective-permute-start.26 = (bf16[128,6144]{1,0:T(8,128)(2,1)S(1)}, bf16[128,6144]{1,0:T(8,128)(2,1)S(1)}, u32[]{:S(2)}, u32[]{:S(2)}) collective-permute-start(bf16[128,6144]{1,0:T(8,128)(2,1)S(1)} %constant_dynamic-update-slice_fusion.4.rows_mine), channel_id=1, source_target_pairs={{0,16},{1,17},{2,18},{3,19},{4,20},{5,21},{6,22},{7,23},{8,24},{9,... | collective-permute-start | bytes 4718600 | tf_op jit(solution)/shard_map/ppermute | solution.py:23
  119.4 27.8 %copy-start.1 = (f32[128,2]{0,1:T(2,128)S(1)}, f32[128,2]{0,1:T(2,128)}, u32[]{:S(2)}) copy-start(f32[128,2]{0,1:T(2,128)} %param.11) | copy-start | bytes 3076

commit v10 on v8

--- a/solution.py
+++ b/solution.py
@@ -79,6 +79,58 @@
     copy = pltpu.make_async_copy(source, out, done)
     copy.start()
     copy.wait()
+
+
+def heads_kernel(count, tokens, *refs):
+    weights, outs = refs[:count], refs[count : 2 * count]
+    held, *held_weights, arrived = refs[2 * count :]
+    chunks = arrived.shape[1]
+    deep = tokens.shape[1] // chunks
+    copies = []
+    for n in range(chunks):
+        part = pl.ds(n * deep, deep)
+        copies.append(
+            [pltpu.make_async_copy(tokens.at[:, part], held.at[:, part], arrived.at[count, n])]
+            + [
+                pltpu.make_async_copy(weight.at[part, :], here.at[part, :], arrived.at[k, n])
+                for k, (weight, here) in enumerate(zip(weights, held_weights))
+            ]
+        )
+        for copy in copies[-1]:
+            copy.start()
+    totals = [None] * count
+    for n in range(chunks):
+        part = pl.ds(n * deep, deep)
+        for copy in copies[n]:
+            copy.wait()
+        for k, here in enumerate(held_weights):
+            product = jnp.dot(held[:, part], here[part, :], preferred_element_type=F32)
+            totals[k] = product if totals[k] is None else totals[k] + product
+    for out, total in zip(outs, totals):
+        out[...] = total.astype(BF16)
+
+
+def heads(tokens, *weights):
+    rows, width = tokens.shape
+    columns = weights[0].shape[1]
+    count = len(weights)
+    chunks = 4 if width % 512 == 0 else 1
+    return pl.pallas_call(
+        functools.partial(heads_kernel, count),
+        out_shape=[jax.ShapeDtypeStruct((rows, columns), BF16)] * count,
+        in_specs=[pl.BlockSpec(memory_space=pltpu.HBM)] * (1 + count),
+        out_specs=[WHOLE] * count,
+        scratch_shapes=[pltpu.VMEM((rows, width), BF16)]
+        + [pltpu.VMEM((width, columns), BF16)] * count
+        + [pltpu.SemaphoreType.DMA((count + 1, chunks))],
+        compiler_params=pltpu.CompilerParams(vmem_limit_bytes=16 * 1024 * 1024),
+        cost_estimate=pl.CostEstimate(
+            flops=2 * rows * width * columns * count,
+            bytes_accessed=2 * width * (rows + columns * count),
+            transcendentals=0,
+        ),
+        name="heads",
+    )(leave(tokens), *[leave(w) for w in weights])
 
 
 def combine_kernel(at, mine, theirs, chip):
@@ -278,8 +330,7 @@
     offset = (((x * CORE + c) * Z + z) * Y + y) * vocab_local
     scalars = jnp.stack([x, c, z, y, p, q, offset, offset]).astype(jnp.int32)
 
-    keys = jnp.dot(tokens, k_weight, preferred_element_type=F32).astype(BF16).reshape(view)
-    values = jnp.dot(tokens, v_weight, preferred_element_type=F32).astype(BF16).reshape(view)
+    keys, values = (part.reshape(view) for part in heads(tokens, k_weight, v_weight))
     lower = jnp.arange(rows_here)[:, None] >= jnp.arange(rows_here)[None, :]
     cumul = jnp.dot(lower.astype(F32), log_decay, precision=HIGHEST)
     last_cum = cumul[-1]
@@ -304,7 +355,7 @@
     tokens_then, chip = lax.optimization_barrier((tokens, chip))
     arrived = [(s, move(chip, along_x(s))) for s in (3, 2, 1)]
 
-    queries = jnp.dot(tokens_then, q_weight, preferred_element_type=F32).astype(BF16).reshape(view)
+    queries = heads(tokens_then, q_weight)[0].reshape(view)
     scores = jnp.einsum("thd,shd->hts", queries, keys, preferred_element_type=F32)
     diff = jnp.transpose(cumul[:, None, :] - cumul[None, :, :], (2, 0, 1))
     weight = (scores * jnp.exp(jnp.where(lower[None], diff, -1e30))).astype(BF16)

time: 145 us -> 143 us (0.986)
  matrix products: 24.4 us -> 15.3 us
  Pallas kernels: 20.6 us -> 27.2 us
    dot_general x3 -> x0, matrix products: 7.51 us -> none  [the longest x1 3.06 us: shards(): jnp.dot(tokens, k_weight, preferred_element_type=F32).astype(BF16)]
    pallas_call x0 -> x2, Pallas kernels: none -> 6.58 us  [heads(): pl.pallas_call(functools.partial(heads_kernel, count), out_shape=[jax.Sha...]
  transfers between devices with their start and end apart: 26 -> 26, of which waited for: 14 -> 14; matrix products, arithmetic and copies ran while one was open for 12% -> 10% of each run, Pallas kernels for 5% -> 7%
where the time goes in v10:
time: 143 us; the launch traced here: 142 us
  waiting for transfers between devices  41.4 us (29%)
  starting transfers between devices  33.1 us (23%)
  Pallas kernels  27.2 us (19%)
  blocking collectives  21.8 us (15%)
  matrix products  15.3 us (11%)
  local copies, waits for them, and re-layouts  2.15 us (2%)
    ppermute x26, waiting for transfers between devices, move(): return lax.ppermute(array, ALL, pairs)  41.4 us
    ppermute x26, starting transfers between devices, move(): return lax.ppermute(array, ALL, pairs)  33.1 us
    all_to_all x1, blocking collectives, shards(): came = lax.all_to_all(sent, ('z', 'y'), 0, 0)  13.6 us
    dot_general x7, matrix products, dot(): return jnp.dot(rows, vocab, preferred_element_type=F32)  12.5 us
    pallas_call x13, Pallas kernels, local(): pl.pallas_call(kernel, out_shape=outs, in_specs=[SCALARS] + [WHOLE] * len...  11.6 us
    all_to_all x1, blocking collectives, shards(): came = lax.all_to_all(sent, ('x', 'core'), 0, 0)  8.2 us
    pallas_call x2, Pallas kernels, heads(): pl.pallas_call(functools.partial(heads_kernel, count), out_shape=[jax.Sha...  6.58 us
    pallas_call x1, Pallas kernels, shards(): pl.pallas_call(load_kernel, out_shape=on_chip(vocab_weight.shape, BF16),...  4.59 us
  transfers between devices with their start and end apart: 26, of which 14 were waited for; matrix products, arithmetic and copies ran while one was open for 10% of the time, Pallas kernels for 7%

profile of v10, /device:TPU:0, one launch (start us, length us, event | category | flops | bytes accessed | tf_op | source)
XLA Modules:
  0.0 142.3 jit_solution(1401640765121279779)
XLA Ops:
  1.1 3.7 %heads.2 = (bf16[128,256]{1,0:T(8,128)(2,1)S(1)}, bf16[128,256]{1,0:T(8,128)(2,1)S(1)}) custom-call(bf16[128,6144]{1,0:T(8,128)(2,1)} %tokens.2, bf16[6144,256]{1,0:T(8,128)(2,1)} %refs_0_.2, bf16[6144,256]{1,0:T(8,128)(2,1)} %refs_1_.1), custom_call_target="tpu_custom_call" | custom-call | flops 805306368 | bytes 7864320 | tf_op jit(solution)/shard_map/heads/pallas_call | solution.py:118
  7.5 2.9 %collective-permute-start.1 = (bf16[2,144,128]{2,1,0:T(8,128)(2,1)S(1)}, bf16[2,144,128]{2,1,0:T(8,128)(2,1)S(1)}, u32[]{:S(2)}, u32[]{:S(2)}) collective-permute-start(bf16[2,144,128]{2,1,0:T(8,128)(2,1)S(1)} %combine.1), channel_id=1, source_target_pairs={{0,96},{1,97},{2,98},{3,99},{4,100},{5,101},{6,102},{7,103},{8,104... | collective-permute-start | bytes 221192 | tf_op jit(solution)/shard_map/ppermute | solution.py:23
  12.1 2.8 %heads.3 = bf16[128,256]{1,0:T(8,128)(2,1)S(1)} custom-call(bf16[128,6144]{1,0:T(8,128)(2,1)} %tokens.2, bf16[6144,256]{1,0:T(8,128)(2,1)} %refs_0_.3), custom_call_target="tpu_custom_call" | custom-call | flops 402653184 | bytes 4718592 | tf_op jit(solution)/shard_map/heads/pallas_call | solution.py:118
  15.3 1.5 %collective-permute-done.2.two = bf16[2,144,128]{2,1,0:T(8,128)(2,1)S(1)} collective-permute-done((bf16[2,144,128]{2,1,0:T(8,128)(2,1)S(1)}, bf16[2,144,128]{2,1,0:T(8,128)(2,1)S(1)}, u32[]{:S(2)}, u32[]{:S(2)}) %collective-permute-start.2) | collective-permute-done | bytes 73760 | tf_op jit(solution)/shard_map/ppermute | solution.py:23
  18.6 4.4 %project.1 = (f32[32,6144]{1,0:T(8,128)}, bf16[32,6144]{1,0:T(8,128)(2,1)}, bf16[32,6144]{1,0:T(8,128)(2,1)}, bf16[32,6144]{1,0:T(8,128)(2,1)}) custom-call(s32[8]{0:T(128)S(1)} %stack.32.at, bf16[128,256]{1,0:T(8,128)(2,1)S(1)} %copy.26.heads, bf16[256,6144]{1,0:T(8,128)(2,1)} %weight.1), custom_call_target="tpu_custom_call" | custom-call | flops 402653184 | bytes 4718592 | tf_op jit(solution)/shard_map/project/pallas_call | solution.py:385
  23.1 1.6 %collective-permute-start.4 = (bf16[32,6144]{1,0:T(8,128)(2,1)}, bf16[32,6144]{1,0:T(8,128)(2,1)S(1)}, u32[]{:S(2)}, u32[]{:S(2)}) collective-permute-start(bf16[32,6144]{1,0:T(8,128)(2,1)} %get-tuple-element.45), channel_id=1, source_target_pairs={{0,1},{1,2},{2,3},{3,0},{4,5},{5,6},{6,7},{7,4},{8,9},{9,10},{10,1... | collective-permute-start | bytes 1179656 | tf_op jit(solution)/shard_map/ppermute | solution.py:23
  24.6 2.9 %collective-permute-start.5 = (bf16[32,6144]{1,0:T(8,128)(2,1)}, bf16[32,6144]{1,0:T(8,128)(2,1)S(1)}, u32[]{:S(2)}, u32[]{:S(2)}) collective-permute-start(bf16[32,6144]{1,0:T(8,128)(2,1)} %get-tuple-element.46), channel_id=1, source_target_pairs={{0,2},{1,3},{2,0},{3,1},{4,6},{5,7},{6,4},{7,5},{8,10},{9,11},{10,... | collective-permute-start | bytes 1179656 | tf_op jit(solution)/shard_map/ppermute | solution.py:23
  28.9 3.4 %collective-permute-done.4.one = bf16[32,6144]{1,0:T(8,128)(2,1)S(1)} collective-permute-done((bf16[32,6144]{1,0:T(8,128)(2,1)}, bf16[32,6144]{1,0:T(8,128)(2,1)S(1)}, u32[]{:S(2)}, u32[]{:S(2)}) %collective-permute-start.4) | collective-permute-done | bytes 393248 | tf_op jit(solution)/shard_map/ppermute | solution.py:23
  32.3 5.5 %collective-permute-done.5.two = bf16[32,6144]{1,0:T(8,128)(2,1)S(1)} collective-permute-done((bf16[32,6144]{1,0:T(8,128)(2,1)}, bf16[32,6144]{1,0:T(8,128)(2,1)S(1)}, u32[]{:S(2)}, u32[]{:S(2)}) %collective-permute-start.5) | collective-permute-done | bytes 393248 | tf_op jit(solution)/shard_map/ppermute | solution.py:23
  39.2 2.0 %collective-permute-start.7 = (bf16[8,6144]{1,0:T(8,128)(2,1)S(1)}, bf16[8,6144]{1,0:T(8,128)(2,1)S(1)}, u32[]{:S(2)}, u32[]{:S(2)}) collective-permute-start(bf16[8,6144]{1,0:T(8,128)(2,1)S(1)} %get-tuple-element.50), channel_id=1, source_target_pairs={{0,4},{1,5},{2,6},{3,7},{4,8},{5,9},{6,10},{7,11},{8,12},{9,13},{1... | collective-permute-start | bytes 294920 | tf_op jit(solution)/shard_map/ppermute | solution.py:23
  41.2 3.6 %collective-permute-start.8 = (bf16[8,6144]{1,0:T(8,128)(2,1)S(1)}, bf16[8,6144]{1,0:T(8,128)(2,1)S(1)}, u32[]{:S(2)}, u32[]{:S(2)}) collective-permute-start(bf16[8,6144]{1,0:T(8,128)(2,1)S(1)} %get-tuple-element.51), channel_id=1, source_target_pairs={{0,8},{1,9},{2,10},{3,11},{4,12},{5,13},{6,14},{7,15},{8,0},{9,1},... | collective-permute-start | bytes 294920 | tf_op jit(solution)/shard_map/ppermute | solution.py:23
  46.7 1.7 %collective-permute-done.8.two = bf16[8,6144]{1,0:T(8,128)(2,1)S(1)} collective-permute-done((bf16[8,6144]{1,0:T(8,128)(2,1)S(1)}, bf16[8,6144]{1,0:T(8,128)(2,1)S(1)}, u32[]{:S(2)}, u32[]{:S(2)}) %collective-permute-start.8) | collective-permute-done | bytes 98336 | tf_op jit(solution)/shard_map/ppermute | solution.py:23
  52.5 2.2 %collective-permute-done.10.b = bf16[8,6144]{1,0:T(8,128)(2,1)S(1)} collective-permute-done((bf16[8,6144]{1,0:T(8,128)(2,1)S(1)}, bf16[8,6144]{1,0:T(8,128)(2,1)S(1)}, u32[]{:S(2)}, u32[]{:S(2)}) %collective-permute-start.10) | collective-permute-done | bytes 98336 | tf_op jit(solution)/shard_map/ppermute | solution.py:23
  54.8 2.1 %collective-permute-done.11.c = bf16[8,6144]{1,0:T(8,128)(2,1)S(1)} collective-permute-done((bf16[8,6144]{1,0:T(8,128)(2,1)S(1)}, bf16[8,6144]{1,0:T(8,128)(2,1)S(1)}, u32[]{:S(2)}, u32[]{:S(2)}) %collective-permute-start.11) | collective-permute-done | bytes 98336 | tf_op jit(solution)/shard_map/ppermute | solution.py:23
  58.5 2.4 %collective-permute-start.13 = (bf16[32,6144]{1,0:T(8,128)(2,1)S(1)}, bf16[32,6144]{1,0:T(8,128)(2,1)S(1)}, u32[]{:S(2)}, u32[]{:S(2)}) collective-permute-start(bf16[32,6144]{1,0:T(8,128)(2,1)S(1)} %stack_x.1.a), channel_id=1, source_target_pairs={{0,3},{1,0},{2,1},{3,2},{4,7},{5,4},{6,5},{7,6},{8,11},{9,8},{10,9... | collective-permute-start | bytes 1179656 | tf_op jit(solution)/shard_map/ppermute | solution.py:23
  62.8 7.6 %collective-permute-done.13.b = bf16[32,6144]{1,0:T(8,128)(2,1)S(1)} collective-permute-done((bf16[32,6144]{1,0:T(8,128)(2,1)S(1)}, bf16[32,6144]{1,0:T(8,128)(2,1)S(1)}, u32[]{:S(2)}, u32[]{:S(2)}) %collective-permute-start.13) | collective-permute-done | bytes 393248 | tf_op jit(solution)/shard_map/ppermute | solution.py:23
  70.4 3.9 %collective-permute-done.15.d = bf16[32,6144]{1,0:T(8,128)(2,1)S(1)} collective-permute-done((bf16[32,6144]{1,0:T(8,128)(2,1)S(1)}, bf16[32,6144]{1,0:T(8,128)(2,1)S(1)}, u32[]{:S(2)}, u32[]{:S(2)}) %collective-permute-start.15) | collective-permute-done | bytes 393248 | tf_op jit(solution)/shard_map/ppermute | solution.py:23
  75.4 4.6 %load.1 = bf16[6144,1024]{1,0:T(8,128)(2,1)S(1)} custom-call(bf16[6144,1024]{1,0:T(8,128)(2,1)} %source), custom_call_target="tpu_custom_call" | custom-call | bytes 25165824 | tf_op jit(solution)/shard_map/load/pallas_call | solution.py:432
  80.7 2.7 %collective-permute-start.20 = (bf16[64,6144]{1,0:T(8,128)(2,1)S(1)}, bf16[64,6144]{1,0:T(8,128)(2,1)S(1)}, u32[]{:S(2)}, u32[]{:S(2)}) collective-permute-start(bf16[64,6144]{1,0:T(8,128)(2,1)S(1)} %get-tuple-element.57), channel_id=1, source_target_pairs={{0,12},{1,13},{2,14},{3,15},{4,0},{5,1},{6,2},{7,3},{8,4},{9,5},{1... | collective-permute-start | bytes 2359304 | tf_op jit(solution)/shard_map/ppermute | solution.py:23
  83.4 1.8 %fusion.24.mine = f32[128,1024]{1,0:T(8,128)S(1)} fusion(bf16[128,6144]{1,0:T(8,128)(2,1)S(1)} %stack_p.1.rows_mine, bf16[6144,1024]{1,0:T(8,128)(2,1)S(1)} %load.1), kind=kOutput, calls=%fused_computation.39 | convolution fusion | flops 1610612736 | bytes 14680064 | tf_op jit(solution)/shard_map/dot_general | solution.py:451
  87.3 6.1 %collective-permute-done.19 = bf16[64,6144]{1,0:T(8,128)(2,1)S(1)} collective-permute-done((bf16[64,6144]{1,0:T(8,128)(2,1)S(1)}, bf16[64,6144]{1,0:T(8,128)(2,1)S(1)}, u32[]{:S(2)}, u32[]{:S(2)}) %collective-permute-start.19) | collective-permute-done | bytes 786464 | tf_op jit(solution)/shard_map/ppermute | solution.py:23
  93.6 1.8 %fusion.25.theirs = f32[128,1024]{1,0:T(8,128)S(1)} fusion(bf16[128,6144]{1,0:T(8,128)(2,1)S(1)} %collective-permute-done.16.rows_theirs, bf16[6144,1024]{1,0:T(8,128)(2,1)S(1)} %load.1), kind=kOutput, calls=%fused_computation.40 | convolution fusion | flops 1610612736 | bytes 14680064 | tf_op jit(solution)/shard_map/dot_general | solution.py:456
  96.9 2.9 %collective-permute-start.23 = (bf16[64,6144]{1,0:T(8,128)(2,1)S(1)}, bf16[64,6144]{1,0:T(8,128)(2,1)S(1)}, u32[]{:S(2)}, u32[]{:S(2)}) collective-permute-start(bf16[64,6144]{1,0:T(8,128)(2,1)S(1)} %collective-permute-done.20), channel_id=1, source_target_pairs={{0,12},{1,13},{2,14},{3,15},{4,0},{5,1},{6,2},{7,3},{8,4},{9,5},{1... | collective-permute-start | bytes 2359304 | tf_op jit(solution)/shard_map/ppermute | solution.py:23
  99.8 1.8 %fusion.26.mine = f32[128,1024]{1,0:T(8,128)S(1)} fusion(bf16[128,6144]{1,0:T(8,128)(2,1)S(1)} %constant_dynamic-update-slice_fusion.rows_mine, bf16[6144,1024]{1,0:T(8,128)(2,1)S(1)} %load.1), kind=kOutput, calls=%fused_computation.41 | convolution fusion | flops 1610612736 | bytes 14680064 | tf_op jit(solution)/shard_map/dot_general | solution.py:456
  101.6 1.8 %fusion.27.theirs = f32[128,1024]{1,0:T(8,128)S(1)} fusion(bf16[128,6144]{1,0:T(8,128)(2,1)S(1)} %collective-permute-done.21.rows_theirs, bf16[6144,1024]{1,0:T(8,128)(2,1)S(1)} %load.1), kind=kOutput, calls=%fused_computation.42 | convolution fusion | flops 1610612736 | bytes 14680064 | tf_op jit(solution)/shard_map/dot_general | solution.py:456
  105.0 1.8 %fusion.28.mine = f32[128,1024]{1,0:T(8,128)S(1)} fusion(bf16[128,6144]{1,0:T(8,128)(2,1)S(1)} %constant_dynamic-update-slice_fusion.2.rows_mine, bf16[6144,1024]{1,0:T(8,128)(2,1)S(1)} %load.1), kind=kOutput, calls=%fused_computation.43 | convolution fusion | flops 1610612736 | bytes 14680064 | tf_op jit(solution)/shard_map/dot_general | solution.py:456
  106.8 3.4 %collective-permute-done.22 = bf16[64,6144]{1,0:T(8,128)(2,1)S(1)} collective-permute-done((bf16[64,6144]{1,0:T(8,128)(2,1)S(1)}, bf16[64,6144]{1,0:T(8,128)(2,1)S(1)}, u32[]{:S(2)}, u32[]{:S(2)}) %collective-permute-start.22) | collective-permute-done | bytes 786464 | tf_op jit(solution)/shard_map/ppermute | solution.py:23
  110.5 1.8 %fusion.30.mine = f32[128,1024]{1,0:T(8,128)S(1)} fusion(bf16[128,6144]{1,0:T(8,128)(2,1)S(1)} %constant_dynamic-update-slice_fusion.4.rows_mine, bf16[6144,1024]{1,0:T(8,128)(2,1)S(1)} %load.1), kind=kOutput, calls=%fused_computation.45 | convolution fusion | flops 1610612736 | bytes 14680064 | tf_op jit(solution)/shard_map/dot_general | solution.py:456
  112.3 1.8 %fusion.29.theirs = f32[128,1024]{1,0:T(8,128)S(1)} fusion(bf16[128,6144]{1,0:T(8,128)(2,1)S(1)} %collective-permute-done.24.rows_theirs, bf16[6144,1024]{1,0:T(8,128)(2,1)S(1)} %load.1), kind=kOutput, calls=%fused_computation.44 | convolution fusion | flops 1610612736 | bytes 14680064 | tf_op jit(solution)/shard_map/dot_general | solution.py:456
  114.1 1.8 %fusion.31.theirs = f32[128,1024]{1,0:T(8,128)S(1)} fusion(bf16[128,6144]{1,0:T(8,128)(2,1)S(1)} %collective-permute-done.25.rows_theirs, bf16[6144,1024]{1,0:T(8,128)(2,1)S(1)} %load.1), kind=kOutput, calls=%fused_computation.46 | convolution fusion | flops 1610612736 | bytes 14680064 | tf_op jit(solution)/shard_map/dot_general | solution.py:456
  118.9 8.2 %all_to_all.10.found = f32[8,8,128]{2,1,0:T(8,128)S(1)} all-to-all(f32[8,8,128]{2,1,0:T(8,128)S(1)} %place.1), channel_id=1, replica_groups=mesh['x'=4,'core'=2,'z'=4,'y'=4] {'x','core'}, dimensions={0} | all-to-all | bytes 65536 | tf_op jit(solution)/shard_map/all_to_all | solution.py:492
  127.7 13.6 %all_to_all.11.found = f32[16,8,128]{2,1,0:T(8,128)S(1)} all-to-all(f32[16,8,128]{2,1,0:T(8,128)S(1)} %block.1), channel_id=1, replica_groups=mesh['x'=4,'core'=2,'z'=4,'y'=4] {'z','y'}, dimensions={0} | all-to-all | bytes 131072 | tf_op jit(solution)/shard_map/all_to_all | solution.py:494
  (85 shorter events, 32.0 us)
Async XLA Ops:
  0.0 0.7 copy-start
  5.5 1.4 %collective-permute-start = (f32[2,136,128]{2,1,0:T(8,128)S(1)}, f32[2,136,128]{2,1,0:T(8,128)S(1)}, u32[]{:S(2)}, u32[]{:S(2)}) collective-permute-start(f32[2,136,128]{2,1,0:T(8,128)S(1)} %pad_maximum_fusion.mine), channel_id=1, source_target_pairs={{0,16},{1,17},{2,18},{3,19},{4,20},{5,21},{6,22},{7,23},{8,24},{9,... | collective-permute-start | bytes 417800 | tf_op jit(solution)/shard_map/ppermute | solution.py:23
  7.5 10.1 %copy-start.2 = (f32[2,128,128]{2,1,0:T(8,128)S(1)}, f32[2,128,128]{2,1,0:T(8,128)}, u32[]{:S(2)}) copy-start(f32[2,128,128]{2,1,0:T(8,128)} %carried.1) | copy-start | bytes 393220
  7.5 7.7 %collective-permute-start.1 = (bf16[2,144,128]{2,1,0:T(8,128)(2,1)S(1)}, bf16[2,144,128]{2,1,0:T(8,128)(2,1)S(1)}, u32[]{:S(2)}, u32[]{:S(2)}) collective-permute-start(bf16[2,144,128]{2,1,0:T(8,128)(2,1)S(1)} %combine.1), channel_id=1, source_target_pairs={{0,96},{1,97},{2,98},{3,99},{4,100},{5,101},{6,102},{7,103},{8,104... | collective-permute-start | bytes 221192 | tf_op jit(solution)/shard_map/ppermute | solution.py:23
  10.4 6.4 %collective-permute-start.2 = (bf16[2,144,128]{2,1,0:T(8,128)(2,1)S(1)}, bf16[2,144,128]{2,1,0:T(8,128)(2,1)S(1)}, u32[]{:S(2)}, u32[]{:S(2)}) collective-permute-start(bf16[2,144,128]{2,1,0:T(8,128)(2,1)S(1)} %combine.1), channel_id=1, source_target_pairs={{0,64},{1,65},{2,66},{3,67},{4,68},{5,69},{6,70},{7,71},{8,72},{9,... | collective-permute-start | bytes 221192 | tf_op jit(solution)/shard_map/ppermute | solution.py:23
  11.2 6.3 %collective-permute-start.3 = (bf16[2,144,128]{2,1,0:T(8,128)(2,1)S(1)}, bf16[2,144,128]{2,1,0:T(8,128)(2,1)S(1)}, u32[]{:S(2)}, u32[]{:S(2)}) collective-permute-start(bf16[2,144,128]{2,1,0:T(8,128)(2,1)S(1)} %combine.1), channel_id=1, source_target_pairs={{0,32},{1,33},{2,34},{3,35},{4,36},{5,37},{6,38},{7,39},{8,40},{9,... | collective-permute-start | bytes 221192 | tf_op jit(solution)/shard_map/ppermute | solution.py:23
  23.1 23.6 %copy-start.3 = (bf16[6144]{0:T(1024)(128)(2,1)S(1)}, bf16[6144]{0:T(1024)(128)(2,1)}, u32[]{:S(2)}) copy-start(bf16[6144]{0:T(1024)(128)(2,1)} %param.17) | copy-start | bytes 36868
  23.1 9.2 %collective-permute-start.4 = (bf16[32,6144]{1,0:T(8,128)(2,1)}, bf16[32,6144]{1,0:T(8,128)(2,1)S(1)}, u32[]{:S(2)}, u32[]{:S(2)}) collective-permute-start(bf16[32,6144]{1,0:T(8,128)(2,1)} %get-tuple-element.45), channel_id=1, source_target_pairs={{0,1},{1,2},{2,3},{3,0},{4,5},{5,6},{6,7},{7,4},{8,9},{9,10},{10,1... | collective-permute-start | bytes 1179656 | tf_op jit(solution)/shard_map/ppermute | solution.py:23
  24.6 13.1 %collective-permute-start.5 = (bf16[32,6144]{1,0:T(8,128)(2,1)}, bf16[32,6144]{1,0:T(8,128)(2,1)S(1)}, u32[]{:S(2)}, u32[]{:S(2)}) collective-permute-start(bf16[32,6144]{1,0:T(8,128)(2,1)} %get-tuple-element.46), channel_id=1, source_target_pairs={{0,2},{1,3},{2,0},{3,1},{4,6},{5,7},{6,4},{7,5},{8,10},{9,11},{10,... | collective-permute-start | bytes 1179656 | tf_op jit(solution)/shard_map/ppermute | solution.py:23
  27.5 10.2 %collective-permute-start.6 = (bf16[32,6144]{1,0:T(8,128)(2,1)}, bf16[32,6144]{1,0:T(8,128)(2,1)S(1)}, u32[]{:S(2)}, u32[]{:S(2)}) collective-permute-start(bf16[32,6144]{1,0:T(8,128)(2,1)} %get-tuple-element.47), channel_id=1, source_target_pairs={{0,3},{1,0},{2,1},{3,2},{4,7},{5,4},{6,5},{7,6},{8,11},{9,8},{10,9... | collective-permute-start | bytes 1179656 | tf_op jit(solution)/shard_map/ppermute | solution.py:23
  39.2 7.5 %collective-permute-start.7 = (bf16[8,6144]{1,0:T(8,128)(2,1)S(1)}, bf16[8,6144]{1,0:T(8,128)(2,1)S(1)}, u32[]{:S(2)}, u32[]{:S(2)}) collective-permute-start(bf16[8,6144]{1,0:T(8,128)(2,1)S(1)} %get-tuple-element.50), channel_id=1, source_target_pairs={{0,4},{1,5},{2,6},{3,7},{4,8},{5,9},{6,10},{7,11},{8,12},{9,13},{1... | collective-permute-start | bytes 294920 | tf_op jit(solution)/shard_map/ppermute | solution.py:23
  41.2 7.2 %collective-permute-start.8 = (bf16[8,6144]{1,0:T(8,128)(2,1)S(1)}, bf16[8,6144]{1,0:T(8,128)(2,1)S(1)}, u32[]{:S(2)}, u32[]{:S(2)}) collective-permute-start(bf16[8,6144]{1,0:T(8,128)(2,1)S(1)} %get-tuple-element.51), channel_id=1, source_target_pairs={{0,8},{1,9},{2,10},{3,11},{4,12},{5,13},{6,14},{7,15},{8,0},{9,1},... | collective-permute-start | bytes 294920 | tf_op jit(solution)/shard_map/ppermute | solution.py:23
  44.7 4.6 %collective-permute-start.9 = (bf16[8,6144]{1,0:T(8,128)(2,1)S(1)}, bf16[8,6144]{1,0:T(8,128)(2,1)S(1)}, u32[]{:S(2)}, u32[]{:S(2)}) collective-permute-start(bf16[8,6144]{1,0:T(8,128)(2,1)S(1)} %get-tuple-element.52), channel_id=1, source_target_pairs={{0,12},{1,13},{2,14},{3,15},{4,0},{5,1},{6,2},{7,3},{8,4},{9,5},{1... | collective-permute-start | bytes 294920 | tf_op jit(solution)/shard_map/ppermute | solution.py:23
  50.1 4.7 %collective-permute-start.10 = (bf16[8,6144]{1,0:T(8,128)(2,1)S(1)}, bf16[8,6144]{1,0:T(8,128)(2,1)S(1)}, u32[]{:S(2)}, u32[]{:S(2)}) collective-permute-start(bf16[8,6144]{1,0:T(8,128)(2,1)S(1)} %norm.1.a), channel_id=1, source_target_pairs={{0,96},{1,97},{2,98},{3,99},{4,100},{5,101},{6,102},{7,103},{8,104... | collective-permute-start | bytes 294920 | tf_op jit(solution)/shard_map/ppermute | solution.py:23
  50.7 6.1 %collective-permute-start.11 = (bf16[8,6144]{1,0:T(8,128)(2,1)S(1)}, bf16[8,6144]{1,0:T(8,128)(2,1)S(1)}, u32[]{:S(2)}, u32[]{:S(2)}) collective-permute-start(bf16[8,6144]{1,0:T(8,128)(2,1)S(1)} %norm.1.a), channel_id=1, source_target_pairs={{0,64},{1,65},{2,66},{3,67},{4,68},{5,69},{6,70},{7,71},{8,72},{9,... | collective-permute-start | bytes 294920 | tf_op jit(solution)/shard_map/ppermute | solution.py:23
  51.8 6.1 %collective-permute-start.12 = (bf16[8,6144]{1,0:T(8,128)(2,1)S(1)}, bf16[8,6144]{1,0:T(8,128)(2,1)S(1)}, u32[]{:S(2)}, u32[]{:S(2)}) collective-permute-start(bf16[8,6144]{1,0:T(8,128)(2,1)S(1)} %norm.1.a), channel_id=1, source_target_pairs={{0,32},{1,33},{2,34},{3,35},{4,36},{5,37},{6,38},{7,39},{8,40},{9,... | collective-permute-start | bytes 294920 | tf_op jit(solution)/shard_map/ppermute | solution.py:23
  58.5 16.6 %copy-start.4 = (s32[1024]{0:T(1024)S(1)}, s32[1024]{0:T(1024)}, u32[]{:S(2)}) copy-start(s32[1024]{0:T(1024)} %param.19) | copy-start | bytes 12292
  58.5 11.9 %collective-permute-start.13 = (bf16[32,6144]{1,0:T(8,128)(2,1)S(1)}, bf16[32,6144]{1,0:T(8,128)(2,1)S(1)}, u32[]{:S(2)}, u32[]{:S(2)}) collective-permute-start(bf16[32,6144]{1,0:T(8,128)(2,1)S(1)} %stack_x.1.a), channel_id=1, source_target_pairs={{0,3},{1,0},{2,1},{3,2},{4,7},{5,4},{6,5},{7,6},{8,11},{9,8},{10,9... | collective-permute-start | bytes 1179656 | tf_op jit(solution)/shard_map/ppermute | solution.py:23
  60.9 9.5 %collective-permute-start.14 = (bf16[32,6144]{1,0:T(8,128)(2,1)S(1)}, bf16[32,6144]{1,0:T(8,128)(2,1)S(1)}, u32[]{:S(2)}, u32[]{:S(2)}) collective-permute-start(bf16[32,6144]{1,0:T(8,128)(2,1)S(1)} %stack_x.1.a), channel_id=1, source_target_pairs={{0,2},{1,3},{2,0},{3,1},{4,6},{5,7},{6,4},{7,5},{8,10},{9,11},{10,... | collective-permute-start | bytes 1179656 | tf_op jit(solution)/shard_map/ppermute | solution.py:23
  62.3 12.1 %collective-permute-start.15 = (bf16[32,6144]{1,0:T(8,128)(2,1)S(1)}, bf16[32,6144]{1,0:T(8,128)(2,1)S(1)}, u32[]{:S(2)}, u32[]{:S(2)}) collective-permute-start(bf16[32,6144]{1,0:T(8,128)(2,1)S(1)} %stack_x.1.a), channel_id=1, source_target_pairs={{0,1},{1,2},{2,3},{3,0},{4,5},{5,6},{6,7},{7,4},{8,9},{9,10},{10,1... | collective-permute-start | bytes 1179656 | tf_op jit(solution)/shard_map/ppermute | solution.py:23
  75.0 5.0 %collective-permute-start.16 = (bf16[128,6144]{1,0:T(8,128)(2,1)S(1)}, bf16[128,6144]{1,0:T(8,128)(2,1)S(1)}, u32[]{:S(2)}, u32[]{:S(2)}) collective-permute-start(bf16[128,6144]{1,0:T(8,128)(2,1)S(1)} %stack_p.1.rows_mine), channel_id=1, source_target_pairs={{0,16},{1,17},{2,18},{3,19},{4,20},{5,21},{6,22},{7,23},{8,24},{9,... | collective-permute-start | bytes 4718600 | tf_op jit(solution)/shard_map/ppermute | solution.py:23
  80.1 13.3 %collective-permute-start.19 = (bf16[64,6144]{1,0:T(8,128)(2,1)S(1)}, bf16[64,6144]{1,0:T(8,128)(2,1)S(1)}, u32[]{:S(2)}, u32[]{:S(2)}) collective-permute-start(bf16[64,6144]{1,0:T(8,128)(2,1)S(1)} %get-tuple-element.56), channel_id=1, source_target_pairs={{0,4},{1,5},{2,6},{3,7},{4,8},{5,9},{6,10},{7,11},{8,12},{9,13},{1... | collective-permute-start | bytes 2359304 | tf_op jit(solution)/shard_map/ppermute | solution.py:23
  80.7 12.7 %collective-permute-start.20 = (bf16[64,6144]{1,0:T(8,128)(2,1)S(1)}, bf16[64,6144]{1,0:T(8,128)(2,1)S(1)}, u32[]{:S(2)}, u32[]{:S(2)}) collective-permute-start(bf16[64,6144]{1,0:T(8,128)(2,1)S(1)} %get-tuple-element.57), channel_id=1, source_target_pairs={{0,12},{1,13},{2,14},{3,15},{4,0},{5,1},{6,2},{7,3},{8,4},{9,5},{1... | collective-permute-start | bytes 2359304 | tf_op jit(solution)/shard_map/ppermute | solution.py:23
  85.2 19.4 %collective-permute-start.17 = (bf16[64,6144]{1,0:T(8,128)(2,1)S(1)}, bf16[64,6144]{1,0:T(8,128)(2,1)S(1)}, u32[]{:S(2)}, u32[]{:S(2)}) collective-permute-start(bf16[64,6144]{1,0:T(8,128)(2,1)S(1)} %get-tuple-element.56), channel_id=1, source_target_pairs={{0,12},{1,13},{2,14},{3,15},{4,0},{5,1},{6,2},{7,3},{8,4},{9,5},{1... | collective-permute-start | bytes 2359304 | tf_op jit(solution)/shard_map/ppermute | solution.py:23
  86.3 18.3 %collective-permute-start.18 = (bf16[64,6144]{1,0:T(8,128)(2,1)S(1)}, bf16[64,6144]{1,0:T(8,128)(2,1)S(1)}, u32[]{:S(2)}, u32[]{:S(2)}) collective-permute-start(bf16[64,6144]{1,0:T(8,128)(2,1)S(1)} %get-tuple-element.57), channel_id=1, source_target_pairs={{0,4},{1,5},{2,6},{3,7},{4,8},{5,9},{6,10},{7,11},{8,12},{9,13},{1... | collective-permute-start | bytes 2359304 | tf_op jit(solution)/shard_map/ppermute | solution.py:23
  93.5 8.1 %collective-permute-start.21 = (bf16[128,6144]{1,0:T(8,128)(2,1)S(1)}, bf16[128,6144]{1,0:T(8,128)(2,1)S(1)}, u32[]{:S(2)}, u32[]{:S(2)}) collective-permute-start(bf16[128,6144]{1,0:T(8,128)(2,1)S(1)} %constant_dynamic-update-slice_fusion.rows_mine), channel_id=1, source_target_pairs={{0,16},{1,17},{2,18},{3,19},{4,20},{5,21},{6,22},{7,23},{8,24},{9,... | collective-permute-start | bytes 4718600 | tf_op jit(solution)/shard_map/ppermute | solution.py:23
  96.5 13.7 %collective-permute-start.22 = (bf16[64,6144]{1,0:T(8,128)(2,1)S(1)}, bf16[64,6144]{1,0:T(8,128)(2,1)S(1)}, u32[]{:S(2)}, u32[]{:S(2)}) collective-permute-start(bf16[64,6144]{1,0:T(8,128)(2,1)S(1)} %collective-permute-done.19), channel_id=1, source_target_pairs={{0,4},{1,5},{2,6},{3,7},{4,8},{5,9},{6,10},{7,11},{8,12},{9,13},{1... | collective-permute-start | bytes 2359304 | tf_op jit(solution)/shard_map/ppermute | solution.py:23
  96.9 13.3 %collective-permute-start.23 = (bf16[64,6144]{1,0:T(8,128)(2,1)S(1)}, bf16[64,6144]{1,0:T(8,128)(2,1)S(1)}, u32[]{:S(2)}, u32[]{:S(2)}) collective-permute-start(bf16[64,6144]{1,0:T(8,128)(2,1)S(1)} %collective-permute-done.20), channel_id=1, source_target_pairs={{0,12},{1,13},{2,14},{3,15},{4,0},{5,1},{6,2},{7,3},{8,4},{9,5},{1... | collective-permute-start | bytes 2359304 | tf_op jit(solution)/shard_map/ppermute | solution.py:23
  104.7 7.5 %collective-permute-start.24 = (bf16[128,6144]{1,0:T(8,128)(2,1)S(1)}, bf16[128,6144]{1,0:T(8,128)(2,1)S(1)}, u32[]{:S(2)}, u32[]{:S(2)}) collective-permute-start(bf16[128,6144]{1,0:T(8,128)(2,1)S(1)} %constant_dynamic-update-slice_fusion.2.rows_mine), channel_id=1, source_target_pairs={{0,16},{1,17},{2,18},{3,19},{4,20},{5,21},{6,22},{7,23},{8,24},{9,... | collective-permute-start | bytes 4718600 | tf_op jit(solution)/shard_map/ppermute | solution.py:23
  110.4 3.7 %collective-permute-start.25 = (bf16[128,6144]{1,0:T(8,128)(2,1)S(1)}, bf16[128,6144]{1,0:T(8,128)(2,1)S(1)}, u32[]{:S(2)}, u32[]{:S(2)}) collective-permute-start(bf16[128,6144]{1,0:T(8,128)(2,1)S(1)} %constant_dynamic-update-slice_fusion.4.rows_mine), channel_id=1, source_target_pairs={{0,16},{1,17},{2,18},{3,19},{4,20},{5,21},{6,22},{7,23},{8,24},{9,... | collective-permute-start | bytes 4718600 | tf_op jit(solution)/shard_map/ppermute | solution.py:23
  115.9 26.5 %copy-start.1 = (f32[128,2]{0,1:T(2,128)S(1)}, f32[128,2]{0,1:T(2,128)}, u32[]{:S(2)}) copy-start(f32[128,2]{0,1:T(2,128)} %param.11) | copy-start | bytes 3076

commit v11 on v10

--- a/solution.py
+++ b/solution.py
@@ -158,18 +158,25 @@
         out[h] = jnp.where(at[1] == 1, part[size : size + 1] * state + part[:size], state)
 
 
-def project_kernel(at, heads, weight, own, one, two, three, rolled):
-    @pl.when(pl.program_id(0) == 0)
-    def _():
-        for s in range(4):
-            start = pl.multiple_of((at[4] + s) % 4 * 32, 32)
-            rolled[pl.ds(32 * s, 32), :] = heads[pl.ds(start, 32), :]
-
-    out = jnp.dot(rolled[...], weight[...], preferred_element_type=F32)
-    own[...] = out[:32]
-    one[...] = out[32:64].astype(BF16)
-    two[...] = out[64:96].astype(BF16)
-    three[...] = out[96:].astype(BF16)
+def project_kernel(at, heads, weight, own, one, two, three, held, rolled, arrived):
+    chunks = arrived.shape[0]
+    wide = weight.shape[1] // chunks
+    copies = []
+    for n in range(chunks):
+        part = pl.ds(n * wide, wide)
+        copies.append(pltpu.make_async_copy(weight.at[:, part], held.at[:, part], arrived.at[n]))
+        copies[-1].start()
+    for s in range(4):
+        start = pl.multiple_of((at[4] + s) % 4 * 32, 32)
+        rolled[pl.ds(32 * s, 32), :] = heads[pl.ds(start, 32), :]
+    for n in range(chunks):
+        part = pl.ds(n * wide, wide)
+        copies[n].wait()
+        out = jnp.dot(rolled[...], held[:, part], preferred_element_type=F32)
+        own[:, part] = out[:32]
+        one[:, part] = out[32:64].astype(BF16)
+        two[:, part] = out[64:96].astype(BF16)
+        three[:, part] = out[96:].astype(BF16)
 
 
 def partial_kernel(at, one, two, three, own, mine, first, second, third, total):
@@ -380,19 +387,17 @@
     flat_heads = normed_heads.astype(BF16).reshape(rows_here, heads_here * head_size)
 
     inner = flat_heads.shape[1]
-    wide = width // 3 if width % 384 == 0 else width
-    share = pl.BlockSpec((32, wide), lambda n: (0, n))
+    chunks = 4 if width % 512 == 0 else 1
     own, *sent = pl.pallas_call(
         project_kernel,
-        out_shape=[in_hbm((32, width), F32)] + [in_hbm((32, width), BF16)] * 3,
-        grid=(width // wide,),
-        in_specs=[
-            SCALARS,
-            pl.BlockSpec((rows_here, inner), lambda n: (0, 0)),
-            pl.BlockSpec((inner, wide), lambda n: (0, n)),
+        out_shape=[in_hbm((32, width), F32)] + [on_chip((32, width), BF16)] * 3,
+        in_specs=[SCALARS, WHOLE, pl.BlockSpec(memory_space=pltpu.HBM)],
+        out_specs=[WHOLE] * 4,
+        scratch_shapes=[
+            pltpu.VMEM(out_weight.shape, BF16),
+            pltpu.VMEM(flat_heads.shape, BF16),
+            pltpu.SemaphoreType.DMA((chunks,)),
         ],
-        out_specs=[share] * 4,
-        scratch_shapes=[pltpu.VMEM((rows_here, inner), BF16)],
         compiler_params=pltpu.CompilerParams(vmem_limit_bytes=12 * 1024 * 1024),
         cost_estimate=pl.CostEstimate(
             flops=2 * rows_here * inner * width,

time: 143 us -> 142 us (level)
  no operation moved by 1% of the time
where the time goes in v11:
time: 142 us; the launch traced here: 141 us
  waiting for transfers between devices  41.1 us (29%)
  starting transfers between devices  33.2 us (23%)
  Pallas kernels  26.4 us (19%)
  blocking collectives  21.8 us (15%)
  matrix products  15.3 us (11%)
  local copies, waits for them, and re-layouts  2.15 us (2%)
    ppermute x26, waiting for transfers between devices, move(): return lax.ppermute(array, ALL, pairs)  41.1 us
    ppermute x26, starting transfers between devices, move(): return lax.ppermute(array, ALL, pairs)  33.2 us
    all_to_all x1, blocking collectives, shards(): came = lax.all_to_all(sent, ('z', 'y'), 0, 0)  13.6 us
    dot_general x7, matrix products, dot(): return jnp.dot(rows, vocab, preferred_element_type=F32)  12.5 us
    pallas_call x13, Pallas kernels, local(): pl.pallas_call(kernel, out_shape=outs, in_specs=[SCALARS] + [WHOLE] * len...  11.6 us
    all_to_all x1, blocking collectives, shards(): came = lax.all_to_all(sent, ('x', 'core'), 0, 0)  8.2 us
    pallas_call x2, Pallas kernels, heads(): pl.pallas_call(functools.partial(heads_kernel, count), out_shape=[jax.Sha...  6.58 us
    pallas_call x1, Pallas kernels, shards(): pl.pallas_call(load_kernel, out_shape=on_chip(vocab_weight.shape, BF16),...  4.59 us
  transfers between devices with their start and end apart: 26, of which 14 were waited for; matrix products, arithmetic and copies ran while one was open for 10% of the time, Pallas kernels for 7%

profile of v11, /device:TPU:0, one launch (start us, length us, event | category | flops | bytes accessed | tf_op | source)
XLA Modules:
  0.0 141.5 jit_solution(4290680452060372030)
XLA Ops:
  1.1 3.7 %heads.2 = (bf16[128,256]{1,0:T(8,128)(2,1)S(1)}, bf16[128,256]{1,0:T(8,128)(2,1)S(1)}) custom-call(bf16[128,6144]{1,0:T(8,128)(2,1)} %tokens.2, bf16[6144,256]{1,0:T(8,128)(2,1)} %refs_0_.2, bf16[6144,256]{1,0:T(8,128)(2,1)} %refs_1_.1), custom_call_target="tpu_custom_call" | custom-call | flops 805306368 | bytes 7864320 | tf_op jit(solution)/shard_map/heads/pallas_call | solution.py:118
  7.5 2.9 %collective-permute-start.1 = (bf16[2,144,128]{2,1,0:T(8,128)(2,1)S(1)}, bf16[2,144,128]{2,1,0:T(8,128)(2,1)S(1)}, u32[]{:S(2)}, u32[]{:S(2)}) collective-permute-start(bf16[2,144,128]{2,1,0:T(8,128)(2,1)S(1)} %combine.1), channel_id=1, source_target_pairs={{0,96},{1,97},{2,98},{3,99},{4,100},{5,101},{6,102},{7,103},{8,104... | collective-permute-start | bytes 221192 | tf_op jit(solution)/shard_map/ppermute | solution.py:23
  12.1 2.8 %heads.3 = bf16[128,256]{1,0:T(8,128)(2,1)S(1)} custom-call(bf16[128,6144]{1,0:T(8,128)(2,1)} %tokens.2, bf16[6144,256]{1,0:T(8,128)(2,1)} %refs_0_.3), custom_call_target="tpu_custom_call" | custom-call | flops 402653184 | bytes 4718592 | tf_op jit(solution)/shard_map/heads/pallas_call | solution.py:118
  15.3 1.5 %collective-permute-done.2.two = bf16[2,144,128]{2,1,0:T(8,128)(2,1)S(1)} collective-permute-done((bf16[2,144,128]{2,1,0:T(8,128)(2,1)S(1)}, bf16[2,144,128]{2,1,0:T(8,128)(2,1)S(1)}, u32[]{:S(2)}, u32[]{:S(2)}) %collective-permute-start.2) | collective-permute-done | bytes 73760 | tf_op jit(solution)/shard_map/ppermute | solution.py:23
  18.6 3.7 %project.1 = (f32[32,6144]{1,0:T(8,128)}, bf16[32,6144]{1,0:T(8,128)(2,1)S(1)}, bf16[32,6144]{1,0:T(8,128)(2,1)S(1)}, bf16[32,6144]{1,0:T(8,128)(2,1)S(1)}) custom-call(s32[8]{0:T(128)S(1)} %stack.32.at, bf16[128,256]{1,0:T(8,128)(2,1)S(1)} %copy.26.heads, bf16[256,6144]{1,0:T(8,128)(2,1)} %weight.1), custom_call_target="tpu_custom_call" | custom-call | flops 402653184 | bytes 4718592 | tf_op jit(solution)/shard_map/project/pallas_call | solution.py:391
  22.3 1.6 %collective-permute-start.4 = (bf16[32,6144]{1,0:T(8,128)(2,1)S(1)}, bf16[32,6144]{1,0:T(8,128)(2,1)S(1)}, u32[]{:S(2)}, u32[]{:S(2)}) collective-permute-start(bf16[32,6144]{1,0:T(8,128)(2,1)S(1)} %get-tuple-element.45), channel_id=1, source_target_pairs={{0,1},{1,2},{2,3},{3,0},{4,5},{5,6},{6,7},{7,4},{8,9},{9,10},{10,1... | collective-permute-start | bytes 1179656 | tf_op jit(solution)/shard_map/ppermute | solution.py:23
  24.0 2.9 %collective-permute-start.5 = (bf16[32,6144]{1,0:T(8,128)(2,1)S(1)}, bf16[32,6144]{1,0:T(8,128)(2,1)S(1)}, u32[]{:S(2)}, u32[]{:S(2)}) collective-permute-start(bf16[32,6144]{1,0:T(8,128)(2,1)S(1)} %get-tuple-element.46), channel_id=1, source_target_pairs={{0,2},{1,3},{2,0},{3,1},{4,6},{5,7},{6,4},{7,5},{8,10},{9,11},{10,... | collective-permute-start | bytes 1179656 | tf_op jit(solution)/shard_map/ppermute | solution.py:23
  28.2 3.2 %collective-permute-done.4.one = bf16[32,6144]{1,0:T(8,128)(2,1)S(1)} collective-permute-done((bf16[32,6144]{1,0:T(8,128)(2,1)S(1)}, bf16[32,6144]{1,0:T(8,128)(2,1)S(1)}, u32[]{:S(2)}, u32[]{:S(2)}) %collective-permute-start.4) | collective-permute-done | bytes 393248 | tf_op jit(solution)/shard_map/ppermute | solution.py:23
  31.4 5.5 %collective-permute-done.5.two = bf16[32,6144]{1,0:T(8,128)(2,1)S(1)} collective-permute-done((bf16[32,6144]{1,0:T(8,128)(2,1)S(1)}, bf16[32,6144]{1,0:T(8,128)(2,1)S(1)}, u32[]{:S(2)}, u32[]{:S(2)}) %collective-permute-start.5) | collective-permute-done | bytes 393248 | tf_op jit(solution)/shard_map/ppermute | solution.py:23
  38.3 2.0 %collective-permute-start.7 = (bf16[8,6144]{1,0:T(8,128)(2,1)S(1)}, bf16[8,6144]{1,0:T(8,128)(2,1)S(1)}, u32[]{:S(2)}, u32[]{:S(2)}) collective-permute-start(bf16[8,6144]{1,0:T(8,128)(2,1)S(1)} %get-tuple-element.50), channel_id=1, source_target_pairs={{0,4},{1,5},{2,6},{3,7},{4,8},{5,9},{6,10},{7,11},{8,12},{9,13},{1... | collective-permute-start | bytes 294920 | tf_op jit(solution)/shard_map/ppermute | solution.py:23
  40.3 3.6 %collective-permute-start.8 = (bf16[8,6144]{1,0:T(8,128)(2,1)S(1)}, bf16[8,6144]{1,0:T(8,128)(2,1)S(1)}, u32[]{:S(2)}, u32[]{:S(2)}) collective-permute-start(bf16[8,6144]{1,0:T(8,128)(2,1)S(1)} %get-tuple-element.51), channel_id=1, source_target_pairs={{0,8},{1,9},{2,10},{3,11},{4,12},{5,13},{6,14},{7,15},{8,0},{9,1},... | collective-permute-start | bytes 294920 | tf_op jit(solution)/shard_map/ppermute | solution.py:23
  45.8 1.7 %collective-permute-done.8.two = bf16[8,6144]{1,0:T(8,128)(2,1)S(1)} collective-permute-done((bf16[8,6144]{1,0:T(8,128)(2,1)S(1)}, bf16[8,6144]{1,0:T(8,128)(2,1)S(1)}, u32[]{:S(2)}, u32[]{:S(2)}) %collective-permute-start.8) | collective-permute-done | bytes 98336 | tf_op jit(solution)/shard_map/ppermute | solution.py:23
  51.7 2.2 %collective-permute-done.10.b = bf16[8,6144]{1,0:T(8,128)(2,1)S(1)} collective-permute-done((bf16[8,6144]{1,0:T(8,128)(2,1)S(1)}, bf16[8,6144]{1,0:T(8,128)(2,1)S(1)}, u32[]{:S(2)}, u32[]{:S(2)}) %collective-permute-start.10) | collective-permute-done | bytes 98336 | tf_op jit(solution)/shard_map/ppermute | solution.py:23
  53.9 2.1 %collective-permute-done.11.c = bf16[8,6144]{1,0:T(8,128)(2,1)S(1)} collective-permute-done((bf16[8,6144]{1,0:T(8,128)(2,1)S(1)}, bf16[8,6144]{1,0:T(8,128)(2,1)S(1)}, u32[]{:S(2)}, u32[]{:S(2)}) %collective-permute-start.11) | collective-permute-done | bytes 98336 | tf_op jit(solution)/shard_map/ppermute | solution.py:23
  57.6 2.4 %collective-permute-start.13 = (bf16[32,6144]{1,0:T(8,128)(2,1)S(1)}, bf16[32,6144]{1,0:T(8,128)(2,1)S(1)}, u32[]{:S(2)}, u32[]{:S(2)}) collective-permute-start(bf16[32,6144]{1,0:T(8,128)(2,1)S(1)} %stack_x.1.a), channel_id=1, source_target_pairs={{0,3},{1,0},{2,1},{3,2},{4,7},{5,4},{6,5},{7,6},{8,11},{9,8},{10,9... | collective-permute-start | bytes 1179656 | tf_op jit(solution)/shard_map/ppermute | solution.py:23
  62.0 7.6 %collective-permute-done.13.b = bf16[32,6144]{1,0:T(8,128)(2,1)S(1)} collective-permute-done((bf16[32,6144]{1,0:T(8,128)(2,1)S(1)}, bf16[32,6144]{1,0:T(8,128)(2,1)S(1)}, u32[]{:S(2)}, u32[]{:S(2)}) %collective-permute-start.13) | collective-permute-done | bytes 393248 | tf_op jit(solution)/shard_map/ppermute | solution.py:23
  69.5 3.9 %collective-permute-done.15.d = bf16[32,6144]{1,0:T(8,128)(2,1)S(1)} collective-permute-done((bf16[32,6144]{1,0:T(8,128)(2,1)S(1)}, bf16[32,6144]{1,0:T(8,128)(2,1)S(1)}, u32[]{:S(2)}, u32[]{:S(2)}) %collective-permute-start.15) | collective-permute-done | bytes 393248 | tf_op jit(solution)/shard_map/ppermute | solution.py:23
  74.5 4.6 %load.1 = bf16[6144,1024]{1,0:T(8,128)(2,1)S(1)} custom-call(bf16[6144,1024]{1,0:T(8,128)(2,1)} %source), custom_call_target="tpu_custom_call" | custom-call | bytes 25165824 | tf_op jit(solution)/shard_map/load/pallas_call | solution.py:437
  79.8 2.7 %collective-permute-start.20 = (bf16[64,6144]{1,0:T(8,128)(2,1)S(1)}, bf16[64,6144]{1,0:T(8,128)(2,1)S(1)}, u32[]{:S(2)}, u32[]{:S(2)}) collective-permute-start(bf16[64,6144]{1,0:T(8,128)(2,1)S(1)} %get-tuple-element.57), channel_id=1, source_target_pairs={{0,12},{1,13},{2,14},{3,15},{4,0},{5,1},{6,2},{7,3},{8,4},{9,5},{1... | collective-permute-start | bytes 2359304 | tf_op jit(solution)/shard_map/ppermute | solution.py:23
  82.5 1.8 %fusion.24.mine = f32[128,1024]{1,0:T(8,128)S(1)} fusion(bf16[128,6144]{1,0:T(8,128)(2,1)S(1)} %stack_p.1.rows_mine, bf16[6144,1024]{1,0:T(8,128)(2,1)S(1)} %load.1), kind=kOutput, calls=%fused_computation.39 | convolution fusion | flops 1610612736 | bytes 14680064 | tf_op jit(solution)/shard_map/dot_general | solution.py:456
  86.4 6.1 %collective-permute-done.19 = bf16[64,6144]{1,0:T(8,128)(2,1)S(1)} collective-permute-done((bf16[64,6144]{1,0:T(8,128)(2,1)S(1)}, bf16[64,6144]{1,0:T(8,128)(2,1)S(1)}, u32[]{:S(2)}, u32[]{:S(2)}) %collective-permute-start.19) | collective-permute-done | bytes 786464 | tf_op jit(solution)/shard_map/ppermute | solution.py:23
  92.7 1.8 %fusion.25.theirs = f32[128,1024]{1,0:T(8,128)S(1)} fusion(bf16[128,6144]{1,0:T(8,128)(2,1)S(1)} %collective-permute-done.16.rows_theirs, bf16[6144,1024]{1,0:T(8,128)(2,1)S(1)} %load.1), kind=kOutput, calls=%fused_computation.40 | convolution fusion | flops 1610612736 | bytes 14680064 | tf_op jit(solution)/shard_map/dot_general | solution.py:461
  96.0 2.9 %collective-permute-start.23 = (bf16[64,6144]{1,0:T(8,128)(2,1)S(1)}, bf16[64,6144]{1,0:T(8,128)(2,1)S(1)}, u32[]{:S(2)}, u32[]{:S(2)}) collective-permute-start(bf16[64,6144]{1,0:T(8,128)(2,1)S(1)} %collective-permute-done.20), channel_id=1, source_target_pairs={{0,12},{1,13},{2,14},{3,15},{4,0},{5,1},{6,2},{7,3},{8,4},{9,5},{1... | collective-permute-start | bytes 2359304 | tf_op jit(solution)/shard_map/ppermute | solution.py:23
  98.9 1.8 %fusion.26.mine = f32[128,1024]{1,0:T(8,128)S(1)} fusion(bf16[128,6144]{1,0:T(8,128)(2,1)S(1)} %constant_dynamic-update-slice_fusion.rows_mine, bf16[6144,1024]{1,0:T(8,128)(2,1)S(1)} %load.1), kind=kOutput, calls=%fused_computation.41 | convolution fusion | flops 1610612736 | bytes 14680064 | tf_op jit(solution)/shard_map/dot_general | solution.py:461
  100.7 1.8 %fusion.27.theirs = f32[128,1024]{1,0:T(8,128)S(1)} fusion(bf16[128,6144]{1,0:T(8,128)(2,1)S(1)} %collective-permute-done.21.rows_theirs, bf16[6144,1024]{1,0:T(8,128)(2,1)S(1)} %load.1), kind=kOutput, calls=%fused_computation.42 | convolution fusion | flops 1610612736 | bytes 14680064 | tf_op jit(solution)/shard_map/dot_general | solution.py:461
  104.2 1.8 %fusion.28.mine = f32[128,1024]{1,0:T(8,128)S(1)} fusion(bf16[128,6144]{1,0:T(8,128)(2,1)S(1)} %constant_dynamic-update-slice_fusion.2.rows_mine, bf16[6144,1024]{1,0:T(8,128)(2,1)S(1)} %load.1), kind=kOutput, calls=%fused_computation.43 | convolution fusion | flops 1610612736 | bytes 14680064 | tf_op jit(solution)/shard_map/dot_general | solution.py:461
  106.0 3.4 %collective-permute-done.22 = bf16[64,6144]{1,0:T(8,128)(2,1)S(1)} collective-permute-done((bf16[64,6144]{1,0:T(8,128)(2,1)S(1)}, bf16[64,6144]{1,0:T(8,128)(2,1)S(1)}, u32[]{:S(2)}, u32[]{:S(2)}) %collective-permute-start.22) | collective-permute-done | bytes 786464 | tf_op jit(solution)/shard_map/ppermute | solution.py:23
  109.6 1.8 %fusion.30.mine = f32[128,1024]{1,0:T(8,128)S(1)} fusion(bf16[128,6144]{1,0:T(8,128)(2,1)S(1)} %constant_dynamic-update-slice_fusion.4.rows_mine, bf16[6144,1024]{1,0:T(8,128)(2,1)S(1)} %load.1), kind=kOutput, calls=%fused_computation.45 | convolution fusion | flops 1610612736 | bytes 14680064 | tf_op jit(solution)/shard_map/dot_general | solution.py:461
  111.4 1.8 %fusion.29.theirs = f32[128,1024]{1,0:T(8,128)S(1)} fusion(bf16[128,6144]{1,0:T(8,128)(2,1)S(1)} %collective-permute-done.24.rows_theirs, bf16[6144,1024]{1,0:T(8,128)(2,1)S(1)} %load.1), kind=kOutput, calls=%fused_computation.44 | convolution fusion | flops 1610612736 | bytes 14680064 | tf_op jit(solution)/shard_map/dot_general | solution.py:461
  113.2 1.8 %fusion.31.theirs = f32[128,1024]{1,0:T(8,128)S(1)} fusion(bf16[128,6144]{1,0:T(8,128)(2,1)S(1)} %collective-permute-done.25.rows_theirs, bf16[6144,1024]{1,0:T(8,128)(2,1)S(1)} %load.1), kind=kOutput, calls=%fused_computation.46 | convolution fusion | flops 1610612736 | bytes 14680064 | tf_op jit(solution)/shard_map/dot_general | solution.py:461
  118.0 8.2 %all_to_all.10.found = f32[8,8,128]{2,1,0:T(8,128)S(1)} all-to-all(f32[8,8,128]{2,1,0:T(8,128)S(1)} %place.1), channel_id=1, replica_groups=mesh['x'=4,'core'=2,'z'=4,'y'=4] {'x','core'}, dimensions={0} | all-to-all | bytes 65536 | tf_op jit(solution)/shard_map/all_to_all | solution.py:497
  126.8 13.6 %all_to_all.11.found = f32[16,8,128]{2,1,0:T(8,128)S(1)} all-to-all(f32[16,8,128]{2,1,0:T(8,128)S(1)} %block.1), channel_id=1, replica_groups=mesh['x'=4,'core'=2,'z'=4,'y'=4] {'z','y'}, dimensions={0} | all-to-all | bytes 131072 | tf_op jit(solution)/shard_map/all_to_all | solution.py:499
  (85 shorter events, 32.0 us)
Async XLA Ops:
  0.0 0.7 copy-start
  5.5 1.4 %collective-permute-start = (f32[2,136,128]{2,1,0:T(8,128)S(1)}, f32[2,136,128]{2,1,0:T(8,128)S(1)}, u32[]{:S(2)}, u32[]{:S(2)}) collective-permute-start(f32[2,136,128]{2,1,0:T(8,128)S(1)} %pad_maximum_fusion.mine), channel_id=1, source_target_pairs={{0,16},{1,17},{2,18},{3,19},{4,20},{5,21},{6,22},{7,23},{8,24},{9,... | collective-permute-start | bytes 417800 | tf_op jit(solution)/shard_map/ppermute | solution.py:23
  7.5 10.1 %copy-start.2 = (f32[2,128,128]{2,1,0:T(8,128)S(1)}, f32[2,128,128]{2,1,0:T(8,128)}, u32[]{:S(2)}) copy-start(f32[2,128,128]{2,1,0:T(8,128)} %carried.1) | copy-start | bytes 393220
  7.5 7.7 %collective-permute-start.1 = (bf16[2,144,128]{2,1,0:T(8,128)(2,1)S(1)}, bf16[2,144,128]{2,1,0:T(8,128)(2,1)S(1)}, u32[]{:S(2)}, u32[]{:S(2)}) collective-permute-start(bf16[2,144,128]{2,1,0:T(8,128)(2,1)S(1)} %combine.1), channel_id=1, source_target_pairs={{0,96},{1,97},{2,98},{3,99},{4,100},{5,101},{6,102},{7,103},{8,104... | collective-permute-start | bytes 221192 | tf_op jit(solution)/shard_map/ppermute | solution.py:23
  10.4 6.4 %collective-permute-start.2 = (bf16[2,144,128]{2,1,0:T(8,128)(2,1)S(1)}, bf16[2,144,128]{2,1,0:T(8,128)(2,1)S(1)}, u32[]{:S(2)}, u32[]{:S(2)}) collective-permute-start(bf16[2,144,128]{2,1,0:T(8,128)(2,1)S(1)} %combine.1), channel_id=1, source_target_pairs={{0,64},{1,65},{2,66},{3,67},{4,68},{5,69},{6,70},{7,71},{8,72},{9,... | collective-permute-start | bytes 221192 | tf_op jit(solution)/shard_map/ppermute | solution.py:23
  11.2 6.3 %collective-permute-start.3 = (bf16[2,144,128]{2,1,0:T(8,128)(2,1)S(1)}, bf16[2,144,128]{2,1,0:T(8,128)(2,1)S(1)}, u32[]{:S(2)}, u32[]{:S(2)}) collective-permute-start(bf16[2,144,128]{2,1,0:T(8,128)(2,1)S(1)} %combine.1), channel_id=1, source_target_pairs={{0,32},{1,33},{2,34},{3,35},{4,36},{5,37},{6,38},{7,39},{8,40},{9,... | collective-permute-start | bytes 221192 | tf_op jit(solution)/shard_map/ppermute | solution.py:23
  22.3 23.5 %copy-start.3 = (bf16[6144]{0:T(1024)(128)(2,1)S(1)}, bf16[6144]{0:T(1024)(128)(2,1)}, u32[]{:S(2)}) copy-start(bf16[6144]{0:T(1024)(128)(2,1)} %param.17) | copy-start | bytes 36868
  22.3 9.1 %collective-permute-start.4 = (bf16[32,6144]{1,0:T(8,128)(2,1)S(1)}, bf16[32,6144]{1,0:T(8,128)(2,1)S(1)}, u32[]{:S(2)}, u32[]{:S(2)}) collective-permute-start(bf16[32,6144]{1,0:T(8,128)(2,1)S(1)} %get-tuple-element.45), channel_id=1, source_target_pairs={{0,1},{1,2},{2,3},{3,0},{4,5},{5,6},{6,7},{7,4},{8,9},{9,10},{10,1... | collective-permute-start | bytes 1179656 | tf_op jit(solution)/shard_map/ppermute | solution.py:23
  24.0 12.9 %collective-permute-start.5 = (bf16[32,6144]{1,0:T(8,128)(2,1)S(1)}, bf16[32,6144]{1,0:T(8,128)(2,1)S(1)}, u32[]{:S(2)}, u32[]{:S(2)}) collective-permute-start(bf16[32,6144]{1,0:T(8,128)(2,1)S(1)} %get-tuple-element.46), channel_id=1, source_target_pairs={{0,2},{1,3},{2,0},{3,1},{4,6},{5,7},{6,4},{7,5},{8,10},{9,11},{10,... | collective-permute-start | bytes 1179656 | tf_op jit(solution)/shard_map/ppermute | solution.py:23
  26.9 10.0 %collective-permute-start.6 = (bf16[32,6144]{1,0:T(8,128)(2,1)S(1)}, bf16[32,6144]{1,0:T(8,128)(2,1)S(1)}, u32[]{:S(2)}, u32[]{:S(2)}) collective-permute-start(bf16[32,6144]{1,0:T(8,128)(2,1)S(1)} %get-tuple-element.47), channel_id=1, source_target_pairs={{0,3},{1,0},{2,1},{3,2},{4,7},{5,4},{6,5},{7,6},{8,11},{9,8},{10,9... | collective-permute-start | bytes 1179656 | tf_op jit(solution)/shard_map/ppermute | solution.py:23
  38.3 7.5 %collective-permute-start.7 = (bf16[8,6144]{1,0:T(8,128)(2,1)S(1)}, bf16[8,6144]{1,0:T(8,128)(2,1)S(1)}, u32[]{:S(2)}, u32[]{:S(2)}) collective-permute-start(bf16[8,6144]{1,0:T(8,128)(2,1)S(1)} %get-tuple-element.50), channel_id=1, source_target_pairs={{0,4},{1,5},{2,6},{3,7},{4,8},{5,9},{6,10},{7,11},{8,12},{9,13},{1... | collective-permute-start | bytes 294920 | tf_op jit(solution)/shard_map/ppermute | solution.py:23
  40.3 7.2 %collective-permute-start.8 = (bf16[8,6144]{1,0:T(8,128)(2,1)S(1)}, bf16[8,6144]{1,0:T(8,128)(2,1)S(1)}, u32[]{:S(2)}, u32[]{:S(2)}) collective-permute-start(bf16[8,6144]{1,0:T(8,128)(2,1)S(1)} %get-tuple-element.51), channel_id=1, source_target_pairs={{0,8},{1,9},{2,10},{3,11},{4,12},{5,13},{6,14},{7,15},{8,0},{9,1},... | collective-permute-start | bytes 294920 | tf_op jit(solution)/shard_map/ppermute | solution.py:23
  43.9 4.6 %collective-permute-start.9 = (bf16[8,6144]{1,0:T(8,128)(2,1)S(1)}, bf16[8,6144]{1,0:T(8,128)(2,1)S(1)}, u32[]{:S(2)}, u32[]{:S(2)}) collective-permute-start(bf16[8,6144]{1,0:T(8,128)(2,1)S(1)} %get-tuple-element.52), channel_id=1, source_target_pairs={{0,12},{1,13},{2,14},{3,15},{4,0},{5,1},{6,2},{7,3},{8,4},{9,5},{1... | collective-permute-start | bytes 294920 | tf_op jit(solution)/shard_map/ppermute | solution.py:23
  49.2 4.7 %collective-permute-start.10 = (bf16[8,6144]{1,0:T(8,128)(2,1)S(1)}, bf16[8,6144]{1,0:T(8,128)(2,1)S(1)}, u32[]{:S(2)}, u32[]{:S(2)}) collective-permute-start(bf16[8,6144]{1,0:T(8,128)(2,1)S(1)} %norm.1.a), channel_id=1, source_target_pairs={{0,96},{1,97},{2,98},{3,99},{4,100},{5,101},{6,102},{7,103},{8,104... | collective-permute-start | bytes 294920 | tf_op jit(solution)/shard_map/ppermute | solution.py:23
  49.8 6.1 %collective-permute-start.11 = (bf16[8,6144]{1,0:T(8,128)(2,1)S(1)}, bf16[8,6144]{1,0:T(8,128)(2,1)S(1)}, u32[]{:S(2)}, u32[]{:S(2)}) collective-permute-start(bf16[8,6144]{1,0:T(8,128)(2,1)S(1)} %norm.1.a), channel_id=1, source_target_pairs={{0,64},{1,65},{2,66},{3,67},{4,68},{5,69},{6,70},{7,71},{8,72},{9,... | collective-permute-start | bytes 294920 | tf_op jit(solution)/shard_map/ppermute | solution.py:23
  50.9 6.1 %collective-permute-start.12 = (bf16[8,6144]{1,0:T(8,128)(2,1)S(1)}, bf16[8,6144]{1,0:T(8,128)(2,1)S(1)}, u32[]{:S(2)}, u32[]{:S(2)}) collective-permute-start(bf16[8,6144]{1,0:T(8,128)(2,1)S(1)} %norm.1.a), channel_id=1, source_target_pairs={{0,32},{1,33},{2,34},{3,35},{4,36},{5,37},{6,38},{7,39},{8,40},{9,... | collective-permute-start | bytes 294920 | tf_op jit(solution)/shard_map/ppermute | solution.py:23
  57.6 16.6 %copy-start.4 = (s32[1024]{0:T(1024)S(1)}, s32[1024]{0:T(1024)}, u32[]{:S(2)}) copy-start(s32[1024]{0:T(1024)} %param.19) | copy-start | bytes 12292
  57.6 11.9 %collective-permute-start.13 = (bf16[32,6144]{1,0:T(8,128)(2,1)S(1)}, bf16[32,6144]{1,0:T(8,128)(2,1)S(1)}, u32[]{:S(2)}, u32[]{:S(2)}) collective-permute-start(bf16[32,6144]{1,0:T(8,128)(2,1)S(1)} %stack_x.1.a), channel_id=1, source_target_pairs={{0,3},{1,0},{2,1},{3,2},{4,7},{5,4},{6,5},{7,6},{8,11},{9,8},{10,9... | collective-permute-start | bytes 1179656 | tf_op jit(solution)/shard_map/ppermute | solution.py:23
  60.0 9.5 %collective-permute-start.14 = (bf16[32,6144]{1,0:T(8,128)(2,1)S(1)}, bf16[32,6144]{1,0:T(8,128)(2,1)S(1)}, u32[]{:S(2)}, u32[]{:S(2)}) collective-permute-start(bf16[32,6144]{1,0:T(8,128)(2,1)S(1)} %stack_x.1.a), channel_id=1, source_target_pairs={{0,2},{1,3},{2,0},{3,1},{4,6},{5,7},{6,4},{7,5},{8,10},{9,11},{10,... | collective-permute-start | bytes 1179656 | tf_op jit(solution)/shard_map/ppermute | solution.py:23
  61.4 12.1 %collective-permute-start.15 = (bf16[32,6144]{1,0:T(8,128)(2,1)S(1)}, bf16[32,6144]{1,0:T(8,128)(2,1)S(1)}, u32[]{:S(2)}, u32[]{:S(2)}) collective-permute-start(bf16[32,6144]{1,0:T(8,128)(2,1)S(1)} %stack_x.1.a), channel_id=1, source_target_pairs={{0,1},{1,2},{2,3},{3,0},{4,5},{5,6},{6,7},{7,4},{8,9},{9,10},{10,1... | collective-permute-start | bytes 1179656 | tf_op jit(solution)/shard_map/ppermute | solution.py:23
  74.1 5.0 %collective-permute-start.16 = (bf16[128,6144]{1,0:T(8,128)(2,1)S(1)}, bf16[128,6144]{1,0:T(8,128)(2,1)S(1)}, u32[]{:S(2)}, u32[]{:S(2)}) collective-permute-start(bf16[128,6144]{1,0:T(8,128)(2,1)S(1)} %stack_p.1.rows_mine), channel_id=1, source_target_pairs={{0,16},{1,17},{2,18},{3,19},{4,20},{5,21},{6,22},{7,23},{8,24},{9,... | collective-permute-start | bytes 4718600 | tf_op jit(solution)/shard_map/ppermute | solution.py:23
  79.2 13.3 %collective-permute-start.19 = (bf16[64,6144]{1,0:T(8,128)(2,1)S(1)}, bf16[64,6144]{1,0:T(8,128)(2,1)S(1)}, u32[]{:S(2)}, u32[]{:S(2)}) collective-permute-start(bf16[64,6144]{1,0:T(8,128)(2,1)S(1)} %get-tuple-element.56), channel_id=1, source_target_pairs={{0,4},{1,5},{2,6},{3,7},{4,8},{5,9},{6,10},{7,11},{8,12},{9,13},{1... | collective-permute-start | bytes 2359304 | tf_op jit(solution)/shard_map/ppermute | solution.py:23
  79.8 12.7 %collective-permute-start.20 = (bf16[64,6144]{1,0:T(8,128)(2,1)S(1)}, bf16[64,6144]{1,0:T(8,128)(2,1)S(1)}, u32[]{:S(2)}, u32[]{:S(2)}) collective-permute-start(bf16[64,6144]{1,0:T(8,128)(2,1)S(1)} %get-tuple-element.57), channel_id=1, source_target_pairs={{0,12},{1,13},{2,14},{3,15},{4,0},{5,1},{6,2},{7,3},{8,4},{9,5},{1... | collective-permute-start | bytes 2359304 | tf_op jit(solution)/shard_map/ppermute | solution.py:23
  84.3 19.4 %collective-permute-start.17 = (bf16[64,6144]{1,0:T(8,128)(2,1)S(1)}, bf16[64,6144]{1,0:T(8,128)(2,1)S(1)}, u32[]{:S(2)}, u32[]{:S(2)}) collective-permute-start(bf16[64,6144]{1,0:T(8,128)(2,1)S(1)} %get-tuple-element.56), channel_id=1, source_target_pairs={{0,12},{1,13},{2,14},{3,15},{4,0},{5,1},{6,2},{7,3},{8,4},{9,5},{1... | collective-permute-start | bytes 2359304 | tf_op jit(solution)/shard_map/ppermute | solution.py:23
  85.4 18.3 %collective-permute-start.18 = (bf16[64,6144]{1,0:T(8,128)(2,1)S(1)}, bf16[64,6144]{1,0:T(8,128)(2,1)S(1)}, u32[]{:S(2)}, u32[]{:S(2)}) collective-permute-start(bf16[64,6144]{1,0:T(8,128)(2,1)S(1)} %get-tuple-element.57), channel_id=1, source_target_pairs={{0,4},{1,5},{2,6},{3,7},{4,8},{5,9},{6,10},{7,11},{8,12},{9,13},{1... | collective-permute-start | bytes 2359304 | tf_op jit(solution)/shard_map/ppermute | solution.py:23
  92.6 8.1 %collective-permute-start.21 = (bf16[128,6144]{1,0:T(8,128)(2,1)S(1)}, bf16[128,6144]{1,0:T(8,128)(2,1)S(1)}, u32[]{:S(2)}, u32[]{:S(2)}) collective-permute-start(bf16[128,6144]{1,0:T(8,128)(2,1)S(1)} %constant_dynamic-update-slice_fusion.rows_mine), channel_id=1, source_target_pairs={{0,16},{1,17},{2,18},{3,19},{4,20},{5,21},{6,22},{7,23},{8,24},{9,... | collective-permute-start | bytes 4718600 | tf_op jit(solution)/shard_map/ppermute | solution.py:23
  95.7 13.7 %collective-permute-start.22 = (bf16[64,6144]{1,0:T(8,128)(2,1)S(1)}, bf16[64,6144]{1,0:T(8,128)(2,1)S(1)}, u32[]{:S(2)}, u32[]{:S(2)}) collective-permute-start(bf16[64,6144]{1,0:T(8,128)(2,1)S(1)} %collective-permute-done.19), channel_id=1, source_target_pairs={{0,4},{1,5},{2,6},{3,7},{4,8},{5,9},{6,10},{7,11},{8,12},{9,13},{1... | collective-permute-start | bytes 2359304 | tf_op jit(solution)/shard_map/ppermute | solution.py:23
  96.0 13.3 %collective-permute-start.23 = (bf16[64,6144]{1,0:T(8,128)(2,1)S(1)}, bf16[64,6144]{1,0:T(8,128)(2,1)S(1)}, u32[]{:S(2)}, u32[]{:S(2)}) collective-permute-start(bf16[64,6144]{1,0:T(8,128)(2,1)S(1)} %collective-permute-done.20), channel_id=1, source_target_pairs={{0,12},{1,13},{2,14},{3,15},{4,0},{5,1},{6,2},{7,3},{8,4},{9,5},{1... | collective-permute-start | bytes 2359304 | tf_op jit(solution)/shard_map/ppermute | solution.py:23
  103.9 7.5 %collective-permute-start.24 = (bf16[128,6144]{1,0:T(8,128)(2,1)S(1)}, bf16[128,6144]{1,0:T(8,128)(2,1)S(1)}, u32[]{:S(2)}, u32[]{:S(2)}) collective-permute-start(bf16[128,6144]{1,0:T(8,128)(2,1)S(1)} %constant_dynamic-update-slice_fusion.2.rows_mine), channel_id=1, source_target_pairs={{0,16},{1,17},{2,18},{3,19},{4,20},{5,21},{6,22},{7,23},{8,24},{9,... | collective-permute-start | bytes 4718600 | tf_op jit(solution)/shard_map/ppermute | solution.py:23
  109.5 3.7 %collective-permute-start.25 = (bf16[128,6144]{1,0:T(8,128)(2,1)S(1)}, bf16[128,6144]{1,0:T(8,128)(2,1)S(1)}, u32[]{:S(2)}, u32[]{:S(2)}) collective-permute-start(bf16[128,6144]{1,0:T(8,128)(2,1)S(1)} %constant_dynamic-update-slice_fusion.4.rows_mine), channel_id=1, source_target_pairs={{0,16},{1,17},{2,18},{3,19},{4,20},{5,21},{6,22},{7,23},{8,24},{9,... | collective-permute-start | bytes 4718600 | tf_op jit(solution)/shard_map/ppermute | solution.py:23
  115.0 26.5 %copy-start.1 = (f32[128,2]{0,1:T(2,128)S(1)}, f32[128,2]{0,1:T(2,128)}, u32[]{:S(2)}) copy-start(f32[128,2]{0,1:T(2,128)} %param.11) | copy-start | bytes 3076

commit v12 on v11

--- a/solution.py
+++ b/solution.py
@@ -448,7 +448,6 @@
     )(leave(source))
     ours = gather(on_x, along_p, scalars, "stack_p")
     theirs = move(ours, other_core)
-    ours, theirs = lax.optimization_barrier((ours, theirs))
     lines = jnp.transpose(targets.reshape(X, CORE, 4, 4, 8), (1, 3, 2, 0, 4)).reshape(8, 128)
     half = ours.shape[0] // 2
     low, high = ours[:half], ours[half:]

time: 142 us -> 136 us (0.958)
  waiting for transfers between devices: 41.1 us -> 36.1 us
    ppermute x26, waiting for transfers between devices: 41.1 us -> 36.1 us  [move(): return lax.ppermute(array, ALL, pairs)]
  transfers between devices with their start and end apart: 26 -> 26, of which waited for: 14 -> 14; matrix products, arithmetic and copies ran while one was open for 10% -> 11% of each run, Pallas kernels for 7% -> 7%
where the time goes in v12:
time: 136 us
  waiting for transfers between devices  36.1 us (27%)
  starting transfers between devices  33.3 us (24%)
  Pallas kernels  26.4 us (19%)
  blocking collectives  21.1 us (16%)
  matrix products  15.3 us (11%)
  local copies, waits for them, and re-layouts  2.18 us (2%)
    ppermute x26, waiting for transfers between devices, move(): return lax.ppermute(array, ALL, pairs)  36.1 us
    ppermute x26, starting transfers between devices, move(): return lax.ppermute(array, ALL, pairs)  33.3 us
    all_to_all x1, blocking collectives, shards(): came = lax.all_to_all(sent, ('z', 'y'), 0, 0)  12.9 us
    dot_general x7, matrix products, dot(): return jnp.dot(rows, vocab, preferred_element_type=F32)  12.5 us
    pallas_call x13, Pallas kernels, local(): pl.pallas_call(kernel, out_shape=outs, in_specs=[SCALARS] + [WHOLE] * len...  11.6 us
    all_to_all x1, blocking collectives, shards(): came = lax.all_to_all(sent, ('x', 'core'), 0, 0)  8.2 us
    pallas_call x2, Pallas kernels, heads(): pl.pallas_call(functools.partial(heads_kernel, count), out_shape=[jax.Sha...  6.58 us
    pallas_call x1, Pallas kernels, shards(): pl.pallas_call(load_kernel, out_shape=on_chip(vocab_weight.shape, BF16),...  4.59 us
  transfers between devices with their start and end apart: 26, of which 14 were waited for; matrix products, arithmetic and copies ran while one was open for 11% of the time, Pallas kernels for 7%

profile of v12, /device:TPU:0, one launch (start us, length us, event | category | flops | bytes accessed | tf_op | source)
XLA Modules:
  0.0 136.0 jit_solution(4156108235138812997)
XLA Ops:
  1.1 3.7 %heads.2 = (bf16[128,256]{1,0:T(8,128)(2,1)S(1)}, bf16[128,256]{1,0:T(8,128)(2,1)S(1)}) custom-call(bf16[128,6144]{1,0:T(8,128)(2,1)} %tokens.2, bf16[6144,256]{1,0:T(8,128)(2,1)} %refs_0_.2, bf16[6144,256]{1,0:T(8,128)(2,1)} %refs_1_.1), custom_call_target="tpu_custom_call" | custom-call | flops 805306368 | bytes 7864320 | tf_op jit(solution)/shard_map/heads/pallas_call | solution.py:118
  7.5 2.9 %collective-permute-start.1 = (bf16[2,144,128]{2,1,0:T(8,128)(2,1)S(1)}, bf16[2,144,128]{2,1,0:T(8,128)(2,1)S(1)}, u32[]{:S(2)}, u32[]{:S(2)}) collective-permute-start(bf16[2,144,128]{2,1,0:T(8,128)(2,1)S(1)} %combine.1), channel_id=1, source_target_pairs={{0,96},{1,97},{2,98},{3,99},{4,100},{5,101},{6,102},{7,103},{8,104... | collective-permute-start | bytes 221192 | tf_op jit(solution)/shard_map/ppermute | solution.py:23
  12.1 2.8 %heads.3 = bf16[128,256]{1,0:T(8,128)(2,1)S(1)} custom-call(bf16[128,6144]{1,0:T(8,128)(2,1)} %tokens.2, bf16[6144,256]{1,0:T(8,128)(2,1)} %refs_0_.3), custom_call_target="tpu_custom_call" | custom-call | flops 402653184 | bytes 4718592 | tf_op jit(solution)/shard_map/heads/pallas_call | solution.py:118
  15.3 1.5 %collective-permute-done.2.two = bf16[2,144,128]{2,1,0:T(8,128)(2,1)S(1)} collective-permute-done((bf16[2,144,128]{2,1,0:T(8,128)(2,1)S(1)}, bf16[2,144,128]{2,1,0:T(8,128)(2,1)S(1)}, u32[]{:S(2)}, u32[]{:S(2)}) %collective-permute-start.2) | collective-permute-done | bytes 73760 | tf_op jit(solution)/shard_map/ppermute | solution.py:23
  18.6 3.7 %project.1 = (f32[32,6144]{1,0:T(8,128)}, bf16[32,6144]{1,0:T(8,128)(2,1)S(1)}, bf16[32,6144]{1,0:T(8,128)(2,1)S(1)}, bf16[32,6144]{1,0:T(8,128)(2,1)S(1)}) custom-call(s32[8]{0:T(128)S(1)} %stack.32.at, bf16[128,256]{1,0:T(8,128)(2,1)S(1)} %copy.26.heads, bf16[256,6144]{1,0:T(8,128)(2,1)} %weight.1), custom_call_target="tpu_custom_call" | custom-call | flops 402653184 | bytes 4718592 | tf_op jit(solution)/shard_map/project/pallas_call | solution.py:391
  22.3 1.6 %collective-permute-start.4 = (bf16[32,6144]{1,0:T(8,128)(2,1)S(1)}, bf16[32,6144]{1,0:T(8,128)(2,1)S(1)}, u32[]{:S(2)}, u32[]{:S(2)}) collective-permute-start(bf16[32,6144]{1,0:T(8,128)(2,1)S(1)} %get-tuple-element.43), channel_id=1, source_target_pairs={{0,1},{1,2},{2,3},{3,0},{4,5},{5,6},{6,7},{7,4},{8,9},{9,10},{10,1... | collective-permute-start | bytes 1179656 | tf_op jit(solution)/shard_map/ppermute | solution.py:23
  24.0 2.9 %collective-permute-start.5 = (bf16[32,6144]{1,0:T(8,128)(2,1)S(1)}, bf16[32,6144]{1,0:T(8,128)(2,1)S(1)}, u32[]{:S(2)}, u32[]{:S(2)}) collective-permute-start(bf16[32,6144]{1,0:T(8,128)(2,1)S(1)} %get-tuple-element.44), channel_id=1, source_target_pairs={{0,2},{1,3},{2,0},{3,1},{4,6},{5,7},{6,4},{7,5},{8,10},{9,11},{10,... | collective-permute-start | bytes 1179656 | tf_op jit(solution)/shard_map/ppermute | solution.py:23
  28.2 3.2 %collective-permute-done.4.one = bf16[32,6144]{1,0:T(8,128)(2,1)S(1)} collective-permute-done((bf16[32,6144]{1,0:T(8,128)(2,1)S(1)}, bf16[32,6144]{1,0:T(8,128)(2,1)S(1)}, u32[]{:S(2)}, u32[]{:S(2)}) %collective-permute-start.4) | collective-permute-done | bytes 393248 | tf_op jit(solution)/shard_map/ppermute | solution.py:23
  31.4 5.5 %collective-permute-done.5.two = bf16[32,6144]{1,0:T(8,128)(2,1)S(1)} collective-permute-done((bf16[32,6144]{1,0:T(8,128)(2,1)S(1)}, bf16[32,6144]{1,0:T(8,128)(2,1)S(1)}, u32[]{:S(2)}, u32[]{:S(2)}) %collective-permute-start.5) | collective-permute-done | bytes 393248 | tf_op jit(solution)/shard_map/ppermute | solution.py:23
  38.3 2.0 %collective-permute-start.7 = (bf16[8,6144]{1,0:T(8,128)(2,1)S(1)}, bf16[8,6144]{1,0:T(8,128)(2,1)S(1)}, u32[]{:S(2)}, u32[]{:S(2)}) collective-permute-start(bf16[8,6144]{1,0:T(8,128)(2,1)S(1)} %get-tuple-element.48), channel_id=1, source_target_pairs={{0,4},{1,5},{2,6},{3,7},{4,8},{5,9},{6,10},{7,11},{8,12},{9,13},{1... | collective-permute-start | bytes 294920 | tf_op jit(solution)/shard_map/ppermute | solution.py:23
  40.3 3.6 %collective-permute-start.8 = (bf16[8,6144]{1,0:T(8,128)(2,1)S(1)}, bf16[8,6144]{1,0:T(8,128)(2,1)S(1)}, u32[]{:S(2)}, u32[]{:S(2)}) collective-permute-start(bf16[8,6144]{1,0:T(8,128)(2,1)S(1)} %get-tuple-element.49), channel_id=1, source_target_pairs={{0,8},{1,9},{2,10},{3,11},{4,12},{5,13},{6,14},{7,15},{8,0},{9,1},... | collective-permute-start | bytes 294920 | tf_op jit(solution)/shard_map/ppermute | solution.py:23
  45.8 1.7 %collective-permute-done.8.two = bf16[8,6144]{1,0:T(8,128)(2,1)S(1)} collective-permute-done((bf16[8,6144]{1,0:T(8,128)(2,1)S(1)}, bf16[8,6144]{1,0:T(8,128)(2,1)S(1)}, u32[]{:S(2)}, u32[]{:S(2)}) %collective-permute-start.8) | collective-permute-done | bytes 98336 | tf_op jit(solution)/shard_map/ppermute | solution.py:23
  51.7 2.2 %collective-permute-done.10.b = bf16[8,6144]{1,0:T(8,128)(2,1)S(1)} collective-permute-done((bf16[8,6144]{1,0:T(8,128)(2,1)S(1)}, bf16[8,6144]{1,0:T(8,128)(2,1)S(1)}, u32[]{:S(2)}, u32[]{:S(2)}) %collective-permute-start.10) | collective-permute-done | bytes 98336 | tf_op jit(solution)/shard_map/ppermute | solution.py:23
  53.9 2.1 %collective-permute-done.11.c = bf16[8,6144]{1,0:T(8,128)(2,1)S(1)} collective-permute-done((bf16[8,6144]{1,0:T(8,128)(2,1)S(1)}, bf16[8,6144]{1,0:T(8,128)(2,1)S(1)}, u32[]{:S(2)}, u32[]{:S(2)}) %collective-permute-start.11) | collective-permute-done | bytes 98336 | tf_op jit(solution)/shard_map/ppermute | solution.py:23
  57.6 2.4 %collective-permute-start.13 = (bf16[32,6144]{1,0:T(8,128)(2,1)S(1)}, bf16[32,6144]{1,0:T(8,128)(2,1)S(1)}, u32[]{:S(2)}, u32[]{:S(2)}) collective-permute-start(bf16[32,6144]{1,0:T(8,128)(2,1)S(1)} %stack_x.1.a), channel_id=1, source_target_pairs={{0,3},{1,0},{2,1},{3,2},{4,7},{5,4},{6,5},{7,6},{8,11},{9,8},{10,9... | collective-permute-start | bytes 1179656 | tf_op jit(solution)/shard_map/ppermute | solution.py:23
  62.3 4.6 %load.1 = bf16[6144,1024]{1,0:T(8,128)(2,1)S(1)} custom-call(bf16[6144,1024]{1,0:T(8,128)(2,1)} %source), custom_call_target="tpu_custom_call" | custom-call | bytes 25165824 | tf_op jit(solution)/shard_map/load/pallas_call | solution.py:437
  66.9 2.7 %collective-permute-done.13.b = bf16[32,6144]{1,0:T(8,128)(2,1)S(1)} collective-permute-done((bf16[32,6144]{1,0:T(8,128)(2,1)S(1)}, bf16[32,6144]{1,0:T(8,128)(2,1)S(1)}, u32[]{:S(2)}, u32[]{:S(2)}) %collective-permute-start.13) | collective-permute-done | bytes 393248 | tf_op jit(solution)/shard_map/ppermute | solution.py:23
  69.5 3.9 %collective-permute-done.15.d = bf16[32,6144]{1,0:T(8,128)(2,1)S(1)} collective-permute-done((bf16[32,6144]{1,0:T(8,128)(2,1)S(1)}, bf16[32,6144]{1,0:T(8,128)(2,1)S(1)}, u32[]{:S(2)}, u32[]{:S(2)}) %collective-permute-start.15) | collective-permute-done | bytes 393248 | tf_op jit(solution)/shard_map/ppermute | solution.py:23
  75.0 2.7 %collective-permute-start.20 = (bf16[64,6144]{1,0:T(8,128)(2,1)S(1)}, bf16[64,6144]{1,0:T(8,128)(2,1)S(1)}, u32[]{:S(2)}, u32[]{:S(2)}) collective-permute-start(bf16[64,6144]{1,0:T(8,128)(2,1)S(1)} %get-tuple-element.54), channel_id=1, source_target_pairs={{0,12},{1,13},{2,14},{3,15},{4,0},{5,1},{6,2},{7,3},{8,4},{9,5},{1... | collective-permute-start | bytes 2359304 | tf_op jit(solution)/shard_map/ppermute | solution.py:23
  77.7 1.8 %fusion.24.mine = f32[128,1024]{1,0:T(8,128)S(1)} fusion(bf16[128,6144]{1,0:T(8,128)(2,1)S(1)} %stack_p.1.rows_mine, bf16[6144,1024]{1,0:T(8,128)(2,1)S(1)} %load.1), kind=kOutput, calls=%fused_computation.39 | convolution fusion | flops 1610612736 | bytes 14680064 | tf_op jit(solution)/shard_map/dot_general | solution.py:455
  81.6 6.1 %collective-permute-done.19 = bf16[64,6144]{1,0:T(8,128)(2,1)S(1)} collective-permute-done((bf16[64,6144]{1,0:T(8,128)(2,1)S(1)}, bf16[64,6144]{1,0:T(8,128)(2,1)S(1)}, u32[]{:S(2)}, u32[]{:S(2)}) %collective-permute-start.19) | collective-permute-done | bytes 786464 | tf_op jit(solution)/shard_map/ppermute | solution.py:23
  88.3 1.8 %fusion.26.mine = f32[128,1024]{1,0:T(8,128)S(1)} fusion(bf16[128,6144]{1,0:T(8,128)(2,1)S(1)} %constant_dynamic-update-slice_fusion.rows_mine, bf16[6144,1024]{1,0:T(8,128)(2,1)S(1)} %load.1), kind=kOutput, calls=%fused_computation.41 | convolution fusion | flops 1610612736 | bytes 14680064 | tf_op jit(solution)/shard_map/dot_general | solution.py:460
  90.1 3.0 %collective-permute-start.23 = (bf16[64,6144]{1,0:T(8,128)(2,1)S(1)}, bf16[64,6144]{1,0:T(8,128)(2,1)S(1)}, u32[]{:S(2)}, u32[]{:S(2)}) collective-permute-start(bf16[64,6144]{1,0:T(8,128)(2,1)S(1)} %collective-permute-done.20), channel_id=1, source_target_pairs={{0,12},{1,13},{2,14},{3,15},{4,0},{5,1},{6,2},{7,3},{8,4},{9,5},{1... | collective-permute-start | bytes 2359304 | tf_op jit(solution)/shard_map/ppermute | solution.py:23
  93.0 1.8 %fusion.25.theirs = f32[128,1024]{1,0:T(8,128)S(1)} fusion(bf16[128,6144]{1,0:T(8,128)(2,1)S(1)} %collective-permute-done.18.rows_theirs, bf16[6144,1024]{1,0:T(8,128)(2,1)S(1)} %load.1), kind=kOutput, calls=%fused_computation.40 | convolution fusion | flops 1610612736 | bytes 14680064 | tf_op jit(solution)/shard_map/dot_general | solution.py:460
  96.0 1.8 %fusion.27.theirs = f32[128,1024]{1,0:T(8,128)S(1)} fusion(bf16[128,6144]{1,0:T(8,128)(2,1)S(1)} %collective-permute-done.21.rows_theirs, bf16[6144,1024]{1,0:T(8,128)(2,1)S(1)} %load.1), kind=kOutput, calls=%fused_computation.42 | convolution fusion | flops 1610612736 | bytes 14680064 | tf_op jit(solution)/shard_map/dot_general | solution.py:460
  99.4 1.8 %fusion.28.mine = f32[128,1024]{1,0:T(8,128)S(1)} fusion(bf16[128,6144]{1,0:T(8,128)(2,1)S(1)} %constant_dynamic-update-slice_fusion.2.rows_mine, bf16[6144,1024]{1,0:T(8,128)(2,1)S(1)} %load.1), kind=kOutput, calls=%fused_computation.43 | convolution fusion | flops 1610612736 | bytes 14680064 | tf_op jit(solution)/shard_map/dot_general | solution.py:460
  101.2 3.3 %collective-permute-done.22 = bf16[64,6144]{1,0:T(8,128)(2,1)S(1)} collective-permute-done((bf16[64,6144]{1,0:T(8,128)(2,1)S(1)}, bf16[64,6144]{1,0:T(8,128)(2,1)S(1)}, u32[]{:S(2)}, u32[]{:S(2)}) %collective-permute-start.22) | collective-permute-done | bytes 786464 | tf_op jit(solution)/shard_map/ppermute | solution.py:23
  104.7 1.8 %fusion.30.mine = f32[128,1024]{1,0:T(8,128)S(1)} fusion(bf16[128,6144]{1,0:T(8,128)(2,1)S(1)} %constant_dynamic-update-slice_fusion.4.rows_mine, bf16[6144,1024]{1,0:T(8,128)(2,1)S(1)} %load.1), kind=kOutput, calls=%fused_computation.45 | convolution fusion | flops 1610612736 | bytes 14680064 | tf_op jit(solution)/shard_map/dot_general | solution.py:460
  106.5 1.8 %fusion.29.theirs = f32[128,1024]{1,0:T(8,128)S(1)} fusion(bf16[128,6144]{1,0:T(8,128)(2,1)S(1)} %collective-permute-done.24.rows_theirs, bf16[6144,1024]{1,0:T(8,128)(2,1)S(1)} %load.1), kind=kOutput, calls=%fused_computation.44 | convolution fusion | flops 1610612736 | bytes 14680064 | tf_op jit(solution)/shard_map/dot_general | solution.py:460
  108.3 1.8 %fusion.31.theirs = f32[128,1024]{1,0:T(8,128)S(1)} fusion(bf16[128,6144]{1,0:T(8,128)(2,1)S(1)} %collective-permute-done.25.rows_theirs, bf16[6144,1024]{1,0:T(8,128)(2,1)S(1)} %load.1), kind=kOutput, calls=%fused_computation.46 | convolution fusion | flops 1610612736 | bytes 14680064 | tf_op jit(solution)/shard_map/dot_general | solution.py:460
  113.2 8.2 %all_to_all.10.found = f32[8,8,128]{2,1,0:T(8,128)S(1)} all-to-all(f32[8,8,128]{2,1,0:T(8,128)S(1)} %place.1), channel_id=1, replica_groups=mesh['x'=4,'core'=2,'z'=4,'y'=4] {'x','core'}, dimensions={0} | all-to-all | bytes 65536 | tf_op jit(solution)/shard_map/all_to_all | solution.py:496
  121.9 12.9 %all_to_all.11.found = f32[16,8,128]{2,1,0:T(8,128)S(1)} all-to-all(f32[16,8,128]{2,1,0:T(8,128)S(1)} %block.1), channel_id=1, replica_groups=mesh['x'=4,'core'=2,'z'=4,'y'=4] {'z','y'}, dimensions={0} | all-to-all | bytes 131072 | tf_op jit(solution)/shard_map/all_to_all | solution.py:498
  (85 shorter events, 32.0 us)
Async XLA Ops:
  0.0 0.7 copy-start
  5.5 1.4 %collective-permute-start = (f32[2,136,128]{2,1,0:T(8,128)S(1)}, f32[2,136,128]{2,1,0:T(8,128)S(1)}, u32[]{:S(2)}, u32[]{:S(2)}) collective-permute-start(f32[2,136,128]{2,1,0:T(8,128)S(1)} %pad_maximum_fusion.mine), channel_id=1, source_target_pairs={{0,16},{1,17},{2,18},{3,19},{4,20},{5,21},{6,22},{7,23},{8,24},{9,... | collective-permute-start | bytes 417800 | tf_op jit(solution)/shard_map/ppermute | solution.py:23
  7.5 10.1 %copy-start.2 = (f32[2,128,128]{2,1,0:T(8,128)S(1)}, f32[2,128,128]{2,1,0:T(8,128)}, u32[]{:S(2)}) copy-start(f32[2,128,128]{2,1,0:T(8,128)} %carried.1) | copy-start | bytes 393220
  7.5 7.7 %collective-permute-start.1 = (bf16[2,144,128]{2,1,0:T(8,128)(2,1)S(1)}, bf16[2,144,128]{2,1,0:T(8,128)(2,1)S(1)}, u32[]{:S(2)}, u32[]{:S(2)}) collective-permute-start(bf16[2,144,128]{2,1,0:T(8,128)(2,1)S(1)} %combine.1), channel_id=1, source_target_pairs={{0,96},{1,97},{2,98},{3,99},{4,100},{5,101},{6,102},{7,103},{8,104... | collective-permute-start | bytes 221192 | tf_op jit(solution)/shard_map/ppermute | solution.py:23
  10.4 6.4 %collective-permute-start.2 = (bf16[2,144,128]{2,1,0:T(8,128)(2,1)S(1)}, bf16[2,144,128]{2,1,0:T(8,128)(2,1)S(1)}, u32[]{:S(2)}, u32[]{:S(2)}) collective-permute-start(bf16[2,144,128]{2,1,0:T(8,128)(2,1)S(1)} %combine.1), channel_id=1, source_target_pairs={{0,64},{1,65},{2,66},{3,67},{4,68},{5,69},{6,70},{7,71},{8,72},{9,... | collective-permute-start | bytes 221192 | tf_op jit(solution)/shard_map/ppermute | solution.py:23
  11.2 6.3 %collective-permute-start.3 = (bf16[2,144,128]{2,1,0:T(8,128)(2,1)S(1)}, bf16[2,144,128]{2,1,0:T(8,128)(2,1)S(1)}, u32[]{:S(2)}, u32[]{:S(2)}) collective-permute-start(bf16[2,144,128]{2,1,0:T(8,128)(2,1)S(1)} %combine.1), channel_id=1, source_target_pairs={{0,32},{1,33},{2,34},{3,35},{4,36},{5,37},{6,38},{7,39},{8,40},{9,... | collective-permute-start | bytes 221192 | tf_op jit(solution)/shard_map/ppermute | solution.py:23
  22.3 23.5 %copy-start.3 = (bf16[6144]{0:T(1024)(128)(2,1)S(1)}, bf16[6144]{0:T(1024)(128)(2,1)}, u32[]{:S(2)}) copy-start(bf16[6144]{0:T(1024)(128)(2,1)} %param.17) | copy-start | bytes 36868
  22.3 9.1 %collective-permute-start.4 = (bf16[32,6144]{1,0:T(8,128)(2,1)S(1)}, bf16[32,6144]{1,0:T(8,128)(2,1)S(1)}, u32[]{:S(2)}, u32[]{:S(2)}) collective-permute-start(bf16[32,6144]{1,0:T(8,128)(2,1)S(1)} %get-tuple-element.43), channel_id=1, source_target_pairs={{0,1},{1,2},{2,3},{3,0},{4,5},{5,6},{6,7},{7,4},{8,9},{9,10},{10,1... | collective-permute-start | bytes 1179656 | tf_op jit(solution)/shard_map/ppermute | solution.py:23
  24.0 12.9 %collective-permute-start.5 = (bf16[32,6144]{1,0:T(8,128)(2,1)S(1)}, bf16[32,6144]{1,0:T(8,128)(2,1)S(1)}, u32[]{:S(2)}, u32[]{:S(2)}) collective-permute-start(bf16[32,6144]{1,0:T(8,128)(2,1)S(1)} %get-tuple-element.44), channel_id=1, source_target_pairs={{0,2},{1,3},{2,0},{3,1},{4,6},{5,7},{6,4},{7,5},{8,10},{9,11},{10,... | collective-permute-start | bytes 1179656 | tf_op jit(solution)/shard_map/ppermute | solution.py:23
  26.9 10.0 %collective-permute-start.6 = (bf16[32,6144]{1,0:T(8,128)(2,1)S(1)}, bf16[32,6144]{1,0:T(8,128)(2,1)S(1)}, u32[]{:S(2)}, u32[]{:S(2)}) collective-permute-start(bf16[32,6144]{1,0:T(8,128)(2,1)S(1)} %get-tuple-element.45), channel_id=1, source_target_pairs={{0,3},{1,0},{2,1},{3,2},{4,7},{5,4},{6,5},{7,6},{8,11},{9,8},{10,9... | collective-permute-start | bytes 1179656 | tf_op jit(solution)/shard_map/ppermute | solution.py:23
  36.9 25.1 %copy-start.4 = (s32[1024]{0:T(1024)S(1)}, s32[1024]{0:T(1024)}, u32[]{:S(2)}) copy-start(s32[1024]{0:T(1024)} %param.19) | copy-start | bytes 12292
  38.3 7.5 %collective-permute-start.7 = (bf16[8,6144]{1,0:T(8,128)(2,1)S(1)}, bf16[8,6144]{1,0:T(8,128)(2,1)S(1)}, u32[]{:S(2)}, u32[]{:S(2)}) collective-permute-start(bf16[8,6144]{1,0:T(8,128)(2,1)S(1)} %get-tuple-element.48), channel_id=1, source_target_pairs={{0,4},{1,5},{2,6},{3,7},{4,8},{5,9},{6,10},{7,11},{8,12},{9,13},{1... | collective-permute-start | bytes 294920 | tf_op jit(solution)/shard_map/ppermute | solution.py:23
  40.3 7.2 %collective-permute-start.8 = (bf16[8,6144]{1,0:T(8,128)(2,1)S(1)}, bf16[8,6144]{1,0:T(8,128)(2,1)S(1)}, u32[]{:S(2)}, u32[]{:S(2)}) collective-permute-start(bf16[8,6144]{1,0:T(8,128)(2,1)S(1)} %get-tuple-element.49), channel_id=1, source_target_pairs={{0,8},{1,9},{2,10},{3,11},{4,12},{5,13},{6,14},{7,15},{8,0},{9,1},... | collective-permute-start | bytes 294920 | tf_op jit(solution)/shard_map/ppermute | solution.py:23
  43.9 4.6 %collective-permute-start.9 = (bf16[8,6144]{1,0:T(8,128)(2,1)S(1)}, bf16[8,6144]{1,0:T(8,128)(2,1)S(1)}, u32[]{:S(2)}, u32[]{:S(2)}) collective-permute-start(bf16[8,6144]{1,0:T(8,128)(2,1)S(1)} %get-tuple-element.50), channel_id=1, source_target_pairs={{0,12},{1,13},{2,14},{3,15},{4,0},{5,1},{6,2},{7,3},{8,4},{9,5},{1... | collective-permute-start | bytes 294920 | tf_op jit(solution)/shard_map/ppermute | solution.py:23
  49.2 4.7 %collective-permute-start.10 = (bf16[8,6144]{1,0:T(8,128)(2,1)S(1)}, bf16[8,6144]{1,0:T(8,128)(2,1)S(1)}, u32[]{:S(2)}, u32[]{:S(2)}) collective-permute-start(bf16[8,6144]{1,0:T(8,128)(2,1)S(1)} %norm.1.a), channel_id=1, source_target_pairs={{0,96},{1,97},{2,98},{3,99},{4,100},{5,101},{6,102},{7,103},{8,104... | collective-permute-start | bytes 294920 | tf_op jit(solution)/shard_map/ppermute | solution.py:23
  49.9 6.1 %collective-permute-start.11 = (bf16[8,6144]{1,0:T(8,128)(2,1)S(1)}, bf16[8,6144]{1,0:T(8,128)(2,1)S(1)}, u32[]{:S(2)}, u32[]{:S(2)}) collective-permute-start(bf16[8,6144]{1,0:T(8,128)(2,1)S(1)} %norm.1.a), channel_id=1, source_target_pairs={{0,64},{1,65},{2,66},{3,67},{4,68},{5,69},{6,70},{7,71},{8,72},{9,... | collective-permute-start | bytes 294920 | tf_op jit(solution)/shard_map/ppermute | solution.py:23
  50.9 6.1 %collective-permute-start.12 = (bf16[8,6144]{1,0:T(8,128)(2,1)S(1)}, bf16[8,6144]{1,0:T(8,128)(2,1)S(1)}, u32[]{:S(2)}, u32[]{:S(2)}) collective-permute-start(bf16[8,6144]{1,0:T(8,128)(2,1)S(1)} %norm.1.a), channel_id=1, source_target_pairs={{0,32},{1,33},{2,34},{3,35},{4,36},{5,37},{6,38},{7,39},{8,40},{9,... | collective-permute-start | bytes 294920 | tf_op jit(solution)/shard_map/ppermute | solution.py:23
  57.6 11.9 %collective-permute-start.13 = (bf16[32,6144]{1,0:T(8,128)(2,1)S(1)}, bf16[32,6144]{1,0:T(8,128)(2,1)S(1)}, u32[]{:S(2)}, u32[]{:S(2)}) collective-permute-start(bf16[32,6144]{1,0:T(8,128)(2,1)S(1)} %stack_x.1.a), channel_id=1, source_target_pairs={{0,3},{1,0},{2,1},{3,2},{4,7},{5,4},{6,5},{7,6},{8,11},{9,8},{10,9... | collective-permute-start | bytes 1179656 | tf_op jit(solution)/shard_map/ppermute | solution.py:23
  60.0 9.5 %collective-permute-start.14 = (bf16[32,6144]{1,0:T(8,128)(2,1)S(1)}, bf16[32,6144]{1,0:T(8,128)(2,1)S(1)}, u32[]{:S(2)}, u32[]{:S(2)}) collective-permute-start(bf16[32,6144]{1,0:T(8,128)(2,1)S(1)} %stack_x.1.a), channel_id=1, source_target_pairs={{0,2},{1,3},{2,0},{3,1},{4,6},{5,7},{6,4},{7,5},{8,10},{9,11},{10,... | collective-permute-start | bytes 1179656 | tf_op jit(solution)/shard_map/ppermute | solution.py:23
  61.4 12.1 %collective-permute-start.15 = (bf16[32,6144]{1,0:T(8,128)(2,1)S(1)}, bf16[32,6144]{1,0:T(8,128)(2,1)S(1)}, u32[]{:S(2)}, u32[]{:S(2)}) collective-permute-start(bf16[32,6144]{1,0:T(8,128)(2,1)S(1)} %stack_x.1.a), channel_id=1, source_target_pairs={{0,1},{1,2},{2,3},{3,0},{4,5},{5,6},{6,7},{7,4},{8,9},{9,10},{10,1... | collective-permute-start | bytes 1179656 | tf_op jit(solution)/shard_map/ppermute | solution.py:23
  74.3 15.8 %collective-permute-start.18 = (bf16[128,6144]{1,0:T(8,128)(2,1)S(1)}, bf16[128,6144]{1,0:T(8,128)(2,1)S(1)}, u32[]{:S(2)}, u32[]{:S(2)}) collective-permute-start(bf16[128,6144]{1,0:T(8,128)(2,1)S(1)} %stack_p.1.rows_mine), channel_id=1, source_target_pairs={{0,16},{1,17},{2,18},{3,19},{4,20},{5,21},{6,22},{7,23},{8,24},{9,... | collective-permute-start | bytes 4718600 | tf_op jit(solution)/shard_map/ppermute | solution.py:23
  74.4 13.3 %collective-permute-start.19 = (bf16[64,6144]{1,0:T(8,128)(2,1)S(1)}, bf16[64,6144]{1,0:T(8,128)(2,1)S(1)}, u32[]{:S(2)}, u32[]{:S(2)}) collective-permute-start(bf16[64,6144]{1,0:T(8,128)(2,1)S(1)} %get-tuple-element.53), channel_id=1, source_target_pairs={{0,4},{1,5},{2,6},{3,7},{4,8},{5,9},{6,10},{7,11},{8,12},{9,13},{1... | collective-permute-start | bytes 2359304 | tf_op jit(solution)/shard_map/ppermute | solution.py:23
  75.0 12.7 %collective-permute-start.20 = (bf16[64,6144]{1,0:T(8,128)(2,1)S(1)}, bf16[64,6144]{1,0:T(8,128)(2,1)S(1)}, u32[]{:S(2)}, u32[]{:S(2)}) collective-permute-start(bf16[64,6144]{1,0:T(8,128)(2,1)S(1)} %get-tuple-element.54), channel_id=1, source_target_pairs={{0,12},{1,13},{2,14},{3,15},{4,0},{5,1},{6,2},{7,3},{8,4},{9,5},{1... | collective-permute-start | bytes 2359304 | tf_op jit(solution)/shard_map/ppermute | solution.py:23
  79.5 19.5 %collective-permute-start.16 = (bf16[64,6144]{1,0:T(8,128)(2,1)S(1)}, bf16[64,6144]{1,0:T(8,128)(2,1)S(1)}, u32[]{:S(2)}, u32[]{:S(2)}) collective-permute-start(bf16[64,6144]{1,0:T(8,128)(2,1)S(1)} %get-tuple-element.53), channel_id=1, source_target_pairs={{0,12},{1,13},{2,14},{3,15},{4,0},{5,1},{6,2},{7,3},{8,4},{9,5},{1... | collective-permute-start | bytes 2359304 | tf_op jit(solution)/shard_map/ppermute | solution.py:23
  80.6 18.4 %collective-permute-start.17 = (bf16[64,6144]{1,0:T(8,128)(2,1)S(1)}, bf16[64,6144]{1,0:T(8,128)(2,1)S(1)}, u32[]{:S(2)}, u32[]{:S(2)}) collective-permute-start(bf16[64,6144]{1,0:T(8,128)(2,1)S(1)} %get-tuple-element.54), channel_id=1, source_target_pairs={{0,4},{1,5},{2,6},{3,7},{4,8},{5,9},{6,10},{7,11},{8,12},{9,13},{1... | collective-permute-start | bytes 2359304 | tf_op jit(solution)/shard_map/ppermute | solution.py:23
  87.8 8.2 %collective-permute-start.21 = (bf16[128,6144]{1,0:T(8,128)(2,1)S(1)}, bf16[128,6144]{1,0:T(8,128)(2,1)S(1)}, u32[]{:S(2)}, u32[]{:S(2)}) collective-permute-start(bf16[128,6144]{1,0:T(8,128)(2,1)S(1)} %constant_dynamic-update-slice_fusion.rows_mine), channel_id=1, source_target_pairs={{0,16},{1,17},{2,18},{3,19},{4,20},{5,21},{6,22},{7,23},{8,24},{9,... | collective-permute-start | bytes 4718600 | tf_op jit(solution)/shard_map/ppermute | solution.py:23
  87.9 16.6 %collective-permute-start.22 = (bf16[64,6144]{1,0:T(8,128)(2,1)S(1)}, bf16[64,6144]{1,0:T(8,128)(2,1)S(1)}, u32[]{:S(2)}, u32[]{:S(2)}) collective-permute-start(bf16[64,6144]{1,0:T(8,128)(2,1)S(1)} %collective-permute-done.19), channel_id=1, source_target_pairs={{0,4},{1,5},{2,6},{3,7},{4,8},{5,9},{6,10},{7,11},{8,12},{9,13},{1... | collective-permute-start | bytes 2359304 | tf_op jit(solution)/shard_map/ppermute | solution.py:23
  90.1 14.4 %collective-permute-start.23 = (bf16[64,6144]{1,0:T(8,128)(2,1)S(1)}, bf16[64,6144]{1,0:T(8,128)(2,1)S(1)}, u32[]{:S(2)}, u32[]{:S(2)}) collective-permute-start(bf16[64,6144]{1,0:T(8,128)(2,1)S(1)} %collective-permute-done.20), channel_id=1, source_target_pairs={{0,12},{1,13},{2,14},{3,15},{4,0},{5,1},{6,2},{7,3},{8,4},{9,5},{1... | collective-permute-start | bytes 2359304 | tf_op jit(solution)/shard_map/ppermute | solution.py:23
  99.1 7.4 %collective-permute-start.24 = (bf16[128,6144]{1,0:T(8,128)(2,1)S(1)}, bf16[128,6144]{1,0:T(8,128)(2,1)S(1)}, u32[]{:S(2)}, u32[]{:S(2)}) collective-permute-start(bf16[128,6144]{1,0:T(8,128)(2,1)S(1)} %constant_dynamic-update-slice_fusion.2.rows_mine), channel_id=1, source_target_pairs={{0,16},{1,17},{2,18},{3,19},{4,20},{5,21},{6,22},{7,23},{8,24},{9,... | collective-permute-start | bytes 4718600 | tf_op jit(solution)/shard_map/ppermute | solution.py:23
  104.6 3.7 %collective-permute-start.25 = (bf16[128,6144]{1,0:T(8,128)(2,1)S(1)}, bf16[128,6144]{1,0:T(8,128)(2,1)S(1)}, u32[]{:S(2)}, u32[]{:S(2)}) collective-permute-start(bf16[128,6144]{1,0:T(8,128)(2,1)S(1)} %constant_dynamic-update-slice_fusion.4.rows_mine), channel_id=1, source_target_pairs={{0,16},{1,17},{2,18},{3,19},{4,20},{5,21},{6,22},{7,23},{8,24},{9,... | collective-permute-start | bytes 4718600 | tf_op jit(solution)/shard_map/ppermute | solution.py:23
  110.1 25.8 %copy-start.1 = (f32[128,2]{0,1:T(2,128)S(1)}, f32[128,2]{0,1:T(2,128)}, u32[]{:S(2)}) copy-start(f32[128,2]{0,1:T(2,128)} %param.11) | copy-start | bytes 3076
